TPU v7x, 32 devices: a whole 2x2x4 slice. The times are simulated.
32 devices in a mesh: sx: 8 (over z, y), sy: 4 (over x, core).
Axes of the slice: x: 2, y: 2, z: 4, core: 2. Of those that a mesh axis runs over, the one named last changes fastest.
Arguments:
- obs_values: bfloat16 [8192, 64], P(('sx', 'sy')), may hold values from -6 to 6
- obs_dest: int32 [8192, 1], P(('sx', 'sy')), may hold values from 0 to 31; in each aligned block of 256 rows (0 to 255, 256 to 511, ...) at most 16 rows name the same one
- obs_node: int32 [8192], P(('sx', 'sy')), may hold values from 0 to 2047
- schur: bfloat16 [8, 4, 2048, 2048], P('sx', 'sy'), as said below
- local_inverse: bfloat16 [8, 4, 2048, 2048], P('sx', 'sy'), as said below
- coarse_inverse: float32 [256, 256], P(('sx', 'sy')), as said below
Outputs:
- solution_field: float32 [8, 4, 64, 2048], P('sx', 'sy')
- residual: float32 [8, 4, 64, 2048], P('sx', 'sy')
Inputs may be any that keep to these rules, and one draw needn't show every extreme that they name: `obs_dest`: at most 16 observations of one device go to one subdomain. `schur`: symmetric positive definite. `local_inverse`: symmetric positive definite. `coarse_inverse`: symmetric positive definite.
All inputs are finite; a program needn't handle non-finite values.
Results may differ from a plain program's by a relative error of at most 0.04.
Values may be sent and summed in bfloat16 or wider, within the bound.
No kernel may reach another device: no remote copies, remote signals or barrier semaphores. Data moves between devices by JAX's collectives and lax.ppermute only.
A program may use at most 128 MiB of HBM per device.

v0:
```python
import jax
import jax.numpy as jnp
from jax import lax
from jax.sharding import PartitionSpec as P

ITERS = 6


def shortened(array):

    def short(part):
        return part.astype(jnp.bfloat16) if part.dtype == jnp.float32 else part

    return jax.tree.map(short, array)


def padded_2(cells, sides, width):
    for axis, dim in sides:
        count = lax.axis_size(axis)
        ends = count - 1
        head = lax.slice_in_dim(cells, 0, width, axis=dim)
        tail = lax.slice_in_dim(cells, cells.shape[dim] - width, cells.shape[dim], axis=dim)
        cells = jnp.concatenate(
            [
                lax.ppermute(tail, axis, [(i, (i + 1) % count) for i in range(ends)]),
                cells,
                lax.ppermute(head, axis, [((i + 1) % count, i) for i in range(ends)]),
            ],
            axis=dim,
        )
    return cells


def edge_weights(size):
    edge_len = size // 4
    col_index = lax.axis_index("sx")
    row_index = lax.axis_index("sy")
    col_count = lax.axis_size("sx")
    row_count = lax.axis_size("sy")
    sides = (
        jnp.where(col_index > 0, 0.5, 1.0),
        jnp.where(col_index < col_count - 1, 0.5, 1.0),
        jnp.where(row_index > 0, 0.5, 1.0),
        jnp.where(row_index < row_count - 1, 0.5, 1.0),
    )
    return jnp.concatenate([jnp.full((edge_len,), value, jnp.float32) for value in sides])


def coarse_basis(size, count):
    edge_len = size // 4
    node = jnp.arange(size)
    side = node // edge_len
    offset = (node % edge_len).astype(jnp.float32) - (edge_len - 1) / 2.0
    norm_ramp = jnp.sqrt(jnp.float32(edge_len * (edge_len * edge_len - 1) / 12.0))
    column = jnp.arange(count)
    on_edge = side[:, None] == (column // 2)[None, :]
    value = jnp.where(
        (column % 2 == 0)[None, :],
        1.0 / jnp.sqrt(jnp.float32(edge_len)),
        offset[:, None] / norm_ramp,
    )
    return jnp.where(on_edge, value, 0.0)


def assemble(local):
    edge_len = local.shape[1] // 4
    west_part = local[:, 0:edge_len]
    east_part = local[:, edge_len : 2 * edge_len]
    south_part = local[:, 2 * edge_len : 3 * edge_len]
    north_part = local[:, 3 * edge_len :]
    padded = padded_2(shortened(local[None, None]), (("sx", 0), ("sy", 1)), 1)
    west = west_part + padded[0, 1, :, edge_len : 2 * edge_len]
    east = east_part + padded[2, 1, :, 0:edge_len]
    south = south_part + padded[1, 0, :, 3 * edge_len :]
    north = north_part + padded[1, 2, :, 2 * edge_len : 3 * edge_len]
    return jnp.concatenate([west, east, south, north], axis=1)


def gather_coarse(coarse_local):
    return lax.all_gather(coarse_local, ("sx", "sy"), axis=0, tiled=True)


def body(obs_values, obs_dest, obs_node, schur, local_inverse, coarse_inverse):
    hp = lax.Precision.HIGHEST
    size = schur.shape[-1]
    count = coarse_inverse.shape[0]
    realiz = obs_values.shape[1]
    obs_count = obs_values.shape[0]
    row_count = lax.axis_size("sy")
    dev_count = lax.axis_size("sx") * row_count
    target = obs_dest[:, 0]
    capacity = max(2, 2 * obs_count // dev_count)
    match_table = (target[:, None] == jnp.arange(dev_count)[None, :]).astype(jnp.int32)
    slot_index = jnp.sum(jnp.cumsum(match_table, axis=0) * match_table, axis=1) - 1
    position = target * capacity + slot_index
    send_values = (
        jnp.zeros((dev_count * capacity, realiz), jnp.bfloat16).at[position].set(obs_values)
    )
    send_nodes = jnp.zeros((dev_count * capacity,), jnp.int32).at[position].set(obs_node)
    got_values, got_nodes = (
        lax.all_to_all(
            send_values.reshape(dev_count, capacity, realiz),
            ("sx", "sy"),
            split_axis=0,
            concat_axis=0,
            tiled=True,
        ),
        lax.all_to_all(
            send_nodes.reshape(dev_count, capacity),
            ("sx", "sy"),
            split_axis=0,
            concat_axis=0,
            tiled=True,
        ),
    )
    load = jax.ops.segment_sum(
        got_values.reshape(-1, realiz).astype(jnp.float32), got_nodes.reshape(-1), num_segments=size
    )
    rhs = assemble(load.T)
    weight = edge_weights(size)[None, :]
    basis = coarse_basis(size, count)
    schur_mat = schur[0, 0]
    inverse_mat = local_inverse[0, 0]

    def project(vec):
        return jnp.dot(weight * vec, basis, precision=hp).T

    def precond(vec, coarse_all):
        scaled = weight * vec
        part = jnp.dot(scaled.astype(jnp.bfloat16), inverse_mat, preferred_element_type=jnp.float32)
        solved = jnp.dot(coarse_inverse, coarse_all, precision=hp)
        correction = jnp.dot(solved.T, basis.T, precision=hp)
        return assemble(weight * (part + correction))

    def products(left, right):
        return lax.psum(jnp.sum(weight * left * right, axis=1), ("sx", "sy"))

    solution_field = jnp.zeros_like(rhs)
    residual = rhs
    coarse_resid = gather_coarse(project(residual))
    precon = precond(residual, coarse_resid)
    direction = precon
    rz_now = products(residual, precon)
    for step in range(ITERS):
        image = assemble(
            jnp.dot(direction.astype(jnp.bfloat16), schur_mat, preferred_element_type=jnp.float32)
        )
        curv_local = jnp.sum(weight * direction * image, axis=1)
        curv = lax.psum(curv_local, ("sx", "sy"))
        alpha = rz_now / curv
        solution_field = solution_field + alpha[:, None] * direction
        residual = residual - alpha[:, None] * image
        if step < ITERS - 1:
            coarse_resid = gather_coarse(project(residual))
            precon = precond(residual, coarse_resid)
            rz_next = products(residual, precon)
            direction = precon + (rz_next / rz_now)[:, None] * direction
            rz_now = rz_next
    return (solution_field[None, None], residual[None, None])


def solution(mesh):
    placed = (
        P(("sx", "sy"), None),
        P(("sx", "sy"), None),
        P(("sx", "sy")),
        P("sx", "sy", None, None),
        P("sx", "sy", None, None),
        P(("sx", "sy"), None),
    )
    return jax.shard_map(
        body,
        mesh=mesh,
        in_specs=placed,
        out_specs=(P("sx", "sy", None, None), P("sx", "sy", None, None)),
        check_vma=False,
    )
```

profile of v0, /device:TPU:0, one launch (start us, length us, event | category | flops | bytes accessed | tf_op | source)
XLA Modules:
  0.0 1206.0 jit_solution(16191598000364921082)
XLA Ops:
  5.9 7.3 all-to-all-start
  24.1 6.1 all-to-all-done.1
  39.1 5.1 collective-permute-done.1
  58.7 47.3 %all_gather.18 = f32[256,64]{1,0:T(8,128)S(1)} all-gather(f32[8,64]{1,0:T(8,128)S(1)} %fusion.35), channel_id=1, replica_groups=mesh['sx'=8,'sy'=4] {'sx','sy'}, dimensions={0}, use_global_device_ids=true | all-gather | bytes 67584 | tf_op jit(solution)/shard_map/all_gather | solution.py:80
  106.1 5.1 fusion.22
  134.7 5.0 collective-permute-start.8
  146.7 9.9 collective-permute-start.10
  158.8 51.6 %all-reduce = (f32[64]{0:T(128)S(1)}, f32[64]{0:T(128)S(1)}) all-reduce(f32[64]{0:T(128)S(1)} %get-tuple-element.3, f32[64]{0:T(128)S(1)} %get-tuple-element.2), channel_id=1, replica_groups=mesh['sx'=8,'sy'=4] {'sx','sy'}, use_global_device_ids=true, to_apply=%region_7.8 | all-reduce | flops 128 | bytes 1024 | tf_op jit(solution)/shard_map/psum | solution.py:136
  217.9 41.3 %all_gather.19 = f32[256,64]{1,0:T(8,128)S(1)} all-gather(f32[8,64]{1,0:T(8,128)S(1)} %fusion.34), channel_id=1, replica_groups=mesh['sx'=8,'sy'=4] {'sx','sy'}, dimensions={0}, use_global_device_ids=true | all-gather | bytes 67584 | tf_op jit(solution)/shard_map/all_gather | solution.py:80
  280.0 47.9 %psum.86 = f32[64]{0:T(128)S(1)} all-reduce(f32[64]{0:T(128)S(1)} %multiply_reduce_fusion.8), channel_id=1, replica_groups=mesh['sx'=8,'sy'=4] {'sx','sy'}, use_global_device_ids=true, to_apply=%region_11.12 | all-reduce | flops 64 | bytes 512 | tf_op jit(solution)/shard_map/psum | solution.py:136
  344.4 5.8 collective-permute-done.16
  356.7 51.0 %psum.87 = f32[64]{0:T(128)S(1)} all-reduce(f32[64]{0:T(128)S(1)} %multiply_reduce_fusion.7), channel_id=1, replica_groups=mesh['sx'=8,'sy'=4] {'sx','sy'}, use_global_device_ids=true, to_apply=%region_13.14 | all-reduce | flops 64 | bytes 512 | tf_op jit(solution)/shard_map/psum | solution.py:149
  412.0 5.0 fusion.18
  417.0 39.4 %all_gather.20 = f32[256,64]{1,0:T(8,128)S(1)} all-gather(f32[8,64]{1,0:T(8,128)S(1)} %fusion.33), channel_id=1, replica_groups=mesh['sx'=8,'sy'=4] {'sx','sy'}, dimensions={0}, use_global_device_ids=true | all-gather | bytes 67584 | tf_op jit(solution)/shard_map/all_gather | solution.py:80
  478.0 47.9 %psum.88 = f32[64]{0:T(128)S(1)} all-reduce(f32[64]{0:T(128)S(1)} %multiply_reduce_fusion.6), channel_id=1, replica_groups=mesh['sx'=8,'sy'=4] {'sx','sy'}, use_global_device_ids=true, to_apply=%region_15.16 | all-reduce | flops 64 | bytes 512 | tf_op jit(solution)/shard_map/psum | solution.py:136
  542.4 5.8 collective-permute-done.24
  554.7 50.8 %psum.89 = f32[64]{0:T(128)S(1)} all-reduce(f32[64]{0:T(128)S(1)} %multiply_reduce_fusion.5), channel_id=1, replica_groups=mesh['sx'=8,'sy'=4] {'sx','sy'}, use_global_device_ids=true, to_apply=%region_17.18 | all-reduce | flops 64 | bytes 512 | tf_op jit(solution)/shard_map/psum | solution.py:149
  615.4 39.4 %all_gather.21 = f32[256,64]{1,0:T(8,128)S(1)} all-gather(f32[8,64]{1,0:T(8,128)S(1)} %fusion.32), channel_id=1, replica_groups=mesh['sx'=8,'sy'=4] {'sx','sy'}, dimensions={0}, use_global_device_ids=true | all-gather | bytes 67584 | tf_op jit(solution)/shard_map/all_gather | solution.py:80
  675.6 47.9 %psum.90 = f32[64]{0:T(128)S(1)} all-reduce(f32[64]{0:T(128)S(1)} %multiply_reduce_fusion.4), channel_id=1, replica_groups=mesh['sx'=8,'sy'=4] {'sx','sy'}, use_global_device_ids=true, to_apply=%region_19.20 | all-reduce | flops 64 | bytes 512 | tf_op jit(solution)/shard_map/psum | solution.py:136
  740.1 5.8 collective-permute-done.32
  752.5 50.8 %psum.91 = f32[64]{0:T(128)S(1)} all-reduce(f32[64]{0:T(128)S(1)} %multiply_reduce_fusion.3), channel_id=1, replica_groups=mesh['sx'=8,'sy'=4] {'sx','sy'}, use_global_device_ids=true, to_apply=%region_21.22 | all-reduce | flops 64 | bytes 512 | tf_op jit(solution)/shard_map/psum | solution.py:149
  807.5 5.0 fusion.14
  812.5 39.4 %all_gather.22 = f32[256,64]{1,0:T(8,128)S(1)} all-gather(f32[8,64]{1,0:T(8,128)S(1)} %fusion.31), channel_id=1, replica_groups=mesh['sx'=8,'sy'=4] {'sx','sy'}, dimensions={0}, use_global_device_ids=true | all-gather | bytes 67584 | tf_op jit(solution)/shard_map/all_gather | solution.py:80
  873.5 47.9 %psum.92 = f32[64]{0:T(128)S(1)} all-reduce(f32[64]{0:T(128)S(1)} %multiply_reduce_fusion.2), channel_id=1, replica_groups=mesh['sx'=8,'sy'=4] {'sx','sy'}, use_global_device_ids=true, to_apply=%region_23.24 | all-reduce | flops 64 | bytes 512 | tf_op jit(solution)/shard_map/psum | solution.py:136
  938.6 5.8 collective-permute-done.40
  950.9 50.9 %psum.93 = f32[64]{0:T(128)S(1)} all-reduce(f32[64]{0:T(128)S(1)} %multiply_reduce_fusion.1), channel_id=1, replica_groups=mesh['sx'=8,'sy'=4] {'sx','sy'}, use_global_device_ids=true, to_apply=%region_25.26 | all-reduce | flops 64 | bytes 512 | tf_op jit(solution)/shard_map/psum | solution.py:149
  1006.1 5.0 fusion.12
  1011.1 39.4 %all_gather.23 = f32[256,64]{1,0:T(8,128)S(1)} all-gather(f32[8,64]{1,0:T(8,128)S(1)} %fusion.30), channel_id=1, replica_groups=mesh['sx'=8,'sy'=4] {'sx','sy'}, dimensions={0}, use_global_device_ids=true | all-gather | bytes 67584 | tf_op jit(solution)/shard_map/all_gather | solution.py:80
  1071.3 47.9 %psum.94 = f32[64]{0:T(128)S(1)} all-reduce(f32[64]{0:T(128)S(1)} %multiply_reduce_fusion), channel_id=1, replica_groups=mesh['sx'=8,'sy'=4] {'sx','sy'}, use_global_device_ids=true, to_apply=%region_27.28 | all-reduce | flops 64 | bytes 512 | tf_op jit(solution)/shard_map/psum | solution.py:136
  1120.4 5.1 fusion
  1135.2 5.8 collective-permute-done.48
  1148.4 50.6 %psum.95 = f32[64]{0:T(128)S(1)} all-reduce(f32[64]{0:T(128)S(1)} %fusion.48), channel_id=1, replica_groups=mesh['sx'=8,'sy'=4] {'sx','sy'}, use_global_device_ids=true, to_apply=%region_29.30 | all-reduce | flops 64 | bytes 512 | tf_op jit(solution)/shard_map/psum | solution.py:149
  (385 shorter events, 324.3 us)
Async XLA Ops:
  5.9 14.4 %all-to-all-start = ((s32[32,1,16]{2,1,0:T(1,128)}), s32[32,1,16]{2,1,0:T(1,128)S(1)}, u32[]{:S(2)}, u32[]{:S(2)}) async-start(s32[32,1,16]{2,1,0:T(1,128)} %bitcast.5), calls=%async_computation | async-start | bytes 32768 | tf_op jit(solution)/shard_map/all_to_all | solution.py:108
  20.2 10.0 all-to-all-start.1
  33.3 10.9 collective-permute-start.1
  34.6 14.5 %collective-permute-start = (bf16[1,1,64,2048]{3,2,1,0:T(8,128)(2,1)S(1)}, bf16[1,1,64,2048]{3,2,1,0:T(8,128)(2,1)S(1)}, u32[]{:S(2)}, u32[]{:S(2)}) collective-permute-start(bf16[1,1,64,2048]{3,2,1,0:T(8,128)(2,1)S(1)} %convert_bitcast_fusion.12), channel_id=1, source_target_pairs={{0,4},{4,8},{8,12},{12,16},{16,20},{20,24},{24,28},{1,5},{5,9},{9,... | collective-permute-start | bytes 786440 | tf_op jit(solution)/shard_map/ppermute | solution.py:25
  49.1 5.4 collective-permute-start.3
  50.4 5.1 collective-permute-start.2
  113.0 10.4 collective-permute-start.5
  114.3 11.1 collective-permute-start.4
  133.4 8.7 collective-permute-start.9
  134.7 10.7 collective-permute-start.8
  145.4 11.2 collective-permute-start.11
  146.7 11.8 collective-permute-start.10
  261.0 10.4 collective-permute-start.13
  262.3 11.1 collective-permute-start.12
  334.7 9.7 collective-permute-start.17
  336.0 14.2 %collective-permute-start.16 = (bf16[1,1,64,2048]{3,2,1,0:T(8,128)(2,1)S(1)}, bf16[1,1,64,2048]{3,2,1,0:T(8,128)(2,1)S(1)}, u32[]{:S(2)}, u32[]{:S(2)}) collective-permute-start(bf16[1,1,64,2048]{3,2,1,0:T(8,128)(2,1)S(1)} %convert_bitcast_fusion.8), channel_id=1, source_target_pairs={{0,4},{4,8},{8,12},{12,16},{16,20},{20,24},{24,28},{1,5},{5,9},{9,... | collective-permute-start | bytes 786440 | tf_op jit(solution)/shard_map/ppermute | solution.py:25
  458.3 10.4 collective-permute-start.21
  459.6 11.1 collective-permute-start.20
  532.7 9.7 collective-permute-start.25
  534.0 14.2 %collective-permute-start.24 = (bf16[1,1,64,2048]{3,2,1,0:T(8,128)(2,1)S(1)}, bf16[1,1,64,2048]{3,2,1,0:T(8,128)(2,1)S(1)}, u32[]{:S(2)}, u32[]{:S(2)}) collective-permute-start(bf16[1,1,64,2048]{3,2,1,0:T(8,128)(2,1)S(1)} %convert_bitcast_fusion.6), channel_id=1, source_target_pairs={{0,4},{4,8},{8,12},{12,16},{16,20},{20,24},{24,28},{1,5},{5,9},{9,... | collective-permute-start | bytes 786440 | tf_op jit(solution)/shard_map/ppermute | solution.py:25
  656.7 10.4 collective-permute-start.29
  658.0 11.1 collective-permute-start.28
  730.4 9.7 collective-permute-start.33
  731.7 14.2 %collective-permute-start.32 = (bf16[1,1,64,2048]{3,2,1,0:T(8,128)(2,1)S(1)}, bf16[1,1,64,2048]{3,2,1,0:T(8,128)(2,1)S(1)}, u32[]{:S(2)}, u32[]{:S(2)}) collective-permute-start(bf16[1,1,64,2048]{3,2,1,0:T(8,128)(2,1)S(1)} %convert_bitcast_fusion.4), channel_id=1, source_target_pairs={{0,4},{4,8},{8,12},{12,16},{16,20},{20,24},{24,28},{1,5},{5,9},{9,... | collective-permute-start | bytes 786440 | tf_op jit(solution)/shard_map/ppermute | solution.py:25
  853.8 10.4 collective-permute-start.37
  855.1 11.1 collective-permute-start.36
  928.9 9.7 collective-permute-start.41
  930.2 14.2 %collective-permute-start.40 = (bf16[1,1,64,2048]{3,2,1,0:T(8,128)(2,1)S(1)}, bf16[1,1,64,2048]{3,2,1,0:T(8,128)(2,1)S(1)}, u32[]{:S(2)}, u32[]{:S(2)}) collective-permute-start(bf16[1,1,64,2048]{3,2,1,0:T(8,128)(2,1)S(1)} %convert_bitcast_fusion.2), channel_id=1, source_target_pairs={{0,4},{4,8},{8,12},{12,16},{16,20},{20,24},{24,28},{1,5},{5,9},{9,... | collective-permute-start | bytes 786440 | tf_op jit(solution)/shard_map/ppermute | solution.py:25
  1052.3 10.4 collective-permute-start.45
  1053.6 11.1 collective-permute-start.44
  1125.5 9.7 collective-permute-start.49
  1126.8 14.2 %collective-permute-start.48 = (bf16[1,1,64,2048]{3,2,1,0:T(8,128)(2,1)S(1)}, bf16[1,1,64,2048]{3,2,1,0:T(8,128)(2,1)S(1)}, u32[]{:S(2)}, u32[]{:S(2)}) collective-permute-start(bf16[1,1,64,2048]{3,2,1,0:T(8,128)(2,1)S(1)} %convert_bitcast_fusion), channel_id=1, source_target_pairs={{0,4},{4,8},{8,12},{12,16},{16,20},{20,24},{24,28},{1,5},{5,9},{9,... | collective-permute-start | bytes 786440 | tf_op jit(solution)/shard_map/ppermute | solution.py:25
  (103 other events, 3913.9 us)
where the time goes:
time: 1220 us; the launch traced here: 1210 us
  blocking collectives  791 us (65%)
  starting transfers between devices  152 us (12%)
  waiting for transfers between devices  134 us (11%)
  matrix products  83.9 us (7%)
  other arithmetic  27.3 us (2%)
  local copies, waits for them, and re-layouts  13.8 us (1%)
    psum x6, blocking collectives, products(): return lax.psum(jnp.sum(weight * left * right, axis=1), ('sx', 'sy'))  291 us
    psum x5, blocking collectives, body(): curv = lax.psum(curv_local, ('sx', 'sy'))  254 us
    all_gather x6, blocking collectives, gather_coarse(): return lax.all_gather(coarse_local, ('sx', 'sy'), axis=0, tiled=True)  246 us
    ppermute x26, starting transfers between devices, padded_2(): lax.ppermute(tail, axis, [(i, (i + 1) % count) for i in range(ends)])  109 us
    ppermute x26, waiting for transfers between devices, padded_2(): lax.ppermute(tail, axis, [(i, (i + 1) % count) for i in range(ends)])  71.1 us
    ppermute x26, waiting for transfers between devices, padded_2(): lax.ppermute(head, axis, [((i + 1) % count, i) for i in range(ends)])  52.8 us
    ppermute x26, starting transfers between devices, padded_2(): lax.ppermute(head, axis, [((i + 1) % count, i) for i in range(ends)])  33.6 us
    dot_general x6, matrix products, precond(): jnp.dot(scaled.astype(jnp.bfloat16), inverse_mat, preferred_element_type=...  30 us
  transfers between devices with their start and end apart: 54, of which 41 were waited for; matrix products, arithmetic and copies ran while one was open for 0% of the time, Pallas kernels for 0%

commit v1 on v0

v1 whole, which is shorter than its diff:
```python
import functools

import jax
import jax.numpy as jnp
from jax import lax
from jax.experimental import pallas as pl
from jax.experimental.pallas import tpu as pltpu
from jax.sharding import PartitionSpec as P

ITERS = 6
LANES = 128
CHUNK = 256
HP = lax.Precision.HIGHEST
F32 = jnp.float32
BF16 = jnp.bfloat16
VM = pl.BlockSpec(memory_space=pltpu.VMEM)


def call(kernel, outs, args, scratch=(), flops=0):
    size = sum(a.size * a.dtype.itemsize for a in args)
    return pl.pallas_call(
        kernel,
        out_shape=outs,
        in_specs=[VM] * len(args),
        out_specs=jax.tree.map(lambda _: VM, outs),
        scratch_shapes=list(scratch),
        compiler_params=pltpu.CompilerParams(vmem_limit_bytes=8 << 20),
        cost_estimate=pl.CostEstimate(flops=flops, bytes_accessed=size, transcendentals=0),
    )(*args)


def shape(rows, columns, dtype=F32):
    return jax.ShapeDtypeStruct((rows, columns), dtype)


class Place:
    def __init__(self):
        col, row = lax.axis_index("sx"), lax.axis_index("sy")
        cols, rows = lax.axis_size("sx"), lax.axis_size("sy")
        odd_col, odd_row = lax.rem(col, 2), lax.rem(row, 2)
        self.edges = (1 - odd_col, odd_col, 3 - odd_row, 2 + odd_row)
        has = (col > 0, col < cols - 1, row > 0, row < rows - 1)
        self.weights = [jnp.where(there, F32(0.5), F32(1.0)) for there in has]
        far_col = jnp.where(odd_col == 1, col < cols - 1, col > 0)
        far_row = jnp.where(odd_row == 1, row < rows - 1, row > 0)
        self.valid = (None, far_col, None, far_row)


def swaps():
    cols, rows = lax.axis_size("sx"), lax.axis_size("sy")

    def near(count):
        return [(i, i ^ 1) for i in range(count)]

    far_sx = [(0, 0), (cols - 1, cols - 1)]
    for i in range(1, cols - 1, 2):
        far_sx += [(i, i + 1), (i + 1, i)]
    far_sy = []
    for i in range(1, rows, 2):
        far_sy += [(i, (i + 1) % rows), ((i + 1) % rows, i)]
    return (("sx", near(cols)), ("sx", far_sx), ("sy", near(rows)), ("sy", far_sy))


def exchange(edges):
    far_sx, far_sy, near_sx, near_sy = 1, 3, 0, 2
    plan = swaps()
    got = [None] * 4
    for i in (far_sx, far_sy, near_sx, near_sy):
        got[i] = lax.ppermute(edges[i], plan[i][0], plan[i][1])
    return got


def send_edges(value_ref, edge_refs):
    place, edge_len = Place(), value_ref.shape[1] // 4
    for edge, ref in zip(place.edges, edge_refs, strict=True):
        start = pl.multiple_of(edge * edge_len, edge_len)
        ref[...] = value_ref[:, pl.ds(start, edge_len)].astype(BF16)


def add_edges(value_ref, edge_refs):
    place, edge_len = Place(), value_ref.shape[1] // 4
    for edge, valid, ref in zip(place.edges, place.valid, edge_refs, strict=True):
        start = pl.multiple_of(edge * edge_len, edge_len)
        got = ref[...].astype(F32)
        if valid is not None:
            got = jnp.where(valid, got, 0.0)
        value_ref[:, pl.ds(start, edge_len)] += got


def basis_parts(edge_len, start, width):
    node = lax.broadcasted_iota(jnp.int32, (1, width), 1) + start
    offset = node.astype(F32) - (edge_len - 1) / 2.0
    level = 1.0 / jnp.sqrt(F32(edge_len))
    norm = jnp.sqrt(F32(edge_len * (edge_len * edge_len - 1) / 12.0))
    return level, offset / norm


def lane_parts(value):
    return sum(value[:, i : i + LANES] for i in range(LANES, value.shape[1], LANES)) + value[:, :LANES]


def project(value_ref):
    edge_len = value_ref.shape[1] // 4
    columns = []
    for edge in range(4):
        flat = ramped = None
        for start in range(0, edge_len, CHUNK):
            at = edge * edge_len + start
            part = value_ref[:, at : at + CHUNK]
            ramp = basis_parts(edge_len, start, CHUNK)[1]
            one, two = lane_parts(part), lane_parts(part * ramp)
            flat = one if flat is None else flat + one
            ramped = two if ramped is None else ramped + two
        level = basis_parts(edge_len, 0, LANES)[0]
        columns.append(jnp.sum(flat, axis=1, keepdims=True) * level)
        columns.append(jnp.sum(ramped, axis=1, keepdims=True))
    return columns


def write_message(message_ref, columns, gamma, delta):
    rows = gamma.shape[0]
    lane = lax.broadcasted_iota(jnp.int32, (rows, LANES), 1)
    table = jnp.zeros((rows, LANES), F32)
    for i, column in enumerate(columns):
        table = jnp.where(lane == i, column, table)
    table = jnp.where(lane == 8, gamma, table)
    table = jnp.where(lane == 9, delta, table)
    turned = table.T
    lower, upper = turned[0:8], turned[8:16]
    block = jnp.concatenate([lower, upper], axis=1)
    message_ref[...] = jnp.broadcast_to(block[None], message_ref.shape)


def pack_kernel(capacity, values_ref, dest_ref, node_ref, out_ref):
    count = values_ref.shape[0]
    slots = out_ref.shape[0]
    dest = dest_ref[...]
    devices = slots // capacity
    wide = max(LANES, devices)
    lane = lax.broadcasted_iota(jnp.int32, (count, wide), 1)
    hit = (dest == lane).astype(F32)
    before = lax.broadcasted_iota(jnp.int32, (count, count), 0) > lax.broadcasted_iota(jnp.int32, (count, count), 1)
    earlier = jnp.dot(before.astype(BF16), hit.astype(BF16), preferred_element_type=F32)
    rank = jnp.sum(hit * earlier, axis=1, keepdims=True).astype(jnp.int32)
    slot = dest * capacity + rank
    node = node_ref[...]
    realiz = values_ref.shape[1]
    high, low = (node // 64).astype(F32), lax.rem(node, 64).astype(F32)
    side = lax.broadcasted_iota(jnp.int32, (count, LANES - realiz), 1)
    codes = jnp.where(side == 0, high, jnp.where(side == 1, low, 0.0)).astype(BF16)
    full = jnp.concatenate([values_ref[...], codes], axis=1)
    choose = (slot == lax.broadcasted_iota(jnp.int32, (count, slots), 1)).astype(F32).astype(BF16)
    out = lax.dot_general(choose, full, (((0,), (0,)), ((), ())), preferred_element_type=F32)
    out_ref[...] = out.astype(BF16)


def coarse_kernel(row_count, inverse_ref, out_ref):
    size = inverse_ref.shape[1]
    i = lax.broadcasted_iota(jnp.int32, (size, size), 0)
    j = lax.broadcasted_iota(jnp.int32, (size, size), 1)
    kind = (j % 8) // 2
    place = j // 8
    col, row = place // row_count, place % row_count
    cols = size // 8 // row_count
    has = (kind == 0) & (col > 0) | (kind == 1) & (col < cols - 1) | (kind == 2) & (row > 0) | (kind == 3) & (row < row_count - 1)
    step = jnp.where(kind == 0, 2 - 8 * row_count, jnp.where(kind == 1, 8 * row_count - 2, jnp.where(kind == 2, 2 - 8, 8 - 2)))
    pair = has & (i == j + step)
    table = jnp.where(pair, 0.5, jnp.where(i == j, jnp.where(has, 0.5, 1.0), 0.0))
    out_ref[...] = jnp.dot(inverse_ref[...], table, precision=HP, preferred_element_type=F32)


def load_kernel(realiz, got_ref, load_ref, e0, e1, e2, e3, message_ref):
    slots, size = got_ref.shape[0], load_ref.shape[1]
    got = got_ref[...]
    node = got[:, realiz : realiz + 1].astype(F32) * 64.0 + got[:, realiz + 1 : realiz + 2].astype(F32)
    node = node.astype(jnp.int32)
    for start in range(0, size, CHUNK):
        here = (node == lax.broadcasted_iota(jnp.int32, (slots, CHUNK), 1) + start).astype(F32).astype(BF16)
        load = lax.dot_general(got, here, (((0,), (0,)), ((), ())), preferred_element_type=F32)
        load_ref[:, start : start + CHUNK] = load[:realiz]
    send_edges(load_ref, (e0, e1, e2, e3))
    zero = jnp.zeros((realiz, 1), F32)
    write_message(message_ref, project(load_ref), zero, zero)


def local_solve(coarse, inverse_ref, coarse_inverse_ref, resid_ref, columns_of, scaled, part_ref, gamma_ref):
    place = Place()
    size = resid_ref.shape[1]
    edge_len = size // 4
    weight_at = [place.weights[i // edge_len] for i in range(0, size, CHUNK)]
    for start in range(0, size, CHUNK):
        at = pl.ds(start, CHUNK)
        scaled[:, at] = (weight_at[start // CHUNK] * resid_ref[:, at]).astype(BF16)
    solved = jnp.dot(coarse_inverse_ref[...], coarse, precision=HP, preferred_element_type=F32)
    turned = columns_of(solved)
    vec = scaled[...]
    gamma = None
    for start in range(0, size, CHUNK):
        at = pl.ds(start, CHUNK)
        edge, weight = start // edge_len, weight_at[start // CHUNK]
        level, ramp = basis_parts(edge_len, start % edge_len, CHUNK)
        part = jnp.dot(vec, inverse_ref[:, at], preferred_element_type=F32)
        part = part + (turned[2 * edge] * level + turned[2 * edge + 1] * ramp)
        part = weight * part
        part_ref[:, at] = part
        here = lane_parts(resid_ref[:, at] * part)
        gamma = here if gamma is None else gamma + here
    gamma_ref[...] = gamma


def turn(rows, realiz):
    count = rows.shape[0]
    full = jnp.concatenate([rows, jnp.zeros((LANES - count, LANES), F32)], axis=0) if count < LANES else rows
    turned = full.T
    return [turned[:realiz, i : i + 1] for i in range(count)]


def first_kernel(load_ref, g0, g1, g2, g3, gathered_ref, inverse_ref, coarse_inverse_ref,
                 resid_ref, coarse_ref, part_ref, gamma_ref, e0, e1, e2, e3, scaled):
    realiz = load_ref.shape[0]
    resid_ref[...] = load_ref[...]
    add_edges(resid_ref, (g0, g1, g2, g3))
    coarse = gathered_ref[...].reshape(coarse_ref.shape)
    coarse_ref[...] = coarse
    local_solve(coarse, inverse_ref, coarse_inverse_ref, resid_ref, lambda rows: turn(rows, realiz), scaled, part_ref, gamma_ref)
    send_edges(part_ref, (e0, e1, e2, e3))


def image_kernel(part_ref, g0, g1, g2, g3, gamma_ref, schur_ref,
                 precon_ref, image_ref, e0, e1, e2, e3, message_ref, rounded):
    size = part_ref.shape[1]
    precon_ref[...] = part_ref[...]
    add_edges(precon_ref, (g0, g1, g2, g3))
    rounded[...] = precon_ref[...].astype(BF16)
    vec = rounded[...]
    delta = None
    for start in range(0, size, CHUNK):
        at = pl.ds(start, CHUNK)
        image = jnp.dot(vec, schur_ref[:, at], preferred_element_type=F32)
        image_ref[:, at] = image
        here = lane_parts(precon_ref[:, at] * image)
        delta = here if delta is None else delta + here
    send_edges(image_ref, (e0, e1, e2, e3))
    gamma = jnp.sum(gamma_ref[...], axis=1, keepdims=True)
    delta = jnp.sum(delta, axis=1, keepdims=True)
    write_message(message_ref, project(image_ref), gamma, delta)


def step_kernel(mode, last, *refs):
    refs = list(refs)
    take = lambda n: [refs.pop(0) for _ in range(n)]
    image_ref, *edges = take(5)
    gathered_ref, precon_ref, resid_in = take(3)
    if mode != "init":
        direction_in, applied_in, field_in, state_in = take(4)
    if not last:
        coarse_in, = take(1)
        if mode != "init":
            coarse_applied_in, = take(1)
        inverse_ref, coarse_inverse_ref = take(2)
    field_ref, resid_ref = take(2)
    if not last:
        direction_ref, applied_ref, state_ref, coarse_ref, coarse_applied_ref, part_ref, gamma_ref = take(7)
        out_edges = take(4)
    work, = take(1)
    realiz, size = image_ref.shape
    work[...] = image_ref[...]
    add_edges(work, edges)
    total = pltpu.roll(jnp.sum(gathered_ref[...], axis=0), LANES // 2, 1)
    gamma, delta = total[0:1], total[1:2]
    if mode == "init":
        alpha = gamma / delta
        beta = jnp.zeros_like(alpha)
    else:
        beta = gamma / state_in[0:1]
        alpha = gamma / (delta - beta * gamma / state_in[1:2])
    lane = lax.broadcasted_iota(jnp.int32, (1, LANES), 1)
    alpha, beta = (jnp.where(lane < realiz, row, 0.0) for row in (alpha, beta))
    if not last:
        scaled, = take(1)
        state_ref[0:1] = gamma
        state_ref[1:2] = alpha
        applied = gathered_ref[...].reshape(coarse_ref.shape)
        if mode != "init":
            applied = applied + beta * coarse_applied_in[...]
        coarse_applied_ref[...] = applied
        coarse = coarse_in[...] - alpha * applied
        coarse_ref[...] = coarse
    alpha_col, beta_col = turn(jnp.concatenate([alpha, beta, jnp.zeros((6, LANES), F32)], axis=0), realiz)[:2]
    for start in range(0, size, CHUNK):
        at = pl.ds(start, CHUNK)
        direction, applied = precon_ref[:, at], work[:, at]
        if mode == "init":
            field_ref[:, at] = alpha_col * direction
        else:
            direction = direction + beta_col * direction_in[:, at]
            applied = applied + beta_col * applied_in[:, at]
            field_ref[:, at] = field_in[:, at] + alpha_col * direction
        resid_ref[:, at] = resid_in[:, at] - alpha_col * applied
        if not last:
            direction_ref[:, at] = direction
            applied_ref[:, at] = applied
    if not last:
        local_solve(coarse, inverse_ref, coarse_inverse_ref, resid_ref, lambda rows: turn(rows, realiz), scaled, part_ref, gamma_ref)
        send_edges(part_ref, out_edges)


def gather(message):
    return lax.all_to_all(message, ("sx", "sy"), split_axis=0, concat_axis=0, tiled=True)


def body(obs_values, obs_dest, obs_node, schur, local_inverse, coarse_inverse):
    size = schur.shape[-1]
    obs_count, realiz = obs_values.shape
    row_count = lax.axis_size("sy")
    devices = lax.axis_size("sx") * row_count
    capacity = max(2, 2 * obs_count // devices)
    coarse_size = coarse_inverse.shape[1]
    edge = shape(realiz, size // 4, BF16)
    edges = [edge] * 4
    whole = shape(realiz, size)
    message = jax.ShapeDtypeStruct((devices, 8, LANES), F32)
    narrow = shape(realiz, LANES)
    coarse_state = shape(coarse_size, LANES)
    scratch_half, scratch_full = pltpu.VMEM((realiz, size), BF16), pltpu.VMEM((realiz, size), F32)
    flops = 2 * realiz * size * size
    schur_mat, inverse_mat = schur[0, 0], local_inverse[0, 0]

    packed = call(
        functools.partial(pack_kernel, capacity),
        shape(devices * capacity, LANES, BF16),
        (obs_values, obs_dest, obs_node[:, None]),
    )
    got = lax.all_to_all(
        packed.reshape(devices, capacity, LANES), ("sx", "sy"), split_axis=0, concat_axis=0, tiled=True
    ).reshape(devices * capacity, LANES)
    coarse_mat = call(functools.partial(coarse_kernel, row_count), shape(*coarse_inverse.shape), (coarse_inverse,))
    load, *out = call(functools.partial(load_kernel, realiz), [whole, *edges, message], (got,))
    gathered, edges_got = gather(out[4]), exchange(out[:4])
    resid, coarse, part, gamma, *out = call(
        first_kernel,
        [whole, coarse_state, whole, narrow, *edges],
        (load, *edges_got, gathered, inverse_mat, coarse_mat),
        [scratch_half],
        flops,
    )
    field = direction = applied = state = coarse_applied = None
    for step in range(ITERS):
        edges_got = exchange(out)
        precon, image, *out = call(
            image_kernel,
            [whole, whole, *edges, message],
            (part, *edges_got, gamma, schur_mat),
            [scratch_half],
            flops,
        )
        gathered, edges_got = gather(out[4]), exchange(out[:4])
        last = step == ITERS - 1
        mode = "init" if step == 0 else "next"
        args = [image, *edges_got, gathered, precon, resid]
        args += [] if step == 0 else [direction, applied, field, state]
        if last:
            field, resid = call(
                functools.partial(step_kernel, mode, True), [whole, whole], args, [scratch_full]
            )
            break
        args += [coarse] if step == 0 else [coarse, coarse_applied]
        args += [inverse_mat, coarse_mat]
        field, resid, direction, applied, state, coarse, coarse_applied, part, gamma, *out = call(
            functools.partial(step_kernel, mode, False),
            [whole, whole, whole, whole, shape(8, LANES), coarse_state, coarse_state, whole, narrow, *edges],
            args,
            [scratch_full, scratch_half],
            flops,
        )
    return field[None, None], resid[None, None]


def solution(mesh):
    placed = (
        P(("sx", "sy"), None),
        P(("sx", "sy"), None),
        P(("sx", "sy")),
        P("sx", "sy", None, None),
        P("sx", "sy", None, None),
        P(("sx", "sy"), None),
    )
    return jax.shard_map(
        body,
        mesh=mesh,
        in_specs=placed,
        out_specs=(P("sx", "sy", None, None), P("sx", "sy", None, None)),
        check_vma=False,
    )
```

time: 1220 us -> 282 us (0.23)
  blocking collectives: 791 us -> 15.3 us
  waiting for transfers between devices: 134 us -> 30.2 us
  matrix products: 83.9 us -> 0 us
  local copies, waits for them, and re-layouts: 13.8 us -> 92.5 us
  starting transfers between devices: 152 us -> 107 us
  Pallas kernels: 0 us -> 32.7 us
  other arithmetic: 27.3 us -> 0 us
    psum x11 -> x0, blocking collectives: 545 us -> none  [the longest x6 291 us: products(): return lax.psum(jnp.sum(weight * left * right, axis=1), ('sx', 'sy'))]
    all_gather x6 -> x0, blocking collectives: 246 us -> none  [gather_coarse(): return lax.all_gather(coarse_local, ('sx', 'sy'), axis=0, tiled=True)]
    ppermute x52, waiting for transfers between devices: 124 us -> 24.8 us  [exchange(): got[i] = lax.ppermute(edges[i], plan[i][0], plan[i][1])]
    dot_general x30 -> x0, matrix products: 83.9 us -> none  [the longest x6 30 us: precond(): jnp.dot(scaled.astype(jnp.bfloat16), inverse_mat, preferred_element_type=...]
    unnamed x165 -> x182, local copies, waits for them, and re-layouts: 9.25 us -> 91.7 us
    ppermute x52, starting transfers between devices: 143 us -> 62.5 us  [exchange(): got[i] = lax.ppermute(edges[i], plan[i][0], plan[i][1])]
    all_to_all x2 -> x7, starting transfers between devices: 9.87 us -> 44.4 us  [gather(): lax.all_to_all(message, ('sx', 'sy'), split_axis=0, concat_axis=0, tiled=...]
    pallas_call x0 -> x16, Pallas kernels: none -> 32.7 us  [call(): pl.pallas_call(kernel, out_shape=outs, in_specs=[VM] * len(args), out_spe...]
  transfers between devices with their start and end apart: 54 -> 59, of which waited for: 41 -> 32; matrix products, arithmetic and copies ran while one was open for 0% -> 0% of each run, Pallas kernels for 0% -> 0%
where the time goes in v1:
time: 282 us; the launch traced here: 279 us
  starting transfers between devices  107 us (38%)
  local copies, waits for them, and re-layouts  92.5 us (33%)
  Pallas kernels  32.7 us (12%)
  waiting for transfers between devices  30.2 us (11%)
  blocking collectives  15.3 us (5%)
    unnamed x182, local copies, waits for them, and re-layouts  91.7 us
    ppermute x52, starting transfers between devices, exchange(): got[i] = lax.ppermute(edges[i], plan[i][0], plan[i][1])  62.5 us
    all_to_all x7, starting transfers between devices, gather(): lax.all_to_all(message, ('sx', 'sy'), split_axis=0, concat_axis=0, tiled=...  44.4 us
    pallas_call x16, Pallas kernels, call(): pl.pallas_call(kernel, out_shape=outs, in_specs=[VM] * len(args), out_spe...  32.7 us
    ppermute x52, waiting for transfers between devices, exchange(): got[i] = lax.ppermute(edges[i], plan[i][0], plan[i][1])  24.8 us
    all_to_all x1, blocking collectives, body(): lax.all_to_all(packed.reshape(devices, capacity, LANES), ('sx', 'sy'), sp...  15.3 us
  transfers between devices with their start and end apart: 59, of which 32 were waited for; matrix products, arithmetic and copies ran while one was open for 0% of the time, Pallas kernels for 0%

profile of v1, /device:TPU:0, one launch (start us, length us, event | category | flops | bytes accessed | tf_op | source)
XLA Modules:
  0.0 278.8 jit_solution(4000070355188679309)
XLA Ops:
  3.8 15.3 %all_to_all.40 = bf16[32,16,128]{2,1,0:T(8,128)(2,1)S(1)} all-to-all(bf16[32,16,128]{2,1,0:T(8,128)(2,1)S(1)} %bitcast.19), channel_id=1, replica_groups=mesh['sx'=8,'sy'=4] {'sx','sy'}, dimensions={0} | all-to-all | bytes 262144 | tf_op jit(solution)/shard_map/all_to_all | solution.py:334
  20.8 2.6 all-to-all-start.1
  31.6 3.4 %copy-done = bf16[1,1,2048,2048]{3,2,1,0:T(8,128)(2,1)S(1)} copy-done((bf16[1,1,2048,2048]{3,2,1,0:T(8,128)(2,1)S(1)}, bf16[1,1,2048,2048]{3,2,1,0:T(8,128)(2,1)}, u32[]{:S(2)}) %copy-start) | copy-done | bytes 8388632
  36.8 2.5 collective-permute-start.4
  43.9 2.7 shard_map.81
  46.6 6.5 %all-to-all-start.2 = ((f32[32,8,128]{2,1,0:T(8,128)}), f32[32,8,128]{2,1,0:T(8,128)S(1)}, u32[]{:S(2)}, u32[]{:S(2)}) async-start(f32[32,8,128]{2,1,0:T(8,128)} %get-tuple-element.140), calls=%async_computation.2 | async-start | bytes 262144 | tf_op jit(solution)/shard_map/all_to_all | solution.py:309
  61.4 3.4 %copy-done.1 = bf16[1,1,2048,2048]{3,2,1,0:T(8,128)(2,1)S(1)} copy-done((bf16[1,1,2048,2048]{3,2,1,0:T(8,128)(2,1)S(1)}, bf16[1,1,2048,2048]{3,2,1,0:T(8,128)(2,1)}, u32[]{:S(2)}) %copy-start.1) | copy-done | bytes 8388632
  67.7 2.4 collective-permute-start.12
  74.8 3.4 %copy-done.7 = bf16[1,1,2048,2048]{3,2,1,0:T(8,128)(2,1)S(1)} copy-done((bf16[1,1,2048,2048]{3,2,1,0:T(8,128)(2,1)S(1)}, bf16[1,1,2048,2048]{3,2,1,0:T(8,128)(2,1)}, u32[]{:S(2)}) %copy-start.7) | copy-done | bytes 8388632
  78.2 2.7 shard_map.83
  82.5 6.5 %all-to-all-start.3 = ((f32[32,8,128]{2,1,0:T(8,128)}), f32[32,8,128]{2,1,0:T(8,128)S(1)}, u32[]{:S(2)}, u32[]{:S(2)}) async-start(f32[32,8,128]{2,1,0:T(8,128)} %get-tuple-element.155), calls=%async_computation.3 | async-start | bytes 262144 | tf_op jit(solution)/shard_map/all_to_all | solution.py:309
  97.1 3.4 %copy-done.2 = bf16[1,1,2048,2048]{3,2,1,0:T(8,128)(2,1)S(1)} copy-done((bf16[1,1,2048,2048]{3,2,1,0:T(8,128)(2,1)S(1)}, bf16[1,1,2048,2048]{3,2,1,0:T(8,128)(2,1)}, u32[]{:S(2)}) %copy-start.2) | copy-done | bytes 8388632
  112.0 3.1 %collective-permute-start.20 = (bf16[64,512]{1,0:T(8,128)(2,1)S(1)}, bf16[64,512]{1,0:T(8,128)(2,1)S(1)}, u32[]{:S(2)}, u32[]{:S(2)}) collective-permute-start(bf16[64,512]{1,0:T(8,128)(2,1)S(1)} %get-tuple-element.165), channel_id=1, source_target_pairs={{0,4},{4,0},{8,12},{12,8},{16,20},{20,16},{24,28},{28,24},{1,5},{5... | collective-permute-start | bytes 196616 | tf_op jit(solution)/shard_map/ppermute | solution.py:69
  117.8 2.2 collective-permute-done.23.g3
  120.0 3.4 %copy-done.8 = bf16[1,1,2048,2048]{3,2,1,0:T(8,128)(2,1)S(1)} copy-done((bf16[1,1,2048,2048]{3,2,1,0:T(8,128)(2,1)S(1)}, bf16[1,1,2048,2048]{3,2,1,0:T(8,128)(2,1)}, u32[]{:S(2)}) %copy-start.8) | copy-done | bytes 8388632
  123.4 2.7 shard_map.85
  130.1 7.3 %all-to-all-start.4 = ((f32[32,8,128]{2,1,0:T(8,128)}), f32[32,8,128]{2,1,0:T(8,128)S(1)}, u32[]{:S(2)}, u32[]{:S(2)}) async-start(f32[32,8,128]{2,1,0:T(8,128)} %get-tuple-element.175), calls=%async_computation.4 | async-start | bytes 262144 | tf_op jit(solution)/shard_map/all_to_all | solution.py:309
  145.7 3.4 %copy-done.3 = bf16[1,1,2048,2048]{3,2,1,0:T(8,128)(2,1)S(1)} copy-done((bf16[1,1,2048,2048]{3,2,1,0:T(8,128)(2,1)S(1)}, bf16[1,1,2048,2048]{3,2,1,0:T(8,128)(2,1)}, u32[]{:S(2)}) %copy-start.3) | copy-done | bytes 8388632
  156.7 3.3 %collective-permute-start.28 = (bf16[64,512]{1,0:T(8,128)(2,1)S(1)}, bf16[64,512]{1,0:T(8,128)(2,1)S(1)}, u32[]{:S(2)}, u32[]{:S(2)}) collective-permute-start(bf16[64,512]{1,0:T(8,128)(2,1)S(1)} %get-tuple-element.185), channel_id=1, source_target_pairs={{0,4},{4,0},{8,12},{12,8},{16,20},{20,16},{24,28},{28,24},{1,5},{5... | collective-permute-start | bytes 196616 | tf_op jit(solution)/shard_map/ppermute | solution.py:69
  164.7 3.4 %copy-done.9 = bf16[1,1,2048,2048]{3,2,1,0:T(8,128)(2,1)S(1)} copy-done((bf16[1,1,2048,2048]{3,2,1,0:T(8,128)(2,1)S(1)}, bf16[1,1,2048,2048]{3,2,1,0:T(8,128)(2,1)}, u32[]{:S(2)}) %copy-start.9) | copy-done | bytes 8388632
  168.1 2.7 shard_map.87
  172.4 7.3 %all-to-all-start.5 = ((f32[32,8,128]{2,1,0:T(8,128)}), f32[32,8,128]{2,1,0:T(8,128)S(1)}, u32[]{:S(2)}, u32[]{:S(2)}) async-start(f32[32,8,128]{2,1,0:T(8,128)} %get-tuple-element.195), calls=%async_computation.5 | async-start | bytes 262144 | tf_op jit(solution)/shard_map/all_to_all | solution.py:309
  187.9 3.4 %copy-done.4 = bf16[1,1,2048,2048]{3,2,1,0:T(8,128)(2,1)S(1)} copy-done((bf16[1,1,2048,2048]{3,2,1,0:T(8,128)(2,1)S(1)}, bf16[1,1,2048,2048]{3,2,1,0:T(8,128)(2,1)}, u32[]{:S(2)}) %copy-start.4) | copy-done | bytes 8388632
  202.8 3.1 %collective-permute-start.36 = (bf16[64,512]{1,0:T(8,128)(2,1)S(1)}, bf16[64,512]{1,0:T(8,128)(2,1)S(1)}, u32[]{:S(2)}, u32[]{:S(2)}) collective-permute-start(bf16[64,512]{1,0:T(8,128)(2,1)S(1)} %get-tuple-element.205), channel_id=1, source_target_pairs={{0,4},{4,0},{8,12},{12,8},{16,20},{20,16},{24,28},{28,24},{1,5},{5... | collective-permute-start | bytes 196616 | tf_op jit(solution)/shard_map/ppermute | solution.py:69
  210.6 3.4 %copy-done.10 = bf16[1,1,2048,2048]{3,2,1,0:T(8,128)(2,1)S(1)} copy-done((bf16[1,1,2048,2048]{3,2,1,0:T(8,128)(2,1)S(1)}, bf16[1,1,2048,2048]{3,2,1,0:T(8,128)(2,1)}, u32[]{:S(2)}) %copy-start.10) | copy-done | bytes 8388632
  218.6 7.3 %all-to-all-start.6 = ((f32[32,8,128]{2,1,0:T(8,128)}), f32[32,8,128]{2,1,0:T(8,128)S(1)}, u32[]{:S(2)}, u32[]{:S(2)}) async-start(f32[32,8,128]{2,1,0:T(8,128)} %copy-done.48), calls=%async_computation.6 | async-start | bytes 262144 | tf_op jit(solution)/shard_map/all_to_all | solution.py:309
  234.1 3.4 %copy-done.5 = bf16[1,1,2048,2048]{3,2,1,0:T(8,128)(2,1)S(1)} copy-done((bf16[1,1,2048,2048]{3,2,1,0:T(8,128)(2,1)S(1)}, bf16[1,1,2048,2048]{3,2,1,0:T(8,128)(2,1)}, u32[]{:S(2)}) %copy-start.5) | copy-done | bytes 8388632
  240.9 2.6 shard_map.90
  243.5 3.5 %collective-permute-start.44 = (bf16[64,512]{1,0:T(8,128)(2,1)S(1)}, bf16[64,512]{1,0:T(8,128)(2,1)S(1)}, u32[]{:S(2)}, u32[]{:S(2)}) collective-permute-start(bf16[64,512]{1,0:T(8,128)(2,1)S(1)} %get-tuple-element.225), channel_id=1, source_target_pairs={{0,4},{4,0},{8,12},{12,8},{16,20},{20,16},{24,28},{28,24},{1,5},{5... | collective-permute-start | bytes 196616 | tf_op jit(solution)/shard_map/ppermute | solution.py:69
  251.9 3.4 %copy-done.11 = bf16[1,1,2048,2048]{3,2,1,0:T(8,128)(2,1)S(1)} copy-done((bf16[1,1,2048,2048]{3,2,1,0:T(8,128)(2,1)S(1)}, bf16[1,1,2048,2048]{3,2,1,0:T(8,128)(2,1)}, u32[]{:S(2)}) %copy-start.11) | copy-done | bytes 8388632
  255.2 2.7 shard_map.91
  258.0 6.9 %all-to-all-start.7 = ((f32[32,8,128]{2,1,0:T(8,128)}), f32[32,8,128]{2,1,0:T(8,128)S(1)}, u32[]{:S(2)}, u32[]{:S(2)}) async-start(f32[32,8,128]{2,1,0:T(8,128)} %get-tuple-element.235), calls=%async_computation.7 | async-start | bytes 262144 | tf_op jit(solution)/shard_map/all_to_all | solution.py:309
  (286 shorter events, 144.3 us)
Async XLA Ops:
  20.8 10.8 %all-to-all-start.1 = ((f32[32,8,128]{2,1,0:T(8,128)}), f32[32,8,128]{2,1,0:T(8,128)S(1)}, u32[]{:S(2)}, u32[]{:S(2)}) async-start(f32[32,8,128]{2,1,0:T(8,128)} %get-tuple-element.128), calls=%async_computation.1 | async-start | bytes 262144 | tf_op jit(solution)/shard_map/all_to_all | solution.py:309
  23.3 5.0 %collective-permute-start = (bf16[64,512]{1,0:T(8,128)(2,1)S(1)}, bf16[64,512]{1,0:T(8,128)(2,1)S(1)}, u32[]{:S(2)}, u32[]{:S(2)}) collective-permute-start(bf16[64,512]{1,0:T(8,128)(2,1)S(1)} %get-tuple-element.124), channel_id=1, source_target_pairs={{0,4},{4,0},{8,12},{12,8},{16,20},{20,16},{24,28},{28,24},{1,5},{5... | collective-permute-start | bytes 196616 | tf_op jit(solution)/shard_map/ppermute | solution.py:69
  25.8 4.4 %collective-permute-start.3 = (bf16[64,512]{1,0:T(8,128)(2,1)S(1)}, bf16[64,512]{1,0:T(8,128)(2,1)S(1)}, u32[]{:S(2)}, u32[]{:S(2)}) collective-permute-start(bf16[64,512]{1,0:T(8,128)(2,1)S(1)} %get-tuple-element.127), channel_id=1, source_target_pairs={{1,2},{2,1},{3,0},{0,3},{5,6},{6,5},{7,4},{4,7},{9,10},{10,9},{11,... | collective-permute-start | bytes 196616 | tf_op jit(solution)/shard_map/ppermute | solution.py:69
  36.8 5.1 %collective-permute-start.4 = (bf16[64,512]{1,0:T(8,128)(2,1)S(1)}, bf16[64,512]{1,0:T(8,128)(2,1)S(1)}, u32[]{:S(2)}, u32[]{:S(2)}) collective-permute-start(bf16[64,512]{1,0:T(8,128)(2,1)S(1)} %get-tuple-element.130), channel_id=1, source_target_pairs={{0,4},{4,0},{8,12},{12,8},{16,20},{20,16},{24,28},{28,24},{1,5},{5... | collective-permute-start | bytes 196616 | tf_op jit(solution)/shard_map/ppermute | solution.py:69
  40.1 3.8 %collective-permute-start.7 = (bf16[64,512]{1,0:T(8,128)(2,1)S(1)}, bf16[64,512]{1,0:T(8,128)(2,1)S(1)}, u32[]{:S(2)}, u32[]{:S(2)}) collective-permute-start(bf16[64,512]{1,0:T(8,128)(2,1)S(1)} %get-tuple-element.133), channel_id=1, source_target_pairs={{1,2},{2,1},{3,0},{0,3},{5,6},{6,5},{7,4},{4,7},{9,10},{10,9},{11,... | collective-permute-start | bytes 196616 | tf_op jit(solution)/shard_map/ppermute | solution.py:69
  46.6 14.7 %all-to-all-start.2 = ((f32[32,8,128]{2,1,0:T(8,128)}), f32[32,8,128]{2,1,0:T(8,128)S(1)}, u32[]{:S(2)}, u32[]{:S(2)}) async-start(f32[32,8,128]{2,1,0:T(8,128)} %get-tuple-element.140), calls=%async_computation.2 | async-start | bytes 262144 | tf_op jit(solution)/shard_map/all_to_all | solution.py:309
  53.1 4.9 %collective-permute-start.8 = (bf16[64,512]{1,0:T(8,128)(2,1)S(1)}, bf16[64,512]{1,0:T(8,128)(2,1)S(1)}, u32[]{:S(2)}, u32[]{:S(2)}) collective-permute-start(bf16[64,512]{1,0:T(8,128)(2,1)S(1)} %get-tuple-element.136), channel_id=1, source_target_pairs={{0,4},{4,0},{8,12},{12,8},{16,20},{20,16},{24,28},{28,24},{1,5},{5... | collective-permute-start | bytes 196616 | tf_op jit(solution)/shard_map/ppermute | solution.py:69
  55.7 4.4 %collective-permute-start.11 = (bf16[64,512]{1,0:T(8,128)(2,1)S(1)}, bf16[64,512]{1,0:T(8,128)(2,1)S(1)}, u32[]{:S(2)}, u32[]{:S(2)}) collective-permute-start(bf16[64,512]{1,0:T(8,128)(2,1)S(1)} %get-tuple-element.139), channel_id=1, source_target_pairs={{1,2},{2,1},{3,0},{0,3},{5,6},{6,5},{7,4},{4,7},{9,10},{10,9},{11,... | collective-permute-start | bytes 196616 | tf_op jit(solution)/shard_map/ppermute | solution.py:69
  67.7 5.1 %collective-permute-start.12 = (bf16[64,512]{1,0:T(8,128)(2,1)S(1)}, bf16[64,512]{1,0:T(8,128)(2,1)S(1)}, u32[]{:S(2)}, u32[]{:S(2)}) collective-permute-start(bf16[64,512]{1,0:T(8,128)(2,1)S(1)} %get-tuple-element.145), channel_id=1, source_target_pairs={{0,4},{4,0},{8,12},{12,8},{16,20},{20,16},{24,28},{28,24},{1,5},{5... | collective-permute-start | bytes 196616 | tf_op jit(solution)/shard_map/ppermute | solution.py:69
  70.9 3.8 %collective-permute-start.15 = (bf16[64,512]{1,0:T(8,128)(2,1)S(1)}, bf16[64,512]{1,0:T(8,128)(2,1)S(1)}, u32[]{:S(2)}, u32[]{:S(2)}) collective-permute-start(bf16[64,512]{1,0:T(8,128)(2,1)S(1)} %get-tuple-element.148), channel_id=1, source_target_pairs={{1,2},{2,1},{3,0},{0,3},{5,6},{6,5},{7,4},{4,7},{9,10},{10,9},{11,... | collective-permute-start | bytes 196616 | tf_op jit(solution)/shard_map/ppermute | solution.py:69
  82.5 14.7 %all-to-all-start.3 = ((f32[32,8,128]{2,1,0:T(8,128)}), f32[32,8,128]{2,1,0:T(8,128)S(1)}, u32[]{:S(2)}, u32[]{:S(2)}) async-start(f32[32,8,128]{2,1,0:T(8,128)} %get-tuple-element.155), calls=%async_computation.3 | async-start | bytes 262144 | tf_op jit(solution)/shard_map/all_to_all | solution.py:309
  88.9 4.9 %collective-permute-start.16 = (bf16[64,512]{1,0:T(8,128)(2,1)S(1)}, bf16[64,512]{1,0:T(8,128)(2,1)S(1)}, u32[]{:S(2)}, u32[]{:S(2)}) collective-permute-start(bf16[64,512]{1,0:T(8,128)(2,1)S(1)} %get-tuple-element.151), channel_id=1, source_target_pairs={{0,4},{4,0},{8,12},{12,8},{16,20},{20,16},{24,28},{28,24},{1,5},{5... | collective-permute-start | bytes 196616 | tf_op jit(solution)/shard_map/ppermute | solution.py:69
  91.5 4.4 %collective-permute-start.19 = (bf16[64,512]{1,0:T(8,128)(2,1)S(1)}, bf16[64,512]{1,0:T(8,128)(2,1)S(1)}, u32[]{:S(2)}, u32[]{:S(2)}) collective-permute-start(bf16[64,512]{1,0:T(8,128)(2,1)S(1)} %get-tuple-element.154), channel_id=1, source_target_pairs={{1,2},{2,1},{3,0},{0,3},{5,6},{6,5},{7,4},{4,7},{9,10},{10,9},{11,... | collective-permute-start | bytes 196616 | tf_op jit(solution)/shard_map/ppermute | solution.py:69
  112.0 5.7 %collective-permute-start.20 = (bf16[64,512]{1,0:T(8,128)(2,1)S(1)}, bf16[64,512]{1,0:T(8,128)(2,1)S(1)}, u32[]{:S(2)}, u32[]{:S(2)}) collective-permute-start(bf16[64,512]{1,0:T(8,128)(2,1)S(1)} %get-tuple-element.165), channel_id=1, source_target_pairs={{0,4},{4,0},{8,12},{12,8},{16,20},{20,16},{24,28},{28,24},{1,5},{5... | collective-permute-start | bytes 196616 | tf_op jit(solution)/shard_map/ppermute | solution.py:69
  130.1 15.6 %all-to-all-start.4 = ((f32[32,8,128]{2,1,0:T(8,128)}), f32[32,8,128]{2,1,0:T(8,128)S(1)}, u32[]{:S(2)}, u32[]{:S(2)}) async-start(f32[32,8,128]{2,1,0:T(8,128)} %get-tuple-element.175), calls=%async_computation.4 | async-start | bytes 262144 | tf_op jit(solution)/shard_map/all_to_all | solution.py:309
  137.5 5.1 %collective-permute-start.24 = (bf16[64,512]{1,0:T(8,128)(2,1)}, bf16[64,512]{1,0:T(8,128)(2,1)S(1)}, u32[]{:S(2)}, u32[]{:S(2)}) collective-permute-start(bf16[64,512]{1,0:T(8,128)(2,1)} %copy-done.88), channel_id=1, source_target_pairs={{0,4},{4,0},{8,12},{12,8},{16,20},{20,16},{24,28},{28,24},{1,5},{5... | collective-permute-start | bytes 196616 | tf_op jit(solution)/shard_map/ppermute | solution.py:69
  139.3 3.9 %collective-permute-start.25 = (bf16[64,512]{1,0:T(8,128)(2,1)}, bf16[64,512]{1,0:T(8,128)(2,1)S(1)}, u32[]{:S(2)}, u32[]{:S(2)}) collective-permute-start(bf16[64,512]{1,0:T(8,128)(2,1)} %copy-done.86), channel_id=1, source_target_pairs={{0,0},{28,28},{4,8},{8,4},{12,16},{16,12},{20,24},{24,20},{1,1},{2... | collective-permute-start | bytes 196616 | tf_op jit(solution)/shard_map/ppermute | solution.py:69
  140.8 4.2 %collective-permute-start.27 = (bf16[64,512]{1,0:T(8,128)(2,1)}, bf16[64,512]{1,0:T(8,128)(2,1)S(1)}, u32[]{:S(2)}, u32[]{:S(2)}) collective-permute-start(bf16[64,512]{1,0:T(8,128)(2,1)} %copy-done.82), channel_id=1, source_target_pairs={{1,2},{2,1},{3,0},{0,3},{5,6},{6,5},{7,4},{4,7},{9,10},{10,9},{11,... | collective-permute-start | bytes 196616 | tf_op jit(solution)/shard_map/ppermute | solution.py:69
  156.7 5.9 %collective-permute-start.28 = (bf16[64,512]{1,0:T(8,128)(2,1)S(1)}, bf16[64,512]{1,0:T(8,128)(2,1)S(1)}, u32[]{:S(2)}, u32[]{:S(2)}) collective-permute-start(bf16[64,512]{1,0:T(8,128)(2,1)S(1)} %get-tuple-element.185), channel_id=1, source_target_pairs={{0,4},{4,0},{8,12},{12,8},{16,20},{20,16},{24,28},{28,24},{1,5},{5... | collective-permute-start | bytes 196616 | tf_op jit(solution)/shard_map/ppermute | solution.py:69
  172.4 15.6 %all-to-all-start.5 = ((f32[32,8,128]{2,1,0:T(8,128)}), f32[32,8,128]{2,1,0:T(8,128)S(1)}, u32[]{:S(2)}, u32[]{:S(2)}) async-start(f32[32,8,128]{2,1,0:T(8,128)} %get-tuple-element.195), calls=%async_computation.5 | async-start | bytes 262144 | tf_op jit(solution)/shard_map/all_to_all | solution.py:309
  179.7 4.9 %collective-permute-start.32 = (bf16[64,512]{1,0:T(8,128)(2,1)S(1)}, bf16[64,512]{1,0:T(8,128)(2,1)S(1)}, u32[]{:S(2)}, u32[]{:S(2)}) collective-permute-start(bf16[64,512]{1,0:T(8,128)(2,1)S(1)} %get-tuple-element.191), channel_id=1, source_target_pairs={{0,4},{4,0},{8,12},{12,8},{16,20},{20,16},{24,28},{28,24},{1,5},{5... | collective-permute-start | bytes 196616 | tf_op jit(solution)/shard_map/ppermute | solution.py:69
  182.3 4.4 %collective-permute-start.35 = (bf16[64,512]{1,0:T(8,128)(2,1)S(1)}, bf16[64,512]{1,0:T(8,128)(2,1)S(1)}, u32[]{:S(2)}, u32[]{:S(2)}) collective-permute-start(bf16[64,512]{1,0:T(8,128)(2,1)S(1)} %get-tuple-element.194), channel_id=1, source_target_pairs={{1,2},{2,1},{3,0},{0,3},{5,6},{6,5},{7,4},{4,7},{9,10},{10,9},{11,... | collective-permute-start | bytes 196616 | tf_op jit(solution)/shard_map/ppermute | solution.py:69
  202.8 5.7 %collective-permute-start.36 = (bf16[64,512]{1,0:T(8,128)(2,1)S(1)}, bf16[64,512]{1,0:T(8,128)(2,1)S(1)}, u32[]{:S(2)}, u32[]{:S(2)}) collective-permute-start(bf16[64,512]{1,0:T(8,128)(2,1)S(1)} %get-tuple-element.205), channel_id=1, source_target_pairs={{0,4},{4,0},{8,12},{12,8},{16,20},{20,16},{24,28},{28,24},{1,5},{5... | collective-permute-start | bytes 196616 | tf_op jit(solution)/shard_map/ppermute | solution.py:69
  218.6 15.5 %all-to-all-start.6 = ((f32[32,8,128]{2,1,0:T(8,128)}), f32[32,8,128]{2,1,0:T(8,128)S(1)}, u32[]{:S(2)}, u32[]{:S(2)}) async-start(f32[32,8,128]{2,1,0:T(8,128)} %copy-done.48), calls=%async_computation.6 | async-start | bytes 262144 | tf_op jit(solution)/shard_map/all_to_all | solution.py:309
  225.9 5.1 %collective-permute-start.40 = (bf16[64,512]{1,0:T(8,128)(2,1)}, bf16[64,512]{1,0:T(8,128)(2,1)S(1)}, u32[]{:S(2)}, u32[]{:S(2)}) collective-permute-start(bf16[64,512]{1,0:T(8,128)(2,1)} %copy-done.89), channel_id=1, source_target_pairs={{0,4},{4,0},{8,12},{12,8},{16,20},{20,16},{24,28},{28,24},{1,5},{5... | collective-permute-start | bytes 196616 | tf_op jit(solution)/shard_map/ppermute | solution.py:69
  227.7 3.9 %collective-permute-start.41 = (bf16[64,512]{1,0:T(8,128)(2,1)}, bf16[64,512]{1,0:T(8,128)(2,1)S(1)}, u32[]{:S(2)}, u32[]{:S(2)}) collective-permute-start(bf16[64,512]{1,0:T(8,128)(2,1)} %copy-done.87), channel_id=1, source_target_pairs={{0,0},{28,28},{4,8},{8,4},{12,16},{16,12},{20,24},{24,20},{1,1},{2... | collective-permute-start | bytes 196616 | tf_op jit(solution)/shard_map/ppermute | solution.py:69
  229.2 4.2 %collective-permute-start.43 = (bf16[64,512]{1,0:T(8,128)(2,1)}, bf16[64,512]{1,0:T(8,128)(2,1)S(1)}, u32[]{:S(2)}, u32[]{:S(2)}) collective-permute-start(bf16[64,512]{1,0:T(8,128)(2,1)} %copy-done.83), channel_id=1, source_target_pairs={{1,2},{2,1},{3,0},{0,3},{5,6},{6,5},{7,4},{4,7},{9,10},{10,9},{11,... | collective-permute-start | bytes 196616 | tf_op jit(solution)/shard_map/ppermute | solution.py:69
  243.5 6.2 %collective-permute-start.44 = (bf16[64,512]{1,0:T(8,128)(2,1)S(1)}, bf16[64,512]{1,0:T(8,128)(2,1)S(1)}, u32[]{:S(2)}, u32[]{:S(2)}) collective-permute-start(bf16[64,512]{1,0:T(8,128)(2,1)S(1)} %get-tuple-element.225), channel_id=1, source_target_pairs={{0,4},{4,0},{8,12},{12,8},{16,20},{20,16},{24,28},{28,24},{1,5},{5... | collective-permute-start | bytes 196616 | tf_op jit(solution)/shard_map/ppermute | solution.py:69
  247.9 4.0 %collective-permute-start.47 = (bf16[64,512]{1,0:T(8,128)(2,1)S(1)}, bf16[64,512]{1,0:T(8,128)(2,1)S(1)}, u32[]{:S(2)}, u32[]{:S(2)}) collective-permute-start(bf16[64,512]{1,0:T(8,128)(2,1)S(1)} %get-tuple-element.228), channel_id=1, source_target_pairs={{1,2},{2,1},{3,0},{0,3},{5,6},{6,5},{7,4},{4,7},{9,10},{10,9},{11,... | collective-permute-start | bytes 196616 | tf_op jit(solution)/shard_map/ppermute | solution.py:69
  258.0 15.2 %all-to-all-start.7 = ((f32[32,8,128]{2,1,0:T(8,128)}), f32[32,8,128]{2,1,0:T(8,128)S(1)}, u32[]{:S(2)}, u32[]{:S(2)}) async-start(f32[32,8,128]{2,1,0:T(8,128)} %get-tuple-element.235), calls=%async_computation.7 | async-start | bytes 262144 | tf_op jit(solution)/shard_map/all_to_all | solution.py:309
  264.9 4.9 %collective-permute-start.48 = (bf16[64,512]{1,0:T(8,128)(2,1)S(1)}, bf16[64,512]{1,0:T(8,128)(2,1)S(1)}, u32[]{:S(2)}, u32[]{:S(2)}) collective-permute-start(bf16[64,512]{1,0:T(8,128)(2,1)S(1)} %get-tuple-element.231), channel_id=1, source_target_pairs={{0,4},{4,0},{8,12},{12,8},{16,20},{20,16},{24,28},{28,24},{1,5},{5... | collective-permute-start | bytes 196616 | tf_op jit(solution)/shard_map/ppermute | solution.py:69
  267.5 4.4 %collective-permute-start.51 = (bf16[64,512]{1,0:T(8,128)(2,1)S(1)}, bf16[64,512]{1,0:T(8,128)(2,1)S(1)}, u32[]{:S(2)}, u32[]{:S(2)}) collective-permute-start(bf16[64,512]{1,0:T(8,128)(2,1)S(1)} %get-tuple-element.234), channel_id=1, source_target_pairs={{1,2},{2,1},{3,0},{0,3},{5,6},{6,5},{7,4},{4,7},{9,10},{10,9},{11,... | collective-permute-start | bytes 196616 | tf_op jit(solution)/shard_map/ppermute | solution.py:69
  (117 other events, 329.7 us)

commit v2 on v1

--- a/solution.py
+++ b/solution.py
@@ -8,6 +8,7 @@
 from jax.sharding import PartitionSpec as P
 
 ITERS = 6
+EXACT = 2
 LANES = 128
 CHUNK = 256
 HP = lax.Precision.HIGHEST
@@ -48,25 +49,23 @@
 
 def swaps():
     cols, rows = lax.axis_size("sx"), lax.axis_size("sy")
-
-    def near(count):
-        return [(i, i ^ 1) for i in range(count)]
-
-    far_sx = [(0, 0), (cols - 1, cols - 1)]
-    for i in range(1, cols - 1, 2):
-        far_sx += [(i, i + 1), (i + 1, i)]
-    far_sy = []
-    for i in range(1, rows, 2):
-        far_sy += [(i, (i + 1) % rows), ((i + 1) % rows, i)]
-    return (("sx", near(cols)), ("sx", far_sx), ("sy", near(rows)), ("sy", far_sy))
+    plans = [], [], [], []
+    for col in range(cols):
+        for row in range(rows):
+            across = col + (1 if col % 2 else -1)
+            beyond = row + (1 if row % 2 else -1)
+            far_sx = (across, row) if 0 <= across < cols else (col, row ^ 1)
+            partners = (col ^ 1, row), far_sx, (col, row ^ 1), (col, beyond % rows)
+            for plan, (to_col, to_row) in zip(plans, partners, strict=True):
+                plan.append((col * rows + row, to_col * rows + to_row))
+    return plans
 
 
 def exchange(edges):
-    far_sx, far_sy, near_sx, near_sy = 1, 3, 0, 2
-    plan = swaps()
+    plans = swaps()
     got = [None] * 4
-    for i in (far_sx, far_sy, near_sx, near_sy):
-        got[i] = lax.ppermute(edges[i], plan[i][0], plan[i][1])
+    for i in (1, 0, 3, 2):
+        got[i] = lax.ppermute(edges[i], ("sx", "sy"), plans[i])
     return got
 
 
@@ -74,7 +73,7 @@
     place, edge_len = Place(), value_ref.shape[1] // 4
     for edge, ref in zip(place.edges, edge_refs, strict=True):
         start = pl.multiple_of(edge * edge_len, edge_len)
-        ref[...] = value_ref[:, pl.ds(start, edge_len)].astype(BF16)
+        ref[...] = value_ref[:, pl.ds(start, edge_len)].astype(ref.dtype)
 
 
 def add_edges(value_ref, edge_refs):
@@ -309,6 +308,13 @@
     return lax.all_to_all(message, ("sx", "sy"), split_axis=0, concat_axis=0, tiled=True)
 
 
+def gather_then_exchange(out):
+    *edges, message = out
+    gathered = gather(message)
+    gathered, *edges = lax.optimization_barrier((gathered, *edges))
+    return gathered, exchange(edges)
+
+
 def body(obs_values, obs_dest, obs_node, schur, local_inverse, coarse_inverse):
     size = schur.shape[-1]
     obs_count, realiz = obs_values.shape
@@ -318,6 +324,7 @@
     coarse_size = coarse_inverse.shape[1]
     edge = shape(realiz, size // 4, BF16)
     edges = [edge] * 4
+    exact = shape(realiz, size // 4)
     whole = shape(realiz, size)
     message = jax.ShapeDtypeStruct((devices, 8, LANES), F32)
     narrow = shape(realiz, LANES)
@@ -336,7 +343,7 @@
     ).reshape(devices * capacity, LANES)
     coarse_mat = call(functools.partial(coarse_kernel, row_count), shape(*coarse_inverse.shape), (coarse_inverse,))
     load, *out = call(functools.partial(load_kernel, realiz), [whole, *edges, message], (got,))
-    gathered, edges_got = gather(out[4]), exchange(out[:4])
+    gathered, edges_got = gather_then_exchange(out)
     resid, coarse, part, gamma, *out = call(
         first_kernel,
         [whole, coarse_state, whole, narrow, *edges],
@@ -349,12 +356,12 @@
         edges_got = exchange(out)
         precon, image, *out = call(
             image_kernel,
-            [whole, whole, *edges, message],
+            [whole, whole, *([exact] * 4 if step < EXACT else edges), message],
             (part, *edges_got, gamma, schur_mat),
             [scratch_half],
             flops,
         )
-        gathered, edges_got = gather(out[4]), exchange(out[:4])
+        gathered, edges_got = gather_then_exchange(out)
         last = step == ITERS - 1
         mode = "init" if step == 0 else "next"
         args = [image, *edges_got, gathered, precon, resid]

time: 282 us -> 209 us (0.74)
  local copies, waits for them, and re-layouts: 92.5 us -> 9.97 us
  starting transfers between devices: 107 us -> 26.5 us
  blocking collectives: 15.3 us -> 89.2 us
  waiting for transfers between devices: 30.2 us -> 52.9 us
  Pallas kernels: 32.7 us -> 28.4 us
    unnamed x182 -> x16, local copies, waits for them, and re-layouts: 91.7 us -> 9.16 us
    all_to_all x0 -> x7, blocking collectives: none -> 73.9 us  [gather(): lax.all_to_all(message, ('sx', 'sy'), split_axis=0, concat_axis=0, tiled=...]
    all_to_all x7 -> x0, starting transfers between devices: 44.4 us -> none  [gather(): lax.all_to_all(message, ('sx', 'sy'), split_axis=0, concat_axis=0, tiled=...]
    ppermute x52, starting transfers between devices: 62.5 us -> 26.5 us  [exchange(): got[i] = lax.ppermute(edges[i], ('sx', 'sy'), plans[i])]
    ppermute x52, waiting for transfers between devices: 24.8 us -> 52.9 us  [exchange(): got[i] = lax.ppermute(edges[i], ('sx', 'sy'), plans[i])]
    all_to_all x7 -> x0, waiting for transfers between devices: 5.43 us -> none  [gather(): lax.all_to_all(message, ('sx', 'sy'), split_axis=0, concat_axis=0, tiled=...]
    pallas_call x16, Pallas kernels: 32.7 us -> 28.4 us  [call(): pl.pallas_call(kernel, out_shape=outs, in_specs=[VM] * len(args), out_spe...]
  transfers between devices with their start and end apart: 59 -> 52, of which waited for: 32 -> 26; matrix products, arithmetic and copies ran while one was open for 0% -> 0% of each run, Pallas kernels for 0% -> 0%
where the time goes in v2:
time: 209 us; the launch traced here: 208 us
  blocking collectives  89.2 us (43%)
  waiting for transfers between devices  52.9 us (25%)
  Pallas kernels  28.4 us (14%)
  starting transfers between devices  26.5 us (13%)
  local copies, waits for them, and re-layouts  9.97 us (5%)
    all_to_all x7, blocking collectives, gather(): lax.all_to_all(message, ('sx', 'sy'), split_axis=0, concat_axis=0, tiled=...  73.9 us
    ppermute x52, waiting for transfers between devices, exchange(): got[i] = lax.ppermute(edges[i], ('sx', 'sy'), plans[i])  52.9 us
    pallas_call x16, Pallas kernels, call(): pl.pallas_call(kernel, out_shape=outs, in_specs=[VM] * len(args), out_spe...  28.4 us
    ppermute x52, starting transfers between devices, exchange(): got[i] = lax.ppermute(edges[i], ('sx', 'sy'), plans[i])  26.5 us
    all_to_all x1, blocking collectives, body(): lax.all_to_all(packed.reshape(devices, capacity, LANES), ('sx', 'sy'), sp...  15.3 us
    unnamed x16, local copies, waits for them, and re-layouts  9.16 us
  transfers between devices with their start and end apart: 52, of which 26 were waited for; matrix products, arithmetic and copies ran while one was open for 0% of the time, Pallas kernels for 0%

profile of v2, /device:TPU:0, one launch (start us, length us, event | category | flops | bytes accessed | tf_op | source)
XLA Modules:
  0.0 208.1 jit_solution(12839614090615634209)
XLA Ops:
  3.8 15.3 %all_to_all.40 = bf16[32,16,128]{2,1,0:T(8,128)(2,1)S(1)} all-to-all(bf16[32,16,128]{2,1,0:T(8,128)(2,1)S(1)} %bitcast.23), channel_id=1, replica_groups=mesh['sx'=8,'sy'=4] {'sx','sy'}, dimensions={0} | all-to-all | bytes 262144 | tf_op jit(solution)/shard_map/all_to_all | solution.py:341
  20.1 10.0 %all_to_all.41.gathered_ref = f32[32,8,128]{2,1,0:T(8,128)S(1)} all-to-all(f32[32,8,128]{2,1,0:T(8,128)S(1)} %get-tuple-element.159), channel_id=1, replica_groups=mesh['sx'=8,'sy'=4] {'sx','sy'}, dimensions={0} | all-to-all | bytes 262144 | tf_op jit(solution)/shard_map/all_to_all | solution.py:308
  35.5 3.4 %copy-done = bf16[1,1,2048,2048]{3,2,1,0:T(8,128)(2,1)S(1)} copy-done((bf16[1,1,2048,2048]{3,2,1,0:T(8,128)(2,1)S(1)}, bf16[1,1,2048,2048]{3,2,1,0:T(8,128)(2,1)}, u32[]{:S(2)}) %copy-start) | copy-done | bytes 8388632
  43.2 2.7 %collective-permute-done.4.g0 = bf16[64,512]{1,0:T(8,128)(2,1)S(1)} collective-permute-done((bf16[64,512]{1,0:T(8,128)(2,1)S(1)}, bf16[64,512]{1,0:T(8,128)(2,1)S(1)}, u32[]{:S(2)}, u32[]{:S(2)}) %collective-permute-start.4) | collective-permute-done | bytes 65568 | tf_op jit(solution)/shard_map/ppermute | solution.py:68
  47.3 3.4 %copy-done.1 = bf16[1,1,2048,2048]{3,2,1,0:T(8,128)(2,1)S(1)} copy-done((bf16[1,1,2048,2048]{3,2,1,0:T(8,128)(2,1)S(1)}, bf16[1,1,2048,2048]{3,2,1,0:T(8,128)(2,1)}, u32[]{:S(2)}) %copy-start.1) | copy-done | bytes 8388632
  52.8 10.7 %all_to_all.42.refs_5_ = f32[32,8,128]{2,1,0:T(8,128)S(1)} all-to-all(f32[32,8,128]{2,1,0:T(8,128)S(1)} %get-tuple-element.176), channel_id=1, replica_groups=mesh['sx'=8,'sy'=4] {'sx','sy'}, dimensions={0} | all-to-all | bytes 262144 | tf_op jit(solution)/shard_map/all_to_all | solution.py:308
  65.0 4.7 %collective-permute-done.8.refs_1_ = f32[64,512]{1,0:T(8,128)S(1)} collective-permute-done((f32[64,512]{1,0:T(8,128)S(1)}, f32[64,512]{1,0:T(8,128)S(1)}, u32[]{:S(2)}, u32[]{:S(2)}) %collective-permute-start.8) | collective-permute-done | bytes 131104 | tf_op jit(solution)/shard_map/ppermute | solution.py:68
  70.2 2.1 %shard_map.82 = (f32[64,2048]{1,0:T(8,128)S(1)}, f32[64,2048]{1,0:T(8,128)S(1)}, f32[64,2048]{1,0:T(8,128)S(1)}, f32[64,2048]{1,0:T(8,128)S(1)}, f32[8,128]{1,0:...) custom-call(f32[64,2048]{1,0:T(8,128)S(1)} %get-tuple-element.175.re, ...), custom_call_target="tpu_custom_call" | custom-call | flops 536870912 | bytes 10756096 | tf_op jit(solution)/shard_map/pallas_call | solution.py:22
  72.3 2.1 collective-permute-start.12
  75.3 2.2 %collective-permute-done.12.g0 = bf16[64,512]{1,0:T(8,128)(2,1)S(1)} collective-permute-done((bf16[64,512]{1,0:T(8,128)(2,1)S(1)}, bf16[64,512]{1,0:T(8,128)(2,1)S(1)}, u32[]{:S(2)}, u32[]{:S(2)}) %collective-permute-start.12) | collective-permute-done | bytes 65568 | tf_op jit(solution)/shard_map/ppermute | solution.py:68
  81.2 10.6 %all_to_all.43.refs_5_ = f32[32,8,128]{2,1,0:T(8,128)S(1)} all-to-all(f32[32,8,128]{2,1,0:T(8,128)S(1)} %get-tuple-element.196), channel_id=1, replica_groups=mesh['sx'=8,'sy'=4] {'sx','sy'}, dimensions={0} | all-to-all | bytes 262144 | tf_op jit(solution)/shard_map/all_to_all | solution.py:308
  93.4 4.7 %collective-permute-done.16.refs_1_ = f32[64,512]{1,0:T(8,128)S(1)} collective-permute-done((f32[64,512]{1,0:T(8,128)S(1)}, f32[64,512]{1,0:T(8,128)S(1)}, u32[]{:S(2)}, u32[]{:S(2)}) %collective-permute-start.16) | collective-permute-done | bytes 131104 | tf_op jit(solution)/shard_map/ppermute | solution.py:68
  98.6 2.2 %shard_map.84 = (f32[64,2048]{1,0:T(8,128)S(1)}, f32[64,2048]{1,0:T(8,128)S(1)}, f32[64,2048]{1,0:T(8,128)S(1)}, f32[64,2048]{1,0:T(8,128)S(1)}, f32[8,128]{1,0:...) custom-call(f32[64,2048]{1,0:T(8,128)S(1)} %get-tuple-element.195.re, ...), custom_call_target="tpu_custom_call" | custom-call | flops 536870912 | bytes 12464128 | tf_op jit(solution)/shard_map/pallas_call | solution.py:22
  100.8 2.1 collective-permute-start.20
  103.7 2.3 %collective-permute-done.20.g0 = bf16[64,512]{1,0:T(8,128)(2,1)S(1)} collective-permute-done((bf16[64,512]{1,0:T(8,128)(2,1)S(1)}, bf16[64,512]{1,0:T(8,128)(2,1)S(1)}, u32[]{:S(2)}, u32[]{:S(2)}) %collective-permute-start.20) | collective-permute-done | bytes 65568 | tf_op jit(solution)/shard_map/ppermute | solution.py:68
  109.6 10.6 %all_to_all.44.refs_5_ = f32[32,8,128]{2,1,0:T(8,128)S(1)} all-to-all(f32[32,8,128]{2,1,0:T(8,128)S(1)} %get-tuple-element.221), channel_id=1, replica_groups=mesh['sx'=8,'sy'=4] {'sx','sy'}, dimensions={0} | all-to-all | bytes 262144 | tf_op jit(solution)/shard_map/all_to_all | solution.py:308
  121.8 2.7 %collective-permute-done.24.refs_1_ = bf16[64,512]{1,0:T(8,128)(2,1)S(1)} collective-permute-done((bf16[64,512]{1,0:T(8,128)(2,1)S(1)}, bf16[64,512]{1,0:T(8,128)(2,1)S(1)}, u32[]{:S(2)}, u32[]{:S(2)}) %collective-permute-start.24) | collective-permute-done | bytes 65568 | tf_op jit(solution)/shard_map/ppermute | solution.py:68
  125.6 2.2 %shard_map.86 = (f32[64,2048]{1,0:T(8,128)S(1)}, f32[64,2048]{1,0:T(8,128)S(1)}, f32[64,2048]{1,0:T(8,128)S(1)}, f32[64,2048]{1,0:T(8,128)S(1)}, f32[8,128]{1,0:...) custom-call(f32[64,2048]{1,0:T(8,128)S(1)} %get-tuple-element.220.re, ...), custom_call_target="tpu_custom_call" | custom-call | flops 536870912 | bytes 12201984 | tf_op jit(solution)/shard_map/pallas_call | solution.py:22
  130.2 2.7 %collective-permute-done.28.g0 = bf16[64,512]{1,0:T(8,128)(2,1)S(1)} collective-permute-done((bf16[64,512]{1,0:T(8,128)(2,1)S(1)}, bf16[64,512]{1,0:T(8,128)(2,1)S(1)}, u32[]{:S(2)}, u32[]{:S(2)}) %collective-permute-start.28) | collective-permute-done | bytes 65568 | tf_op jit(solution)/shard_map/ppermute | solution.py:68
  134.4 2.0 shard_map.87
  136.4 10.7 %all_to_all.45.refs_5_ = f32[32,8,128]{2,1,0:T(8,128)S(1)} all-to-all(f32[32,8,128]{2,1,0:T(8,128)S(1)} %get-tuple-element.246), channel_id=1, replica_groups=mesh['sx'=8,'sy'=4] {'sx','sy'}, dimensions={0} | all-to-all | bytes 262144 | tf_op jit(solution)/shard_map/all_to_all | solution.py:308
  148.6 2.7 %collective-permute-done.32.refs_1_ = bf16[64,512]{1,0:T(8,128)(2,1)S(1)} collective-permute-done((bf16[64,512]{1,0:T(8,128)(2,1)S(1)}, bf16[64,512]{1,0:T(8,128)(2,1)S(1)}, u32[]{:S(2)}, u32[]{:S(2)}) %collective-permute-start.32) | collective-permute-done | bytes 65568 | tf_op jit(solution)/shard_map/ppermute | solution.py:68
  152.5 2.2 %shard_map.88 = (f32[64,2048]{1,0:T(8,128)S(1)}, f32[64,2048]{1,0:T(8,128)S(1)}, f32[64,2048]{1,0:T(8,128)S(1)}, f32[64,2048]{1,0:T(8,128)S(1)}, f32[8,128]{1,0:...) custom-call(f32[64,2048]{1,0:T(8,128)S(1)} %get-tuple-element.245.re, ...), custom_call_target="tpu_custom_call" | custom-call | flops 536870912 | bytes 12201984 | tf_op jit(solution)/shard_map/pallas_call | solution.py:22
  157.1 2.7 %collective-permute-done.36.g0 = bf16[64,512]{1,0:T(8,128)(2,1)S(1)} collective-permute-done((bf16[64,512]{1,0:T(8,128)(2,1)S(1)}, bf16[64,512]{1,0:T(8,128)(2,1)S(1)}, u32[]{:S(2)}, u32[]{:S(2)}) %collective-permute-start.36) | collective-permute-done | bytes 65568 | tf_op jit(solution)/shard_map/ppermute | solution.py:68
  161.3 2.0 shard_map.89
  163.3 10.7 %all_to_all.46.refs_5_ = f32[32,8,128]{2,1,0:T(8,128)S(1)} all-to-all(f32[32,8,128]{2,1,0:T(8,128)S(1)} %get-tuple-element.271), channel_id=1, replica_groups=mesh['sx'=8,'sy'=4] {'sx','sy'}, dimensions={0} | all-to-all | bytes 262144 | tf_op jit(solution)/shard_map/all_to_all | solution.py:308
  175.5 2.7 %collective-permute-done.40.refs_1_ = bf16[64,512]{1,0:T(8,128)(2,1)S(1)} collective-permute-done((bf16[64,512]{1,0:T(8,128)(2,1)S(1)}, bf16[64,512]{1,0:T(8,128)(2,1)S(1)}, u32[]{:S(2)}, u32[]{:S(2)}) %collective-permute-start.40) | collective-permute-done | bytes 65568 | tf_op jit(solution)/shard_map/ppermute | solution.py:68
  179.3 2.6 %shard_map.90 = (f32[64,2048]{1,0:T(8,128)S(1)}, f32[64,2048]{1,0:T(8,128)S(1)}, f32[64,2048]{1,0:T(8,128)S(1)}, f32[64,2048]{1,0:T(8,128)S(1)}, f32[8,128]{1,0:...) custom-call(f32[64,2048]{1,0:T(8,128)S(1)} %get-tuple-element.270.re, ...), custom_call_target="tpu_custom_call" | custom-call | flops 536870912 | bytes 12201984 | tf_op jit(solution)/shard_map/pallas_call | solution.py:22
  184.3 2.7 %collective-permute-done.44.g0 = bf16[64,512]{1,0:T(8,128)(2,1)S(1)} collective-permute-done((bf16[64,512]{1,0:T(8,128)(2,1)S(1)}, bf16[64,512]{1,0:T(8,128)(2,1)S(1)}, u32[]{:S(2)}, u32[]{:S(2)}) %collective-permute-start.44) | collective-permute-done | bytes 65568 | tf_op jit(solution)/shard_map/ppermute | solution.py:68
  188.5 2.0 shard_map.91
  190.6 10.6 %all_to_all.47.refs_5_ = f32[32,8,128]{2,1,0:T(8,128)S(1)} all-to-all(f32[32,8,128]{2,1,0:T(8,128)S(1)} %get-tuple-element.296), channel_id=1, replica_groups=mesh['sx'=8,'sy'=4] {'sx','sy'}, dimensions={0} | all-to-all | bytes 262144 | tf_op jit(solution)/shard_map/all_to_all | solution.py:308
  202.8 2.7 %collective-permute-done.48.refs_1_ = bf16[64,512]{1,0:T(8,128)(2,1)S(1)} collective-permute-done((bf16[64,512]{1,0:T(8,128)(2,1)S(1)}, bf16[64,512]{1,0:T(8,128)(2,1)S(1)}, u32[]{:S(2)}, u32[]{:S(2)}) %collective-permute-start.48) | collective-permute-done | bytes 65568 | tf_op jit(solution)/shard_map/ppermute | solution.py:68
  (115 shorter events, 54.1 us)
Async XLA Ops:
  30.1 4.3 %collective-permute-start = (bf16[64,512]{1,0:T(8,128)(2,1)S(1)}, bf16[64,512]{1,0:T(8,128)(2,1)S(1)}, u32[]{:S(2)}, u32[]{:S(2)}) collective-permute-start(bf16[64,512]{1,0:T(8,128)(2,1)S(1)} %get-tuple-element.164), channel_id=1, source_target_pairs={{0,4},{1,5},{2,6},{3,7},{4,0},{5,1},{6,2},{7,3},{8,12},{9,13},{10,... | collective-permute-start | bytes 196616 | tf_op jit(solution)/shard_map/ppermute | solution.py:68
  31.3 4.2 %collective-permute-start.3 = (bf16[64,512]{1,0:T(8,128)(2,1)S(1)}, bf16[64,512]{1,0:T(8,128)(2,1)S(1)}, u32[]{:S(2)}, u32[]{:S(2)}) collective-permute-start(bf16[64,512]{1,0:T(8,128)(2,1)S(1)} %get-tuple-element.167), channel_id=1, source_target_pairs={{0,3},{1,2},{2,1},{3,0},{4,7},{5,6},{6,5},{7,4},{8,11},{9,10},{10,... | collective-permute-start | bytes 196616 | tf_op jit(solution)/shard_map/ppermute | solution.py:68
  40.7 5.1 %collective-permute-start.4 = (bf16[64,512]{1,0:T(8,128)(2,1)S(1)}, bf16[64,512]{1,0:T(8,128)(2,1)S(1)}, u32[]{:S(2)}, u32[]{:S(2)}) collective-permute-start(bf16[64,512]{1,0:T(8,128)(2,1)S(1)} %get-tuple-element.170), channel_id=1, source_target_pairs={{0,4},{1,5},{2,6},{3,7},{4,0},{5,1},{6,2},{7,3},{8,12},{9,13},{10,... | collective-permute-start | bytes 196616 | tf_op jit(solution)/shard_map/ppermute | solution.py:68
  43.1 4.2 %collective-permute-start.7 = (bf16[64,512]{1,0:T(8,128)(2,1)S(1)}, bf16[64,512]{1,0:T(8,128)(2,1)S(1)}, u32[]{:S(2)}, u32[]{:S(2)}) collective-permute-start(bf16[64,512]{1,0:T(8,128)(2,1)S(1)} %get-tuple-element.173), channel_id=1, source_target_pairs={{0,3},{1,2},{2,1},{3,0},{4,7},{5,6},{6,5},{7,4},{8,11},{9,10},{10,... | collective-permute-start | bytes 196616 | tf_op jit(solution)/shard_map/ppermute | solution.py:68
  63.4 6.3 %collective-permute-start.8 = (f32[64,512]{1,0:T(8,128)S(1)}, f32[64,512]{1,0:T(8,128)S(1)}, u32[]{:S(2)}, u32[]{:S(2)}) collective-permute-start(f32[64,512]{1,0:T(8,128)S(1)} %get-tuple-element.181), channel_id=1, source_target_pairs={{0,4},{1,5},{2,6},{3,7},{4,0},{5,1},{6,2},{7,3},{8,12},{9,13},{10,... | collective-permute-start | bytes 393224 | tf_op jit(solution)/shard_map/ppermute | solution.py:68
  64.1 5.6 %collective-permute-start.9 = (f32[64,512]{1,0:T(8,128)S(1)}, f32[64,512]{1,0:T(8,128)S(1)}, u32[]{:S(2)}, u32[]{:S(2)}) collective-permute-start(f32[64,512]{1,0:T(8,128)S(1)} %get-tuple-element.182), channel_id=1, source_target_pairs={{0,1},{1,0},{2,3},{3,2},{4,8},{5,9},{6,10},{7,11},{8,4},{9,5},{10,... | collective-permute-start | bytes 393224 | tf_op jit(solution)/shard_map/ppermute | solution.py:68
  64.1 5.6 %collective-permute-start.10 = (f32[64,512]{1,0:T(8,128)S(1)}, f32[64,512]{1,0:T(8,128)S(1)}, u32[]{:S(2)}, u32[]{:S(2)}) collective-permute-start(f32[64,512]{1,0:T(8,128)S(1)} %get-tuple-element.183), channel_id=1, source_target_pairs={{0,1},{1,0},{2,3},{3,2},{4,5},{5,4},{6,7},{7,6},{8,9},{9,8},{10,11... | collective-permute-start | bytes 393224 | tf_op jit(solution)/shard_map/ppermute | solution.py:68
  64.6 5.6 %collective-permute-start.11 = (f32[64,512]{1,0:T(8,128)S(1)}, f32[64,512]{1,0:T(8,128)S(1)}, u32[]{:S(2)}, u32[]{:S(2)}) collective-permute-start(f32[64,512]{1,0:T(8,128)S(1)} %get-tuple-element.184), channel_id=1, source_target_pairs={{0,3},{1,2},{2,1},{3,0},{4,7},{5,6},{6,5},{7,4},{8,11},{9,10},{10,... | collective-permute-start | bytes 393224 | tf_op jit(solution)/shard_map/ppermute | solution.py:68
  72.3 5.2 %collective-permute-start.12 = (bf16[64,512]{1,0:T(8,128)(2,1)S(1)}, bf16[64,512]{1,0:T(8,128)(2,1)S(1)}, u32[]{:S(2)}, u32[]{:S(2)}) collective-permute-start(bf16[64,512]{1,0:T(8,128)(2,1)S(1)} %get-tuple-element.190), channel_id=1, source_target_pairs={{0,4},{1,5},{2,6},{3,7},{4,0},{5,1},{6,2},{7,3},{8,12},{9,13},{10,... | collective-permute-start | bytes 196616 | tf_op jit(solution)/shard_map/ppermute | solution.py:68
  74.9 4.2 %collective-permute-start.15 = (bf16[64,512]{1,0:T(8,128)(2,1)S(1)}, bf16[64,512]{1,0:T(8,128)(2,1)S(1)}, u32[]{:S(2)}, u32[]{:S(2)}) collective-permute-start(bf16[64,512]{1,0:T(8,128)(2,1)S(1)} %get-tuple-element.193), channel_id=1, source_target_pairs={{0,3},{1,2},{2,1},{3,0},{4,7},{5,6},{6,5},{7,4},{8,11},{9,10},{10,... | collective-permute-start | bytes 196616 | tf_op jit(solution)/shard_map/ppermute | solution.py:68
  91.8 6.3 %collective-permute-start.16 = (f32[64,512]{1,0:T(8,128)S(1)}, f32[64,512]{1,0:T(8,128)S(1)}, u32[]{:S(2)}, u32[]{:S(2)}) collective-permute-start(f32[64,512]{1,0:T(8,128)S(1)} %get-tuple-element.201), channel_id=1, source_target_pairs={{0,4},{1,5},{2,6},{3,7},{4,0},{5,1},{6,2},{7,3},{8,12},{9,13},{10,... | collective-permute-start | bytes 393224 | tf_op jit(solution)/shard_map/ppermute | solution.py:68
  92.5 5.6 %collective-permute-start.17 = (f32[64,512]{1,0:T(8,128)S(1)}, f32[64,512]{1,0:T(8,128)S(1)}, u32[]{:S(2)}, u32[]{:S(2)}) collective-permute-start(f32[64,512]{1,0:T(8,128)S(1)} %get-tuple-element.202), channel_id=1, source_target_pairs={{0,1},{1,0},{2,3},{3,2},{4,8},{5,9},{6,10},{7,11},{8,4},{9,5},{10,... | collective-permute-start | bytes 393224 | tf_op jit(solution)/shard_map/ppermute | solution.py:68
  92.5 5.6 %collective-permute-start.18 = (f32[64,512]{1,0:T(8,128)S(1)}, f32[64,512]{1,0:T(8,128)S(1)}, u32[]{:S(2)}, u32[]{:S(2)}) collective-permute-start(f32[64,512]{1,0:T(8,128)S(1)} %get-tuple-element.203), channel_id=1, source_target_pairs={{0,1},{1,0},{2,3},{3,2},{4,5},{5,4},{6,7},{7,6},{8,9},{9,8},{10,11... | collective-permute-start | bytes 393224 | tf_op jit(solution)/shard_map/ppermute | solution.py:68
  93.0 5.6 %collective-permute-start.19 = (f32[64,512]{1,0:T(8,128)S(1)}, f32[64,512]{1,0:T(8,128)S(1)}, u32[]{:S(2)}, u32[]{:S(2)}) collective-permute-start(f32[64,512]{1,0:T(8,128)S(1)} %get-tuple-element.204), channel_id=1, source_target_pairs={{0,3},{1,2},{2,1},{3,0},{4,7},{5,6},{6,5},{7,4},{8,11},{9,10},{10,... | collective-permute-start | bytes 393224 | tf_op jit(solution)/shard_map/ppermute | solution.py:68
  100.8 5.2 %collective-permute-start.20 = (bf16[64,512]{1,0:T(8,128)(2,1)S(1)}, bf16[64,512]{1,0:T(8,128)(2,1)S(1)}, u32[]{:S(2)}, u32[]{:S(2)}) collective-permute-start(bf16[64,512]{1,0:T(8,128)(2,1)S(1)} %get-tuple-element.215), channel_id=1, source_target_pairs={{0,4},{1,5},{2,6},{3,7},{4,0},{5,1},{6,2},{7,3},{8,12},{9,13},{10,... | collective-permute-start | bytes 196616 | tf_op jit(solution)/shard_map/ppermute | solution.py:68
  103.3 4.2 %collective-permute-start.23 = (bf16[64,512]{1,0:T(8,128)(2,1)S(1)}, bf16[64,512]{1,0:T(8,128)(2,1)S(1)}, u32[]{:S(2)}, u32[]{:S(2)}) collective-permute-start(bf16[64,512]{1,0:T(8,128)(2,1)S(1)} %get-tuple-element.218), channel_id=1, source_target_pairs={{0,3},{1,2},{2,1},{3,0},{4,7},{5,6},{6,5},{7,4},{8,11},{9,10},{10,... | collective-permute-start | bytes 196616 | tf_op jit(solution)/shard_map/ppermute | solution.py:68
  120.2 4.3 %collective-permute-start.24 = (bf16[64,512]{1,0:T(8,128)(2,1)S(1)}, bf16[64,512]{1,0:T(8,128)(2,1)S(1)}, u32[]{:S(2)}, u32[]{:S(2)}) collective-permute-start(bf16[64,512]{1,0:T(8,128)(2,1)S(1)} %get-tuple-element.226), channel_id=1, source_target_pairs={{0,4},{1,5},{2,6},{3,7},{4,0},{5,1},{6,2},{7,3},{8,12},{9,13},{10,... | collective-permute-start | bytes 196616 | tf_op jit(solution)/shard_map/ppermute | solution.py:68
  120.9 3.6 %collective-permute-start.26 = (bf16[64,512]{1,0:T(8,128)(2,1)S(1)}, bf16[64,512]{1,0:T(8,128)(2,1)S(1)}, u32[]{:S(2)}, u32[]{:S(2)}) collective-permute-start(bf16[64,512]{1,0:T(8,128)(2,1)S(1)} %get-tuple-element.228), channel_id=1, source_target_pairs={{0,1},{1,0},{2,3},{3,2},{4,5},{5,4},{6,7},{7,6},{8,9},{9,8},{10,11... | collective-permute-start | bytes 196616 | tf_op jit(solution)/shard_map/ppermute | solution.py:68
  121.4 4.2 %collective-permute-start.27 = (bf16[64,512]{1,0:T(8,128)(2,1)S(1)}, bf16[64,512]{1,0:T(8,128)(2,1)S(1)}, u32[]{:S(2)}, u32[]{:S(2)}) collective-permute-start(bf16[64,512]{1,0:T(8,128)(2,1)S(1)} %get-tuple-element.229), channel_id=1, source_target_pairs={{0,3},{1,2},{2,1},{3,0},{4,7},{5,6},{6,5},{7,4},{8,11},{9,10},{10,... | collective-permute-start | bytes 196616 | tf_op jit(solution)/shard_map/ppermute | solution.py:68
  127.8 5.1 %collective-permute-start.28 = (bf16[64,512]{1,0:T(8,128)(2,1)S(1)}, bf16[64,512]{1,0:T(8,128)(2,1)S(1)}, u32[]{:S(2)}, u32[]{:S(2)}) collective-permute-start(bf16[64,512]{1,0:T(8,128)(2,1)S(1)} %get-tuple-element.240), channel_id=1, source_target_pairs={{0,4},{1,5},{2,6},{3,7},{4,0},{5,1},{6,2},{7,3},{8,12},{9,13},{10,... | collective-permute-start | bytes 196616 | tf_op jit(solution)/shard_map/ppermute | solution.py:68
  130.2 4.2 %collective-permute-start.31 = (bf16[64,512]{1,0:T(8,128)(2,1)S(1)}, bf16[64,512]{1,0:T(8,128)(2,1)S(1)}, u32[]{:S(2)}, u32[]{:S(2)}) collective-permute-start(bf16[64,512]{1,0:T(8,128)(2,1)S(1)} %get-tuple-element.243), channel_id=1, source_target_pairs={{0,3},{1,2},{2,1},{3,0},{4,7},{5,6},{6,5},{7,4},{8,11},{9,10},{10,... | collective-permute-start | bytes 196616 | tf_op jit(solution)/shard_map/ppermute | solution.py:68
  147.1 4.3 %collective-permute-start.32 = (bf16[64,512]{1,0:T(8,128)(2,1)S(1)}, bf16[64,512]{1,0:T(8,128)(2,1)S(1)}, u32[]{:S(2)}, u32[]{:S(2)}) collective-permute-start(bf16[64,512]{1,0:T(8,128)(2,1)S(1)} %get-tuple-element.251), channel_id=1, source_target_pairs={{0,4},{1,5},{2,6},{3,7},{4,0},{5,1},{6,2},{7,3},{8,12},{9,13},{10,... | collective-permute-start | bytes 196616 | tf_op jit(solution)/shard_map/ppermute | solution.py:68
  147.8 3.6 %collective-permute-start.33 = (bf16[64,512]{1,0:T(8,128)(2,1)S(1)}, bf16[64,512]{1,0:T(8,128)(2,1)S(1)}, u32[]{:S(2)}, u32[]{:S(2)}) collective-permute-start(bf16[64,512]{1,0:T(8,128)(2,1)S(1)} %get-tuple-element.252), channel_id=1, source_target_pairs={{0,1},{1,0},{2,3},{3,2},{4,8},{5,9},{6,10},{7,11},{8,4},{9,5},{10,... | collective-permute-start | bytes 196616 | tf_op jit(solution)/shard_map/ppermute | solution.py:68
  148.3 4.2 %collective-permute-start.35 = (bf16[64,512]{1,0:T(8,128)(2,1)S(1)}, bf16[64,512]{1,0:T(8,128)(2,1)S(1)}, u32[]{:S(2)}, u32[]{:S(2)}) collective-permute-start(bf16[64,512]{1,0:T(8,128)(2,1)S(1)} %get-tuple-element.254), channel_id=1, source_target_pairs={{0,3},{1,2},{2,1},{3,0},{4,7},{5,6},{6,5},{7,4},{8,11},{9,10},{10,... | collective-permute-start | bytes 196616 | tf_op jit(solution)/shard_map/ppermute | solution.py:68
  154.6 5.1 %collective-permute-start.36 = (bf16[64,512]{1,0:T(8,128)(2,1)S(1)}, bf16[64,512]{1,0:T(8,128)(2,1)S(1)}, u32[]{:S(2)}, u32[]{:S(2)}) collective-permute-start(bf16[64,512]{1,0:T(8,128)(2,1)S(1)} %get-tuple-element.265), channel_id=1, source_target_pairs={{0,4},{1,5},{2,6},{3,7},{4,0},{5,1},{6,2},{7,3},{8,12},{9,13},{10,... | collective-permute-start | bytes 196616 | tf_op jit(solution)/shard_map/ppermute | solution.py:68
  157.0 4.2 %collective-permute-start.39 = (bf16[64,512]{1,0:T(8,128)(2,1)S(1)}, bf16[64,512]{1,0:T(8,128)(2,1)S(1)}, u32[]{:S(2)}, u32[]{:S(2)}) collective-permute-start(bf16[64,512]{1,0:T(8,128)(2,1)S(1)} %get-tuple-element.268), channel_id=1, source_target_pairs={{0,3},{1,2},{2,1},{3,0},{4,7},{5,6},{6,5},{7,4},{8,11},{9,10},{10,... | collective-permute-start | bytes 196616 | tf_op jit(solution)/shard_map/ppermute | solution.py:68
  174.0 4.3 %collective-permute-start.40 = (bf16[64,512]{1,0:T(8,128)(2,1)S(1)}, bf16[64,512]{1,0:T(8,128)(2,1)S(1)}, u32[]{:S(2)}, u32[]{:S(2)}) collective-permute-start(bf16[64,512]{1,0:T(8,128)(2,1)S(1)} %get-tuple-element.276), channel_id=1, source_target_pairs={{0,4},{1,5},{2,6},{3,7},{4,0},{5,1},{6,2},{7,3},{8,12},{9,13},{10,... | collective-permute-start | bytes 196616 | tf_op jit(solution)/shard_map/ppermute | solution.py:68
  175.1 4.2 %collective-permute-start.43 = (bf16[64,512]{1,0:T(8,128)(2,1)S(1)}, bf16[64,512]{1,0:T(8,128)(2,1)S(1)}, u32[]{:S(2)}, u32[]{:S(2)}) collective-permute-start(bf16[64,512]{1,0:T(8,128)(2,1)S(1)} %get-tuple-element.279), channel_id=1, source_target_pairs={{0,3},{1,2},{2,1},{3,0},{4,7},{5,6},{6,5},{7,4},{8,11},{9,10},{10,... | collective-permute-start | bytes 196616 | tf_op jit(solution)/shard_map/ppermute | solution.py:68
  182.0 5.0 %collective-permute-start.44 = (bf16[64,512]{1,0:T(8,128)(2,1)S(1)}, bf16[64,512]{1,0:T(8,128)(2,1)S(1)}, u32[]{:S(2)}, u32[]{:S(2)}) collective-permute-start(bf16[64,512]{1,0:T(8,128)(2,1)S(1)} %get-tuple-element.290), channel_id=1, source_target_pairs={{0,4},{1,5},{2,6},{3,7},{4,0},{5,1},{6,2},{7,3},{8,12},{9,13},{10,... | collective-permute-start | bytes 196616 | tf_op jit(solution)/shard_map/ppermute | solution.py:68
  184.3 4.2 %collective-permute-start.47 = (bf16[64,512]{1,0:T(8,128)(2,1)S(1)}, bf16[64,512]{1,0:T(8,128)(2,1)S(1)}, u32[]{:S(2)}, u32[]{:S(2)}) collective-permute-start(bf16[64,512]{1,0:T(8,128)(2,1)S(1)} %get-tuple-element.293), channel_id=1, source_target_pairs={{0,3},{1,2},{2,1},{3,0},{4,7},{5,6},{6,5},{7,4},{8,11},{9,10},{10,... | collective-permute-start | bytes 196616 | tf_op jit(solution)/shard_map/ppermute | solution.py:68
  201.2 4.3 %collective-permute-start.48 = (bf16[64,512]{1,0:T(8,128)(2,1)S(1)}, bf16[64,512]{1,0:T(8,128)(2,1)S(1)}, u32[]{:S(2)}, u32[]{:S(2)}) collective-permute-start(bf16[64,512]{1,0:T(8,128)(2,1)S(1)} %get-tuple-element.301), channel_id=1, source_target_pairs={{0,4},{1,5},{2,6},{3,7},{4,0},{5,1},{6,2},{7,3},{8,12},{9,13},{10,... | collective-permute-start | bytes 196616 | tf_op jit(solution)/shard_map/ppermute | solution.py:68
  202.4 4.2 %collective-permute-start.51 = (bf16[64,512]{1,0:T(8,128)(2,1)S(1)}, bf16[64,512]{1,0:T(8,128)(2,1)S(1)}, u32[]{:S(2)}, u32[]{:S(2)}) collective-permute-start(bf16[64,512]{1,0:T(8,128)(2,1)S(1)} %get-tuple-element.304), channel_id=1, source_target_pairs={{0,3},{1,2},{2,1},{3,0},{4,7},{5,6},{6,5},{7,4},{8,11},{9,10},{10,... | collective-permute-start | bytes 196616 | tf_op jit(solution)/shard_map/ppermute | solution.py:68
  (27 other events, 162.8 us)

commit v3 on v0

v3 whole, which is shorter than its diff:
```python
import functools

import jax
import jax.numpy as jnp
from jax import lax
from jax.experimental import pallas as pl
from jax.experimental.pallas import tpu as pltpu
from jax.sharding import PartitionSpec as P

ITERS = 6
PAD = 16
COVER = 8e9
LANES = 128
CHUNK = 256
HP = lax.Precision.HIGHEST
F32 = jnp.float32
BF16 = jnp.bfloat16
VM = pl.BlockSpec(memory_space=pltpu.VMEM)
AXES = ("sx", "sy")


def call(kernel, outs, args, scratch=(), flops=0):
    size = sum(a.size * a.dtype.itemsize for a in args)
    return pl.pallas_call(
        kernel,
        out_shape=outs,
        in_specs=[VM] * len(args),
        out_specs=jax.tree.map(lambda _: VM, outs),
        scratch_shapes=list(scratch),
        compiler_params=pltpu.CompilerParams(vmem_limit_bytes=8 << 20),
        cost_estimate=pl.CostEstimate(flops=int(flops), bytes_accessed=size, transcendentals=0),
    )(*args)


def shape(rows, columns, dtype=F32):
    return jax.ShapeDtypeStruct((rows, columns), dtype)


def edge_of(slot, odd_col, odd_row):
    return (1 - odd_col, 3 - odd_row, odd_col, 2 + odd_row)[slot]


class Place:
    def __init__(self):
        col, row = lax.axis_index("sx"), lax.axis_index("sy")
        cols, rows = lax.axis_size("sx"), lax.axis_size("sy")
        odd_col, odd_row = lax.rem(col, 2), lax.rem(row, 2)
        self.edges = [edge_of(slot, odd_col, odd_row) for slot in range(4)]
        far_col = jnp.where(odd_col == 1, col < cols - 1, col > 0)
        far_row = jnp.where(odd_row == 1, row < rows - 1, row > 0)
        self.shared = (None, None, far_col, far_row)

    def weight(self, slot):
        shared = self.shared[slot]
        return F32(0.5) if shared is None else jnp.where(shared, F32(0.5), F32(1.0))


def swaps():
    cols, rows = lax.axis_size("sx"), lax.axis_size("sy")
    plans = [], [], [], []
    for col in range(cols):
        for row in range(rows):
            across = col + (1 if col % 2 else -1)
            beyond = row + (1 if row % 2 else -1)
            far_sx = (across, row) if 0 <= across < cols else (col, row ^ 1)
            partners = (col ^ 1, row), (col, row ^ 1), far_sx, (col, beyond % rows)
            for plan, (to_col, to_row) in zip(plans, partners, strict=True):
                plan.append((col * rows + row, to_col * rows + to_row))
    return plans


def exchange(edges):
    plans = swaps()
    got = [None] * 4
    for slot in (2, 0, 3, 1):
        got[slot] = lax.ppermute(edges[slot], AXES, plans[slot])
    return got


def received(place, slot, ref):
    got = ref[...].astype(F32)
    shared = place.shared[slot]
    return got if shared is None else jnp.where(shared, got, 0.0)


def basis_parts(edge_len, start, width):
    node = lax.broadcasted_iota(jnp.int32, (1, width), 1) + start
    offset = node.astype(F32) - (edge_len - 1) / 2.0
    level = 1.0 / jnp.sqrt(F32(edge_len))
    norm = jnp.sqrt(F32(edge_len * (edge_len * edge_len - 1) / 12.0))
    return level, offset / norm


def lane_parts(value):
    return sum(value[:, i : i + LANES] for i in range(LANES, value.shape[1], LANES)) + value[:, :LANES]


def project(halves):
    edge_len = halves[0].shape[1] // 2
    columns = []
    for slot in range(4):
        flat = ramped = None
        for start in range(0, edge_len, CHUNK):
            at = slot % 2 * edge_len + start
            part = halves[slot // 2][:, at : at + CHUNK]
            ramp = basis_parts(edge_len, start, CHUNK)[1]
            one, two = lane_parts(part), lane_parts(part * ramp)
            flat = one if flat is None else flat + one
            ramped = two if ramped is None else ramped + two
        level = basis_parts(edge_len, 0, LANES)[0]
        columns.append(jnp.sum(flat, axis=1, keepdims=True) * level)
        columns.append(jnp.sum(ramped, axis=1, keepdims=True))
    return columns


def write_message(message_ref, columns, gamma, delta):
    rows = gamma.shape[0]
    lane = lax.broadcasted_iota(jnp.int32, (rows, LANES), 1)
    table = jnp.zeros((rows, LANES), F32)
    order = [*columns[0::2], gamma, *columns[1::2], delta]
    for i, column in enumerate(order):
        table = jnp.where(lane == (i if i < 5 else i + 3), column, table)
    turned = table.T
    block = jnp.concatenate([turned[0:8], turned[8:16]], axis=1)
    for i in range(5):
        row = jnp.broadcast_to(block[i : i + 1][None], (message_ref.shape[0], 1, LANES))
        message_ref[:, :, i * LANES : (i + 1) * LANES] = row


def pack_kernel(capacity, values_ref, dest_ref, node_ref, out_ref):
    realiz, count = values_ref.shape
    slots = out_ref.shape[0]
    dest, node = dest_ref[...], node_ref[...]
    hit = lax.broadcasted_iota(jnp.int32, (slots // capacity, count), 0) == dest
    before = lax.broadcasted_iota(jnp.int32, (count, count), 0) < lax.broadcasted_iota(jnp.int32, (count, count), 1)
    hit = hit.astype(F32)
    earlier = jnp.dot(hit.astype(BF16), before.astype(F32).astype(BF16), preferred_element_type=F32)
    rank = jnp.sum(hit * earlier, axis=0, keepdims=True).astype(jnp.int32)
    slot = dest * capacity + rank
    high, low = (node // 64).astype(F32), lax.rem(node, 64).astype(F32)
    side = lax.broadcasted_iota(jnp.int32, (LANES - realiz, count), 0)
    codes = jnp.where(side == 0, high, jnp.where(side == 1, low, 0.0)).astype(BF16)
    full = jnp.concatenate([values_ref[...], codes], axis=0)
    choose = (lax.broadcasted_iota(jnp.int32, (slots, count), 0) == slot).astype(F32).astype(BF16)
    out = lax.dot_general(choose, full, (((1,), (1,)), ((), ())), preferred_element_type=F32)
    out_ref[...] = out.astype(BF16)


def coarse_kernel(cols, rows, inverse_ref, *out_refs):
    devices = cols * rows
    i = lax.broadcasted_iota(jnp.int32, (8 * devices, 4 * devices), 0)
    j = lax.broadcasted_iota(jnp.int32, (8 * devices, 4 * devices), 1)
    slot, device = j // devices, j % devices
    col, row = device // rows, device % rows
    along_x = (slot == 0) | (slot == 2)
    near = slot < 2
    step_col = jnp.where(near, 1, -1) * (1 - 2 * (col % 2))
    step_row = jnp.where(near, 1, -1) * (1 - 2 * (row % 2))
    to_col = jnp.where(along_x, col + step_col, col)
    to_row = jnp.where(along_x, row, row + step_row)
    shared = (to_col >= 0) & (to_col < cols) & (to_row >= 0) & (to_row < rows)

    def index(col, row):
        odd_col, odd_row = col % 2, row % 2
        edge = jnp.where(slot == 0, 1 - odd_col, jnp.where(slot == 1, 3 - odd_row, jnp.where(slot == 2, odd_col, 2 + odd_row)))
        return (col * rows + row) * 8 + edge * 2

    own, other = index(col, row), index(to_col, to_row)
    place = Place()
    k = lax.broadcasted_iota(jnp.int32, (8, 8), 0)
    from_row = lax.broadcasted_iota(jnp.int32, (8, 8), 1)
    edge = place.edges[3]
    for s in range(3):
        edge = jnp.where(k // 2 == s, place.edges[s], edge)
    pick = (from_row == 2 * edge + k % 2).astype(F32)
    mine = jnp.dot(pick, inverse_ref[...], precision=HP, preferred_element_type=F32)
    for part, out_ref in enumerate(out_refs):
        table = jnp.where(shared & (i == other + part), 0.5, jnp.where(i == own + part, jnp.where(shared, 0.5, 1.0), 0.0))
        out_ref[...] = jnp.dot(mine, table, precision=HP, preferred_element_type=F32)


def load_kernel(realiz, got_ref, near_ref, far_ref, e0, e1, e2, e3, message_ref):
    place, slots, edge_len = Place(), got_ref.shape[0], e0.shape[1]
    got = got_ref[...]
    node = got[:, realiz : realiz + 1].astype(F32) * 64.0 + got[:, realiz + 1 : realiz + 2].astype(F32)
    node = node.astype(jnp.int32)
    halves = near_ref, far_ref
    for slot, edge_ref in enumerate((e0, e1, e2, e3)):
        for start in range(0, edge_len, CHUNK):
            first = place.edges[slot] * edge_len + start
            here = lax.broadcasted_iota(jnp.int32, (slots, CHUNK), 1) + first == node
            load = lax.dot_general(got, here.astype(F32).astype(BF16), (((0,), (0,)), ((), ())), preferred_element_type=F32)
            at = slot % 2 * edge_len + start
            halves[slot // 2][:, at : at + CHUNK] = load[:realiz]
            edge_ref[:realiz, start : start + CHUNK] = load[:realiz]
    zero = jnp.zeros((realiz, 1), F32)
    write_message(message_ref, project(halves), zero, zero)


def half_product(place, half, vec_ref, matrix_ref, slot, start):
    edge_len = vec_ref.shape[1] // 2
    column = pl.multiple_of(place.edges[slot] * edge_len + start, CHUNK)
    total = None
    for i in range(2):
        row = pl.multiple_of(place.edges[2 * half + i] * edge_len, edge_len)
        block = matrix_ref[pl.ds(row, edge_len), pl.ds(column, CHUNK)]
        part = jnp.dot(vec_ref[:, i * edge_len : (i + 1) * edge_len], block, preferred_element_type=F32)
        total = part if total is None else total + part
    return total


def image_near_kernel(part_ref, g0, g1, schur_ref, precon_ref, sum_ref, rounded):
    place, edge_len = Place(), g0.shape[1]
    for i, got in enumerate((g0, g1)):
        at = pl.ds(i * edge_len, edge_len)
        value = part_ref[:, at] + received(place, i, got)
        precon_ref[:, at] = value
        rounded[:, at] = value.astype(BF16)
    for slot in range(4):
        for start in range(0, edge_len, CHUNK):
            sum_ref[:, pl.ds(slot * edge_len + start, CHUNK)] = half_product(place, 0, rounded, schur_ref, slot, start)


def image_far_kernel(part_ref, g2, g3, near_ref, sum_ref, gamma_ref, schur_ref,
                     precon_ref, image_near_ref, image_far_ref, e0, e1, e2, e3, message_ref, rounded):
    place, edge_len = Place(), g2.shape[1]
    for i, got in enumerate((g2, g3)):
        at = pl.ds(i * edge_len, edge_len)
        value = part_ref[:, at] + received(place, 2 + i, got)
        precon_ref[:, at] = value
        rounded[:, at] = value.astype(BF16)
    halves, vectors = (image_near_ref, image_far_ref), (near_ref, precon_ref)
    delta = None
    for slot, edge_ref in enumerate((e0, e1, e2, e3)):
        for start in range(0, edge_len, CHUNK):
            image = sum_ref[:, pl.ds(slot * edge_len + start, CHUNK)] + half_product(place, 1, rounded, schur_ref, slot, start)
            at = pl.ds(slot % 2 * edge_len + start, CHUNK)
            halves[slot // 2][:, at] = image
            edge_ref[: image.shape[0], pl.ds(start, CHUNK)] = image
            here = lane_parts(vectors[slot // 2][:, at] * image)
            delta = here if delta is None else delta + here
    gamma = jnp.sum(gamma_ref[...], axis=1, keepdims=True)
    delta = jnp.sum(delta, axis=1, keepdims=True)
    write_message(message_ref, project(halves), gamma, delta)


def coarse_table(gathered_ref, full):
    devices = gathered_ref.shape[0]
    for slot in range(4):
        full[slot * devices : (slot + 1) * devices] = gathered_ref[:, 0, slot * LANES : (slot + 1) * LANES]


def scalars(mode, gathered_ref, state_in, state_ref, realiz):
    total = jnp.sum(gathered_ref[:, 0, 4 * LANES : 5 * LANES], axis=0, keepdims=True)
    lane = lax.broadcasted_iota(jnp.int32, (1, LANES), 1)
    swapped = pltpu.roll(total, LANES // 2, 1)
    gamma = jnp.where(lane < realiz, total, swapped)
    delta = jnp.where(lane < realiz, swapped, total)
    if mode == "init":
        alpha, beta = gamma / delta, jnp.zeros_like(gamma)
    else:
        beta = gamma / state_in[0:1]
        alpha = gamma / (delta - beta * gamma / state_in[1:2])
    if state_ref is not None:
        state_ref[0:1] = gamma
        state_ref[1:2] = alpha
    return alpha, beta


def turn(rows, realiz):
    count = sum(row.shape[0] for row in rows)
    return jnp.concatenate([*rows, jnp.zeros((LANES - count, LANES), F32)], axis=0).T[:realiz]


def step_half(place, half, mode, image_ref, edges, columns, precon_ref, olds, news, scaled):
    edge_len = edges[0].shape[1]
    resid_in, *olds = olds
    alpha, beta = columns[:, 0:1], columns[:, 1:2]
    for i, got in enumerate(edges):
        slot = 2 * half + i
        for start in range(0, edge_len, CHUNK):
            from_ = pl.ds(start, CHUNK)
            at = pl.ds(i * edge_len + start, CHUNK)
            other = got[: image_ref.shape[0], from_]
            if place.shared[slot] is not None:
                other = jnp.where(place.shared[slot], other, 0.0)
            applied = image_ref[:, at] + other
            if mode == "load":
                resid = applied
            else:
                direction = precon_ref[:, at]
                if mode == "next":
                    direction_in, applied_in, field_in = olds
                    direction = direction + beta * direction_in[:, at]
                    applied = applied + beta * applied_in[:, at]
                    news[1][:, at] = field_in[:, at] + alpha * direction
                else:
                    news[1][:, at] = alpha * direction
                resid = resid_in[:, at] - alpha * applied
                if len(news) > 2:
                    news[2][:, at] = direction
                    news[3][:, at] = applied
            news[0][:, at] = resid
            if scaled is not None:
                scaled[:, pl.ds(slot * edge_len + start, CHUNK)] = (place.weight(slot) * resid).astype(BF16)


def whole_product(place, vec_ref, matrix_ref, slot, start):
    edge_len = vec_ref.shape[1] // 4
    column = pl.multiple_of(place.edges[slot] * edge_len + start, CHUNK)
    total = None
    for i in range(4):
        row = pl.multiple_of(place.edges[i] * edge_len, edge_len)
        block = matrix_ref[pl.ds(row, edge_len), pl.ds(column, CHUNK)]
        part = jnp.dot(vec_ref[:, i * edge_len : (i + 1) * edge_len], block, preferred_element_type=F32)
        total = part if total is None else total + part
    return total


OLD = {"load": 0, "init": 2, "next": 5}


def scalar_kernel(mode, last, gathered_ref, *refs):
    refs = list(refs)
    state_in, coarse_in, applied_in, state_ref = None, None, None, None
    if mode == "next":
        state_in = refs.pop(0)
    if not last:
        if mode != "load":
            coarse_in = refs.pop(0)
        if mode == "next":
            applied_in = refs.pop(0)
        level_mat_ref, ramp_mat_ref = refs.pop(0), refs.pop(0)
    columns_ref = refs.pop(0)
    rows = []
    if mode == "load":
        coarse_ref, = refs
        coarse_table(gathered_ref, coarse_ref)
        coarse = coarse_ref[...]
        rows.append(jnp.zeros((8, LANES), F32))
    else:
        if not last:
            state_ref, coarse_ref, applied_ref = refs
        alpha, beta = scalars(mode, gathered_ref, state_in, state_ref, columns_ref.shape[0])
        rows += [alpha, beta, jnp.zeros((6, LANES), F32)]
        if not last:
            coarse_table(gathered_ref, applied_ref)
            if mode == "next":
                applied_ref[...] = applied_ref[...] + beta * applied_in[...]
            coarse = coarse_in[...] - alpha * applied_ref[...]
            coarse_ref[...] = coarse
    if not last:
        solved = jnp.dot(level_mat_ref[...], coarse, precision=HP, preferred_element_type=F32)
        ramped = jnp.dot(ramp_mat_ref[...], coarse, precision=HP, preferred_element_type=F32)
        rows.append(solved + pltpu.roll(ramped, LANES // 2, 1))
    columns_ref[...] = turn(rows, columns_ref.shape[0])


def step_kernel(mode, *refs):
    refs = list(refs)
    take = lambda n: [refs.pop(0) for _ in range(n)]
    place = Place()
    images, edges, (columns_ref,) = take(2), take(4), take(1)
    olds = [take(OLD[mode]) for _ in range(2)]
    inverse_ref, = take(1)
    news = [take(1 if mode == "load" else 4) for _ in range(2)]
    halves, (gamma_ref,), edge_refs, (scaled,) = take(2), take(1), take(4), take(1)
    edge_len = edges[0].shape[1]
    columns = columns_ref[...]
    for half in range(2):
        precon_ref, *old = olds[half] or [None, None]
        step_half(place, half, mode, images[half], edges[2 * half : 2 * half + 2], columns, precon_ref, old, news[half], scaled)
    gamma = None
    for slot, edge_ref in enumerate(edge_refs):
        flat, ramp_by = (columns[:, 8 + 2 * slot + i : 9 + 2 * slot + i] for i in range(2))
        for start in range(0, edge_len, CHUNK):
            level, ramp = basis_parts(edge_len, start, CHUNK)
            part = whole_product(place, scaled, inverse_ref, slot, start)
            part = place.weight(slot) * (part + (flat * level + ramp_by * ramp))
            at = pl.ds(slot % 2 * edge_len + start, CHUNK)
            halves[slot // 2][:, at] = part
            edge_ref[:, pl.ds(start, CHUNK)] = part.astype(edge_ref.dtype)
            here = lane_parts(news[slot // 2][0][:, at] * part)
            gamma = here if gamma is None else gamma + here
    gamma_ref[...] = gamma


def last_kernel(mode, *refs):
    refs = list(refs)
    take = lambda n: [refs.pop(0) for _ in range(n)]
    place = Place()
    images, edges, (columns_ref,) = take(2), take(4), take(1)
    olds = [take(OLD[mode]) for _ in range(2)]
    field_ref, resid_ref = take(2)
    news = [take(2) for _ in range(2)]
    edge_len = edges[0].shape[1]
    columns = columns_ref[...]
    for half in range(2):
        precon_ref, *old = olds[half]
        step_half(place, half, mode, images[half], edges[2 * half : 2 * half + 2], columns, precon_ref, old, news[half], None)
        for i in range(2):
            to = pl.ds(pl.multiple_of(place.edges[2 * half + i] * edge_len, edge_len), edge_len)
            at = pl.ds(i * edge_len, edge_len)
            resid_ref[:, to] = news[half][0][:, at]
            field_ref[:, to] = news[half][1][:, at]


def gather(message):
    return lax.all_to_all(message, AXES, split_axis=0, concat_axis=0, tiled=True)


def body(obs_values, obs_dest, obs_node, schur, local_inverse, coarse_inverse):
    size = schur.shape[-1]
    obs_count, realiz = obs_values.shape
    cols, rows = lax.axis_size("sx"), lax.axis_size("sy")
    devices = cols * rows
    capacity = max(2, 2 * obs_count // devices)
    edges = [shape(realiz, size // 4, BF16)] * 4
    exact = [shape(realiz + PAD, size // 4)] * 4
    half, whole = shape(realiz, size // 2), shape(realiz, size)
    message = jax.ShapeDtypeStruct((devices, 1, 5 * LANES), F32)
    narrow, state_shape = shape(realiz, LANES), shape(8, LANES)
    coarse_state = shape(4 * devices, LANES)
    scratch_half, scratch_whole = pltpu.VMEM((realiz, size // 2), BF16), pltpu.VMEM((realiz, size), BF16)
    flops = 2 * realiz * size * size
    schur_mat, inverse_mat = schur[0, 0], local_inverse[0, 0]

    packed = call(
        functools.partial(pack_kernel, capacity),
        shape(devices * capacity, LANES, BF16),
        (obs_values.T, obs_dest.reshape(1, obs_count), obs_node.reshape(1, obs_count)),
        flops=COVER,
    )
    coarse_mats = call(
        functools.partial(coarse_kernel, cols, rows), [shape(8, 4 * devices)] * 2, (coarse_inverse,)
    )
    packed, *coarse_mats = lax.optimization_barrier((packed, *coarse_mats))
    got = lax.all_to_all(packed.reshape(devices, capacity, LANES), AXES, split_axis=0, concat_axis=0, tiled=True)
    *image, e0, e1, e2, e3, sent = call(
        functools.partial(load_kernel, realiz),
        [half, half, *exact, message],
        (got.reshape(devices * capacity, LANES),),
        flops=COVER,
    )
    mode, olds, states = "load", ([], []), []
    for step in range(ITERS + 1):
        last = step == ITERS
        g, gathered = exchange((e0, e1, e2, e3)), gather(sent)
        new_states = [] if last else [state_shape, coarse_state, coarse_state][1 if mode == "load" else 0 :]
        new_states = new_states[:1] if mode == "load" else new_states
        columns, *states = call(
            functools.partial(scalar_kernel, mode, last),
            [narrow, *new_states],
            (gathered, *states[:1]) if last else (gathered, *states, *coarse_mats),
        )
        ins = [*image, *g, columns, *olds[0], *olds[1]]
        if last:
            scratch = [pltpu.VMEM((realiz, size // 2), F32)] * 4
            field, resid = call(functools.partial(last_kernel, mode), [whole, whole], ins, scratch)
            return field[None, None], resid[None, None]
        count = 1 if mode == "load" else 4
        outs = call(
            functools.partial(step_kernel, mode),
            [*[half] * (2 * count), half, half, narrow, *edges],
            [*ins, inverse_mat],
            [scratch_whole],
            flops,
        )
        near, far, outs = outs[:count], outs[count : 2 * count], outs[2 * count :]
        part_near, part_far, gamma, e0, e1, e2, e3 = outs
        g = exchange((e0, e1, e2, e3))
        z_near, partial = call(
            image_near_kernel, [half, whole], (part_near, g[0], g[1], schur_mat), [scratch_half], flops // 2
        )
        z_far, *image, e0, e1, e2, e3, sent = call(
            image_far_kernel,
            [half, half, half, *exact, message],
            (part_far, g[2], g[3], z_near, partial, gamma, schur_mat),
            [scratch_half],
            flops // 2,
        )
        mode = "init" if step == 0 else "next"
        olds = [[z, new[0]] + ([] if step == 0 else [new[2], new[3], new[1]]) for z, new in ((z_near, near), (z_far, far))]


def solution(mesh):
    placed = (
        P(AXES, None),
        P(AXES, None),
        P(AXES),
        P("sx", "sy", None, None),
        P("sx", "sy", None, None),
        P(AXES, None),
    )
    return jax.shard_map(
        body,
        mesh=mesh,
        in_specs=placed,
        out_specs=(P("sx", "sy", None, None), P("sx", "sy", None, None)),
        check_vma=False,
    )
```

time: 1220 us -> 175 us (0.14); the launches traced: 1210 us -> 175 us
  blocking collectives: 791 us -> 96.5 us
  starting transfers between devices: 152 us -> 26.8 us
  waiting for transfers between devices: 134 us -> 18.1 us
  matrix products: 83.9 us -> 0 us
  Pallas kernels: 0 us -> 29.7 us
  other arithmetic: 27.3 us -> 0.01 us
    psum x11 -> x0, blocking collectives: 545 us -> none  [the longest x6 291 us: products(): return lax.psum(jnp.sum(weight * left * right, axis=1), ('sx', 'sy'))]
    all_gather x6 -> x0, blocking collectives: 246 us -> none  [gather_coarse(): return lax.all_gather(coarse_local, ('sx', 'sy'), axis=0, tiled=True)]
    ppermute x52, starting transfers between devices: 143 us -> 26.8 us  [exchange(): got[slot] = lax.ppermute(edges[slot], AXES, plans[slot])]
    ppermute x52, waiting for transfers between devices: 124 us -> 18.1 us  [exchange(): got[slot] = lax.ppermute(edges[slot], AXES, plans[slot])]
    all_to_all x0 -> x8, blocking collectives: none -> 96.5 us  [the longest x7 81.1 us: gather(): lax.all_to_all(message, AXES, split_axis=0, concat_axis=0, tiled=True)]
    dot_general x30 -> x0, matrix products: 83.9 us -> none  [the longest x6 30 us: precond(): jnp.dot(scaled.astype(jnp.bfloat16), inverse_mat, preferred_element_type=...]
    pallas_call x0 -> x29, Pallas kernels: none -> 29.7 us  [call(): pl.pallas_call(kernel, out_shape=outs, in_specs=[VM] * len(args), out_spe...]
  transfers between devices with their start and end apart: 54 -> 52, of which waited for: 41 -> 12; matrix products, arithmetic and copies ran while one was open for 0% -> 0% of each run, Pallas kernels for 0% -> 5%
where the time goes in v3:
time: 175 us
  blocking collectives  96.5 us (55%)
  Pallas kernels  29.7 us (17%)
  starting transfers between devices  26.8 us (15%)
  waiting for transfers between devices  18.1 us (10%)
  local copies, waits for them, and re-layouts  2.83 us (2%)
    all_to_all x7, blocking collectives, gather(): lax.all_to_all(message, AXES, split_axis=0, concat_axis=0, tiled=True)  81.1 us
    pallas_call x29, Pallas kernels, call(): pl.pallas_call(kernel, out_shape=outs, in_specs=[VM] * len(args), out_spe...  29.7 us
    ppermute x52, starting transfers between devices, exchange(): got[slot] = lax.ppermute(edges[slot], AXES, plans[slot])  26.8 us
    ppermute x52, waiting for transfers between devices, exchange(): got[slot] = lax.ppermute(edges[slot], AXES, plans[slot])  18.1 us
    all_to_all x1, blocking collectives, body(): lax.all_to_all(packed.reshape(devices, capacity, LANES), AXES, split_axis...  15.3 us
  transfers between devices with their start and end apart: 52, of which 12 were waited for; matrix products, arithmetic and copies ran while one was open for 0% of the time, Pallas kernels for 5%

profile of v3, /device:TPU:0, one launch (start us, length us, event | category | flops | bytes accessed | tf_op | source)
XLA Modules:
  0.0 175.0 jit_solution(18340754416768022290)
XLA Ops:
  4.2 15.3 %all_to_all.40 = bf16[32,16,128]{2,1,0:T(8,128)(2,1)S(1)} all-to-all(bf16[32,16,128]{2,1,0:T(8,128)(2,1)S(1)} %bitcast.32), channel_id=1, replica_groups=mesh['sx'=8,'sy'=4] {'sx','sy'}, dimensions={0} | all-to-all | bytes 262144 | tf_op jit(solution)/shard_map/all_to_all | solution.py:438
  22.1 11.2 %all_to_all.41.gathered_ref = f32[32,1,640]{2,1,0:T(1,128)S(1)} all-to-all(f32[32,1,640]{2,1,0:T(1,128)S(1)} %get-tuple-element.189), channel_id=1, replica_groups=mesh['sx'=8,'sy'=4] {'sx','sy'}, dimensions={0} | all-to-all | bytes 163840 | tf_op jit(solution)/shard_map/all_to_all | solution.py:409
  33.7 1.7 shard_map.81
  37.0 2.8 %collective-permute-done.6.g0 = bf16[64,512]{1,0:T(8,128)(2,1)S(1)} collective-permute-done((bf16[64,512]{1,0:T(8,128)(2,1)S(1)}, bf16[64,512]{1,0:T(8,128)(2,1)S(1)}, u32[]{:S(2)}, u32[]{:S(2)}) %collective-permute-start.6) | collective-permute-done | bytes 65568 | tf_op jit(solution)/shard_map/ppermute | solution.py:76
  40.9 1.2 shard_map.83
  42.1 2.2 %collective-permute-start.8 = (f32[80,512]{1,0:T(8,128)S(1)}, f32[80,512]{1,0:T(8,128)S(1)}, u32[]{:S(2)}, u32[]{:S(2)}) collective-permute-start(f32[80,512]{1,0:T(8,128)S(1)} %get-tuple-element.204), channel_id=1, source_target_pairs={{0,4},{1,5},{2,6},{3,7},{4,0},{5,1},{6,2},{7,3},{8,12},{9,13},{10,... | collective-permute-start | bytes 491528 | tf_op jit(solution)/shard_map/ppermute | solution.py:76
  44.8 11.7 %all_to_all.42.gathered_ref = f32[32,1,640]{2,1,0:T(1,128)S(1)} all-to-all(f32[32,1,640]{2,1,0:T(1,128)S(1)} %get-tuple-element.208), channel_id=1, replica_groups=mesh['sx'=8,'sy'=4] {'sx','sy'}, dimensions={0} | all-to-all | bytes 163840 | tf_op jit(solution)/shard_map/all_to_all | solution.py:409
  56.9 1.8 %shard_map.85 = (f32[64,1024]{1,0:T(8,128)S(1)}, f32[64,1024]{1,0:T(8,128)S(1)}, f32[64,1024]{1,0:T(8,128)S(1)}, f32[64,1024]{1,0:T(8,128)S(1)}, f32[64,1024]{1,...) custom-call(f32[64,1024]{1,0:T(8,128)S(1)} %get-tuple-element.202.re, ...), custom_call_target="tpu_custom_call" | custom-call | flops 536870912 | bytes 10649600 | tf_op jit(solution)/shard_map/pallas_call | solution.py:24
  60.3 2.8 %collective-permute-done.14.g0 = bf16[64,512]{1,0:T(8,128)(2,1)S(1)} collective-permute-done((bf16[64,512]{1,0:T(8,128)(2,1)S(1)}, bf16[64,512]{1,0:T(8,128)(2,1)S(1)}, u32[]{:S(2)}, u32[]{:S(2)}) %collective-permute-start.14) | collective-permute-done | bytes 65568 | tf_op jit(solution)/shard_map/ppermute | solution.py:76
  64.2 1.2 shard_map.87
  65.4 2.2 %collective-permute-start.16 = (f32[80,512]{1,0:T(8,128)S(1)}, f32[80,512]{1,0:T(8,128)S(1)}, u32[]{:S(2)}, u32[]{:S(2)}) collective-permute-start(f32[80,512]{1,0:T(8,128)S(1)} %get-tuple-element.225), channel_id=1, source_target_pairs={{0,4},{1,5},{2,6},{3,7},{4,0},{5,1},{6,2},{7,3},{8,12},{9,13},{10,... | collective-permute-start | bytes 491528 | tf_op jit(solution)/shard_map/ppermute | solution.py:76
  68.1 11.7 %all_to_all.43.gathered_ref = f32[32,1,640]{2,1,0:T(1,128)S(1)} all-to-all(f32[32,1,640]{2,1,0:T(1,128)S(1)} %get-tuple-element.229), channel_id=1, replica_groups=mesh['sx'=8,'sy'=4] {'sx','sy'}, dimensions={0} | all-to-all | bytes 163840 | tf_op jit(solution)/shard_map/all_to_all | solution.py:409
  80.3 1.9 %shard_map.89 = (f32[64,1024]{1,0:T(8,128)S(1)}, f32[64,1024]{1,0:T(8,128)S(1)}, f32[64,1024]{1,0:T(8,128)S(1)}, f32[64,1024]{1,0:T(8,128)S(1)}, f32[64,1024]{1,...) custom-call(f32[64,1024]{1,0:T(8,128)S(1)} %get-tuple-element.223.re, ...), custom_call_target="tpu_custom_call" | custom-call | flops 536870912 | bytes 12222464 | tf_op jit(solution)/shard_map/pallas_call | solution.py:24
  83.7 2.9 %collective-permute-done.22.g0 = bf16[64,512]{1,0:T(8,128)(2,1)S(1)} collective-permute-done((bf16[64,512]{1,0:T(8,128)(2,1)S(1)}, bf16[64,512]{1,0:T(8,128)(2,1)S(1)}, u32[]{:S(2)}, u32[]{:S(2)}) %collective-permute-start.22) | collective-permute-done | bytes 65568 | tf_op jit(solution)/shard_map/ppermute | solution.py:76
  87.5 1.2 shard_map.91
  88.8 2.2 %collective-permute-start.24 = (f32[80,512]{1,0:T(8,128)S(1)}, f32[80,512]{1,0:T(8,128)S(1)}, u32[]{:S(2)}, u32[]{:S(2)}) collective-permute-start(f32[80,512]{1,0:T(8,128)S(1)} %get-tuple-element.254), channel_id=1, source_target_pairs={{0,4},{1,5},{2,6},{3,7},{4,0},{5,1},{6,2},{7,3},{8,12},{9,13},{10,... | collective-permute-start | bytes 491528 | tf_op jit(solution)/shard_map/ppermute | solution.py:76
  91.5 11.7 %all_to_all.44.gathered_ref = f32[32,1,640]{2,1,0:T(1,128)S(1)} all-to-all(f32[32,1,640]{2,1,0:T(1,128)S(1)} %get-tuple-element.258), channel_id=1, replica_groups=mesh['sx'=8,'sy'=4] {'sx','sy'}, dimensions={0} | all-to-all | bytes 163840 | tf_op jit(solution)/shard_map/all_to_all | solution.py:409
  103.6 1.9 %shard_map.93 = (f32[64,1024]{1,0:T(8,128)S(1)}, f32[64,1024]{1,0:T(8,128)S(1)}, f32[64,1024]{1,0:T(8,128)S(1)}, f32[64,1024]{1,0:T(8,128)S(1)}, f32[64,1024]{1,...) custom-call(f32[64,1024]{1,0:T(8,128)S(1)} %get-tuple-element.252.re, ...), custom_call_target="tpu_custom_call" | custom-call | flops 536870912 | bytes 12222464 | tf_op jit(solution)/shard_map/pallas_call | solution.py:24
  107.0 2.9 %collective-permute-done.30.g0 = bf16[64,512]{1,0:T(8,128)(2,1)S(1)} collective-permute-done((bf16[64,512]{1,0:T(8,128)(2,1)S(1)}, bf16[64,512]{1,0:T(8,128)(2,1)S(1)}, u32[]{:S(2)}, u32[]{:S(2)}) %collective-permute-start.30) | collective-permute-done | bytes 65568 | tf_op jit(solution)/shard_map/ppermute | solution.py:76
  112.1 2.2 %collective-permute-start.32 = (f32[80,512]{1,0:T(8,128)S(1)}, f32[80,512]{1,0:T(8,128)S(1)}, u32[]{:S(2)}, u32[]{:S(2)}) collective-permute-start(f32[80,512]{1,0:T(8,128)S(1)} %get-tuple-element.283), channel_id=1, source_target_pairs={{0,4},{1,5},{2,6},{3,7},{4,0},{5,1},{6,2},{7,3},{8,12},{9,13},{10,... | collective-permute-start | bytes 491528 | tf_op jit(solution)/shard_map/ppermute | solution.py:76
  114.9 11.6 %all_to_all.45.gathered_ref = f32[32,1,640]{2,1,0:T(1,128)S(1)} all-to-all(f32[32,1,640]{2,1,0:T(1,128)S(1)} %get-tuple-element.287), channel_id=1, replica_groups=mesh['sx'=8,'sy'=4] {'sx','sy'}, dimensions={0} | all-to-all | bytes 163840 | tf_op jit(solution)/shard_map/all_to_all | solution.py:409
  127.0 1.9 %shard_map.97 = (f32[64,1024]{1,0:T(8,128)S(1)}, f32[64,1024]{1,0:T(8,128)S(1)}, f32[64,1024]{1,0:T(8,128)S(1)}, f32[64,1024]{1,0:T(8,128)S(1)}, f32[64,1024]{1,...) custom-call(f32[64,1024]{1,0:T(8,128)S(1)} %get-tuple-element.281.re, ...), custom_call_target="tpu_custom_call" | custom-call | flops 536870912 | bytes 12222464 | tf_op jit(solution)/shard_map/pallas_call | solution.py:24
  130.4 2.9 %collective-permute-done.38.g0 = bf16[64,512]{1,0:T(8,128)(2,1)S(1)} collective-permute-done((bf16[64,512]{1,0:T(8,128)(2,1)S(1)}, bf16[64,512]{1,0:T(8,128)(2,1)S(1)}, u32[]{:S(2)}, u32[]{:S(2)}) %collective-permute-start.38) | collective-permute-done | bytes 65568 | tf_op jit(solution)/shard_map/ppermute | solution.py:76
  134.3 1.2 shard_map.99
  135.5 2.2 %collective-permute-start.40 = (f32[80,512]{1,0:T(8,128)S(1)}, f32[80,512]{1,0:T(8,128)S(1)}, u32[]{:S(2)}, u32[]{:S(2)}) collective-permute-start(f32[80,512]{1,0:T(8,128)S(1)} %get-tuple-element.312), channel_id=1, source_target_pairs={{0,4},{1,5},{2,6},{3,7},{4,0},{5,1},{6,2},{7,3},{8,12},{9,13},{10,... | collective-permute-start | bytes 491528 | tf_op jit(solution)/shard_map/ppermute | solution.py:76
  138.2 11.7 %all_to_all.46.gathered_ref = f32[32,1,640]{2,1,0:T(1,128)S(1)} all-to-all(f32[32,1,640]{2,1,0:T(1,128)S(1)} %get-tuple-element.316), channel_id=1, replica_groups=mesh['sx'=8,'sy'=4] {'sx','sy'}, dimensions={0} | all-to-all | bytes 163840 | tf_op jit(solution)/shard_map/all_to_all | solution.py:409
  150.7 1.9 %shard_map.101 = (f32[64,1024]{1,0:T(8,128)S(1)}, f32[64,1024]{1,0:T(8,128)S(1)}, f32[64,1024]{1,0:T(8,128)S(1)}, f32[64,1024]{1,0:T(8,128)S(1)}, f32[64,1024]{1...) custom-call(f32[64,1024]{1,0:T(8,128)S(1)} %get-tuple-element.310.re, ...), custom_call_target="tpu_custom_call" | custom-call | flops 536870912 | bytes 12222464 | tf_op jit(solution)/shard_map/pallas_call | solution.py:24
  154.1 2.9 %collective-permute-done.46.g0 = bf16[64,512]{1,0:T(8,128)(2,1)S(1)} collective-permute-done((bf16[64,512]{1,0:T(8,128)(2,1)S(1)}, bf16[64,512]{1,0:T(8,128)(2,1)S(1)}, u32[]{:S(2)}, u32[]{:S(2)}) %collective-permute-start.46) | collective-permute-done | bytes 65568 | tf_op jit(solution)/shard_map/ppermute | solution.py:76
  158.0 1.2 shard_map.103
  159.2 2.2 %collective-permute-start.48 = (f32[80,512]{1,0:T(8,128)S(1)}, f32[80,512]{1,0:T(8,128)S(1)}, u32[]{:S(2)}, u32[]{:S(2)}) collective-permute-start(f32[80,512]{1,0:T(8,128)S(1)} %get-tuple-element.341), channel_id=1, source_target_pairs={{0,4},{1,5},{2,6},{3,7},{4,0},{5,1},{6,2},{7,3},{8,12},{9,13},{10,... | collective-permute-start | bytes 491528 | tf_op jit(solution)/shard_map/ppermute | solution.py:76
  161.9 11.7 %all_to_all.47.gathered_ref = f32[32,1,640]{2,1,0:T(1,128)S(1)} all-to-all(f32[32,1,640]{2,1,0:T(1,128)S(1)} %get-tuple-element.345), channel_id=1, replica_groups=mesh['sx'=8,'sy'=4] {'sx','sy'}, dimensions={0} | all-to-all | bytes 163840 | tf_op jit(solution)/shard_map/all_to_all | solution.py:409
  173.8 1.3 shard_map.105
  (127 shorter events, 28.7 us)
Async XLA Ops:
  20.5 13.2 %collective-permute-start = (f32[80,512]{1,0:T(8,128)S(1)}, f32[80,512]{1,0:T(8,128)S(1)}, u32[]{:S(2)}, u32[]{:S(2)}) collective-permute-start(f32[80,512]{1,0:T(8,128)S(1)} %get-tuple-element.185), channel_id=1, source_target_pairs={{0,4},{1,5},{2,6},{3,7},{4,0},{5,1},{6,2},{7,3},{8,12},{9,13},{10,... | collective-permute-start | bytes 491528 | tf_op jit(solution)/shard_map/ppermute | solution.py:76
  21.2 12.5 %collective-permute-start.1 = (f32[80,512]{1,0:T(8,128)S(1)}, f32[80,512]{1,0:T(8,128)S(1)}, u32[]{:S(2)}, u32[]{:S(2)}) collective-permute-start(f32[80,512]{1,0:T(8,128)S(1)} %get-tuple-element.186), channel_id=1, source_target_pairs={{0,1},{1,0},{2,3},{3,2},{4,5},{5,4},{6,7},{7,6},{8,9},{9,8},{10,11... | collective-permute-start | bytes 491528 | tf_op jit(solution)/shard_map/ppermute | solution.py:76
  21.2 12.5 %collective-permute-start.2 = (f32[80,512]{1,0:T(8,128)S(1)}, f32[80,512]{1,0:T(8,128)S(1)}, u32[]{:S(2)}, u32[]{:S(2)}) collective-permute-start(f32[80,512]{1,0:T(8,128)S(1)} %get-tuple-element.187), channel_id=1, source_target_pairs={{0,1},{1,0},{2,3},{3,2},{4,8},{5,9},{6,10},{7,11},{8,4},{9,5},{10,... | collective-permute-start | bytes 491528 | tf_op jit(solution)/shard_map/ppermute | solution.py:76
  21.7 12.0 %collective-permute-start.3 = (f32[80,512]{1,0:T(8,128)S(1)}, f32[80,512]{1,0:T(8,128)S(1)}, u32[]{:S(2)}, u32[]{:S(2)}) collective-permute-start(f32[80,512]{1,0:T(8,128)S(1)} %get-tuple-element.188), channel_id=1, source_target_pairs={{0,3},{1,2},{2,1},{3,0},{4,7},{5,6},{6,5},{7,4},{8,11},{9,10},{10,... | collective-permute-start | bytes 491528 | tf_op jit(solution)/shard_map/ppermute | solution.py:76
  42.1 14.8 %collective-permute-start.8 = (f32[80,512]{1,0:T(8,128)S(1)}, f32[80,512]{1,0:T(8,128)S(1)}, u32[]{:S(2)}, u32[]{:S(2)}) collective-permute-start(f32[80,512]{1,0:T(8,128)S(1)} %get-tuple-element.204), channel_id=1, source_target_pairs={{0,4},{1,5},{2,6},{3,7},{4,0},{5,1},{6,2},{7,3},{8,12},{9,13},{10,... | collective-permute-start | bytes 491528 | tf_op jit(solution)/shard_map/ppermute | solution.py:76
  44.3 12.6 %collective-permute-start.9 = (f32[80,512]{1,0:T(8,128)S(1)}, f32[80,512]{1,0:T(8,128)S(1)}, u32[]{:S(2)}, u32[]{:S(2)}) collective-permute-start(f32[80,512]{1,0:T(8,128)S(1)} %get-tuple-element.205), channel_id=1, source_target_pairs={{0,1},{1,0},{2,3},{3,2},{4,5},{5,4},{6,7},{7,6},{8,9},{9,8},{10,11... | collective-permute-start | bytes 491528 | tf_op jit(solution)/shard_map/ppermute | solution.py:76
  44.3 12.6 %collective-permute-start.10 = (f32[80,512]{1,0:T(8,128)S(1)}, f32[80,512]{1,0:T(8,128)S(1)}, u32[]{:S(2)}, u32[]{:S(2)}) collective-permute-start(f32[80,512]{1,0:T(8,128)S(1)} %get-tuple-element.206), channel_id=1, source_target_pairs={{0,1},{1,0},{2,3},{3,2},{4,8},{5,9},{6,10},{7,11},{8,4},{9,5},{10,... | collective-permute-start | bytes 491528 | tf_op jit(solution)/shard_map/ppermute | solution.py:76
  44.8 12.2 %collective-permute-start.11 = (f32[80,512]{1,0:T(8,128)S(1)}, f32[80,512]{1,0:T(8,128)S(1)}, u32[]{:S(2)}, u32[]{:S(2)}) collective-permute-start(f32[80,512]{1,0:T(8,128)S(1)} %get-tuple-element.207), channel_id=1, source_target_pairs={{0,3},{1,2},{2,1},{3,0},{4,7},{5,6},{6,5},{7,4},{8,11},{9,10},{10,... | collective-permute-start | bytes 491528 | tf_op jit(solution)/shard_map/ppermute | solution.py:76
  65.4 14.8 %collective-permute-start.16 = (f32[80,512]{1,0:T(8,128)S(1)}, f32[80,512]{1,0:T(8,128)S(1)}, u32[]{:S(2)}, u32[]{:S(2)}) collective-permute-start(f32[80,512]{1,0:T(8,128)S(1)} %get-tuple-element.225), channel_id=1, source_target_pairs={{0,4},{1,5},{2,6},{3,7},{4,0},{5,1},{6,2},{7,3},{8,12},{9,13},{10,... | collective-permute-start | bytes 491528 | tf_op jit(solution)/shard_map/ppermute | solution.py:76
  67.6 12.6 %collective-permute-start.17 = (f32[80,512]{1,0:T(8,128)S(1)}, f32[80,512]{1,0:T(8,128)S(1)}, u32[]{:S(2)}, u32[]{:S(2)}) collective-permute-start(f32[80,512]{1,0:T(8,128)S(1)} %get-tuple-element.226), channel_id=1, source_target_pairs={{0,1},{1,0},{2,3},{3,2},{4,5},{5,4},{6,7},{7,6},{8,9},{9,8},{10,11... | collective-permute-start | bytes 491528 | tf_op jit(solution)/shard_map/ppermute | solution.py:76
  67.6 12.6 %collective-permute-start.18 = (f32[80,512]{1,0:T(8,128)S(1)}, f32[80,512]{1,0:T(8,128)S(1)}, u32[]{:S(2)}, u32[]{:S(2)}) collective-permute-start(f32[80,512]{1,0:T(8,128)S(1)} %get-tuple-element.227), channel_id=1, source_target_pairs={{0,1},{1,0},{2,3},{3,2},{4,8},{5,9},{6,10},{7,11},{8,4},{9,5},{10,... | collective-permute-start | bytes 491528 | tf_op jit(solution)/shard_map/ppermute | solution.py:76
  68.1 12.2 %collective-permute-start.19 = (f32[80,512]{1,0:T(8,128)S(1)}, f32[80,512]{1,0:T(8,128)S(1)}, u32[]{:S(2)}, u32[]{:S(2)}) collective-permute-start(f32[80,512]{1,0:T(8,128)S(1)} %get-tuple-element.228), channel_id=1, source_target_pairs={{0,3},{1,2},{2,1},{3,0},{4,7},{5,6},{6,5},{7,4},{8,11},{9,10},{10,... | collective-permute-start | bytes 491528 | tf_op jit(solution)/shard_map/ppermute | solution.py:76
  82.8 4.6 %collective-permute-start.20 = (bf16[64,512]{1,0:T(8,128)(2,1)S(1)}, bf16[64,512]{1,0:T(8,128)(2,1)S(1)}, u32[]{:S(2)}, u32[]{:S(2)}) collective-permute-start(bf16[64,512]{1,0:T(8,128)(2,1)S(1)} %get-tuple-element.244), channel_id=1, source_target_pairs={{0,1},{1,0},{2,3},{3,2},{4,8},{5,9},{6,10},{7,11},{8,4},{9,5},{10,... | collective-permute-start | bytes 196616 | tf_op jit(solution)/shard_map/ppermute | solution.py:76
  88.8 14.8 %collective-permute-start.24 = (f32[80,512]{1,0:T(8,128)S(1)}, f32[80,512]{1,0:T(8,128)S(1)}, u32[]{:S(2)}, u32[]{:S(2)}) collective-permute-start(f32[80,512]{1,0:T(8,128)S(1)} %get-tuple-element.254), channel_id=1, source_target_pairs={{0,4},{1,5},{2,6},{3,7},{4,0},{5,1},{6,2},{7,3},{8,12},{9,13},{10,... | collective-permute-start | bytes 491528 | tf_op jit(solution)/shard_map/ppermute | solution.py:76
  91.0 12.6 %collective-permute-start.25 = (f32[80,512]{1,0:T(8,128)S(1)}, f32[80,512]{1,0:T(8,128)S(1)}, u32[]{:S(2)}, u32[]{:S(2)}) collective-permute-start(f32[80,512]{1,0:T(8,128)S(1)} %get-tuple-element.255), channel_id=1, source_target_pairs={{0,1},{1,0},{2,3},{3,2},{4,5},{5,4},{6,7},{7,6},{8,9},{9,8},{10,11... | collective-permute-start | bytes 491528 | tf_op jit(solution)/shard_map/ppermute | solution.py:76
  91.0 12.7 %collective-permute-start.26 = (f32[80,512]{1,0:T(8,128)S(1)}, f32[80,512]{1,0:T(8,128)S(1)}, u32[]{:S(2)}, u32[]{:S(2)}) collective-permute-start(f32[80,512]{1,0:T(8,128)S(1)} %get-tuple-element.256), channel_id=1, source_target_pairs={{0,1},{1,0},{2,3},{3,2},{4,8},{5,9},{6,10},{7,11},{8,4},{9,5},{10,... | collective-permute-start | bytes 491528 | tf_op jit(solution)/shard_map/ppermute | solution.py:76
  91.5 12.2 %collective-permute-start.27 = (f32[80,512]{1,0:T(8,128)S(1)}, f32[80,512]{1,0:T(8,128)S(1)}, u32[]{:S(2)}, u32[]{:S(2)}) collective-permute-start(f32[80,512]{1,0:T(8,128)S(1)} %get-tuple-element.257), channel_id=1, source_target_pairs={{0,3},{1,2},{2,1},{3,0},{4,7},{5,6},{6,5},{7,4},{8,11},{9,10},{10,... | collective-permute-start | bytes 491528 | tf_op jit(solution)/shard_map/ppermute | solution.py:76
  106.2 4.6 %collective-permute-start.28 = (bf16[64,512]{1,0:T(8,128)(2,1)S(1)}, bf16[64,512]{1,0:T(8,128)(2,1)S(1)}, u32[]{:S(2)}, u32[]{:S(2)}) collective-permute-start(bf16[64,512]{1,0:T(8,128)(2,1)S(1)} %get-tuple-element.273), channel_id=1, source_target_pairs={{0,1},{1,0},{2,3},{3,2},{4,8},{5,9},{6,10},{7,11},{8,4},{9,5},{10,... | collective-permute-start | bytes 196616 | tf_op jit(solution)/shard_map/ppermute | solution.py:76
  112.1 14.8 %collective-permute-start.32 = (f32[80,512]{1,0:T(8,128)S(1)}, f32[80,512]{1,0:T(8,128)S(1)}, u32[]{:S(2)}, u32[]{:S(2)}) collective-permute-start(f32[80,512]{1,0:T(8,128)S(1)} %get-tuple-element.283), channel_id=1, source_target_pairs={{0,4},{1,5},{2,6},{3,7},{4,0},{5,1},{6,2},{7,3},{8,12},{9,13},{10,... | collective-permute-start | bytes 491528 | tf_op jit(solution)/shard_map/ppermute | solution.py:76
  114.3 12.6 %collective-permute-start.33 = (f32[80,512]{1,0:T(8,128)S(1)}, f32[80,512]{1,0:T(8,128)S(1)}, u32[]{:S(2)}, u32[]{:S(2)}) collective-permute-start(f32[80,512]{1,0:T(8,128)S(1)} %get-tuple-element.284), channel_id=1, source_target_pairs={{0,1},{1,0},{2,3},{3,2},{4,5},{5,4},{6,7},{7,6},{8,9},{9,8},{10,11... | collective-permute-start | bytes 491528 | tf_op jit(solution)/shard_map/ppermute | solution.py:76
  114.4 12.6 %collective-permute-start.34 = (f32[80,512]{1,0:T(8,128)S(1)}, f32[80,512]{1,0:T(8,128)S(1)}, u32[]{:S(2)}, u32[]{:S(2)}) collective-permute-start(f32[80,512]{1,0:T(8,128)S(1)} %get-tuple-element.285), channel_id=1, source_target_pairs={{0,1},{1,0},{2,3},{3,2},{4,8},{5,9},{6,10},{7,11},{8,4},{9,5},{10,... | collective-permute-start | bytes 491528 | tf_op jit(solution)/shard_map/ppermute | solution.py:76
  114.9 12.1 %collective-permute-start.35 = (f32[80,512]{1,0:T(8,128)S(1)}, f32[80,512]{1,0:T(8,128)S(1)}, u32[]{:S(2)}, u32[]{:S(2)}) collective-permute-start(f32[80,512]{1,0:T(8,128)S(1)} %get-tuple-element.286), channel_id=1, source_target_pairs={{0,3},{1,2},{2,1},{3,0},{4,7},{5,6},{6,5},{7,4},{8,11},{9,10},{10,... | collective-permute-start | bytes 491528 | tf_op jit(solution)/shard_map/ppermute | solution.py:76
  129.6 4.6 %collective-permute-start.36 = (bf16[64,512]{1,0:T(8,128)(2,1)S(1)}, bf16[64,512]{1,0:T(8,128)(2,1)S(1)}, u32[]{:S(2)}, u32[]{:S(2)}) collective-permute-start(bf16[64,512]{1,0:T(8,128)(2,1)S(1)} %get-tuple-element.302), channel_id=1, source_target_pairs={{0,1},{1,0},{2,3},{3,2},{4,8},{5,9},{6,10},{7,11},{8,4},{9,5},{10,... | collective-permute-start | bytes 196616 | tf_op jit(solution)/shard_map/ppermute | solution.py:76
  135.5 15.1 %collective-permute-start.40 = (f32[80,512]{1,0:T(8,128)S(1)}, f32[80,512]{1,0:T(8,128)S(1)}, u32[]{:S(2)}, u32[]{:S(2)}) collective-permute-start(f32[80,512]{1,0:T(8,128)S(1)} %get-tuple-element.312), channel_id=1, source_target_pairs={{0,4},{1,5},{2,6},{3,7},{4,0},{5,1},{6,2},{7,3},{8,12},{9,13},{10,... | collective-permute-start | bytes 491528 | tf_op jit(solution)/shard_map/ppermute | solution.py:76
  137.7 12.9 %collective-permute-start.41 = (f32[80,512]{1,0:T(8,128)S(1)}, f32[80,512]{1,0:T(8,128)S(1)}, u32[]{:S(2)}, u32[]{:S(2)}) collective-permute-start(f32[80,512]{1,0:T(8,128)S(1)} %get-tuple-element.313), channel_id=1, source_target_pairs={{0,1},{1,0},{2,3},{3,2},{4,5},{5,4},{6,7},{7,6},{8,9},{9,8},{10,11... | collective-permute-start | bytes 491528 | tf_op jit(solution)/shard_map/ppermute | solution.py:76
  137.7 12.9 %collective-permute-start.42 = (f32[80,512]{1,0:T(8,128)S(1)}, f32[80,512]{1,0:T(8,128)S(1)}, u32[]{:S(2)}, u32[]{:S(2)}) collective-permute-start(f32[80,512]{1,0:T(8,128)S(1)} %get-tuple-element.314), channel_id=1, source_target_pairs={{0,1},{1,0},{2,3},{3,2},{4,8},{5,9},{6,10},{7,11},{8,4},{9,5},{10,... | collective-permute-start | bytes 491528 | tf_op jit(solution)/shard_map/ppermute | solution.py:76
  138.2 12.4 %collective-permute-start.43 = (f32[80,512]{1,0:T(8,128)S(1)}, f32[80,512]{1,0:T(8,128)S(1)}, u32[]{:S(2)}, u32[]{:S(2)}) collective-permute-start(f32[80,512]{1,0:T(8,128)S(1)} %get-tuple-element.315), channel_id=1, source_target_pairs={{0,3},{1,2},{2,1},{3,0},{4,7},{5,6},{6,5},{7,4},{8,11},{9,10},{10,... | collective-permute-start | bytes 491528 | tf_op jit(solution)/shard_map/ppermute | solution.py:76
  153.2 4.6 %collective-permute-start.44 = (bf16[64,512]{1,0:T(8,128)(2,1)S(1)}, bf16[64,512]{1,0:T(8,128)(2,1)S(1)}, u32[]{:S(2)}, u32[]{:S(2)}) collective-permute-start(bf16[64,512]{1,0:T(8,128)(2,1)S(1)} %get-tuple-element.331), channel_id=1, source_target_pairs={{0,1},{1,0},{2,3},{3,2},{4,8},{5,9},{6,10},{7,11},{8,4},{9,5},{10,... | collective-permute-start | bytes 196616 | tf_op jit(solution)/shard_map/ppermute | solution.py:76
  159.2 14.6 %collective-permute-start.48 = (f32[80,512]{1,0:T(8,128)S(1)}, f32[80,512]{1,0:T(8,128)S(1)}, u32[]{:S(2)}, u32[]{:S(2)}) collective-permute-start(f32[80,512]{1,0:T(8,128)S(1)} %get-tuple-element.341), channel_id=1, source_target_pairs={{0,4},{1,5},{2,6},{3,7},{4,0},{5,1},{6,2},{7,3},{8,12},{9,13},{10,... | collective-permute-start | bytes 491528 | tf_op jit(solution)/shard_map/ppermute | solution.py:76
  161.4 12.4 %collective-permute-start.49 = (f32[80,512]{1,0:T(8,128)S(1)}, f32[80,512]{1,0:T(8,128)S(1)}, u32[]{:S(2)}, u32[]{:S(2)}) collective-permute-start(f32[80,512]{1,0:T(8,128)S(1)} %get-tuple-element.342), channel_id=1, source_target_pairs={{0,1},{1,0},{2,3},{3,2},{4,5},{5,4},{6,7},{7,6},{8,9},{9,8},{10,11... | collective-permute-start | bytes 491528 | tf_op jit(solution)/shard_map/ppermute | solution.py:76
  161.4 12.4 %collective-permute-start.50 = (f32[80,512]{1,0:T(8,128)S(1)}, f32[80,512]{1,0:T(8,128)S(1)}, u32[]{:S(2)}, u32[]{:S(2)}) collective-permute-start(f32[80,512]{1,0:T(8,128)S(1)} %get-tuple-element.343), channel_id=1, source_target_pairs={{0,1},{1,0},{2,3},{3,2},{4,8},{5,9},{6,10},{7,11},{8,4},{9,5},{10,... | collective-permute-start | bytes 491528 | tf_op jit(solution)/shard_map/ppermute | solution.py:76
  161.9 11.9 %collective-permute-start.51 = (f32[80,512]{1,0:T(8,128)S(1)}, f32[80,512]{1,0:T(8,128)S(1)}, u32[]{:S(2)}, u32[]{:S(2)}) collective-permute-start(f32[80,512]{1,0:T(8,128)S(1)} %get-tuple-element.344), channel_id=1, source_target_pairs={{0,3},{1,2},{2,1},{3,0},{4,7},{5,6},{6,5},{7,4},{8,11},{9,10},{10,... | collective-permute-start | bytes 491528 | tf_op jit(solution)/shard_map/ppermute | solution.py:76
  (28 other events, 169.9 us)

commit v4 on v3

--- a/solution.py
+++ b/solution.py
@@ -19,15 +19,15 @@
 AXES = ("sx", "sy")
 
 
-def call(kernel, outs, args, scratch=(), flops=0):
+def call(kernel, outs, args, scratch=(), flops=0, spec=VM):
     size = sum(a.size * a.dtype.itemsize for a in args)
     return pl.pallas_call(
         kernel,
         out_shape=outs,
-        in_specs=[VM] * len(args),
+        in_specs=[spec] * len(args),
         out_specs=jax.tree.map(lambda _: VM, outs),
         scratch_shapes=list(scratch),
-        compiler_params=pltpu.CompilerParams(vmem_limit_bytes=8 << 20),
+        compiler_params=pltpu.CompilerParams(vmem_limit_bytes=(8 if spec is VM else 56) << 20),
         cost_estimate=pl.CostEstimate(flops=int(flops), bytes_accessed=size, transcendentals=0),
     )(*args)
 
@@ -77,12 +77,6 @@
     return got
 
 
-def received(place, slot, ref):
-    got = ref[...].astype(F32)
-    shared = place.shared[slot]
-    return got if shared is None else jnp.where(shared, got, 0.0)
-
-
 def basis_parts(edge_len, start, width):
     node = lax.broadcasted_iota(jnp.int32, (1, width), 1) + start
     offset = node.astype(F32) - (edge_len - 1) / 2.0
@@ -127,7 +121,19 @@
         message_ref[:, :, i * LANES : (i + 1) * LANES] = row
 
 
-def pack_kernel(capacity, values_ref, dest_ref, node_ref, out_ref):
+def first_kernel(capacity, cols, rows, values_in, dest_in, node_in, inverse_in, out_ref, level_mat_ref, ramp_mat_ref,
+                 values_ref, dest_ref, node_ref, inverse_ref, sems):
+    pairs = ((values_in, values_ref), (dest_in, dest_ref), (node_in, node_ref), (inverse_in, inverse_ref))
+    copies = [pltpu.make_async_copy(source, to, sems.at[i]) for i, (source, to) in enumerate(pairs)]
+    for copy in copies:
+        copy.start()
+    for copy in copies:
+        copy.wait()
+    pack(capacity, values_ref, dest_ref, node_ref, out_ref)
+    coarse_matrices(cols, rows, inverse_ref, (level_mat_ref, ramp_mat_ref))
+
+
+def pack(capacity, values_ref, dest_ref, node_ref, out_ref):
     realiz, count = values_ref.shape
     slots = out_ref.shape[0]
     dest, node = dest_ref[...], node_ref[...]
@@ -146,7 +152,7 @@
     out_ref[...] = out.astype(BF16)
 
 
-def coarse_kernel(cols, rows, inverse_ref, *out_refs):
+def coarse_matrices(cols, rows, inverse_ref, out_refs):
     devices = cols * rows
     i = lax.broadcasted_iota(jnp.int32, (8 * devices, 4 * devices), 0)
     j = lax.broadcasted_iota(jnp.int32, (8 * devices, 4 * devices), 1)
@@ -197,12 +203,12 @@
     write_message(message_ref, project(halves), zero, zero)
 
 
-def half_product(place, half, vec_ref, matrix_ref, slot, start):
-    edge_len = vec_ref.shape[1] // 2
+def product(place, slots, vec_ref, matrix_ref, slot, start):
+    edge_len = vec_ref.shape[1] // len(slots)
     column = pl.multiple_of(place.edges[slot] * edge_len + start, CHUNK)
     total = None
-    for i in range(2):
-        row = pl.multiple_of(place.edges[2 * half + i] * edge_len, edge_len)
+    for i, source in enumerate(slots):
+        row = pl.multiple_of(place.edges[source] * edge_len, edge_len)
         block = matrix_ref[pl.ds(row, edge_len), pl.ds(column, CHUNK)]
         part = jnp.dot(vec_ref[:, i * edge_len : (i + 1) * edge_len], block, preferred_element_type=F32)
         total = part if total is None else total + part
@@ -213,27 +219,27 @@
     place, edge_len = Place(), g0.shape[1]
     for i, got in enumerate((g0, g1)):
         at = pl.ds(i * edge_len, edge_len)
-        value = part_ref[:, at] + received(place, i, got)
+        value = part_ref[:, at] + got[...].astype(F32)
         precon_ref[:, at] = value
         rounded[:, at] = value.astype(BF16)
     for slot in range(4):
         for start in range(0, edge_len, CHUNK):
-            sum_ref[:, pl.ds(slot * edge_len + start, CHUNK)] = half_product(place, 0, rounded, schur_ref, slot, start)
-
-
-def image_far_kernel(part_ref, g2, g3, near_ref, sum_ref, gamma_ref, schur_ref,
-                     precon_ref, image_near_ref, image_far_ref, e0, e1, e2, e3, message_ref, rounded):
+            sum_ref[:, pl.ds(slot * edge_len + start, CHUNK)] = product(place, (0, 1), rounded, schur_ref, slot, start)
+
+
+def image_far_kernel(part_ref, g2, g3, near_ref, sum_ref, gamma_ref, schur_ref, *refs):
+    precon_ref, image_near_ref, image_far_ref, e0, e1, e2, e3, message_ref, rounded = refs[-9:]
     place, edge_len = Place(), g2.shape[1]
     for i, got in enumerate((g2, g3)):
         at = pl.ds(i * edge_len, edge_len)
-        value = part_ref[:, at] + received(place, 2 + i, got)
+        value = part_ref[:, at] + jnp.where(place.shared[2 + i], got[...].astype(F32), 0.0)
         precon_ref[:, at] = value
         rounded[:, at] = value.astype(BF16)
     halves, vectors = (image_near_ref, image_far_ref), (near_ref, precon_ref)
     delta = None
     for slot, edge_ref in enumerate((e0, e1, e2, e3)):
         for start in range(0, edge_len, CHUNK):
-            image = sum_ref[:, pl.ds(slot * edge_len + start, CHUNK)] + half_product(place, 1, rounded, schur_ref, slot, start)
+            image = sum_ref[:, pl.ds(slot * edge_len + start, CHUNK)] + product(place, (2, 3), rounded, schur_ref, slot, start)
             at = pl.ds(slot % 2 * edge_len + start, CHUNK)
             halves[slot // 2][:, at] = image
             edge_ref[: image.shape[0], pl.ds(start, CHUNK)] = image
@@ -272,137 +278,112 @@
     return jnp.concatenate([*rows, jnp.zeros((LANES - count, LANES), F32)], axis=0).T[:realiz]
 
 
-def step_half(place, half, mode, image_ref, edges, columns, precon_ref, olds, news, scaled):
-    edge_len = edges[0].shape[1]
-    resid_in, *olds = olds
-    alpha, beta = columns[:, 0:1], columns[:, 1:2]
-    for i, got in enumerate(edges):
-        slot = 2 * half + i
-        for start in range(0, edge_len, CHUNK):
-            from_ = pl.ds(start, CHUNK)
-            at = pl.ds(i * edge_len + start, CHUNK)
-            other = got[: image_ref.shape[0], from_]
-            if place.shared[slot] is not None:
-                other = jnp.where(place.shared[slot], other, 0.0)
-            applied = image_ref[:, at] + other
-            if mode == "load":
-                resid = applied
-            else:
-                direction = precon_ref[:, at]
-                if mode == "next":
-                    direction_in, applied_in, field_in = olds
-                    direction = direction + beta * direction_in[:, at]
-                    applied = applied + beta * applied_in[:, at]
-                    news[1][:, at] = field_in[:, at] + alpha * direction
-                else:
-                    news[1][:, at] = alpha * direction
-                resid = resid_in[:, at] - alpha * applied
-                if len(news) > 2:
-                    news[2][:, at] = direction
-                    news[3][:, at] = applied
-            news[0][:, at] = resid
-            if scaled is not None:
-                scaled[:, pl.ds(slot * edge_len + start, CHUNK)] = (place.weight(slot) * resid).astype(BF16)
-
-
-def whole_product(place, vec_ref, matrix_ref, slot, start):
-    edge_len = vec_ref.shape[1] // 4
-    column = pl.multiple_of(place.edges[slot] * edge_len + start, CHUNK)
-    total = None
-    for i in range(4):
-        row = pl.multiple_of(place.edges[i] * edge_len, edge_len)
-        block = matrix_ref[pl.ds(row, edge_len), pl.ds(column, CHUNK)]
-        part = jnp.dot(vec_ref[:, i * edge_len : (i + 1) * edge_len], block, preferred_element_type=F32)
-        total = part if total is None else total + part
-    return total
-
-
-OLD = {"load": 0, "init": 2, "next": 5}
-
-
-def scalar_kernel(mode, last, gathered_ref, *refs):
-    refs = list(refs)
-    state_in, coarse_in, applied_in, state_ref = None, None, None, None
+def new_residual(place, slot, mode, columns, image_ref, got_ref, old, at, start):
+    got = got_ref[: image_ref.shape[0], pl.ds(start, CHUNK)]
+    shared = place.shared[slot]
+    applied = image_ref[:, at] + (got if shared is None else jnp.where(shared, got, 0.0))
+    if mode == "load":
+        return None, applied
     if mode == "next":
-        state_in = refs.pop(0)
-    if not last:
-        if mode != "load":
-            coarse_in = refs.pop(0)
-        if mode == "next":
-            applied_in = refs.pop(0)
-        level_mat_ref, ramp_mat_ref = refs.pop(0), refs.pop(0)
-    columns_ref = refs.pop(0)
-    rows = []
-    if mode == "load":
-        coarse_ref, = refs
-        coarse_table(gathered_ref, coarse_ref)
-        coarse = coarse_ref[...]
-        rows.append(jnp.zeros((8, LANES), F32))
-    else:
-        if not last:
-            state_ref, coarse_ref, applied_ref = refs
-        alpha, beta = scalars(mode, gathered_ref, state_in, state_ref, columns_ref.shape[0])
-        rows += [alpha, beta, jnp.zeros((6, LANES), F32)]
-        if not last:
-            coarse_table(gathered_ref, applied_ref)
-            if mode == "next":
-                applied_ref[...] = applied_ref[...] + beta * applied_in[...]
-            coarse = coarse_in[...] - alpha * applied_ref[...]
-            coarse_ref[...] = coarse
-    if not last:
-        solved = jnp.dot(level_mat_ref[...], coarse, precision=HP, preferred_element_type=F32)
-        ramped = jnp.dot(ramp_mat_ref[...], coarse, precision=HP, preferred_element_type=F32)
-        rows.append(solved + pltpu.roll(ramped, LANES // 2, 1))
-    columns_ref[...] = turn(rows, columns_ref.shape[0])
+        applied = applied + columns[:, 1:2] * old[1][:, at]
+    return applied, old[0][:, at] - columns[:, 0:1] * applied
+
+
+def new_field(mode, columns, precon_ref, old, at):
+    direction = precon_ref[:, at]
+    if mode == "init":
+        return direction, columns[:, 0:1] * direction
+    direction = direction + columns[:, 1:2] * old[0][:, at]
+    return direction, old[1][:, at] + columns[:, 0:1] * direction
+
+
+OLD = {"load": 0, "init": 1, "next": 2}
 
 
 def step_kernel(mode, *refs):
     refs = list(refs)
     take = lambda n: [refs.pop(0) for _ in range(n)]
     place = Place()
-    images, edges, (columns_ref,) = take(2), take(4), take(1)
+    images, edges, (gathered_ref,) = take(2), take(4), take(1)
     olds = [take(OLD[mode]) for _ in range(2)]
-    inverse_ref, = take(1)
-    news = [take(1 if mode == "load" else 4) for _ in range(2)]
+    state_in, = take(1) if mode == "next" else (None,)
+    coarse_in, = take(1) if mode != "load" else (None,)
+    applied_in, = take(1) if mode == "next" else (None,)
+    level_mat_ref, ramp_mat_ref, inverse_ref = take(3)
+    news = [take(1 if mode == "load" else 2) for _ in range(2)]
+    columns_ref, coarse_ref = take(2)
+    state_ref, applied_ref = take(2) if mode != "load" else (None, None)
     halves, (gamma_ref,), edge_refs, (scaled,) = take(2), take(1), take(4), take(1)
-    edge_len = edges[0].shape[1]
-    columns = columns_ref[...]
-    for half in range(2):
-        precon_ref, *old = olds[half] or [None, None]
-        step_half(place, half, mode, images[half], edges[2 * half : 2 * half + 2], columns, precon_ref, old, news[half], scaled)
+    realiz, edge_len = images[0].shape[0], edges[0].shape[1]
+    if mode == "load":
+        coarse_table(gathered_ref, coarse_ref)
+        coarse = coarse_ref[...]
+        rows, columns = [jnp.zeros((8, LANES), F32)], None
+    else:
+        alpha, beta = scalars(mode, gathered_ref, state_in, state_ref, realiz)
+        columns = turn([alpha, beta], realiz)
+        coarse_table(gathered_ref, applied_ref)
+        if mode == "next":
+            applied_ref[...] = applied_ref[...] + beta * applied_in[...]
+        coarse = coarse_in[...] - alpha * applied_ref[...]
+        coarse_ref[...] = coarse
+        rows = [alpha, beta, jnp.zeros((6, LANES), F32)]
+    for slot in range(4):
+        half = slot // 2
+        for start in range(0, edge_len, CHUNK):
+            at = pl.ds(slot % 2 * edge_len + start, CHUNK)
+            applied, resid = new_residual(place, slot, mode, columns, images[half], edges[slot], olds[half], at, start)
+            news[half][0][:, at] = resid
+            if applied is not None:
+                news[half][1][:, at] = applied
+            scaled[:, pl.ds(slot * edge_len + start, CHUNK)] = (place.weight(slot) * resid).astype(BF16)
+    level = jnp.dot(level_mat_ref[...], coarse, precision=HP, preferred_element_type=F32)
+    ramp = jnp.dot(ramp_mat_ref[...], coarse, precision=HP, preferred_element_type=F32)
+    rows.append(level + pltpu.roll(ramp, LANES // 2, 1))
+    columns = turn(rows, realiz)
+    columns_ref[...] = columns
     gamma = None
     for slot, edge_ref in enumerate(edge_refs):
         flat, ramp_by = (columns[:, 8 + 2 * slot + i : 9 + 2 * slot + i] for i in range(2))
         for start in range(0, edge_len, CHUNK):
             level, ramp = basis_parts(edge_len, start, CHUNK)
-            part = whole_product(place, scaled, inverse_ref, slot, start)
+            part = product(place, (0, 1, 2, 3), scaled, inverse_ref, slot, start)
             part = place.weight(slot) * (part + (flat * level + ramp_by * ramp))
             at = pl.ds(slot % 2 * edge_len + start, CHUNK)
             halves[slot // 2][:, at] = part
-            edge_ref[:, pl.ds(start, CHUNK)] = part.astype(edge_ref.dtype)
+            edge_ref[:, pl.ds(start, CHUNK)] = part.astype(BF16)
             here = lane_parts(news[slot // 2][0][:, at] * part)
             gamma = here if gamma is None else gamma + here
     gamma_ref[...] = gamma
 
 
-def last_kernel(mode, *refs):
+def field_kernel(mode, columns_ref, *refs):
+    old = 0 if mode == "init" else 2
+    columns = columns_ref[...]
+    for half in range(2):
+        precon_ref, *olds = refs[half * (1 + old) : (half + 1) * (1 + old)]
+        direction_ref, field_ref = refs[2 * (1 + old) + 2 * half : 2 * (1 + old) + 2 * half + 2]
+        for start in range(0, precon_ref.shape[1], CHUNK):
+            at = pl.ds(start, CHUNK)
+            direction_ref[:, at], field_ref[:, at] = new_field(mode, columns, precon_ref, olds, at)
+
+
+def last_kernel(*refs):
     refs = list(refs)
     take = lambda n: [refs.pop(0) for _ in range(n)]
     place = Place()
-    images, edges, (columns_ref,) = take(2), take(4), take(1)
-    olds = [take(OLD[mode]) for _ in range(2)]
-    field_ref, resid_ref = take(2)
-    news = [take(2) for _ in range(2)]
-    edge_len = edges[0].shape[1]
-    columns = columns_ref[...]
-    for half in range(2):
-        precon_ref, *old = olds[half]
-        step_half(place, half, mode, images[half], edges[2 * half : 2 * half + 2], columns, precon_ref, old, news[half], None)
-        for i in range(2):
-            to = pl.ds(pl.multiple_of(place.edges[2 * half + i] * edge_len, edge_len), edge_len)
-            at = pl.ds(i * edge_len, edge_len)
-            resid_ref[:, to] = news[half][0][:, at]
-            field_ref[:, to] = news[half][1][:, at]
+    images, edges, (gathered_ref,) = take(2), take(4), take(1)
+    olds, (state_in,), tracks = [take(2) for _ in range(2)], take(1), [take(3) for _ in range(2)]
+    field_ref, resid_ref = refs
+    realiz, edge_len = images[0].shape[0], edges[0].shape[1]
+    columns = turn(scalars("next", gathered_ref, state_in, None, realiz), realiz)
+    for slot in range(4):
+        half = slot // 2
+        for start in range(0, edge_len, CHUNK):
+            at = pl.ds(slot % 2 * edge_len + start, CHUNK)
+            to = pl.ds(pl.multiple_of(place.edges[slot] * edge_len + start, CHUNK), CHUNK)
+            _, resid_ref[:, to] = new_residual(place, slot, "next", columns, images[half], edges[slot], olds[half], at, start)
+            _, field_ref[:, to] = new_field("next", columns, tracks[half][0], tracks[half][1:], at)
 
 
 def gather(message):
@@ -415,26 +396,29 @@
     cols, rows = lax.axis_size("sx"), lax.axis_size("sy")
     devices = cols * rows
     capacity = max(2, 2 * obs_count // devices)
-    edges = [shape(realiz, size // 4, BF16)] * 4
+    edge = shape(realiz, size // 4, BF16)
     exact = [shape(realiz + PAD, size // 4)] * 4
     half, whole = shape(realiz, size // 2), shape(realiz, size)
     message = jax.ShapeDtypeStruct((devices, 1, 5 * LANES), F32)
     narrow, state_shape = shape(realiz, LANES), shape(8, LANES)
     coarse_state = shape(4 * devices, LANES)
-    scratch_half, scratch_whole = pltpu.VMEM((realiz, size // 2), BF16), pltpu.VMEM((realiz, size), BF16)
+    scratch_half = pltpu.VMEM((realiz, size // 2), BF16)
     flops = 2 * realiz * size * size
     schur_mat, inverse_mat = schur[0, 0], local_inverse[0, 0]
 
-    packed = call(
-        functools.partial(pack_kernel, capacity),
-        shape(devices * capacity, LANES, BF16),
-        (obs_values.T, obs_dest.reshape(1, obs_count), obs_node.reshape(1, obs_count)),
-        flops=COVER,
+    packed, *coarse_mats = call(
+        functools.partial(first_kernel, capacity, cols, rows),
+        [shape(devices * capacity, LANES, BF16), *[shape(8, 4 * devices)] * 2],
+        (obs_values.T, obs_dest.reshape(1, obs_count), obs_node.reshape(1, obs_count), coarse_inverse),
+        [
+            pltpu.VMEM((realiz, obs_count), BF16),
+            *[pltpu.VMEM((1, obs_count), jnp.int32)] * 2,
+            pltpu.VMEM(coarse_inverse.shape, F32),
+            pltpu.SemaphoreType.DMA((4,)),
+        ],
+        COVER,
+        pl.BlockSpec(memory_space=pltpu.HBM),
     )
-    coarse_mats = call(
-        functools.partial(coarse_kernel, cols, rows), [shape(8, 4 * devices)] * 2, (coarse_inverse,)
-    )
-    packed, *coarse_mats = lax.optimization_barrier((packed, *coarse_mats))
     got = lax.all_to_all(packed.reshape(devices, capacity, LANES), AXES, split_axis=0, concat_axis=0, tiled=True)
     *image, e0, e1, e2, e3, sent = call(
         functools.partial(load_kernel, realiz),
@@ -444,43 +428,42 @@
     )
     mode, olds, states = "load", ([], []), []
     for step in range(ITERS + 1):
-        last = step == ITERS
         g, gathered = exchange((e0, e1, e2, e3)), gather(sent)
-        new_states = [] if last else [state_shape, coarse_state, coarse_state][1 if mode == "load" else 0 :]
-        new_states = new_states[:1] if mode == "load" else new_states
-        columns, *states = call(
-            functools.partial(scalar_kernel, mode, last),
-            [narrow, *new_states],
-            (gathered, *states[:1]) if last else (gathered, *states, *coarse_mats),
-        )
-        ins = [*image, *g, columns, *olds[0], *olds[1]]
-        if last:
-            scratch = [pltpu.VMEM((realiz, size // 2), F32)] * 4
-            field, resid = call(functools.partial(last_kernel, mode), [whole, whole], ins, scratch)
+        ins = [*image, *g, gathered, *olds[0], *olds[1]]
+        if step == ITERS:
+            field, resid = call(last_kernel, [whole, whole], [*ins, states[0], z[0], *track[0], z[1], *track[1]])
             return field[None, None], resid[None, None]
-        count = 1 if mode == "load" else 4
+        count, state_count = (1, 1) if mode == "load" else (2, 3)
         outs = call(
             functools.partial(step_kernel, mode),
-            [*[half] * (2 * count), half, half, narrow, *edges],
-            [*ins, inverse_mat],
-            [scratch_whole],
+            [*[half] * (2 * count), narrow, *[coarse_state, state_shape, coarse_state][:state_count], half, half, narrow, *[edge] * 4],
+            [*ins, *states, *coarse_mats, inverse_mat],
+            [pltpu.VMEM((realiz, size), BF16)],
             flops,
         )
-        near, far, outs = outs[:count], outs[count : 2 * count], outs[2 * count :]
+        olds, (columns, coarse), outs = (outs[:count], outs[count : 2 * count]), outs[2 * count : 2 * count + 2], outs[2 * count + 2 :]
+        states, outs = [*outs[:1], coarse, *outs[1:2]] if mode != "load" else [coarse], outs[state_count - 1 :]
         part_near, part_far, gamma, e0, e1, e2, e3 = outs
         g = exchange((e0, e1, e2, e3))
+        if step == 0:
+            track = (), ()
+        else:
+            outs = call(
+                functools.partial(field_kernel, mode), [half] * 4, (columns, z[0], *track[0], z[1], *track[1]), flops=1
+            )
+            track = outs[:2], outs[2:]
         z_near, partial = call(
             image_near_kernel, [half, whole], (part_near, g[0], g[1], schur_mat), [scratch_half], flops // 2
         )
         z_far, *image, e0, e1, e2, e3, sent = call(
             image_far_kernel,
             [half, half, half, *exact, message],
-            (part_far, g[2], g[3], z_near, partial, gamma, schur_mat),
+            (part_far, g[2], g[3], z_near, partial, gamma, schur_mat, *track[0][:1]),
             [scratch_half],
             flops // 2,
         )
+        z = z_near, z_far
         mode = "init" if step == 0 else "next"
-        olds = [[z, new[0]] + ([] if step == 0 else [new[2], new[3], new[1]]) for z, new in ((z_near, near), (z_far, far))]
 
 
 def solution(mesh):

time: 175 us -> 172 us (0.983)
  local copies, waits for them, and re-layouts: 2.83 us -> 0.03 us
    unnamed x16 -> x12, local copies, waits for them, and re-layouts: 2.83 us -> 0.03 us
    pallas_call x29 -> x26, Pallas kernels: 29.7 us -> 30.1 us  [call(): pl.pallas_call(kernel, out_shape=outs, in_specs=[spec] * len(args), out_s...]
  transfers between devices with their start and end apart: 52 -> 52, of which waited for: 12 -> 12; matrix products, arithmetic and copies ran while one was open for 0% -> 0% of each run, Pallas kernels for 5% -> 3%
where the time goes in v4:
time: 172 us
  blocking collectives  96.7 us (56%)
  Pallas kernels  30.1 us (18%)
  starting transfers between devices  26.6 us (15%)
  waiting for transfers between devices  17.3 us (10%)
    all_to_all x7, blocking collectives, gather(): lax.all_to_all(message, AXES, split_axis=0, concat_axis=0, tiled=True)  81.1 us
    pallas_call x26, Pallas kernels, call(): pl.pallas_call(kernel, out_shape=outs, in_specs=[spec] * len(args), out_s...  30.1 us
    ppermute x52, starting transfers between devices, exchange(): got[slot] = lax.ppermute(edges[slot], AXES, plans[slot])  26.6 us
    ppermute x52, waiting for transfers between devices, exchange(): got[slot] = lax.ppermute(edges[slot], AXES, plans[slot])  17.3 us
    all_to_all x1, blocking collectives, body(): lax.all_to_all(packed.reshape(devices, capacity, LANES), AXES, split_axis...  15.5 us
  transfers between devices with their start and end apart: 52, of which 12 were waited for; matrix products, arithmetic and copies ran while one was open for 0% of the time, Pallas kernels for 3%

profile of v4, /device:TPU:0, one launch (start us, length us, event | category | flops | bytes accessed | tf_op | source)
XLA Modules:
  0.0 171.8 jit_solution(10363520389386554351)
XLA Ops:
  0.6 2.0 %shard_map.77 = (bf16[512,128]{1,0:T(8,128)(2,1)}, f32[8,128]{1,0:T(8,128)}, f32[8,128]{1,0:T(8,128)}) custom-call(bf16[64,256]{1,0:T(8,128)(2,1)} %bitcast.35, s32[1,256]{1,0:T(1,128)} %bitcast.36, s32[1,256]{1,0:T(1,128)} %bitcast.37, f32[8,256]{1,0:T(8,128)} %inverse_in.1), custom_call_target="tpu_custom_call" | custom-call | flops 8000000000 | bytes 43008 | tf_op jit(solution)/shard_map/pallas_call | solution.py:24
  2.7 15.5 %all_to_all.40 = bf16[32,16,128]{2,1,0:T(8,128)(2,1)S(1)} all-to-all(bf16[32,16,128]{2,1,0:T(8,128)(2,1)} %bitcast.32), channel_id=1, replica_groups=mesh['sx'=8,'sy'=4] {'sx','sy'}, dimensions={0} | all-to-all | bytes 262144 | tf_op jit(solution)/shard_map/all_to_all | solution.py:422
  20.8 11.2 %all_to_all.41.refs_6_ = f32[32,1,640]{2,1,0:T(1,128)S(1)} all-to-all(f32[32,1,640]{2,1,0:T(1,128)S(1)} %get-tuple-element.184), channel_id=1, replica_groups=mesh['sx'=8,'sy'=4] {'sx','sy'}, dimensions={0} | all-to-all | bytes 163840 | tf_op jit(solution)/shard_map/all_to_all | solution.py:390
  32.1 2.2 %shard_map.79 = (f32[64,1024]{1,0:T(8,128)S(1)}, f32[64,1024]{1,0:T(8,128)S(1)}, f32[64,128]{1,0:T(8,128)}, f32[128,128]{1,0:T(8,128)S(1)}, f32[64,1024]{1,0:T(8...) custom-call(f32[64,1024]{1,0:T(8,128)S(1)} %get-tuple-element.178.re, ...), custom_call_target="tpu_custom_call" | custom-call | flops 536870912 | bytes 9658368 | tf_op jit(solution)/shard_map/pallas_call | solution.py:24
  35.7 2.8 %collective-permute-done.6.g0 = bf16[64,512]{1,0:T(8,128)(2,1)S(1)} collective-permute-done((bf16[64,512]{1,0:T(8,128)(2,1)S(1)}, bf16[64,512]{1,0:T(8,128)(2,1)S(1)}, u32[]{:S(2)}, u32[]{:S(2)}) %collective-permute-start.6) | collective-permute-done | bytes 65568 | tf_op jit(solution)/shard_map/ppermute | solution.py:76
  39.6 1.2 shard_map.81
  40.8 2.2 %collective-permute-start.8 = (f32[80,512]{1,0:T(8,128)S(1)}, f32[80,512]{1,0:T(8,128)S(1)}, u32[]{:S(2)}, u32[]{:S(2)}) collective-permute-start(f32[80,512]{1,0:T(8,128)S(1)} %get-tuple-element.198), channel_id=1, source_target_pairs={{0,4},{1,5},{2,6},{3,7},{4,0},{5,1},{6,2},{7,3},{8,12},{9,13},{10,... | collective-permute-start | bytes 491528 | tf_op jit(solution)/shard_map/ppermute | solution.py:76
  43.5 11.6 %all_to_all.42.refs_6_ = f32[32,1,640]{2,1,0:T(1,128)S(1)} all-to-all(f32[32,1,640]{2,1,0:T(1,128)S(1)} %get-tuple-element.202), channel_id=1, replica_groups=mesh['sx'=8,'sy'=4] {'sx','sy'}, dimensions={0} | all-to-all | bytes 163840 | tf_op jit(solution)/shard_map/all_to_all | solution.py:390
  55.2 2.0 %shard_map.82 = (f32[64,1024]{1,0:T(8,128)S(1)}, f32[64,1024]{1,0:T(8,128)S(1)}, f32[64,1024]{1,0:T(8,128)S(1)}, f32[64,1024]{1,0:T(8,128)S(1)}, f32[64,128]{1,0...) custom-call(f32[64,1024]{1,0:T(8,128)S(1)} %get-tuple-element.196.re, ...), custom_call_target="tpu_custom_call" | custom-call | flops 536870912 | bytes 10248192 | tf_op jit(solution)/shard_map/pallas_call | solution.py:24
  58.8 2.7 %collective-permute-done.14.g0 = bf16[64,512]{1,0:T(8,128)(2,1)S(1)} collective-permute-done((bf16[64,512]{1,0:T(8,128)(2,1)S(1)}, bf16[64,512]{1,0:T(8,128)(2,1)S(1)}, u32[]{:S(2)}, u32[]{:S(2)}) %collective-permute-start.14) | collective-permute-done | bytes 65568 | tf_op jit(solution)/shard_map/ppermute | solution.py:76
  63.8 2.2 %collective-permute-start.16 = (f32[80,512]{1,0:T(8,128)S(1)}, f32[80,512]{1,0:T(8,128)S(1)}, u32[]{:S(2)}, u32[]{:S(2)}) collective-permute-start(f32[80,512]{1,0:T(8,128)S(1)} %get-tuple-element.220), channel_id=1, source_target_pairs={{0,4},{1,5},{2,6},{3,7},{4,0},{5,1},{6,2},{7,3},{8,12},{9,13},{10,... | collective-permute-start | bytes 491528 | tf_op jit(solution)/shard_map/ppermute | solution.py:76
  66.5 11.6 %all_to_all.43.refs_6_ = f32[32,1,640]{2,1,0:T(1,128)S(1)} all-to-all(f32[32,1,640]{2,1,0:T(1,128)S(1)} %get-tuple-element.224), channel_id=1, replica_groups=mesh['sx'=8,'sy'=4] {'sx','sy'}, dimensions={0} | all-to-all | bytes 163840 | tf_op jit(solution)/shard_map/all_to_all | solution.py:390
  78.1 2.0 %shard_map.86 = (f32[64,1024]{1,0:T(8,128)S(1)}, f32[64,1024]{1,0:T(8,128)S(1)}, f32[64,1024]{1,0:T(8,128)S(1)}, f32[64,1024]{1,0:T(8,128)S(1)}, f32[64,128]{1,0...) custom-call(f32[64,1024]{1,0:T(8,128)S(1)} %get-tuple-element.218.re, ...), custom_call_target="tpu_custom_call" | custom-call | flops 536870912 | bytes 10842112 | tf_op jit(solution)/shard_map/pallas_call | solution.py:24
  81.8 2.7 %collective-permute-done.22.g0 = bf16[64,512]{1,0:T(8,128)(2,1)S(1)} collective-permute-done((bf16[64,512]{1,0:T(8,128)(2,1)S(1)}, bf16[64,512]{1,0:T(8,128)(2,1)S(1)}, u32[]{:S(2)}, u32[]{:S(2)}) %collective-permute-start.22) | collective-permute-done | bytes 65568 | tf_op jit(solution)/shard_map/ppermute | solution.py:76
  85.5 1.2 shard_map.89
  86.7 2.2 %collective-permute-start.24 = (f32[80,512]{1,0:T(8,128)S(1)}, f32[80,512]{1,0:T(8,128)S(1)}, u32[]{:S(2)}, u32[]{:S(2)}) collective-permute-start(f32[80,512]{1,0:T(8,128)S(1)} %get-tuple-element.249), channel_id=1, source_target_pairs={{0,4},{1,5},{2,6},{3,7},{4,0},{5,1},{6,2},{7,3},{8,12},{9,13},{10,... | collective-permute-start | bytes 491528 | tf_op jit(solution)/shard_map/ppermute | solution.py:76
  89.5 11.6 %all_to_all.44.refs_6_ = f32[32,1,640]{2,1,0:T(1,128)S(1)} all-to-all(f32[32,1,640]{2,1,0:T(1,128)S(1)} %get-tuple-element.253), channel_id=1, replica_groups=mesh['sx'=8,'sy'=4] {'sx','sy'}, dimensions={0} | all-to-all | bytes 163840 | tf_op jit(solution)/shard_map/all_to_all | solution.py:390
  101.1 2.0 %shard_map.90 = (f32[64,1024]{1,0:T(8,128)S(1)}, f32[64,1024]{1,0:T(8,128)S(1)}, f32[64,1024]{1,0:T(8,128)S(1)}, f32[64,1024]{1,0:T(8,128)S(1)}, f32[64,128]{1,0...) custom-call(f32[64,1024]{1,0:T(8,128)S(1)} %get-tuple-element.247.re, ...), custom_call_target="tpu_custom_call" | custom-call | flops 536870912 | bytes 10842112 | tf_op jit(solution)/shard_map/pallas_call | solution.py:24
  104.8 2.7 %collective-permute-done.30.g0 = bf16[64,512]{1,0:T(8,128)(2,1)S(1)} collective-permute-done((bf16[64,512]{1,0:T(8,128)(2,1)S(1)}, bf16[64,512]{1,0:T(8,128)(2,1)S(1)}, u32[]{:S(2)}, u32[]{:S(2)}) %collective-permute-start.30) | collective-permute-done | bytes 65568 | tf_op jit(solution)/shard_map/ppermute | solution.py:76
  108.5 1.2 shard_map.93
  109.7 2.2 %collective-permute-start.32 = (f32[80,512]{1,0:T(8,128)S(1)}, f32[80,512]{1,0:T(8,128)S(1)}, u32[]{:S(2)}, u32[]{:S(2)}) collective-permute-start(f32[80,512]{1,0:T(8,128)S(1)} %get-tuple-element.278), channel_id=1, source_target_pairs={{0,4},{1,5},{2,6},{3,7},{4,0},{5,1},{6,2},{7,3},{8,12},{9,13},{10,... | collective-permute-start | bytes 491528 | tf_op jit(solution)/shard_map/ppermute | solution.py:76
  112.4 11.7 %all_to_all.45.refs_6_ = f32[32,1,640]{2,1,0:T(1,128)S(1)} all-to-all(f32[32,1,640]{2,1,0:T(1,128)S(1)} %get-tuple-element.282), channel_id=1, replica_groups=mesh['sx'=8,'sy'=4] {'sx','sy'}, dimensions={0} | all-to-all | bytes 163840 | tf_op jit(solution)/shard_map/all_to_all | solution.py:390
  124.1 2.0 %shard_map.94 = (f32[64,1024]{1,0:T(8,128)S(1)}, f32[64,1024]{1,0:T(8,128)S(1)}, f32[64,1024]{1,0:T(8,128)S(1)}, f32[64,1024]{1,0:T(8,128)S(1)}, f32[64,128]{1,0...) custom-call(f32[64,1024]{1,0:T(8,128)S(1)} %get-tuple-element.276.re, ...), custom_call_target="tpu_custom_call" | custom-call | flops 536870912 | bytes 10842112 | tf_op jit(solution)/shard_map/pallas_call | solution.py:24
  127.8 2.7 %collective-permute-done.38.g0 = bf16[64,512]{1,0:T(8,128)(2,1)S(1)} collective-permute-done((bf16[64,512]{1,0:T(8,128)(2,1)S(1)}, bf16[64,512]{1,0:T(8,128)(2,1)S(1)}, u32[]{:S(2)}, u32[]{:S(2)}) %collective-permute-start.38) | collective-permute-done | bytes 65568 | tf_op jit(solution)/shard_map/ppermute | solution.py:76
  132.7 2.2 %collective-permute-start.40 = (f32[80,512]{1,0:T(8,128)S(1)}, f32[80,512]{1,0:T(8,128)S(1)}, u32[]{:S(2)}, u32[]{:S(2)}) collective-permute-start(f32[80,512]{1,0:T(8,128)S(1)} %get-tuple-element.307), channel_id=1, source_target_pairs={{0,4},{1,5},{2,6},{3,7},{4,0},{5,1},{6,2},{7,3},{8,12},{9,13},{10,... | collective-permute-start | bytes 491528 | tf_op jit(solution)/shard_map/ppermute | solution.py:76
  135.4 11.7 %all_to_all.46.refs_6_ = f32[32,1,640]{2,1,0:T(1,128)S(1)} all-to-all(f32[32,1,640]{2,1,0:T(1,128)S(1)} %get-tuple-element.311), channel_id=1, replica_groups=mesh['sx'=8,'sy'=4] {'sx','sy'}, dimensions={0} | all-to-all | bytes 163840 | tf_op jit(solution)/shard_map/all_to_all | solution.py:390
  147.1 2.3 %shard_map.98 = (f32[64,1024]{1,0:T(8,128)S(1)}, f32[64,1024]{1,0:T(8,128)S(1)}, f32[64,1024]{1,0:T(8,128)S(1)}, f32[64,1024]{1,0:T(8,128)S(1)}, f32[64,128]{1,0...) custom-call(f32[64,1024]{1,0:T(8,128)S(1)} %get-tuple-element.305.re, ...), custom_call_target="tpu_custom_call" | custom-call | flops 536870912 | bytes 10842112 | tf_op jit(solution)/shard_map/pallas_call | solution.py:24
  151.0 2.7 %collective-permute-done.46.g0 = bf16[64,512]{1,0:T(8,128)(2,1)S(1)} collective-permute-done((bf16[64,512]{1,0:T(8,128)(2,1)S(1)}, bf16[64,512]{1,0:T(8,128)(2,1)S(1)}, u32[]{:S(2)}, u32[]{:S(2)}) %collective-permute-start.46) | collective-permute-done | bytes 65568 | tf_op jit(solution)/shard_map/ppermute | solution.py:76
  154.8 1.2 shard_map.101
  156.0 2.2 %collective-permute-start.48 = (f32[80,512]{1,0:T(8,128)S(1)}, f32[80,512]{1,0:T(8,128)S(1)}, u32[]{:S(2)}, u32[]{:S(2)}) collective-permute-start(f32[80,512]{1,0:T(8,128)S(1)} %get-tuple-element.336), channel_id=1, source_target_pairs={{0,4},{1,5},{2,6},{3,7},{4,0},{5,1},{6,2},{7,3},{8,12},{9,13},{10,... | collective-permute-start | bytes 491528 | tf_op jit(solution)/shard_map/ppermute | solution.py:76
  158.7 11.7 %all_to_all.47.refs_6_ = f32[32,1,640]{2,1,0:T(1,128)S(1)} all-to-all(f32[32,1,640]{2,1,0:T(1,128)S(1)} %get-tuple-element.340), channel_id=1, replica_groups=mesh['sx'=8,'sy'=4] {'sx','sy'}, dimensions={0} | all-to-all | bytes 163840 | tf_op jit(solution)/shard_map/all_to_all | solution.py:390
  170.4 1.4 shard_map.102
  (120 shorter events, 24.0 us)
Async XLA Ops:
  19.2 12.8 %collective-permute-start = (f32[80,512]{1,0:T(8,128)S(1)}, f32[80,512]{1,0:T(8,128)S(1)}, u32[]{:S(2)}, u32[]{:S(2)}) collective-permute-start(f32[80,512]{1,0:T(8,128)S(1)} %get-tuple-element.180), channel_id=1, source_target_pairs={{0,4},{1,5},{2,6},{3,7},{4,0},{5,1},{6,2},{7,3},{8,12},{9,13},{10,... | collective-permute-start | bytes 491528 | tf_op jit(solution)/shard_map/ppermute | solution.py:76
  19.9 12.1 %collective-permute-start.1 = (f32[80,512]{1,0:T(8,128)S(1)}, f32[80,512]{1,0:T(8,128)S(1)}, u32[]{:S(2)}, u32[]{:S(2)}) collective-permute-start(f32[80,512]{1,0:T(8,128)S(1)} %get-tuple-element.181), channel_id=1, source_target_pairs={{0,1},{1,0},{2,3},{3,2},{4,5},{5,4},{6,7},{7,6},{8,9},{9,8},{10,11... | collective-permute-start | bytes 491528 | tf_op jit(solution)/shard_map/ppermute | solution.py:76
  19.9 12.1 %collective-permute-start.2 = (f32[80,512]{1,0:T(8,128)S(1)}, f32[80,512]{1,0:T(8,128)S(1)}, u32[]{:S(2)}, u32[]{:S(2)}) collective-permute-start(f32[80,512]{1,0:T(8,128)S(1)} %get-tuple-element.182), channel_id=1, source_target_pairs={{0,1},{1,0},{2,3},{3,2},{4,8},{5,9},{6,10},{7,11},{8,4},{9,5},{10,... | collective-permute-start | bytes 491528 | tf_op jit(solution)/shard_map/ppermute | solution.py:76
  20.4 11.6 %collective-permute-start.3 = (f32[80,512]{1,0:T(8,128)S(1)}, f32[80,512]{1,0:T(8,128)S(1)}, u32[]{:S(2)}, u32[]{:S(2)}) collective-permute-start(f32[80,512]{1,0:T(8,128)S(1)} %get-tuple-element.183), channel_id=1, source_target_pairs={{0,3},{1,2},{2,1},{3,0},{4,7},{5,6},{6,5},{7,4},{8,11},{9,10},{10,... | collective-permute-start | bytes 491528 | tf_op jit(solution)/shard_map/ppermute | solution.py:76
  40.8 14.3 %collective-permute-start.8 = (f32[80,512]{1,0:T(8,128)S(1)}, f32[80,512]{1,0:T(8,128)S(1)}, u32[]{:S(2)}, u32[]{:S(2)}) collective-permute-start(f32[80,512]{1,0:T(8,128)S(1)} %get-tuple-element.198), channel_id=1, source_target_pairs={{0,4},{1,5},{2,6},{3,7},{4,0},{5,1},{6,2},{7,3},{8,12},{9,13},{10,... | collective-permute-start | bytes 491528 | tf_op jit(solution)/shard_map/ppermute | solution.py:76
  43.0 12.2 %collective-permute-start.9 = (f32[80,512]{1,0:T(8,128)S(1)}, f32[80,512]{1,0:T(8,128)S(1)}, u32[]{:S(2)}, u32[]{:S(2)}) collective-permute-start(f32[80,512]{1,0:T(8,128)S(1)} %get-tuple-element.199), channel_id=1, source_target_pairs={{0,1},{1,0},{2,3},{3,2},{4,5},{5,4},{6,7},{7,6},{8,9},{9,8},{10,11... | collective-permute-start | bytes 491528 | tf_op jit(solution)/shard_map/ppermute | solution.py:76
  43.0 12.2 %collective-permute-start.10 = (f32[80,512]{1,0:T(8,128)S(1)}, f32[80,512]{1,0:T(8,128)S(1)}, u32[]{:S(2)}, u32[]{:S(2)}) collective-permute-start(f32[80,512]{1,0:T(8,128)S(1)} %get-tuple-element.200), channel_id=1, source_target_pairs={{0,1},{1,0},{2,3},{3,2},{4,8},{5,9},{6,10},{7,11},{8,4},{9,5},{10,... | collective-permute-start | bytes 491528 | tf_op jit(solution)/shard_map/ppermute | solution.py:76
  43.5 11.7 %collective-permute-start.11 = (f32[80,512]{1,0:T(8,128)S(1)}, f32[80,512]{1,0:T(8,128)S(1)}, u32[]{:S(2)}, u32[]{:S(2)}) collective-permute-start(f32[80,512]{1,0:T(8,128)S(1)} %get-tuple-element.201), channel_id=1, source_target_pairs={{0,3},{1,2},{2,1},{3,0},{4,7},{5,6},{6,5},{7,4},{8,11},{9,10},{10,... | collective-permute-start | bytes 491528 | tf_op jit(solution)/shard_map/ppermute | solution.py:76
  57.8 4.5 %collective-permute-start.12 = (bf16[64,512]{1,0:T(8,128)(2,1)S(1)}, bf16[64,512]{1,0:T(8,128)(2,1)S(1)}, u32[]{:S(2)}, u32[]{:S(2)}) collective-permute-start(bf16[64,512]{1,0:T(8,128)(2,1)S(1)} %get-tuple-element.207), channel_id=1, source_target_pairs={{0,1},{1,0},{2,3},{3,2},{4,8},{5,9},{6,10},{7,11},{8,4},{9,5},{10,... | collective-permute-start | bytes 196616 | tf_op jit(solution)/shard_map/ppermute | solution.py:76
  63.8 14.4 %collective-permute-start.16 = (f32[80,512]{1,0:T(8,128)S(1)}, f32[80,512]{1,0:T(8,128)S(1)}, u32[]{:S(2)}, u32[]{:S(2)}) collective-permute-start(f32[80,512]{1,0:T(8,128)S(1)} %get-tuple-element.220), channel_id=1, source_target_pairs={{0,4},{1,5},{2,6},{3,7},{4,0},{5,1},{6,2},{7,3},{8,12},{9,13},{10,... | collective-permute-start | bytes 491528 | tf_op jit(solution)/shard_map/ppermute | solution.py:76
  65.9 12.2 %collective-permute-start.17 = (f32[80,512]{1,0:T(8,128)S(1)}, f32[80,512]{1,0:T(8,128)S(1)}, u32[]{:S(2)}, u32[]{:S(2)}) collective-permute-start(f32[80,512]{1,0:T(8,128)S(1)} %get-tuple-element.221), channel_id=1, source_target_pairs={{0,1},{1,0},{2,3},{3,2},{4,5},{5,4},{6,7},{7,6},{8,9},{9,8},{10,11... | collective-permute-start | bytes 491528 | tf_op jit(solution)/shard_map/ppermute | solution.py:76
  66.0 12.2 %collective-permute-start.18 = (f32[80,512]{1,0:T(8,128)S(1)}, f32[80,512]{1,0:T(8,128)S(1)}, u32[]{:S(2)}, u32[]{:S(2)}) collective-permute-start(f32[80,512]{1,0:T(8,128)S(1)} %get-tuple-element.222), channel_id=1, source_target_pairs={{0,1},{1,0},{2,3},{3,2},{4,8},{5,9},{6,10},{7,11},{8,4},{9,5},{10,... | collective-permute-start | bytes 491528 | tf_op jit(solution)/shard_map/ppermute | solution.py:76
  66.5 11.7 %collective-permute-start.19 = (f32[80,512]{1,0:T(8,128)S(1)}, f32[80,512]{1,0:T(8,128)S(1)}, u32[]{:S(2)}, u32[]{:S(2)}) collective-permute-start(f32[80,512]{1,0:T(8,128)S(1)} %get-tuple-element.223), channel_id=1, source_target_pairs={{0,3},{1,2},{2,1},{3,0},{4,7},{5,6},{6,5},{7,4},{8,11},{9,10},{10,... | collective-permute-start | bytes 491528 | tf_op jit(solution)/shard_map/ppermute | solution.py:76
  80.8 4.5 %collective-permute-start.20 = (bf16[64,512]{1,0:T(8,128)(2,1)S(1)}, bf16[64,512]{1,0:T(8,128)(2,1)S(1)}, u32[]{:S(2)}, u32[]{:S(2)}) collective-permute-start(bf16[64,512]{1,0:T(8,128)(2,1)S(1)} %get-tuple-element.233), channel_id=1, source_target_pairs={{0,1},{1,0},{2,3},{3,2},{4,8},{5,9},{6,10},{7,11},{8,4},{9,5},{10,... | collective-permute-start | bytes 196616 | tf_op jit(solution)/shard_map/ppermute | solution.py:76
  86.7 14.4 %collective-permute-start.24 = (f32[80,512]{1,0:T(8,128)S(1)}, f32[80,512]{1,0:T(8,128)S(1)}, u32[]{:S(2)}, u32[]{:S(2)}) collective-permute-start(f32[80,512]{1,0:T(8,128)S(1)} %get-tuple-element.249), channel_id=1, source_target_pairs={{0,4},{1,5},{2,6},{3,7},{4,0},{5,1},{6,2},{7,3},{8,12},{9,13},{10,... | collective-permute-start | bytes 491528 | tf_op jit(solution)/shard_map/ppermute | solution.py:76
  88.9 12.2 %collective-permute-start.25 = (f32[80,512]{1,0:T(8,128)S(1)}, f32[80,512]{1,0:T(8,128)S(1)}, u32[]{:S(2)}, u32[]{:S(2)}) collective-permute-start(f32[80,512]{1,0:T(8,128)S(1)} %get-tuple-element.250), channel_id=1, source_target_pairs={{0,1},{1,0},{2,3},{3,2},{4,5},{5,4},{6,7},{7,6},{8,9},{9,8},{10,11... | collective-permute-start | bytes 491528 | tf_op jit(solution)/shard_map/ppermute | solution.py:76
  88.9 12.2 %collective-permute-start.26 = (f32[80,512]{1,0:T(8,128)S(1)}, f32[80,512]{1,0:T(8,128)S(1)}, u32[]{:S(2)}, u32[]{:S(2)}) collective-permute-start(f32[80,512]{1,0:T(8,128)S(1)} %get-tuple-element.251), channel_id=1, source_target_pairs={{0,1},{1,0},{2,3},{3,2},{4,8},{5,9},{6,10},{7,11},{8,4},{9,5},{10,... | collective-permute-start | bytes 491528 | tf_op jit(solution)/shard_map/ppermute | solution.py:76
  89.4 11.7 %collective-permute-start.27 = (f32[80,512]{1,0:T(8,128)S(1)}, f32[80,512]{1,0:T(8,128)S(1)}, u32[]{:S(2)}, u32[]{:S(2)}) collective-permute-start(f32[80,512]{1,0:T(8,128)S(1)} %get-tuple-element.252), channel_id=1, source_target_pairs={{0,3},{1,2},{2,1},{3,0},{4,7},{5,6},{6,5},{7,4},{8,11},{9,10},{10,... | collective-permute-start | bytes 491528 | tf_op jit(solution)/shard_map/ppermute | solution.py:76
  103.8 4.6 %collective-permute-start.28 = (bf16[64,512]{1,0:T(8,128)(2,1)S(1)}, bf16[64,512]{1,0:T(8,128)(2,1)S(1)}, u32[]{:S(2)}, u32[]{:S(2)}) collective-permute-start(bf16[64,512]{1,0:T(8,128)(2,1)S(1)} %get-tuple-element.262), channel_id=1, source_target_pairs={{0,1},{1,0},{2,3},{3,2},{4,8},{5,9},{6,10},{7,11},{8,4},{9,5},{10,... | collective-permute-start | bytes 196616 | tf_op jit(solution)/shard_map/ppermute | solution.py:76
  109.7 14.4 %collective-permute-start.32 = (f32[80,512]{1,0:T(8,128)S(1)}, f32[80,512]{1,0:T(8,128)S(1)}, u32[]{:S(2)}, u32[]{:S(2)}) collective-permute-start(f32[80,512]{1,0:T(8,128)S(1)} %get-tuple-element.278), channel_id=1, source_target_pairs={{0,4},{1,5},{2,6},{3,7},{4,0},{5,1},{6,2},{7,3},{8,12},{9,13},{10,... | collective-permute-start | bytes 491528 | tf_op jit(solution)/shard_map/ppermute | solution.py:76
  111.9 12.2 %collective-permute-start.33 = (f32[80,512]{1,0:T(8,128)S(1)}, f32[80,512]{1,0:T(8,128)S(1)}, u32[]{:S(2)}, u32[]{:S(2)}) collective-permute-start(f32[80,512]{1,0:T(8,128)S(1)} %get-tuple-element.279), channel_id=1, source_target_pairs={{0,1},{1,0},{2,3},{3,2},{4,5},{5,4},{6,7},{7,6},{8,9},{9,8},{10,11... | collective-permute-start | bytes 491528 | tf_op jit(solution)/shard_map/ppermute | solution.py:76
  111.9 12.2 %collective-permute-start.34 = (f32[80,512]{1,0:T(8,128)S(1)}, f32[80,512]{1,0:T(8,128)S(1)}, u32[]{:S(2)}, u32[]{:S(2)}) collective-permute-start(f32[80,512]{1,0:T(8,128)S(1)} %get-tuple-element.280), channel_id=1, source_target_pairs={{0,1},{1,0},{2,3},{3,2},{4,8},{5,9},{6,10},{7,11},{8,4},{9,5},{10,... | collective-permute-start | bytes 491528 | tf_op jit(solution)/shard_map/ppermute | solution.py:76
  112.4 11.7 %collective-permute-start.35 = (f32[80,512]{1,0:T(8,128)S(1)}, f32[80,512]{1,0:T(8,128)S(1)}, u32[]{:S(2)}, u32[]{:S(2)}) collective-permute-start(f32[80,512]{1,0:T(8,128)S(1)} %get-tuple-element.281), channel_id=1, source_target_pairs={{0,3},{1,2},{2,1},{3,0},{4,7},{5,6},{6,5},{7,4},{8,11},{9,10},{10,... | collective-permute-start | bytes 491528 | tf_op jit(solution)/shard_map/ppermute | solution.py:76
  126.8 4.6 %collective-permute-start.36 = (bf16[64,512]{1,0:T(8,128)(2,1)S(1)}, bf16[64,512]{1,0:T(8,128)(2,1)S(1)}, u32[]{:S(2)}, u32[]{:S(2)}) collective-permute-start(bf16[64,512]{1,0:T(8,128)(2,1)S(1)} %get-tuple-element.291), channel_id=1, source_target_pairs={{0,1},{1,0},{2,3},{3,2},{4,8},{5,9},{6,10},{7,11},{8,4},{9,5},{10,... | collective-permute-start | bytes 196616 | tf_op jit(solution)/shard_map/ppermute | solution.py:76
  132.7 14.4 %collective-permute-start.40 = (f32[80,512]{1,0:T(8,128)S(1)}, f32[80,512]{1,0:T(8,128)S(1)}, u32[]{:S(2)}, u32[]{:S(2)}) collective-permute-start(f32[80,512]{1,0:T(8,128)S(1)} %get-tuple-element.307), channel_id=1, source_target_pairs={{0,4},{1,5},{2,6},{3,7},{4,0},{5,1},{6,2},{7,3},{8,12},{9,13},{10,... | collective-permute-start | bytes 491528 | tf_op jit(solution)/shard_map/ppermute | solution.py:76
  134.9 12.2 %collective-permute-start.41 = (f32[80,512]{1,0:T(8,128)S(1)}, f32[80,512]{1,0:T(8,128)S(1)}, u32[]{:S(2)}, u32[]{:S(2)}) collective-permute-start(f32[80,512]{1,0:T(8,128)S(1)} %get-tuple-element.308), channel_id=1, source_target_pairs={{0,1},{1,0},{2,3},{3,2},{4,5},{5,4},{6,7},{7,6},{8,9},{9,8},{10,11... | collective-permute-start | bytes 491528 | tf_op jit(solution)/shard_map/ppermute | solution.py:76
  134.9 12.2 %collective-permute-start.42 = (f32[80,512]{1,0:T(8,128)S(1)}, f32[80,512]{1,0:T(8,128)S(1)}, u32[]{:S(2)}, u32[]{:S(2)}) collective-permute-start(f32[80,512]{1,0:T(8,128)S(1)} %get-tuple-element.309), channel_id=1, source_target_pairs={{0,1},{1,0},{2,3},{3,2},{4,8},{5,9},{6,10},{7,11},{8,4},{9,5},{10,... | collective-permute-start | bytes 491528 | tf_op jit(solution)/shard_map/ppermute | solution.py:76
  135.4 11.7 %collective-permute-start.43 = (f32[80,512]{1,0:T(8,128)S(1)}, f32[80,512]{1,0:T(8,128)S(1)}, u32[]{:S(2)}, u32[]{:S(2)}) collective-permute-start(f32[80,512]{1,0:T(8,128)S(1)} %get-tuple-element.310), channel_id=1, source_target_pairs={{0,3},{1,2},{2,1},{3,0},{4,7},{5,6},{6,5},{7,4},{8,11},{9,10},{10,... | collective-permute-start | bytes 491528 | tf_op jit(solution)/shard_map/ppermute | solution.py:76
  156.0 14.4 %collective-permute-start.48 = (f32[80,512]{1,0:T(8,128)S(1)}, f32[80,512]{1,0:T(8,128)S(1)}, u32[]{:S(2)}, u32[]{:S(2)}) collective-permute-start(f32[80,512]{1,0:T(8,128)S(1)} %get-tuple-element.336), channel_id=1, source_target_pairs={{0,4},{1,5},{2,6},{3,7},{4,0},{5,1},{6,2},{7,3},{8,12},{9,13},{10,... | collective-permute-start | bytes 491528 | tf_op jit(solution)/shard_map/ppermute | solution.py:76
  158.2 12.2 %collective-permute-start.49 = (f32[80,512]{1,0:T(8,128)S(1)}, f32[80,512]{1,0:T(8,128)S(1)}, u32[]{:S(2)}, u32[]{:S(2)}) collective-permute-start(f32[80,512]{1,0:T(8,128)S(1)} %get-tuple-element.337), channel_id=1, source_target_pairs={{0,1},{1,0},{2,3},{3,2},{4,5},{5,4},{6,7},{7,6},{8,9},{9,8},{10,11... | collective-permute-start | bytes 491528 | tf_op jit(solution)/shard_map/ppermute | solution.py:76
  158.2 12.2 %collective-permute-start.50 = (f32[80,512]{1,0:T(8,128)S(1)}, f32[80,512]{1,0:T(8,128)S(1)}, u32[]{:S(2)}, u32[]{:S(2)}) collective-permute-start(f32[80,512]{1,0:T(8,128)S(1)} %get-tuple-element.338), channel_id=1, source_target_pairs={{0,1},{1,0},{2,3},{3,2},{4,8},{5,9},{6,10},{7,11},{8,4},{9,5},{10,... | collective-permute-start | bytes 491528 | tf_op jit(solution)/shard_map/ppermute | solution.py:76
  158.7 11.7 %collective-permute-start.51 = (f32[80,512]{1,0:T(8,128)S(1)}, f32[80,512]{1,0:T(8,128)S(1)}, u32[]{:S(2)}, u32[]{:S(2)}) collective-permute-start(f32[80,512]{1,0:T(8,128)S(1)} %get-tuple-element.339), channel_id=1, source_target_pairs={{0,3},{1,2},{2,1},{3,0},{4,7},{5,6},{6,5},{7,4},{8,11},{9,10},{10,... | collective-permute-start | bytes 491528 | tf_op jit(solution)/shard_map/ppermute | solution.py:76
  (26 other events, 211.3 us)

commit v5 on v4

--- a/solution.py
+++ b/solution.py
@@ -8,6 +8,7 @@
 from jax.sharding import PartitionSpec as P
 
 ITERS = 6
+ORDER = (1, 0, 2, 3)
 PAD = 16
 COVER = 8e9
 LANES = 128
@@ -215,7 +216,17 @@
     return total
 
 
-def image_near_kernel(part_ref, g0, g1, schur_ref, precon_ref, sum_ref, rounded):
+def image_first_kernel(part_ref, got_ref, schur_ref, precon_ref, sum_ref, rounded):
+    place, edge_len = Place(), got_ref.shape[1]
+    value = part_ref[...] + jnp.where(place.shared[2], got_ref[...].astype(F32), 0.0)
+    precon_ref[...] = value
+    rounded[...] = value.astype(BF16)
+    for slot in range(4):
+        for start in range(0, edge_len, CHUNK):
+            sum_ref[:, pl.ds(slot * edge_len + start, CHUNK)] = product(place, (2,), rounded, schur_ref, slot, start)
+
+
+def image_near_kernel(part_ref, g0, g1, sum_in, schur_ref, precon_ref, sum_ref, rounded):
     place, edge_len = Place(), g0.shape[1]
     for i, got in enumerate((g0, g1)):
         at = pl.ds(i * edge_len, edge_len)
@@ -224,22 +235,22 @@
         rounded[:, at] = value.astype(BF16)
     for slot in range(4):
         for start in range(0, edge_len, CHUNK):
-            sum_ref[:, pl.ds(slot * edge_len + start, CHUNK)] = product(place, (0, 1), rounded, schur_ref, slot, start)
-
-
-def image_far_kernel(part_ref, g2, g3, near_ref, sum_ref, gamma_ref, schur_ref, *refs):
+            at = pl.ds(slot * edge_len + start, CHUNK)
+            sum_ref[:, at] = sum_in[:, at] + product(place, (0, 1), rounded, schur_ref, slot, start)
+
+
+def image_last_kernel(part_ref, g3, first_ref, near_ref, sum_ref, gamma_ref, schur_ref, *refs):
     precon_ref, image_near_ref, image_far_ref, e0, e1, e2, e3, message_ref, rounded = refs[-9:]
-    place, edge_len = Place(), g2.shape[1]
-    for i, got in enumerate((g2, g3)):
-        at = pl.ds(i * edge_len, edge_len)
-        value = part_ref[:, at] + jnp.where(place.shared[2 + i], got[...].astype(F32), 0.0)
-        precon_ref[:, at] = value
-        rounded[:, at] = value.astype(BF16)
+    place, edge_len = Place(), g3.shape[1]
+    value = part_ref[...] + jnp.where(place.shared[3], g3[...].astype(F32), 0.0)
+    precon_ref[:, pl.ds(0, edge_len)] = first_ref[...]
+    precon_ref[:, pl.ds(edge_len, edge_len)] = value
+    rounded[...] = value.astype(BF16)
     halves, vectors = (image_near_ref, image_far_ref), (near_ref, precon_ref)
     delta = None
     for slot, edge_ref in enumerate((e0, e1, e2, e3)):
         for start in range(0, edge_len, CHUNK):
-            image = sum_ref[:, pl.ds(slot * edge_len + start, CHUNK)] + product(place, (2, 3), rounded, schur_ref, slot, start)
+            image = sum_ref[:, pl.ds(slot * edge_len + start, CHUNK)] + product(place, (3,), rounded, schur_ref, slot, start)
             at = pl.ds(slot % 2 * edge_len + start, CHUNK)
             halves[slot // 2][:, at] = image
             edge_ref[: image.shape[0], pl.ds(start, CHUNK)] = image
@@ -278,6 +289,10 @@
     return jnp.concatenate([*rows, jnp.zeros((LANES - count, LANES), F32)], axis=0).T[:realiz]
 
 
+def in_slots(refs):
+    return [refs[ORDER.index(slot)] for slot in range(4)]
+
+
 def new_residual(place, slot, mode, columns, image_ref, got_ref, old, at, start):
     got = got_ref[: image_ref.shape[0], pl.ds(start, CHUNK)]
     shared = place.shared[slot]
@@ -297,6 +312,22 @@
     return direction, old[1][:, at] + columns[:, 0:1] * direction
 
 
+def precondition(place, columns, scaled, inverse_ref, slots, resid_refs, part_at, edge_refs, gamma):
+    edge_len = scaled.shape[1] // 4
+    for slot in slots:
+        flat, ramp_by = (columns[:, 8 + 2 * slot + i : 9 + 2 * slot + i] for i in range(2))
+        for start in range(0, edge_len, CHUNK):
+            level, ramp = basis_parts(edge_len, start, CHUNK)
+            part = product(place, (0, 1, 2, 3), scaled, inverse_ref, slot, start)
+            part = place.weight(slot) * (part + (flat * level + ramp_by * ramp))
+            part_ref, first = part_at[slot]
+            part_ref[:, pl.ds(first + start, CHUNK)] = part
+            edge_refs[slot][:, pl.ds(start, CHUNK)] = part.astype(BF16)
+            here = lane_parts(resid_refs[slot // 2][:, pl.ds(slot % 2 * edge_len + start, CHUNK)] * part)
+            gamma = here if gamma is None else gamma + here
+    return gamma
+
+
 OLD = {"load": 0, "init": 1, "next": 2}
 
 
@@ -304,7 +335,7 @@
     refs = list(refs)
     take = lambda n: [refs.pop(0) for _ in range(n)]
     place = Place()
-    images, edges, (gathered_ref,) = take(2), take(4), take(1)
+    images, edges, (gathered_ref,) = take(2), in_slots(take(4)), take(1)
     olds = [take(OLD[mode]) for _ in range(2)]
     state_in, = take(1) if mode == "next" else (None,)
     coarse_in, = take(1) if mode != "load" else (None,)
@@ -313,7 +344,7 @@
     news = [take(1 if mode == "load" else 2) for _ in range(2)]
     columns_ref, coarse_ref = take(2)
     state_ref, applied_ref = take(2) if mode != "load" else (None, None)
-    halves, (gamma_ref,), edge_refs, (scaled,) = take(2), take(1), take(4), take(1)
+    scaled, part_ref, edge_ref, gamma_ref = take(4)
     realiz, edge_len = images[0].shape[0], edges[0].shape[1]
     if mode == "load":
         coarse_table(gathered_ref, coarse_ref)
@@ -342,19 +373,16 @@
     rows.append(level + pltpu.roll(ramp, LANES // 2, 1))
     columns = turn(rows, realiz)
     columns_ref[...] = columns
-    gamma = None
-    for slot, edge_ref in enumerate(edge_refs):
-        flat, ramp_by = (columns[:, 8 + 2 * slot + i : 9 + 2 * slot + i] for i in range(2))
-        for start in range(0, edge_len, CHUNK):
-            level, ramp = basis_parts(edge_len, start, CHUNK)
-            part = product(place, (0, 1, 2, 3), scaled, inverse_ref, slot, start)
-            part = place.weight(slot) * (part + (flat * level + ramp_by * ramp))
-            at = pl.ds(slot % 2 * edge_len + start, CHUNK)
-            halves[slot // 2][:, at] = part
-            edge_ref[:, pl.ds(start, CHUNK)] = part.astype(BF16)
-            here = lane_parts(news[slot // 2][0][:, at] * part)
-            gamma = here if gamma is None else gamma + here
-    gamma_ref[...] = gamma
+    resids = [new[0] for new in news]
+    gamma_ref[...] = precondition(place, columns, scaled, inverse_ref, (2,), resids, {2: (part_ref, 0)}, {2: edge_ref}, None)
+
+
+def rest_kernel(columns_ref, scaled, near_ref, far_ref, gamma_in, inverse_ref, part_near_ref, part_ref, gamma_ref, e0, e1, e3):
+    edge_len = scaled.shape[1] // 4
+    part_at = {0: (part_near_ref, 0), 1: (part_near_ref, edge_len), 3: (part_ref, 0)}
+    gamma_ref[...] = precondition(
+        Place(), columns_ref[...], scaled, inverse_ref, (0, 3, 1), (near_ref, far_ref), part_at, {0: e0, 1: e1, 3: e3}, gamma_in[...]
+    )
 
 
 def field_kernel(mode, columns_ref, *refs):
@@ -372,7 +400,7 @@
     refs = list(refs)
     take = lambda n: [refs.pop(0) for _ in range(n)]
     place = Place()
-    images, edges, (gathered_ref,) = take(2), take(4), take(1)
+    images, edges, (gathered_ref,) = take(2), in_slots(take(4)), take(1)
     olds, (state_in,), tracks = [take(2) for _ in range(2)], take(1), [take(3) for _ in range(2)]
     field_ref, resid_ref = refs
     realiz, edge_len = images[0].shape[0], edges[0].shape[1]
@@ -396,13 +424,13 @@
     cols, rows = lax.axis_size("sx"), lax.axis_size("sy")
     devices = cols * rows
     capacity = max(2, 2 * obs_count // devices)
-    edge = shape(realiz, size // 4, BF16)
+    edge, quarter = shape(realiz, size // 4, BF16), shape(realiz, size // 4)
     exact = [shape(realiz + PAD, size // 4)] * 4
     half, whole = shape(realiz, size // 2), shape(realiz, size)
     message = jax.ShapeDtypeStruct((devices, 1, 5 * LANES), F32)
     narrow, state_shape = shape(realiz, LANES), shape(8, LANES)
     coarse_state = shape(4 * devices, LANES)
-    scratch_half = pltpu.VMEM((realiz, size // 2), BF16)
+    scratch_half, scratch_quarter = pltpu.VMEM((realiz, size // 2), BF16), pltpu.VMEM((realiz, size // 4), BF16)
     flops = 2 * realiz * size * size
     schur_mat, inverse_mat = schur[0, 0], local_inverse[0, 0]
 
@@ -429,21 +457,26 @@
     mode, olds, states = "load", ([], []), []
     for step in range(ITERS + 1):
         g, gathered = exchange((e0, e1, e2, e3)), gather(sent)
-        ins = [*image, *g, gathered, *olds[0], *olds[1]]
+        ins = [*image, *[g[slot] for slot in ORDER], gathered, *olds[0], *olds[1]]
         if step == ITERS:
             field, resid = call(last_kernel, [whole, whole], [*ins, states[0], z[0], *track[0], z[1], *track[1]])
             return field[None, None], resid[None, None]
         count, state_count = (1, 1) if mode == "load" else (2, 3)
         outs = call(
             functools.partial(step_kernel, mode),
-            [*[half] * (2 * count), narrow, *[coarse_state, state_shape, coarse_state][:state_count], half, half, narrow, *[edge] * 4],
+            [*[half] * (2 * count), narrow, *[coarse_state, state_shape, coarse_state][:state_count], shape(realiz, size, BF16), quarter, edge, narrow],
             [*ins, *states, *coarse_mats, inverse_mat],
-            [pltpu.VMEM((realiz, size), BF16)],
-            flops,
+            flops=flops // 4,
         )
         olds, (columns, coarse), outs = (outs[:count], outs[count : 2 * count]), outs[2 * count : 2 * count + 2], outs[2 * count + 2 :]
         states, outs = [*outs[:1], coarse, *outs[1:2]] if mode != "load" else [coarse], outs[state_count - 1 :]
-        part_near, part_far, gamma, e0, e1, e2, e3 = outs
+        scaled, part_first, e2, gamma = outs
+        part_near, part_last, gamma, e0, e1, e3 = call(
+            rest_kernel,
+            [half, quarter, narrow, edge, edge, edge],
+            (columns, scaled, olds[0][0], olds[1][0], gamma, inverse_mat),
+            flops=flops * 3 // 4,
+        )
         g = exchange((e0, e1, e2, e3))
         if step == 0:
             track = (), ()
@@ -452,15 +485,18 @@
                 functools.partial(field_kernel, mode), [half] * 4, (columns, z[0], *track[0], z[1], *track[1]), flops=1
             )
             track = outs[:2], outs[2:]
+        z_first, partial = call(
+            image_first_kernel, [quarter, whole], (part_first, g[2], schur_mat), [scratch_quarter], flops // 4
+        )
         z_near, partial = call(
-            image_near_kernel, [half, whole], (part_near, g[0], g[1], schur_mat), [scratch_half], flops // 2
+            image_near_kernel, [half, whole], (part_near, g[0], g[1], partial, schur_mat), [scratch_half], flops // 2
         )
         z_far, *image, e0, e1, e2, e3, sent = call(
-            image_far_kernel,
+            image_last_kernel,
             [half, half, half, *exact, message],
-            (part_far, g[2], g[3], z_near, partial, gamma, schur_mat, *track[0][:1]),
-            [scratch_half],
-            flops // 2,
+            (part_last, g[3], z_first, z_near, partial, gamma, schur_mat, *track[0][:1]),
+            [scratch_quarter],
+            flops // 4,
         )
         z = z_near, z_far
         mode = "init" if step == 0 else "next"

time: 172 us -> 169 us (0.983)
  waiting for transfers between devices: 17.3 us -> 10.2 us
  starting transfers between devices: 26.6 us -> 30.6 us
    ppermute x52, waiting for transfers between devices: 17.3 us -> 10.2 us  [exchange(): got[slot] = lax.ppermute(edges[slot], AXES, plans[slot])]
    ppermute x52, starting transfers between devices: 26.6 us -> 30.6 us  [exchange(): got[slot] = lax.ppermute(edges[slot], AXES, plans[slot])]
    pallas_call x26 -> x38, Pallas kernels: 30.1 us -> 31.6 us  [call(): pl.pallas_call(kernel, out_shape=outs, in_specs=[spec] * len(args), out_s...]
  transfers between devices with their start and end apart: 52 -> 52, of which waited for: 12 -> 12; matrix products, arithmetic and copies ran while one was open for 0% -> 0% of each run, Pallas kernels for 3% -> 10%
where the time goes in v5:
time: 169 us
  blocking collectives  95.2 us (56%)
  Pallas kernels  31.6 us (19%)
  starting transfers between devices  30.6 us (18%)
  waiting for transfers between devices  10.2 us (6%)
    all_to_all x7, blocking collectives, gather(): lax.all_to_all(message, AXES, split_axis=0, concat_axis=0, tiled=True)  79.6 us
    pallas_call x38, Pallas kernels, call(): pl.pallas_call(kernel, out_shape=outs, in_specs=[spec] * len(args), out_s...  31.6 us
    ppermute x52, starting transfers between devices, exchange(): got[slot] = lax.ppermute(edges[slot], AXES, plans[slot])  30.6 us
    all_to_all x1, blocking collectives, body(): lax.all_to_all(packed.reshape(devices, capacity, LANES), AXES, split_axis...  15.5 us
    ppermute x52, waiting for transfers between devices, exchange(): got[slot] = lax.ppermute(edges[slot], AXES, plans[slot])  10.2 us
  transfers between devices with their start and end apart: 52, of which 12 were waited for; matrix products, arithmetic and copies ran while one was open for 0% of the time, Pallas kernels for 10%

profile of v5, /device:TPU:0, one launch (start us, length us, event | category | flops | bytes accessed | tf_op | source)
XLA Modules:
  0.0 168.7 jit_solution(6338495563734797713)
XLA Ops:
  0.6 2.0 %shard_map.77 = (bf16[512,128]{1,0:T(8,128)(2,1)}, f32[8,128]{1,0:T(8,128)}, f32[8,128]{1,0:T(8,128)}) custom-call(bf16[64,256]{1,0:T(8,128)(2,1)} %bitcast.47, s32[1,256]{1,0:T(1,128)} %bitcast.48, s32[1,256]{1,0:T(1,128)} %bitcast.49, f32[8,256]{1,0:T(8,128)} %inverse_in.1), custom_call_target="tpu_custom_call" | custom-call | flops 8000000000 | bytes 43008 | tf_op jit(solution)/shard_map/pallas_call | solution.py:25
  2.7 15.5 %all_to_all.40 = bf16[32,16,128]{2,1,0:T(8,128)(2,1)S(1)} all-to-all(bf16[32,16,128]{2,1,0:T(8,128)(2,1)} %bitcast.44), channel_id=1, replica_groups=mesh['sx'=8,'sy'=4] {'sx','sy'}, dimensions={0} | all-to-all | bytes 262144 | tf_op jit(solution)/shard_map/all_to_all | solution.py:450
  20.9 11.1 %all_to_all.41.refs_6_ = f32[32,1,640]{2,1,0:T(1,128)S(1)} all-to-all(f32[32,1,640]{2,1,0:T(1,128)S(1)} %get-tuple-element.215), channel_id=1, replica_groups=mesh['sx'=8,'sy'=4] {'sx','sy'}, dimensions={0} | all-to-all | bytes 163840 | tf_op jit(solution)/shard_map/all_to_all | solution.py:418
  32.9 1.3 shard_map.80
  34.2 2.0 %collective-permute-start.6 = (bf16[64,512]{1,0:T(8,128)(2,1)S(1)}, bf16[64,512]{1,0:T(8,128)(2,1)S(1)}, u32[]{:S(2)}, u32[]{:S(2)}) collective-permute-start(bf16[64,512]{1,0:T(8,128)(2,1)S(1)} %get-tuple-element.229), channel_id=1, source_target_pairs={{0,4},{1,5},{2,6},{3,7},{4,0},{5,1},{6,2},{7,3},{8,12},{9,13},{10,... | collective-permute-start | bytes 196616 | tf_op jit(solution)/shard_map/ppermute | solution.py:77
  37.3 1.4 collective-permute-done.6.g0
  41.4 1.1 collective-permute-start.9
  43.0 11.4 %all_to_all.42.refs_6_ = f32[32,1,640]{2,1,0:T(1,128)S(1)} all-to-all(f32[32,1,640]{2,1,0:T(1,128)S(1)} %get-tuple-element.241), channel_id=1, replica_groups=mesh['sx'=8,'sy'=4] {'sx','sy'}, dimensions={0} | all-to-all | bytes 163840 | tf_op jit(solution)/shard_map/all_to_all | solution.py:418
  55.4 1.3 shard_map.85
  56.7 2.0 %collective-permute-start.14 = (bf16[64,512]{1,0:T(8,128)(2,1)S(1)}, bf16[64,512]{1,0:T(8,128)(2,1)S(1)}, u32[]{:S(2)}, u32[]{:S(2)}) collective-permute-start(bf16[64,512]{1,0:T(8,128)(2,1)S(1)} %get-tuple-element.254), channel_id=1, source_target_pairs={{0,4},{1,5},{2,6},{3,7},{4,0},{5,1},{6,2},{7,3},{8,12},{9,13},{10,... | collective-permute-start | bytes 196616 | tf_op jit(solution)/shard_map/ppermute | solution.py:77
  59.9 1.3 collective-permute-done.14.g0
  65.4 11.4 %all_to_all.43.refs_6_ = f32[32,1,640]{2,1,0:T(1,128)S(1)} all-to-all(f32[32,1,640]{2,1,0:T(1,128)S(1)} %get-tuple-element.268), channel_id=1, replica_groups=mesh['sx'=8,'sy'=4] {'sx','sy'}, dimensions={0} | all-to-all | bytes 163840 | tf_op jit(solution)/shard_map/all_to_all | solution.py:418
  77.8 1.3 shard_map.91
  79.1 2.0 %collective-permute-start.22 = (bf16[64,512]{1,0:T(8,128)(2,1)S(1)}, bf16[64,512]{1,0:T(8,128)(2,1)S(1)}, u32[]{:S(2)}, u32[]{:S(2)}) collective-permute-start(bf16[64,512]{1,0:T(8,128)(2,1)S(1)} %get-tuple-element.285), channel_id=1, source_target_pairs={{0,4},{1,5},{2,6},{3,7},{4,0},{5,1},{6,2},{7,3},{8,12},{9,13},{10,... | collective-permute-start | bytes 196616 | tf_op jit(solution)/shard_map/ppermute | solution.py:77
  82.4 1.3 collective-permute-done.22.g0
  87.9 11.4 %all_to_all.44.refs_6_ = f32[32,1,640]{2,1,0:T(1,128)S(1)} all-to-all(f32[32,1,640]{2,1,0:T(1,128)S(1)} %get-tuple-element.302), channel_id=1, replica_groups=mesh['sx'=8,'sy'=4] {'sx','sy'}, dimensions={0} | all-to-all | bytes 163840 | tf_op jit(solution)/shard_map/all_to_all | solution.py:418
  100.3 1.3 shard_map.97
  101.6 2.0 %collective-permute-start.30 = (bf16[64,512]{1,0:T(8,128)(2,1)S(1)}, bf16[64,512]{1,0:T(8,128)(2,1)S(1)}, u32[]{:S(2)}, u32[]{:S(2)}) collective-permute-start(bf16[64,512]{1,0:T(8,128)(2,1)S(1)} %get-tuple-element.319), channel_id=1, source_target_pairs={{0,4},{1,5},{2,6},{3,7},{4,0},{5,1},{6,2},{7,3},{8,12},{9,13},{10,... | collective-permute-start | bytes 196616 | tf_op jit(solution)/shard_map/ppermute | solution.py:77
  104.9 1.2 collective-permute-done.30.g0
  108.8 1.0 collective-permute-start.33
  110.4 11.4 %all_to_all.45.refs_6_ = f32[32,1,640]{2,1,0:T(1,128)S(1)} all-to-all(f32[32,1,640]{2,1,0:T(1,128)S(1)} %get-tuple-element.336), channel_id=1, replica_groups=mesh['sx'=8,'sy'=4] {'sx','sy'}, dimensions={0} | all-to-all | bytes 163840 | tf_op jit(solution)/shard_map/all_to_all | solution.py:418
  122.8 1.3 shard_map.103
  124.1 2.0 %collective-permute-start.38 = (bf16[64,512]{1,0:T(8,128)(2,1)S(1)}, bf16[64,512]{1,0:T(8,128)(2,1)S(1)}, u32[]{:S(2)}, u32[]{:S(2)}) collective-permute-start(bf16[64,512]{1,0:T(8,128)(2,1)S(1)} %get-tuple-element.353), channel_id=1, source_target_pairs={{0,4},{1,5},{2,6},{3,7},{4,0},{5,1},{6,2},{7,3},{8,12},{9,13},{10,... | collective-permute-start | bytes 196616 | tf_op jit(solution)/shard_map/ppermute | solution.py:77
  127.4 1.2 collective-permute-done.38.g0
  132.9 11.4 %all_to_all.46.refs_6_ = f32[32,1,640]{2,1,0:T(1,128)S(1)} all-to-all(f32[32,1,640]{2,1,0:T(1,128)S(1)} %get-tuple-element.370), channel_id=1, replica_groups=mesh['sx'=8,'sy'=4] {'sx','sy'}, dimensions={0} | all-to-all | bytes 163840 | tf_op jit(solution)/shard_map/all_to_all | solution.py:418
  144.3 1.3 shard_map.108
  145.7 1.3 shard_map.109
  147.1 2.0 %collective-permute-start.46 = (bf16[64,512]{1,0:T(8,128)(2,1)S(1)}, bf16[64,512]{1,0:T(8,128)(2,1)S(1)}, u32[]{:S(2)}, u32[]{:S(2)}) collective-permute-start(bf16[64,512]{1,0:T(8,128)(2,1)S(1)} %get-tuple-element.387), channel_id=1, source_target_pairs={{0,4},{1,5},{2,6},{3,7},{4,0},{5,1},{6,2},{7,3},{8,12},{9,13},{10,... | collective-permute-start | bytes 196616 | tf_op jit(solution)/shard_map/ppermute | solution.py:77
  150.3 1.2 collective-permute-done.46.g0
  154.2 1.1 collective-permute-start.49
  155.8 11.4 %all_to_all.47.refs_6_ = f32[32,1,640]{2,1,0:T(1,128)S(1)} all-to-all(f32[32,1,640]{2,1,0:T(1,128)S(1)} %get-tuple-element.404), channel_id=1, replica_groups=mesh['sx'=8,'sy'=4] {'sx','sy'}, dimensions={0} | all-to-all | bytes 163840 | tf_op jit(solution)/shard_map/all_to_all | solution.py:418
  167.2 1.4 shard_map.114
  (132 shorter events, 36.6 us)
Async XLA Ops:
  19.2 12.8 %collective-permute-start = (f32[80,512]{1,0:T(8,128)S(1)}, f32[80,512]{1,0:T(8,128)S(1)}, u32[]{:S(2)}, u32[]{:S(2)}) collective-permute-start(f32[80,512]{1,0:T(8,128)S(1)} %get-tuple-element.211), channel_id=1, source_target_pairs={{0,1},{1,0},{2,3},{3,2},{4,5},{5,4},{6,7},{7,6},{8,9},{9,8},{10,11... | collective-permute-start | bytes 491528 | tf_op jit(solution)/shard_map/ppermute | solution.py:77
  19.5 12.5 %collective-permute-start.1 = (f32[80,512]{1,0:T(8,128)S(1)}, f32[80,512]{1,0:T(8,128)S(1)}, u32[]{:S(2)}, u32[]{:S(2)}) collective-permute-start(f32[80,512]{1,0:T(8,128)S(1)} %get-tuple-element.212), channel_id=1, source_target_pairs={{0,4},{1,5},{2,6},{3,7},{4,0},{5,1},{6,2},{7,3},{8,12},{9,13},{10,... | collective-permute-start | bytes 491528 | tf_op jit(solution)/shard_map/ppermute | solution.py:77
  20.0 12.0 %collective-permute-start.2 = (f32[80,512]{1,0:T(8,128)S(1)}, f32[80,512]{1,0:T(8,128)S(1)}, u32[]{:S(2)}, u32[]{:S(2)}) collective-permute-start(f32[80,512]{1,0:T(8,128)S(1)} %get-tuple-element.213), channel_id=1, source_target_pairs={{0,1},{1,0},{2,3},{3,2},{4,8},{5,9},{6,10},{7,11},{8,4},{9,5},{10,... | collective-permute-start | bytes 491528 | tf_op jit(solution)/shard_map/ppermute | solution.py:77
  20.1 11.8 %collective-permute-start.3 = (f32[80,512]{1,0:T(8,128)S(1)}, f32[80,512]{1,0:T(8,128)S(1)}, u32[]{:S(2)}, u32[]{:S(2)}) collective-permute-start(f32[80,512]{1,0:T(8,128)S(1)} %get-tuple-element.214), channel_id=1, source_target_pairs={{0,3},{1,2},{2,1},{3,0},{4,7},{5,6},{6,5},{7,4},{8,11},{9,10},{10,... | collective-permute-start | bytes 491528 | tf_op jit(solution)/shard_map/ppermute | solution.py:77
  34.2 4.5 %collective-permute-start.6 = (bf16[64,512]{1,0:T(8,128)(2,1)S(1)}, bf16[64,512]{1,0:T(8,128)(2,1)S(1)}, u32[]{:S(2)}, u32[]{:S(2)}) collective-permute-start(bf16[64,512]{1,0:T(8,128)(2,1)S(1)} %get-tuple-element.229), channel_id=1, source_target_pairs={{0,4},{1,5},{2,6},{3,7},{4,0},{5,1},{6,2},{7,3},{8,12},{9,13},{10,... | collective-permute-start | bytes 196616 | tf_op jit(solution)/shard_map/ppermute | solution.py:77
  40.9 13.5 %collective-permute-start.8 = (f32[80,512]{1,0:T(8,128)S(1)}, f32[80,512]{1,0:T(8,128)S(1)}, u32[]{:S(2)}, u32[]{:S(2)}) collective-permute-start(f32[80,512]{1,0:T(8,128)S(1)} %get-tuple-element.237), channel_id=1, source_target_pairs={{0,1},{1,0},{2,3},{3,2},{4,5},{5,4},{6,7},{7,6},{8,9},{9,8},{10,11... | collective-permute-start | bytes 491528 | tf_op jit(solution)/shard_map/ppermute | solution.py:77
  41.4 13.0 %collective-permute-start.9 = (f32[80,512]{1,0:T(8,128)S(1)}, f32[80,512]{1,0:T(8,128)S(1)}, u32[]{:S(2)}, u32[]{:S(2)}) collective-permute-start(f32[80,512]{1,0:T(8,128)S(1)} %get-tuple-element.238), channel_id=1, source_target_pairs={{0,4},{1,5},{2,6},{3,7},{4,0},{5,1},{6,2},{7,3},{8,12},{9,13},{10,... | collective-permute-start | bytes 491528 | tf_op jit(solution)/shard_map/ppermute | solution.py:77
  42.5 11.9 %collective-permute-start.10 = (f32[80,512]{1,0:T(8,128)S(1)}, f32[80,512]{1,0:T(8,128)S(1)}, u32[]{:S(2)}, u32[]{:S(2)}) collective-permute-start(f32[80,512]{1,0:T(8,128)S(1)} %get-tuple-element.239), channel_id=1, source_target_pairs={{0,1},{1,0},{2,3},{3,2},{4,8},{5,9},{6,10},{7,11},{8,4},{9,5},{10,... | collective-permute-start | bytes 491528 | tf_op jit(solution)/shard_map/ppermute | solution.py:77
  42.6 11.8 %collective-permute-start.11 = (f32[80,512]{1,0:T(8,128)S(1)}, f32[80,512]{1,0:T(8,128)S(1)}, u32[]{:S(2)}, u32[]{:S(2)}) collective-permute-start(f32[80,512]{1,0:T(8,128)S(1)} %get-tuple-element.240), channel_id=1, source_target_pairs={{0,3},{1,2},{2,1},{3,0},{4,7},{5,6},{6,5},{7,4},{8,11},{9,10},{10,... | collective-permute-start | bytes 491528 | tf_op jit(solution)/shard_map/ppermute | solution.py:77
  56.7 4.5 %collective-permute-start.14 = (bf16[64,512]{1,0:T(8,128)(2,1)S(1)}, bf16[64,512]{1,0:T(8,128)(2,1)S(1)}, u32[]{:S(2)}, u32[]{:S(2)}) collective-permute-start(bf16[64,512]{1,0:T(8,128)(2,1)S(1)} %get-tuple-element.254), channel_id=1, source_target_pairs={{0,4},{1,5},{2,6},{3,7},{4,0},{5,1},{6,2},{7,3},{8,12},{9,13},{10,... | collective-permute-start | bytes 196616 | tf_op jit(solution)/shard_map/ppermute | solution.py:77
  63.3 13.5 %collective-permute-start.16 = (f32[80,512]{1,0:T(8,128)S(1)}, f32[80,512]{1,0:T(8,128)S(1)}, u32[]{:S(2)}, u32[]{:S(2)}) collective-permute-start(f32[80,512]{1,0:T(8,128)S(1)} %get-tuple-element.264), channel_id=1, source_target_pairs={{0,1},{1,0},{2,3},{3,2},{4,5},{5,4},{6,7},{7,6},{8,9},{9,8},{10,11... | collective-permute-start | bytes 491528 | tf_op jit(solution)/shard_map/ppermute | solution.py:77
  63.8 13.0 %collective-permute-start.17 = (f32[80,512]{1,0:T(8,128)S(1)}, f32[80,512]{1,0:T(8,128)S(1)}, u32[]{:S(2)}, u32[]{:S(2)}) collective-permute-start(f32[80,512]{1,0:T(8,128)S(1)} %get-tuple-element.265), channel_id=1, source_target_pairs={{0,4},{1,5},{2,6},{3,7},{4,0},{5,1},{6,2},{7,3},{8,12},{9,13},{10,... | collective-permute-start | bytes 491528 | tf_op jit(solution)/shard_map/ppermute | solution.py:77
  64.9 11.9 %collective-permute-start.18 = (f32[80,512]{1,0:T(8,128)S(1)}, f32[80,512]{1,0:T(8,128)S(1)}, u32[]{:S(2)}, u32[]{:S(2)}) collective-permute-start(f32[80,512]{1,0:T(8,128)S(1)} %get-tuple-element.266), channel_id=1, source_target_pairs={{0,1},{1,0},{2,3},{3,2},{4,8},{5,9},{6,10},{7,11},{8,4},{9,5},{10,... | collective-permute-start | bytes 491528 | tf_op jit(solution)/shard_map/ppermute | solution.py:77
  65.1 11.8 %collective-permute-start.19 = (f32[80,512]{1,0:T(8,128)S(1)}, f32[80,512]{1,0:T(8,128)S(1)}, u32[]{:S(2)}, u32[]{:S(2)}) collective-permute-start(f32[80,512]{1,0:T(8,128)S(1)} %get-tuple-element.267), channel_id=1, source_target_pairs={{0,3},{1,2},{2,1},{3,0},{4,7},{5,6},{6,5},{7,4},{8,11},{9,10},{10,... | collective-permute-start | bytes 491528 | tf_op jit(solution)/shard_map/ppermute | solution.py:77
  85.8 13.5 %collective-permute-start.24 = (f32[80,512]{1,0:T(8,128)S(1)}, f32[80,512]{1,0:T(8,128)S(1)}, u32[]{:S(2)}, u32[]{:S(2)}) collective-permute-start(f32[80,512]{1,0:T(8,128)S(1)} %get-tuple-element.298), channel_id=1, source_target_pairs={{0,1},{1,0},{2,3},{3,2},{4,5},{5,4},{6,7},{7,6},{8,9},{9,8},{10,11... | collective-permute-start | bytes 491528 | tf_op jit(solution)/shard_map/ppermute | solution.py:77
  86.3 13.0 %collective-permute-start.25 = (f32[80,512]{1,0:T(8,128)S(1)}, f32[80,512]{1,0:T(8,128)S(1)}, u32[]{:S(2)}, u32[]{:S(2)}) collective-permute-start(f32[80,512]{1,0:T(8,128)S(1)} %get-tuple-element.299), channel_id=1, source_target_pairs={{0,4},{1,5},{2,6},{3,7},{4,0},{5,1},{6,2},{7,3},{8,12},{9,13},{10,... | collective-permute-start | bytes 491528 | tf_op jit(solution)/shard_map/ppermute | solution.py:77
  87.4 12.0 %collective-permute-start.26 = (f32[80,512]{1,0:T(8,128)S(1)}, f32[80,512]{1,0:T(8,128)S(1)}, u32[]{:S(2)}, u32[]{:S(2)}) collective-permute-start(f32[80,512]{1,0:T(8,128)S(1)} %get-tuple-element.300), channel_id=1, source_target_pairs={{0,1},{1,0},{2,3},{3,2},{4,8},{5,9},{6,10},{7,11},{8,4},{9,5},{10,... | collective-permute-start | bytes 491528 | tf_op jit(solution)/shard_map/ppermute | solution.py:77
  87.5 11.8 %collective-permute-start.27 = (f32[80,512]{1,0:T(8,128)S(1)}, f32[80,512]{1,0:T(8,128)S(1)}, u32[]{:S(2)}, u32[]{:S(2)}) collective-permute-start(f32[80,512]{1,0:T(8,128)S(1)} %get-tuple-element.301), channel_id=1, source_target_pairs={{0,3},{1,2},{2,1},{3,0},{4,7},{5,6},{6,5},{7,4},{8,11},{9,10},{10,... | collective-permute-start | bytes 491528 | tf_op jit(solution)/shard_map/ppermute | solution.py:77
  101.6 4.5 %collective-permute-start.30 = (bf16[64,512]{1,0:T(8,128)(2,1)S(1)}, bf16[64,512]{1,0:T(8,128)(2,1)S(1)}, u32[]{:S(2)}, u32[]{:S(2)}) collective-permute-start(bf16[64,512]{1,0:T(8,128)(2,1)S(1)} %get-tuple-element.319), channel_id=1, source_target_pairs={{0,4},{1,5},{2,6},{3,7},{4,0},{5,1},{6,2},{7,3},{8,12},{9,13},{10,... | collective-permute-start | bytes 196616 | tf_op jit(solution)/shard_map/ppermute | solution.py:77
  108.3 13.5 %collective-permute-start.32 = (f32[80,512]{1,0:T(8,128)S(1)}, f32[80,512]{1,0:T(8,128)S(1)}, u32[]{:S(2)}, u32[]{:S(2)}) collective-permute-start(f32[80,512]{1,0:T(8,128)S(1)} %get-tuple-element.332), channel_id=1, source_target_pairs={{0,1},{1,0},{2,3},{3,2},{4,5},{5,4},{6,7},{7,6},{8,9},{9,8},{10,11... | collective-permute-start | bytes 491528 | tf_op jit(solution)/shard_map/ppermute | solution.py:77
  108.8 13.0 %collective-permute-start.33 = (f32[80,512]{1,0:T(8,128)S(1)}, f32[80,512]{1,0:T(8,128)S(1)}, u32[]{:S(2)}, u32[]{:S(2)}) collective-permute-start(f32[80,512]{1,0:T(8,128)S(1)} %get-tuple-element.333), channel_id=1, source_target_pairs={{0,4},{1,5},{2,6},{3,7},{4,0},{5,1},{6,2},{7,3},{8,12},{9,13},{10,... | collective-permute-start | bytes 491528 | tf_op jit(solution)/shard_map/ppermute | solution.py:77
  109.8 12.0 %collective-permute-start.34 = (f32[80,512]{1,0:T(8,128)S(1)}, f32[80,512]{1,0:T(8,128)S(1)}, u32[]{:S(2)}, u32[]{:S(2)}) collective-permute-start(f32[80,512]{1,0:T(8,128)S(1)} %get-tuple-element.334), channel_id=1, source_target_pairs={{0,1},{1,0},{2,3},{3,2},{4,8},{5,9},{6,10},{7,11},{8,4},{9,5},{10,... | collective-permute-start | bytes 491528 | tf_op jit(solution)/shard_map/ppermute | solution.py:77
  110.0 11.8 %collective-permute-start.35 = (f32[80,512]{1,0:T(8,128)S(1)}, f32[80,512]{1,0:T(8,128)S(1)}, u32[]{:S(2)}, u32[]{:S(2)}) collective-permute-start(f32[80,512]{1,0:T(8,128)S(1)} %get-tuple-element.335), channel_id=1, source_target_pairs={{0,3},{1,2},{2,1},{3,0},{4,7},{5,6},{6,5},{7,4},{8,11},{9,10},{10,... | collective-permute-start | bytes 491528 | tf_op jit(solution)/shard_map/ppermute | solution.py:77
  130.8 13.5 %collective-permute-start.40 = (f32[80,512]{1,0:T(8,128)S(1)}, f32[80,512]{1,0:T(8,128)S(1)}, u32[]{:S(2)}, u32[]{:S(2)}) collective-permute-start(f32[80,512]{1,0:T(8,128)S(1)} %get-tuple-element.366), channel_id=1, source_target_pairs={{0,1},{1,0},{2,3},{3,2},{4,5},{5,4},{6,7},{7,6},{8,9},{9,8},{10,11... | collective-permute-start | bytes 491528 | tf_op jit(solution)/shard_map/ppermute | solution.py:77
  131.3 13.0 %collective-permute-start.41 = (f32[80,512]{1,0:T(8,128)S(1)}, f32[80,512]{1,0:T(8,128)S(1)}, u32[]{:S(2)}, u32[]{:S(2)}) collective-permute-start(f32[80,512]{1,0:T(8,128)S(1)} %get-tuple-element.367), channel_id=1, source_target_pairs={{0,4},{1,5},{2,6},{3,7},{4,0},{5,1},{6,2},{7,3},{8,12},{9,13},{10,... | collective-permute-start | bytes 491528 | tf_op jit(solution)/shard_map/ppermute | solution.py:77
  132.3 12.0 %collective-permute-start.42 = (f32[80,512]{1,0:T(8,128)S(1)}, f32[80,512]{1,0:T(8,128)S(1)}, u32[]{:S(2)}, u32[]{:S(2)}) collective-permute-start(f32[80,512]{1,0:T(8,128)S(1)} %get-tuple-element.368), channel_id=1, source_target_pairs={{0,1},{1,0},{2,3},{3,2},{4,8},{5,9},{6,10},{7,11},{8,4},{9,5},{10,... | collective-permute-start | bytes 491528 | tf_op jit(solution)/shard_map/ppermute | solution.py:77
  132.5 11.8 %collective-permute-start.43 = (f32[80,512]{1,0:T(8,128)S(1)}, f32[80,512]{1,0:T(8,128)S(1)}, u32[]{:S(2)}, u32[]{:S(2)}) collective-permute-start(f32[80,512]{1,0:T(8,128)S(1)} %get-tuple-element.369), channel_id=1, source_target_pairs={{0,3},{1,2},{2,1},{3,0},{4,7},{5,6},{6,5},{7,4},{8,11},{9,10},{10,... | collective-permute-start | bytes 491528 | tf_op jit(solution)/shard_map/ppermute | solution.py:77
  147.1 4.5 %collective-permute-start.46 = (bf16[64,512]{1,0:T(8,128)(2,1)S(1)}, bf16[64,512]{1,0:T(8,128)(2,1)S(1)}, u32[]{:S(2)}, u32[]{:S(2)}) collective-permute-start(bf16[64,512]{1,0:T(8,128)(2,1)S(1)} %get-tuple-element.387), channel_id=1, source_target_pairs={{0,4},{1,5},{2,6},{3,7},{4,0},{5,1},{6,2},{7,3},{8,12},{9,13},{10,... | collective-permute-start | bytes 196616 | tf_op jit(solution)/shard_map/ppermute | solution.py:77
  153.7 13.5 %collective-permute-start.48 = (f32[80,512]{1,0:T(8,128)S(1)}, f32[80,512]{1,0:T(8,128)S(1)}, u32[]{:S(2)}, u32[]{:S(2)}) collective-permute-start(f32[80,512]{1,0:T(8,128)S(1)} %get-tuple-element.400), channel_id=1, source_target_pairs={{0,1},{1,0},{2,3},{3,2},{4,5},{5,4},{6,7},{7,6},{8,9},{9,8},{10,11... | collective-permute-start | bytes 491528 | tf_op jit(solution)/shard_map/ppermute | solution.py:77
  154.2 13.0 %collective-permute-start.49 = (f32[80,512]{1,0:T(8,128)S(1)}, f32[80,512]{1,0:T(8,128)S(1)}, u32[]{:S(2)}, u32[]{:S(2)}) collective-permute-start(f32[80,512]{1,0:T(8,128)S(1)} %get-tuple-element.401), channel_id=1, source_target_pairs={{0,4},{1,5},{2,6},{3,7},{4,0},{5,1},{6,2},{7,3},{8,12},{9,13},{10,... | collective-permute-start | bytes 491528 | tf_op jit(solution)/shard_map/ppermute | solution.py:77
  155.3 12.0 %collective-permute-start.50 = (f32[80,512]{1,0:T(8,128)S(1)}, f32[80,512]{1,0:T(8,128)S(1)}, u32[]{:S(2)}, u32[]{:S(2)}) collective-permute-start(f32[80,512]{1,0:T(8,128)S(1)} %get-tuple-element.402), channel_id=1, source_target_pairs={{0,1},{1,0},{2,3},{3,2},{4,8},{5,9},{6,10},{7,11},{8,4},{9,5},{10,... | collective-permute-start | bytes 491528 | tf_op jit(solution)/shard_map/ppermute | solution.py:77
  155.4 11.8 %collective-permute-start.51 = (f32[80,512]{1,0:T(8,128)S(1)}, f32[80,512]{1,0:T(8,128)S(1)}, u32[]{:S(2)}, u32[]{:S(2)}) collective-permute-start(f32[80,512]{1,0:T(8,128)S(1)} %get-tuple-element.403), channel_id=1, source_target_pairs={{0,3},{1,2},{2,1},{3,0},{4,7},{5,6},{6,5},{7,4},{8,11},{9,10},{10,... | collective-permute-start | bytes 491528 | tf_op jit(solution)/shard_map/ppermute | solution.py:77
  (26 other events, 169.2 us)

commit v6 on v5

--- a/solution.py
+++ b/solution.py
@@ -216,41 +216,31 @@
     return total
 
 
-def image_first_kernel(part_ref, got_ref, schur_ref, precon_ref, sum_ref, rounded):
-    place, edge_len = Place(), got_ref.shape[1]
-    value = part_ref[...] + jnp.where(place.shared[2], got_ref[...].astype(F32), 0.0)
-    precon_ref[...] = value
-    rounded[...] = value.astype(BF16)
+def image_far_kernel(part_ref, g3, g2, schur_ref, precon_ref, sum_ref, rounded):
+    place, edge_len = Place(), g2.shape[1]
+    for i, got in enumerate((g2, g3)):
+        at = pl.ds(i * edge_len, edge_len)
+        value = part_ref[:, at] + jnp.where(place.shared[2 + i], got[...].astype(F32), 0.0)
+        precon_ref[:, at] = value
+        rounded[:, at] = value.astype(BF16)
     for slot in range(4):
         for start in range(0, edge_len, CHUNK):
-            sum_ref[:, pl.ds(slot * edge_len + start, CHUNK)] = product(place, (2,), rounded, schur_ref, slot, start)
-
-
-def image_near_kernel(part_ref, g0, g1, sum_in, schur_ref, precon_ref, sum_ref, rounded):
+            sum_ref[:, pl.ds(slot * edge_len + start, CHUNK)] = product(place, (2, 3), rounded, schur_ref, slot, start)
+
+
+def image_near_kernel(part_ref, g0, g1, far_ref, sum_ref, gamma_ref, schur_ref, *refs):
+    precon_ref, image_near_ref, image_far_ref, e0, e1, e2, e3, message_ref, rounded = refs[-9:]
     place, edge_len = Place(), g0.shape[1]
     for i, got in enumerate((g0, g1)):
         at = pl.ds(i * edge_len, edge_len)
         value = part_ref[:, at] + got[...].astype(F32)
         precon_ref[:, at] = value
         rounded[:, at] = value.astype(BF16)
-    for slot in range(4):
-        for start in range(0, edge_len, CHUNK):
-            at = pl.ds(slot * edge_len + start, CHUNK)
-            sum_ref[:, at] = sum_in[:, at] + product(place, (0, 1), rounded, schur_ref, slot, start)
-
-
-def image_last_kernel(part_ref, g3, first_ref, near_ref, sum_ref, gamma_ref, schur_ref, *refs):
-    precon_ref, image_near_ref, image_far_ref, e0, e1, e2, e3, message_ref, rounded = refs[-9:]
-    place, edge_len = Place(), g3.shape[1]
-    value = part_ref[...] + jnp.where(place.shared[3], g3[...].astype(F32), 0.0)
-    precon_ref[:, pl.ds(0, edge_len)] = first_ref[...]
-    precon_ref[:, pl.ds(edge_len, edge_len)] = value
-    rounded[...] = value.astype(BF16)
-    halves, vectors = (image_near_ref, image_far_ref), (near_ref, precon_ref)
+    halves, vectors = (image_near_ref, image_far_ref), (precon_ref, far_ref)
     delta = None
     for slot, edge_ref in enumerate((e0, e1, e2, e3)):
         for start in range(0, edge_len, CHUNK):
-            image = sum_ref[:, pl.ds(slot * edge_len + start, CHUNK)] + product(place, (3,), rounded, schur_ref, slot, start)
+            image = sum_ref[:, pl.ds(slot * edge_len + start, CHUNK)] + product(place, (0, 1), rounded, schur_ref, slot, start)
             at = pl.ds(slot % 2 * edge_len + start, CHUNK)
             halves[slot // 2][:, at] = image
             edge_ref[: image.shape[0], pl.ds(start, CHUNK)] = image
@@ -312,9 +302,9 @@
     return direction, old[1][:, at] + columns[:, 0:1] * direction
 
 
-def precondition(place, columns, scaled, inverse_ref, slots, resid_refs, part_at, edge_refs, gamma):
+def precondition(place, columns, scaled, inverse_ref, part_at, resid_refs, edge_refs, gamma):
     edge_len = scaled.shape[1] // 4
-    for slot in slots:
+    for slot in part_at:
         flat, ramp_by = (columns[:, 8 + 2 * slot + i : 9 + 2 * slot + i] for i in range(2))
         for start in range(0, edge_len, CHUNK):
             level, ramp = basis_parts(edge_len, start, CHUNK)
@@ -344,7 +334,7 @@
     news = [take(1 if mode == "load" else 2) for _ in range(2)]
     columns_ref, coarse_ref = take(2)
     state_ref, applied_ref = take(2) if mode != "load" else (None, None)
-    scaled, part_ref, edge_ref, gamma_ref = take(4)
+    scaled, part_ref, e2, e3, gamma_ref = take(5)
     realiz, edge_len = images[0].shape[0], edges[0].shape[1]
     if mode == "load":
         coarse_table(gathered_ref, coarse_ref)
@@ -374,14 +364,14 @@
     columns = turn(rows, realiz)
     columns_ref[...] = columns
     resids = [new[0] for new in news]
-    gamma_ref[...] = precondition(place, columns, scaled, inverse_ref, (2,), resids, {2: (part_ref, 0)}, {2: edge_ref}, None)
-
-
-def rest_kernel(columns_ref, scaled, near_ref, far_ref, gamma_in, inverse_ref, part_near_ref, part_ref, gamma_ref, e0, e1, e3):
-    edge_len = scaled.shape[1] // 4
-    part_at = {0: (part_near_ref, 0), 1: (part_near_ref, edge_len), 3: (part_ref, 0)}
+    part_at = {2: (part_ref, 0), 3: (part_ref, edge_len)}
+    gamma_ref[...] = precondition(place, columns, scaled, inverse_ref, part_at, resids, {2: e2, 3: e3}, None)
+
+
+def rest_kernel(columns_ref, scaled, near_ref, far_ref, gamma_in, inverse_ref, part_ref, e0, e1, gamma_ref):
+    part_at = {0: (part_ref, 0), 1: (part_ref, scaled.shape[1] // 4)}
     gamma_ref[...] = precondition(
-        Place(), columns_ref[...], scaled, inverse_ref, (0, 3, 1), (near_ref, far_ref), part_at, {0: e0, 1: e1, 3: e3}, gamma_in[...]
+        Place(), columns_ref[...], scaled, inverse_ref, part_at, (near_ref, far_ref), {0: e0, 1: e1}, gamma_in[...]
     )
 
 
@@ -424,13 +414,13 @@
     cols, rows = lax.axis_size("sx"), lax.axis_size("sy")
     devices = cols * rows
     capacity = max(2, 2 * obs_count // devices)
-    edge, quarter = shape(realiz, size // 4, BF16), shape(realiz, size // 4)
+    edge = shape(realiz, size // 4, BF16)
     exact = [shape(realiz + PAD, size // 4)] * 4
     half, whole = shape(realiz, size // 2), shape(realiz, size)
     message = jax.ShapeDtypeStruct((devices, 1, 5 * LANES), F32)
     narrow, state_shape = shape(realiz, LANES), shape(8, LANES)
     coarse_state = shape(4 * devices, LANES)
-    scratch_half, scratch_quarter = pltpu.VMEM((realiz, size // 2), BF16), pltpu.VMEM((realiz, size // 4), BF16)
+    scratch_half = pltpu.VMEM((realiz, size // 2), BF16)
     flops = 2 * realiz * size * size
     schur_mat, inverse_mat = schur[0, 0], local_inverse[0, 0]
 
@@ -464,18 +454,18 @@
         count, state_count = (1, 1) if mode == "load" else (2, 3)
         outs = call(
             functools.partial(step_kernel, mode),
-            [*[half] * (2 * count), narrow, *[coarse_state, state_shape, coarse_state][:state_count], shape(realiz, size, BF16), quarter, edge, narrow],
+            [*[half] * (2 * count), narrow, *[coarse_state, state_shape, coarse_state][:state_count], shape(realiz, size, BF16), half, edge, edge, narrow],
             [*ins, *states, *coarse_mats, inverse_mat],
-            flops=flops // 4,
+            flops=flops // 2,
         )
         olds, (columns, coarse), outs = (outs[:count], outs[count : 2 * count]), outs[2 * count : 2 * count + 2], outs[2 * count + 2 :]
         states, outs = [*outs[:1], coarse, *outs[1:2]] if mode != "load" else [coarse], outs[state_count - 1 :]
-        scaled, part_first, e2, gamma = outs
-        part_near, part_last, gamma, e0, e1, e3 = call(
+        scaled, part_far, e2, e3, gamma = outs
+        part_near, e0, e1, gamma = call(
             rest_kernel,
-            [half, quarter, narrow, edge, edge, edge],
+            [half, edge, edge, narrow],
             (columns, scaled, olds[0][0], olds[1][0], gamma, inverse_mat),
-            flops=flops * 3 // 4,
+            flops=flops // 2,
         )
         g = exchange((e0, e1, e2, e3))
         if step == 0:
@@ -485,18 +475,15 @@
                 functools.partial(field_kernel, mode), [half] * 4, (columns, z[0], *track[0], z[1], *track[1]), flops=1
             )
             track = outs[:2], outs[2:]
-        z_first, partial = call(
-            image_first_kernel, [quarter, whole], (part_first, g[2], schur_mat), [scratch_quarter], flops // 4
+        z_far, partial = call(
+            image_far_kernel, [half, whole], (part_far, g[3], g[2], schur_mat), [scratch_half], flops // 2
         )
-        z_near, partial = call(
-            image_near_kernel, [half, whole], (part_near, g[0], g[1], partial, schur_mat), [scratch_half], flops // 2
-        )
-        z_far, *image, e0, e1, e2, e3, sent = call(
-            image_last_kernel,
+        z_near, *image, e0, e1, e2, e3, sent = call(
+            image_near_kernel,
             [half, half, half, *exact, message],
-            (part_last, g[3], z_first, z_near, partial, gamma, schur_mat, *track[0][:1]),
-            [scratch_quarter],
-            flops // 4,
+            (part_near, g[0], g[1], z_far, partial, gamma, schur_mat, *track[0][:1]),
+            [scratch_half],
+            flops // 2,
         )
         z = z_near, z_far
         mode = "init" if step == 0 else "next"

time: 169 us -> 168 us (level)
  starting transfers between devices: 30.6 us -> 37.6 us
  blocking collectives: 95.2 us -> 88.5 us
    ppermute x52, starting transfers between devices: 30.6 us -> 37.6 us  [exchange(): got[slot] = lax.ppermute(edges[slot], AXES, plans[slot])]
    all_to_all x7, blocking collectives: 79.6 us -> 73 us  [gather(): lax.all_to_all(message, AXES, split_axis=0, concat_axis=0, tiled=True)]
    pallas_call x38 -> x32, Pallas kernels: 31.6 us -> 30.7 us  [call(): pl.pallas_call(kernel, out_shape=outs, in_specs=[spec] * len(args), out_s...]
  transfers between devices with their start and end apart: 52 -> 52, of which waited for: 12 -> 12; matrix products, arithmetic and copies ran while one was open for 0% -> 0% of each run, Pallas kernels for 10% -> 7%
where the time goes in v6:
time: 168 us; the launch traced here: 167 us
  blocking collectives  88.5 us (53%)
  starting transfers between devices  37.6 us (22%)
  Pallas kernels  30.7 us (18%)
  waiting for transfers between devices  9.32 us (6%)
    all_to_all x7, blocking collectives, gather(): lax.all_to_all(message, AXES, split_axis=0, concat_axis=0, tiled=True)  73 us
    ppermute x52, starting transfers between devices, exchange(): got[slot] = lax.ppermute(edges[slot], AXES, plans[slot])  37.6 us
    pallas_call x32, Pallas kernels, call(): pl.pallas_call(kernel, out_shape=outs, in_specs=[spec] * len(args), out_s...  30.7 us
    all_to_all x1, blocking collectives, body(): lax.all_to_all(packed.reshape(devices, capacity, LANES), AXES, split_axis...  15.5 us
    ppermute x52, waiting for transfers between devices, exchange(): got[slot] = lax.ppermute(edges[slot], AXES, plans[slot])  9.32 us
  transfers between devices with their start and end apart: 52, of which 12 were waited for; matrix products, arithmetic and copies ran while one was open for 0% of the time, Pallas kernels for 7%

profile of v6, /device:TPU:0, one launch (start us, length us, event | category | flops | bytes accessed | tf_op | source)
XLA Modules:
  0.0 167.3 jit_solution(1903320179611901080)
XLA Ops:
  0.6 2.0 %shard_map.77 = (bf16[512,128]{1,0:T(8,128)(2,1)}, f32[8,128]{1,0:T(8,128)}, f32[8,128]{1,0:T(8,128)}) custom-call(bf16[64,256]{1,0:T(8,128)(2,1)} %bitcast.41, s32[1,256]{1,0:T(1,128)} %bitcast.42, s32[1,256]{1,0:T(1,128)} %bitcast.43, f32[8,256]{1,0:T(8,128)} %inverse_in.1), custom_call_target="tpu_custom_call" | custom-call | flops 8000000000 | bytes 43008 | tf_op jit(solution)/shard_map/pallas_call | solution.py:25
  2.7 15.5 %all_to_all.40 = bf16[32,16,128]{2,1,0:T(8,128)(2,1)S(1)} all-to-all(bf16[32,16,128]{2,1,0:T(8,128)(2,1)} %bitcast.38), channel_id=1, replica_groups=mesh['sx'=8,'sy'=4] {'sx','sy'}, dimensions={0} | all-to-all | bytes 262144 | tf_op jit(solution)/shard_map/all_to_all | solution.py:440
  20.9 11.1 %all_to_all.41.refs_6_ = f32[32,1,640]{2,1,0:T(1,128)S(1)} all-to-all(f32[32,1,640]{2,1,0:T(1,128)S(1)} %get-tuple-element.197), channel_id=1, replica_groups=mesh['sx'=8,'sy'=4] {'sx','sy'}, dimensions={0} | all-to-all | bytes 163840 | tf_op jit(solution)/shard_map/all_to_all | solution.py:408
  34.6 1.8 %collective-permute-start.4 = (bf16[64,512]{1,0:T(8,128)(2,1)S(1)}, bf16[64,512]{1,0:T(8,128)(2,1)S(1)}, u32[]{:S(2)}, u32[]{:S(2)}) collective-permute-start(bf16[64,512]{1,0:T(8,128)(2,1)S(1)} %get-tuple-element.206), channel_id=1, source_target_pairs={{0,4},{1,5},{2,6},{3,7},{4,0},{5,1},{6,2},{7,3},{8,12},{9,13},{10,... | collective-permute-start | bytes 196616 | tf_op jit(solution)/shard_map/ppermute | solution.py:77
  39.0 1.2 shard_map.82
  40.3 2.0 %collective-permute-start.9 = (f32[80,512]{1,0:T(8,128)S(1)}, f32[80,512]{1,0:T(8,128)S(1)}, u32[]{:S(2)}, u32[]{:S(2)}) collective-permute-start(f32[80,512]{1,0:T(8,128)S(1)} %get-tuple-element.217), channel_id=1, source_target_pairs={{0,4},{1,5},{2,6},{3,7},{4,0},{5,1},{6,2},{7,3},{8,12},{9,13},{10,... | collective-permute-start | bytes 491528 | tf_op jit(solution)/shard_map/ppermute | solution.py:77
  42.5 1.3 collective-permute-start.11
  43.8 10.3 %all_to_all.42.refs_6_ = f32[32,1,640]{2,1,0:T(1,128)S(1)} all-to-all(f32[32,1,640]{2,1,0:T(1,128)S(1)} %get-tuple-element.220), channel_id=1, replica_groups=mesh['sx'=8,'sy'=4] {'sx','sy'}, dimensions={0} | all-to-all | bytes 163840 | tf_op jit(solution)/shard_map/all_to_all | solution.py:408
  56.9 1.8 %collective-permute-start.12 = (bf16[64,512]{1,0:T(8,128)(2,1)S(1)}, bf16[64,512]{1,0:T(8,128)(2,1)S(1)}, u32[]{:S(2)}, u32[]{:S(2)}) collective-permute-start(bf16[64,512]{1,0:T(8,128)(2,1)S(1)} %get-tuple-element.228), channel_id=1, source_target_pairs={{0,4},{1,5},{2,6},{3,7},{4,0},{5,1},{6,2},{7,3},{8,12},{9,13},{10,... | collective-permute-start | bytes 196616 | tf_op jit(solution)/shard_map/ppermute | solution.py:77
  61.2 1.2 shard_map.87
  62.5 2.0 %collective-permute-start.17 = (f32[80,512]{1,0:T(8,128)S(1)}, f32[80,512]{1,0:T(8,128)S(1)}, u32[]{:S(2)}, u32[]{:S(2)}) collective-permute-start(f32[80,512]{1,0:T(8,128)S(1)} %get-tuple-element.241), channel_id=1, source_target_pairs={{0,4},{1,5},{2,6},{3,7},{4,0},{5,1},{6,2},{7,3},{8,12},{9,13},{10,... | collective-permute-start | bytes 491528 | tf_op jit(solution)/shard_map/ppermute | solution.py:77
  64.7 1.3 collective-permute-start.19
  66.0 10.3 %all_to_all.43.refs_6_ = f32[32,1,640]{2,1,0:T(1,128)S(1)} all-to-all(f32[32,1,640]{2,1,0:T(1,128)S(1)} %get-tuple-element.244), channel_id=1, replica_groups=mesh['sx'=8,'sy'=4] {'sx','sy'}, dimensions={0} | all-to-all | bytes 163840 | tf_op jit(solution)/shard_map/all_to_all | solution.py:408
  79.1 1.8 %collective-permute-start.20 = (bf16[64,512]{1,0:T(8,128)(2,1)S(1)}, bf16[64,512]{1,0:T(8,128)(2,1)S(1)}, u32[]{:S(2)}, u32[]{:S(2)}) collective-permute-start(bf16[64,512]{1,0:T(8,128)(2,1)S(1)} %get-tuple-element.256), channel_id=1, source_target_pairs={{0,4},{1,5},{2,6},{3,7},{4,0},{5,1},{6,2},{7,3},{8,12},{9,13},{10,... | collective-permute-start | bytes 196616 | tf_op jit(solution)/shard_map/ppermute | solution.py:77
  83.4 1.2 shard_map.92
  84.7 2.1 %collective-permute-start.25 = (f32[80,512]{1,0:T(8,128)S(1)}, f32[80,512]{1,0:T(8,128)S(1)}, u32[]{:S(2)}, u32[]{:S(2)}) collective-permute-start(f32[80,512]{1,0:T(8,128)S(1)} %get-tuple-element.272), channel_id=1, source_target_pairs={{0,4},{1,5},{2,6},{3,7},{4,0},{5,1},{6,2},{7,3},{8,12},{9,13},{10,... | collective-permute-start | bytes 491528 | tf_op jit(solution)/shard_map/ppermute | solution.py:77
  87.0 1.3 collective-permute-start.27
  88.3 10.3 %all_to_all.44.refs_6_ = f32[32,1,640]{2,1,0:T(1,128)S(1)} all-to-all(f32[32,1,640]{2,1,0:T(1,128)S(1)} %get-tuple-element.275), channel_id=1, replica_groups=mesh['sx'=8,'sy'=4] {'sx','sy'}, dimensions={0} | all-to-all | bytes 163840 | tf_op jit(solution)/shard_map/all_to_all | solution.py:408
  101.3 1.8 %collective-permute-start.28 = (bf16[64,512]{1,0:T(8,128)(2,1)S(1)}, bf16[64,512]{1,0:T(8,128)(2,1)S(1)}, u32[]{:S(2)}, u32[]{:S(2)}) collective-permute-start(bf16[64,512]{1,0:T(8,128)(2,1)S(1)} %get-tuple-element.287), channel_id=1, source_target_pairs={{0,4},{1,5},{2,6},{3,7},{4,0},{5,1},{6,2},{7,3},{8,12},{9,13},{10,... | collective-permute-start | bytes 196616 | tf_op jit(solution)/shard_map/ppermute | solution.py:77
  107.0 2.1 %collective-permute-start.33 = (f32[80,512]{1,0:T(8,128)S(1)}, f32[80,512]{1,0:T(8,128)S(1)}, u32[]{:S(2)}, u32[]{:S(2)}) collective-permute-start(f32[80,512]{1,0:T(8,128)S(1)} %get-tuple-element.303), channel_id=1, source_target_pairs={{0,4},{1,5},{2,6},{3,7},{4,0},{5,1},{6,2},{7,3},{8,12},{9,13},{10,... | collective-permute-start | bytes 491528 | tf_op jit(solution)/shard_map/ppermute | solution.py:77
  109.2 1.3 collective-permute-start.35
  110.6 10.3 %all_to_all.45.refs_6_ = f32[32,1,640]{2,1,0:T(1,128)S(1)} all-to-all(f32[32,1,640]{2,1,0:T(1,128)S(1)} %get-tuple-element.306), channel_id=1, replica_groups=mesh['sx'=8,'sy'=4] {'sx','sy'}, dimensions={0} | all-to-all | bytes 163840 | tf_op jit(solution)/shard_map/all_to_all | solution.py:408
  123.6 1.8 %collective-permute-start.36 = (bf16[64,512]{1,0:T(8,128)(2,1)S(1)}, bf16[64,512]{1,0:T(8,128)(2,1)S(1)}, u32[]{:S(2)}, u32[]{:S(2)}) collective-permute-start(bf16[64,512]{1,0:T(8,128)(2,1)S(1)} %get-tuple-element.318), channel_id=1, source_target_pairs={{0,4},{1,5},{2,6},{3,7},{4,0},{5,1},{6,2},{7,3},{8,12},{9,13},{10,... | collective-permute-start | bytes 196616 | tf_op jit(solution)/shard_map/ppermute | solution.py:77
  129.3 2.1 %collective-permute-start.41 = (f32[80,512]{1,0:T(8,128)S(1)}, f32[80,512]{1,0:T(8,128)S(1)}, u32[]{:S(2)}, u32[]{:S(2)}) collective-permute-start(f32[80,512]{1,0:T(8,128)S(1)} %get-tuple-element.334), channel_id=1, source_target_pairs={{0,4},{1,5},{2,6},{3,7},{4,0},{5,1},{6,2},{7,3},{8,12},{9,13},{10,... | collective-permute-start | bytes 491528 | tf_op jit(solution)/shard_map/ppermute | solution.py:77
  131.5 1.3 collective-permute-start.43
  132.8 10.3 %all_to_all.46.refs_6_ = f32[32,1,640]{2,1,0:T(1,128)S(1)} all-to-all(f32[32,1,640]{2,1,0:T(1,128)S(1)} %get-tuple-element.337), channel_id=1, replica_groups=mesh['sx'=8,'sy'=4] {'sx','sy'}, dimensions={0} | all-to-all | bytes 163840 | tf_op jit(solution)/shard_map/all_to_all | solution.py:408
  143.2 1.7 %shard_map.103 = (f32[64,1024]{1,0:T(8,128)S(1)}, f32[64,1024]{1,0:T(8,128)S(1)}, f32[64,1024]{1,0:T(8,128)S(1)}, f32[64,1024]{1,0:T(8,128)S(1)}, f32[64,128]{1,...) custom-call(f32[64,1024]{1,0:T(8,128)S(1)} %get-tuple-element.331.re, ...), custom_call_target="tpu_custom_call" | custom-call | flops 268435456 | bytes 10842112 | tf_op jit(solution)/shard_map/pallas_call | solution.py:25
  146.3 1.8 %collective-permute-start.44 = (bf16[64,512]{1,0:T(8,128)(2,1)S(1)}, bf16[64,512]{1,0:T(8,128)(2,1)S(1)}, u32[]{:S(2)}, u32[]{:S(2)}) collective-permute-start(bf16[64,512]{1,0:T(8,128)(2,1)S(1)} %get-tuple-element.349), channel_id=1, source_target_pairs={{0,4},{1,5},{2,6},{3,7},{4,0},{5,1},{6,2},{7,3},{8,12},{9,13},{10,... | collective-permute-start | bytes 196616 | tf_op jit(solution)/shard_map/ppermute | solution.py:77
  152.0 2.1 %collective-permute-start.49 = (f32[80,512]{1,0:T(8,128)S(1)}, f32[80,512]{1,0:T(8,128)S(1)}, u32[]{:S(2)}, u32[]{:S(2)}) collective-permute-start(f32[80,512]{1,0:T(8,128)S(1)} %get-tuple-element.365), channel_id=1, source_target_pairs={{0,4},{1,5},{2,6},{3,7},{4,0},{5,1},{6,2},{7,3},{8,12},{9,13},{10,... | collective-permute-start | bytes 491528 | tf_op jit(solution)/shard_map/ppermute | solution.py:77
  154.2 1.3 collective-permute-start.51
  155.5 10.3 %all_to_all.47.refs_6_ = f32[32,1,640]{2,1,0:T(1,128)S(1)} all-to-all(f32[32,1,640]{2,1,0:T(1,128)S(1)} %get-tuple-element.368), channel_id=1, replica_groups=mesh['sx'=8,'sy'=4] {'sx','sy'}, dimensions={0} | all-to-all | bytes 163840 | tf_op jit(solution)/shard_map/all_to_all | solution.py:408
  165.9 1.4 shard_map.108
  (126 shorter events, 37.8 us)
Async XLA Ops:
  19.2 12.8 %collective-permute-start = (f32[80,512]{1,0:T(8,128)S(1)}, f32[80,512]{1,0:T(8,128)S(1)}, u32[]{:S(2)}, u32[]{:S(2)}) collective-permute-start(f32[80,512]{1,0:T(8,128)S(1)} %get-tuple-element.193), channel_id=1, source_target_pairs={{0,1},{1,0},{2,3},{3,2},{4,5},{5,4},{6,7},{7,6},{8,9},{9,8},{10,11... | collective-permute-start | bytes 491528 | tf_op jit(solution)/shard_map/ppermute | solution.py:77
  19.5 12.5 %collective-permute-start.1 = (f32[80,512]{1,0:T(8,128)S(1)}, f32[80,512]{1,0:T(8,128)S(1)}, u32[]{:S(2)}, u32[]{:S(2)}) collective-permute-start(f32[80,512]{1,0:T(8,128)S(1)} %get-tuple-element.194), channel_id=1, source_target_pairs={{0,4},{1,5},{2,6},{3,7},{4,0},{5,1},{6,2},{7,3},{8,12},{9,13},{10,... | collective-permute-start | bytes 491528 | tf_op jit(solution)/shard_map/ppermute | solution.py:77
  20.0 12.0 %collective-permute-start.2 = (f32[80,512]{1,0:T(8,128)S(1)}, f32[80,512]{1,0:T(8,128)S(1)}, u32[]{:S(2)}, u32[]{:S(2)}) collective-permute-start(f32[80,512]{1,0:T(8,128)S(1)} %get-tuple-element.195), channel_id=1, source_target_pairs={{0,1},{1,0},{2,3},{3,2},{4,8},{5,9},{6,10},{7,11},{8,4},{9,5},{10,... | collective-permute-start | bytes 491528 | tf_op jit(solution)/shard_map/ppermute | solution.py:77
  20.1 11.8 %collective-permute-start.3 = (f32[80,512]{1,0:T(8,128)S(1)}, f32[80,512]{1,0:T(8,128)S(1)}, u32[]{:S(2)}, u32[]{:S(2)}) collective-permute-start(f32[80,512]{1,0:T(8,128)S(1)} %get-tuple-element.196), channel_id=1, source_target_pairs={{0,3},{1,2},{2,1},{3,0},{4,7},{5,6},{6,5},{7,4},{8,11},{9,10},{10,... | collective-permute-start | bytes 491528 | tf_op jit(solution)/shard_map/ppermute | solution.py:77
  34.6 4.3 %collective-permute-start.4 = (bf16[64,512]{1,0:T(8,128)(2,1)S(1)}, bf16[64,512]{1,0:T(8,128)(2,1)S(1)}, u32[]{:S(2)}, u32[]{:S(2)}) collective-permute-start(bf16[64,512]{1,0:T(8,128)(2,1)S(1)} %get-tuple-element.206), channel_id=1, source_target_pairs={{0,4},{1,5},{2,6},{3,7},{4,0},{5,1},{6,2},{7,3},{8,12},{9,13},{10,... | collective-permute-start | bytes 196616 | tf_op jit(solution)/shard_map/ppermute | solution.py:77
  40.2 13.9 %collective-permute-start.8 = (f32[80,512]{1,0:T(8,128)S(1)}, f32[80,512]{1,0:T(8,128)S(1)}, u32[]{:S(2)}, u32[]{:S(2)}) collective-permute-start(f32[80,512]{1,0:T(8,128)S(1)} %get-tuple-element.216), channel_id=1, source_target_pairs={{0,1},{1,0},{2,3},{3,2},{4,5},{5,4},{6,7},{7,6},{8,9},{9,8},{10,11... | collective-permute-start | bytes 491528 | tf_op jit(solution)/shard_map/ppermute | solution.py:77
  40.3 13.9 %collective-permute-start.9 = (f32[80,512]{1,0:T(8,128)S(1)}, f32[80,512]{1,0:T(8,128)S(1)}, u32[]{:S(2)}, u32[]{:S(2)}) collective-permute-start(f32[80,512]{1,0:T(8,128)S(1)} %get-tuple-element.217), channel_id=1, source_target_pairs={{0,4},{1,5},{2,6},{3,7},{4,0},{5,1},{6,2},{7,3},{8,12},{9,13},{10,... | collective-permute-start | bytes 491528 | tf_op jit(solution)/shard_map/ppermute | solution.py:77
  42.3 11.8 %collective-permute-start.10 = (f32[80,512]{1,0:T(8,128)S(1)}, f32[80,512]{1,0:T(8,128)S(1)}, u32[]{:S(2)}, u32[]{:S(2)}) collective-permute-start(f32[80,512]{1,0:T(8,128)S(1)} %get-tuple-element.218), channel_id=1, source_target_pairs={{0,1},{1,0},{2,3},{3,2},{4,8},{5,9},{6,10},{7,11},{8,4},{9,5},{10,... | collective-permute-start | bytes 491528 | tf_op jit(solution)/shard_map/ppermute | solution.py:77
  42.5 11.7 %collective-permute-start.11 = (f32[80,512]{1,0:T(8,128)S(1)}, f32[80,512]{1,0:T(8,128)S(1)}, u32[]{:S(2)}, u32[]{:S(2)}) collective-permute-start(f32[80,512]{1,0:T(8,128)S(1)} %get-tuple-element.219), channel_id=1, source_target_pairs={{0,3},{1,2},{2,1},{3,0},{4,7},{5,6},{6,5},{7,4},{8,11},{9,10},{10,... | collective-permute-start | bytes 491528 | tf_op jit(solution)/shard_map/ppermute | solution.py:77
  56.9 4.3 %collective-permute-start.12 = (bf16[64,512]{1,0:T(8,128)(2,1)S(1)}, bf16[64,512]{1,0:T(8,128)(2,1)S(1)}, u32[]{:S(2)}, u32[]{:S(2)}) collective-permute-start(bf16[64,512]{1,0:T(8,128)(2,1)S(1)} %get-tuple-element.228), channel_id=1, source_target_pairs={{0,4},{1,5},{2,6},{3,7},{4,0},{5,1},{6,2},{7,3},{8,12},{9,13},{10,... | collective-permute-start | bytes 196616 | tf_op jit(solution)/shard_map/ppermute | solution.py:77
  62.4 13.9 %collective-permute-start.16 = (f32[80,512]{1,0:T(8,128)S(1)}, f32[80,512]{1,0:T(8,128)S(1)}, u32[]{:S(2)}, u32[]{:S(2)}) collective-permute-start(f32[80,512]{1,0:T(8,128)S(1)} %get-tuple-element.240), channel_id=1, source_target_pairs={{0,1},{1,0},{2,3},{3,2},{4,5},{5,4},{6,7},{7,6},{8,9},{9,8},{10,11... | collective-permute-start | bytes 491528 | tf_op jit(solution)/shard_map/ppermute | solution.py:77
  62.5 13.9 %collective-permute-start.17 = (f32[80,512]{1,0:T(8,128)S(1)}, f32[80,512]{1,0:T(8,128)S(1)}, u32[]{:S(2)}, u32[]{:S(2)}) collective-permute-start(f32[80,512]{1,0:T(8,128)S(1)} %get-tuple-element.241), channel_id=1, source_target_pairs={{0,4},{1,5},{2,6},{3,7},{4,0},{5,1},{6,2},{7,3},{8,12},{9,13},{10,... | collective-permute-start | bytes 491528 | tf_op jit(solution)/shard_map/ppermute | solution.py:77
  64.5 11.8 %collective-permute-start.18 = (f32[80,512]{1,0:T(8,128)S(1)}, f32[80,512]{1,0:T(8,128)S(1)}, u32[]{:S(2)}, u32[]{:S(2)}) collective-permute-start(f32[80,512]{1,0:T(8,128)S(1)} %get-tuple-element.242), channel_id=1, source_target_pairs={{0,1},{1,0},{2,3},{3,2},{4,8},{5,9},{6,10},{7,11},{8,4},{9,5},{10,... | collective-permute-start | bytes 491528 | tf_op jit(solution)/shard_map/ppermute | solution.py:77
  64.7 11.7 %collective-permute-start.19 = (f32[80,512]{1,0:T(8,128)S(1)}, f32[80,512]{1,0:T(8,128)S(1)}, u32[]{:S(2)}, u32[]{:S(2)}) collective-permute-start(f32[80,512]{1,0:T(8,128)S(1)} %get-tuple-element.243), channel_id=1, source_target_pairs={{0,3},{1,2},{2,1},{3,0},{4,7},{5,6},{6,5},{7,4},{8,11},{9,10},{10,... | collective-permute-start | bytes 491528 | tf_op jit(solution)/shard_map/ppermute | solution.py:77
  79.1 4.3 %collective-permute-start.20 = (bf16[64,512]{1,0:T(8,128)(2,1)S(1)}, bf16[64,512]{1,0:T(8,128)(2,1)S(1)}, u32[]{:S(2)}, u32[]{:S(2)}) collective-permute-start(bf16[64,512]{1,0:T(8,128)(2,1)S(1)} %get-tuple-element.256), channel_id=1, source_target_pairs={{0,4},{1,5},{2,6},{3,7},{4,0},{5,1},{6,2},{7,3},{8,12},{9,13},{10,... | collective-permute-start | bytes 196616 | tf_op jit(solution)/shard_map/ppermute | solution.py:77
  84.7 14.0 %collective-permute-start.24 = (f32[80,512]{1,0:T(8,128)S(1)}, f32[80,512]{1,0:T(8,128)S(1)}, u32[]{:S(2)}, u32[]{:S(2)}) collective-permute-start(f32[80,512]{1,0:T(8,128)S(1)} %get-tuple-element.271), channel_id=1, source_target_pairs={{0,1},{1,0},{2,3},{3,2},{4,5},{5,4},{6,7},{7,6},{8,9},{9,8},{10,11... | collective-permute-start | bytes 491528 | tf_op jit(solution)/shard_map/ppermute | solution.py:77
  84.7 13.9 %collective-permute-start.25 = (f32[80,512]{1,0:T(8,128)S(1)}, f32[80,512]{1,0:T(8,128)S(1)}, u32[]{:S(2)}, u32[]{:S(2)}) collective-permute-start(f32[80,512]{1,0:T(8,128)S(1)} %get-tuple-element.272), channel_id=1, source_target_pairs={{0,4},{1,5},{2,6},{3,7},{4,0},{5,1},{6,2},{7,3},{8,12},{9,13},{10,... | collective-permute-start | bytes 491528 | tf_op jit(solution)/shard_map/ppermute | solution.py:77
  86.8 11.8 %collective-permute-start.26 = (f32[80,512]{1,0:T(8,128)S(1)}, f32[80,512]{1,0:T(8,128)S(1)}, u32[]{:S(2)}, u32[]{:S(2)}) collective-permute-start(f32[80,512]{1,0:T(8,128)S(1)} %get-tuple-element.273), channel_id=1, source_target_pairs={{0,1},{1,0},{2,3},{3,2},{4,8},{5,9},{6,10},{7,11},{8,4},{9,5},{10,... | collective-permute-start | bytes 491528 | tf_op jit(solution)/shard_map/ppermute | solution.py:77
  87.0 11.7 %collective-permute-start.27 = (f32[80,512]{1,0:T(8,128)S(1)}, f32[80,512]{1,0:T(8,128)S(1)}, u32[]{:S(2)}, u32[]{:S(2)}) collective-permute-start(f32[80,512]{1,0:T(8,128)S(1)} %get-tuple-element.274), channel_id=1, source_target_pairs={{0,3},{1,2},{2,1},{3,0},{4,7},{5,6},{6,5},{7,4},{8,11},{9,10},{10,... | collective-permute-start | bytes 491528 | tf_op jit(solution)/shard_map/ppermute | solution.py:77
  101.3 4.3 %collective-permute-start.28 = (bf16[64,512]{1,0:T(8,128)(2,1)S(1)}, bf16[64,512]{1,0:T(8,128)(2,1)S(1)}, u32[]{:S(2)}, u32[]{:S(2)}) collective-permute-start(bf16[64,512]{1,0:T(8,128)(2,1)S(1)} %get-tuple-element.287), channel_id=1, source_target_pairs={{0,4},{1,5},{2,6},{3,7},{4,0},{5,1},{6,2},{7,3},{8,12},{9,13},{10,... | collective-permute-start | bytes 196616 | tf_op jit(solution)/shard_map/ppermute | solution.py:77
  106.9 14.0 %collective-permute-start.32 = (f32[80,512]{1,0:T(8,128)S(1)}, f32[80,512]{1,0:T(8,128)S(1)}, u32[]{:S(2)}, u32[]{:S(2)}) collective-permute-start(f32[80,512]{1,0:T(8,128)S(1)} %get-tuple-element.302), channel_id=1, source_target_pairs={{0,1},{1,0},{2,3},{3,2},{4,5},{5,4},{6,7},{7,6},{8,9},{9,8},{10,11... | collective-permute-start | bytes 491528 | tf_op jit(solution)/shard_map/ppermute | solution.py:77
  107.0 13.9 %collective-permute-start.33 = (f32[80,512]{1,0:T(8,128)S(1)}, f32[80,512]{1,0:T(8,128)S(1)}, u32[]{:S(2)}, u32[]{:S(2)}) collective-permute-start(f32[80,512]{1,0:T(8,128)S(1)} %get-tuple-element.303), channel_id=1, source_target_pairs={{0,4},{1,5},{2,6},{3,7},{4,0},{5,1},{6,2},{7,3},{8,12},{9,13},{10,... | collective-permute-start | bytes 491528 | tf_op jit(solution)/shard_map/ppermute | solution.py:77
  109.1 11.8 %collective-permute-start.34 = (f32[80,512]{1,0:T(8,128)S(1)}, f32[80,512]{1,0:T(8,128)S(1)}, u32[]{:S(2)}, u32[]{:S(2)}) collective-permute-start(f32[80,512]{1,0:T(8,128)S(1)} %get-tuple-element.304), channel_id=1, source_target_pairs={{0,1},{1,0},{2,3},{3,2},{4,8},{5,9},{6,10},{7,11},{8,4},{9,5},{10,... | collective-permute-start | bytes 491528 | tf_op jit(solution)/shard_map/ppermute | solution.py:77
  109.2 11.7 %collective-permute-start.35 = (f32[80,512]{1,0:T(8,128)S(1)}, f32[80,512]{1,0:T(8,128)S(1)}, u32[]{:S(2)}, u32[]{:S(2)}) collective-permute-start(f32[80,512]{1,0:T(8,128)S(1)} %get-tuple-element.305), channel_id=1, source_target_pairs={{0,3},{1,2},{2,1},{3,0},{4,7},{5,6},{6,5},{7,4},{8,11},{9,10},{10,... | collective-permute-start | bytes 491528 | tf_op jit(solution)/shard_map/ppermute | solution.py:77
  129.2 14.0 %collective-permute-start.40 = (f32[80,512]{1,0:T(8,128)S(1)}, f32[80,512]{1,0:T(8,128)S(1)}, u32[]{:S(2)}, u32[]{:S(2)}) collective-permute-start(f32[80,512]{1,0:T(8,128)S(1)} %get-tuple-element.333), channel_id=1, source_target_pairs={{0,1},{1,0},{2,3},{3,2},{4,5},{5,4},{6,7},{7,6},{8,9},{9,8},{10,11... | collective-permute-start | bytes 491528 | tf_op jit(solution)/shard_map/ppermute | solution.py:77
  129.3 13.9 %collective-permute-start.41 = (f32[80,512]{1,0:T(8,128)S(1)}, f32[80,512]{1,0:T(8,128)S(1)}, u32[]{:S(2)}, u32[]{:S(2)}) collective-permute-start(f32[80,512]{1,0:T(8,128)S(1)} %get-tuple-element.334), channel_id=1, source_target_pairs={{0,4},{1,5},{2,6},{3,7},{4,0},{5,1},{6,2},{7,3},{8,12},{9,13},{10,... | collective-permute-start | bytes 491528 | tf_op jit(solution)/shard_map/ppermute | solution.py:77
  131.3 11.8 %collective-permute-start.42 = (f32[80,512]{1,0:T(8,128)S(1)}, f32[80,512]{1,0:T(8,128)S(1)}, u32[]{:S(2)}, u32[]{:S(2)}) collective-permute-start(f32[80,512]{1,0:T(8,128)S(1)} %get-tuple-element.335), channel_id=1, source_target_pairs={{0,1},{1,0},{2,3},{3,2},{4,8},{5,9},{6,10},{7,11},{8,4},{9,5},{10,... | collective-permute-start | bytes 491528 | tf_op jit(solution)/shard_map/ppermute | solution.py:77
  131.5 11.7 %collective-permute-start.43 = (f32[80,512]{1,0:T(8,128)S(1)}, f32[80,512]{1,0:T(8,128)S(1)}, u32[]{:S(2)}, u32[]{:S(2)}) collective-permute-start(f32[80,512]{1,0:T(8,128)S(1)} %get-tuple-element.336), channel_id=1, source_target_pairs={{0,3},{1,2},{2,1},{3,0},{4,7},{5,6},{6,5},{7,4},{8,11},{9,10},{10,... | collective-permute-start | bytes 491528 | tf_op jit(solution)/shard_map/ppermute | solution.py:77
  151.9 14.0 %collective-permute-start.48 = (f32[80,512]{1,0:T(8,128)S(1)}, f32[80,512]{1,0:T(8,128)S(1)}, u32[]{:S(2)}, u32[]{:S(2)}) collective-permute-start(f32[80,512]{1,0:T(8,128)S(1)} %get-tuple-element.364), channel_id=1, source_target_pairs={{0,1},{1,0},{2,3},{3,2},{4,5},{5,4},{6,7},{7,6},{8,9},{9,8},{10,11... | collective-permute-start | bytes 491528 | tf_op jit(solution)/shard_map/ppermute | solution.py:77
  152.0 13.9 %collective-permute-start.49 = (f32[80,512]{1,0:T(8,128)S(1)}, f32[80,512]{1,0:T(8,128)S(1)}, u32[]{:S(2)}, u32[]{:S(2)}) collective-permute-start(f32[80,512]{1,0:T(8,128)S(1)} %get-tuple-element.365), channel_id=1, source_target_pairs={{0,4},{1,5},{2,6},{3,7},{4,0},{5,1},{6,2},{7,3},{8,12},{9,13},{10,... | collective-permute-start | bytes 491528 | tf_op jit(solution)/shard_map/ppermute | solution.py:77
  154.0 11.8 %collective-permute-start.50 = (f32[80,512]{1,0:T(8,128)S(1)}, f32[80,512]{1,0:T(8,128)S(1)}, u32[]{:S(2)}, u32[]{:S(2)}) collective-permute-start(f32[80,512]{1,0:T(8,128)S(1)} %get-tuple-element.366), channel_id=1, source_target_pairs={{0,1},{1,0},{2,3},{3,2},{4,8},{5,9},{6,10},{7,11},{8,4},{9,5},{10,... | collective-permute-start | bytes 491528 | tf_op jit(solution)/shard_map/ppermute | solution.py:77
  154.2 11.7 %collective-permute-start.51 = (f32[80,512]{1,0:T(8,128)S(1)}, f32[80,512]{1,0:T(8,128)S(1)}, u32[]{:S(2)}, u32[]{:S(2)}) collective-permute-start(f32[80,512]{1,0:T(8,128)S(1)} %get-tuple-element.367), channel_id=1, source_target_pairs={{0,3},{1,2},{2,1},{3,0},{4,7},{5,6},{6,5},{7,4},{8,11},{9,10},{10,... | collective-permute-start | bytes 491528 | tf_op jit(solution)/shard_map/ppermute | solution.py:77
  (26 other events, 171.5 us)

commit v7 on v6

--- a/solution.py
+++ b/solution.py
@@ -12,7 +12,7 @@
 PAD = 16
 COVER = 8e9
 LANES = 128
-CHUNK = 256
+CHUNK = 512
 HP = lax.Precision.HIGHEST
 F32 = jnp.float32
 BF16 = jnp.bfloat16

time: 168 us -> 167 us (level)
  no operation moved by 1% of the time
where the time goes in v7:
time: 167 us; the launch traced here: 166 us
  blocking collectives  88.3 us (53%)
  starting transfers between devices  37.8 us (23%)
  Pallas kernels  29.5 us (18%)
  waiting for transfers between devices  9.45 us (6%)
    all_to_all x7, blocking collectives, gather(): lax.all_to_all(message, AXES, split_axis=0, concat_axis=0, tiled=True)  72.8 us
    ppermute x52, starting transfers between devices, exchange(): got[slot] = lax.ppermute(edges[slot], AXES, plans[slot])  37.8 us
    pallas_call x32, Pallas kernels, call(): pl.pallas_call(kernel, out_shape=outs, in_specs=[spec] * len(args), out_s...  29.5 us
    all_to_all x1, blocking collectives, body(): lax.all_to_all(packed.reshape(devices, capacity, LANES), AXES, split_axis...  15.5 us
    ppermute x52, waiting for transfers between devices, exchange(): got[slot] = lax.ppermute(edges[slot], AXES, plans[slot])  9.45 us
  transfers between devices with their start and end apart: 52, of which 12 were waited for; matrix products, arithmetic and copies ran while one was open for 0% of the time, Pallas kernels for 7%

profile of v7, /device:TPU:0, one launch (start us, length us, event | category | flops | bytes accessed | tf_op | source)
XLA Modules:
  0.0 166.3 jit_solution(17512273282073777056)
XLA Ops:
  0.6 2.0 %shard_map.77 = (bf16[512,128]{1,0:T(8,128)(2,1)}, f32[8,128]{1,0:T(8,128)}, f32[8,128]{1,0:T(8,128)}) custom-call(bf16[64,256]{1,0:T(8,128)(2,1)} %bitcast.41, s32[1,256]{1,0:T(1,128)} %bitcast.42, s32[1,256]{1,0:T(1,128)} %bitcast.43, f32[8,256]{1,0:T(8,128)} %inverse_in.1), custom_call_target="tpu_custom_call" | custom-call | flops 8000000000 | bytes 43008 | tf_op jit(solution)/shard_map/pallas_call | solution.py:25
  2.7 15.5 %all_to_all.40 = bf16[32,16,128]{2,1,0:T(8,128)(2,1)S(1)} all-to-all(bf16[32,16,128]{2,1,0:T(8,128)(2,1)} %bitcast.38), channel_id=1, replica_groups=mesh['sx'=8,'sy'=4] {'sx','sy'}, dimensions={0} | all-to-all | bytes 262144 | tf_op jit(solution)/shard_map/all_to_all | solution.py:440
  20.9 11.1 %all_to_all.41.refs_6_ = f32[32,1,640]{2,1,0:T(1,128)S(1)} all-to-all(f32[32,1,640]{2,1,0:T(1,128)S(1)} %get-tuple-element.197), channel_id=1, replica_groups=mesh['sx'=8,'sy'=4] {'sx','sy'}, dimensions={0} | all-to-all | bytes 163840 | tf_op jit(solution)/shard_map/all_to_all | solution.py:408
  34.6 1.8 %collective-permute-start.4 = (bf16[64,512]{1,0:T(8,128)(2,1)S(1)}, bf16[64,512]{1,0:T(8,128)(2,1)S(1)}, u32[]{:S(2)}, u32[]{:S(2)}) collective-permute-start(bf16[64,512]{1,0:T(8,128)(2,1)S(1)} %get-tuple-element.206), channel_id=1, source_target_pairs={{0,4},{1,5},{2,6},{3,7},{4,0},{5,1},{6,2},{7,3},{8,12},{9,13},{10,... | collective-permute-start | bytes 196616 | tf_op jit(solution)/shard_map/ppermute | solution.py:77
  38.9 1.2 shard_map.82
  40.2 2.1 %collective-permute-start.9 = (f32[80,512]{1,0:T(8,128)S(1)}, f32[80,512]{1,0:T(8,128)S(1)}, u32[]{:S(2)}, u32[]{:S(2)}) collective-permute-start(f32[80,512]{1,0:T(8,128)S(1)} %get-tuple-element.217), channel_id=1, source_target_pairs={{0,4},{1,5},{2,6},{3,7},{4,0},{5,1},{6,2},{7,3},{8,12},{9,13},{10,... | collective-permute-start | bytes 491528 | tf_op jit(solution)/shard_map/ppermute | solution.py:77
  42.4 1.3 collective-permute-start.11
  43.7 10.3 %all_to_all.42.refs_6_ = f32[32,1,640]{2,1,0:T(1,128)S(1)} all-to-all(f32[32,1,640]{2,1,0:T(1,128)S(1)} %get-tuple-element.220), channel_id=1, replica_groups=mesh['sx'=8,'sy'=4] {'sx','sy'}, dimensions={0} | all-to-all | bytes 163840 | tf_op jit(solution)/shard_map/all_to_all | solution.py:408
  56.6 1.8 %collective-permute-start.12 = (bf16[64,512]{1,0:T(8,128)(2,1)S(1)}, bf16[64,512]{1,0:T(8,128)(2,1)S(1)}, u32[]{:S(2)}, u32[]{:S(2)}) collective-permute-start(bf16[64,512]{1,0:T(8,128)(2,1)S(1)} %get-tuple-element.228), channel_id=1, source_target_pairs={{0,4},{1,5},{2,6},{3,7},{4,0},{5,1},{6,2},{7,3},{8,12},{9,13},{10,... | collective-permute-start | bytes 196616 | tf_op jit(solution)/shard_map/ppermute | solution.py:77
  61.0 1.2 shard_map.87
  62.2 2.1 %collective-permute-start.17 = (f32[80,512]{1,0:T(8,128)S(1)}, f32[80,512]{1,0:T(8,128)S(1)}, u32[]{:S(2)}, u32[]{:S(2)}) collective-permute-start(f32[80,512]{1,0:T(8,128)S(1)} %get-tuple-element.241), channel_id=1, source_target_pairs={{0,4},{1,5},{2,6},{3,7},{4,0},{5,1},{6,2},{7,3},{8,12},{9,13},{10,... | collective-permute-start | bytes 491528 | tf_op jit(solution)/shard_map/ppermute | solution.py:77
  64.5 1.3 collective-permute-start.19
  65.8 10.3 %all_to_all.43.refs_6_ = f32[32,1,640]{2,1,0:T(1,128)S(1)} all-to-all(f32[32,1,640]{2,1,0:T(1,128)S(1)} %get-tuple-element.244), channel_id=1, replica_groups=mesh['sx'=8,'sy'=4] {'sx','sy'}, dimensions={0} | all-to-all | bytes 163840 | tf_op jit(solution)/shard_map/all_to_all | solution.py:408
  78.7 1.8 %collective-permute-start.20 = (bf16[64,512]{1,0:T(8,128)(2,1)S(1)}, bf16[64,512]{1,0:T(8,128)(2,1)S(1)}, u32[]{:S(2)}, u32[]{:S(2)}) collective-permute-start(bf16[64,512]{1,0:T(8,128)(2,1)S(1)} %get-tuple-element.256), channel_id=1, source_target_pairs={{0,4},{1,5},{2,6},{3,7},{4,0},{5,1},{6,2},{7,3},{8,12},{9,13},{10,... | collective-permute-start | bytes 196616 | tf_op jit(solution)/shard_map/ppermute | solution.py:77
  84.3 2.1 %collective-permute-start.25 = (f32[80,512]{1,0:T(8,128)S(1)}, f32[80,512]{1,0:T(8,128)S(1)}, u32[]{:S(2)}, u32[]{:S(2)}) collective-permute-start(f32[80,512]{1,0:T(8,128)S(1)} %get-tuple-element.272), channel_id=1, source_target_pairs={{0,4},{1,5},{2,6},{3,7},{4,0},{5,1},{6,2},{7,3},{8,12},{9,13},{10,... | collective-permute-start | bytes 491528 | tf_op jit(solution)/shard_map/ppermute | solution.py:77
  86.6 1.3 collective-permute-start.27
  87.9 10.3 %all_to_all.44.refs_6_ = f32[32,1,640]{2,1,0:T(1,128)S(1)} all-to-all(f32[32,1,640]{2,1,0:T(1,128)S(1)} %get-tuple-element.275), channel_id=1, replica_groups=mesh['sx'=8,'sy'=4] {'sx','sy'}, dimensions={0} | all-to-all | bytes 163840 | tf_op jit(solution)/shard_map/all_to_all | solution.py:408
  100.8 1.8 %collective-permute-start.28 = (bf16[64,512]{1,0:T(8,128)(2,1)S(1)}, bf16[64,512]{1,0:T(8,128)(2,1)S(1)}, u32[]{:S(2)}, u32[]{:S(2)}) collective-permute-start(bf16[64,512]{1,0:T(8,128)(2,1)S(1)} %get-tuple-element.287), channel_id=1, source_target_pairs={{0,4},{1,5},{2,6},{3,7},{4,0},{5,1},{6,2},{7,3},{8,12},{9,13},{10,... | collective-permute-start | bytes 196616 | tf_op jit(solution)/shard_map/ppermute | solution.py:77
  105.2 1.2 shard_map.97
  106.4 2.1 %collective-permute-start.33 = (f32[80,512]{1,0:T(8,128)S(1)}, f32[80,512]{1,0:T(8,128)S(1)}, u32[]{:S(2)}, u32[]{:S(2)}) collective-permute-start(f32[80,512]{1,0:T(8,128)S(1)} %get-tuple-element.303), channel_id=1, source_target_pairs={{0,4},{1,5},{2,6},{3,7},{4,0},{5,1},{6,2},{7,3},{8,12},{9,13},{10,... | collective-permute-start | bytes 491528 | tf_op jit(solution)/shard_map/ppermute | solution.py:77
  108.7 1.3 collective-permute-start.35
  110.0 10.3 %all_to_all.45.refs_6_ = f32[32,1,640]{2,1,0:T(1,128)S(1)} all-to-all(f32[32,1,640]{2,1,0:T(1,128)S(1)} %get-tuple-element.306), channel_id=1, replica_groups=mesh['sx'=8,'sy'=4] {'sx','sy'}, dimensions={0} | all-to-all | bytes 163840 | tf_op jit(solution)/shard_map/all_to_all | solution.py:408
  122.9 1.8 %collective-permute-start.36 = (bf16[64,512]{1,0:T(8,128)(2,1)S(1)}, bf16[64,512]{1,0:T(8,128)(2,1)S(1)}, u32[]{:S(2)}, u32[]{:S(2)}) collective-permute-start(bf16[64,512]{1,0:T(8,128)(2,1)S(1)} %get-tuple-element.318), channel_id=1, source_target_pairs={{0,4},{1,5},{2,6},{3,7},{4,0},{5,1},{6,2},{7,3},{8,12},{9,13},{10,... | collective-permute-start | bytes 196616 | tf_op jit(solution)/shard_map/ppermute | solution.py:77
  128.5 2.1 %collective-permute-start.41 = (f32[80,512]{1,0:T(8,128)S(1)}, f32[80,512]{1,0:T(8,128)S(1)}, u32[]{:S(2)}, u32[]{:S(2)}) collective-permute-start(f32[80,512]{1,0:T(8,128)S(1)} %get-tuple-element.334), channel_id=1, source_target_pairs={{0,4},{1,5},{2,6},{3,7},{4,0},{5,1},{6,2},{7,3},{8,12},{9,13},{10,... | collective-permute-start | bytes 491528 | tf_op jit(solution)/shard_map/ppermute | solution.py:77
  130.8 1.3 collective-permute-start.43
  132.1 10.3 %all_to_all.46.refs_6_ = f32[32,1,640]{2,1,0:T(1,128)S(1)} all-to-all(f32[32,1,640]{2,1,0:T(1,128)S(1)} %get-tuple-element.337), channel_id=1, replica_groups=mesh['sx'=8,'sy'=4] {'sx','sy'}, dimensions={0} | all-to-all | bytes 163840 | tf_op jit(solution)/shard_map/all_to_all | solution.py:408
  142.4 1.5 shard_map.103
  145.3 1.8 %collective-permute-start.44 = (bf16[64,512]{1,0:T(8,128)(2,1)S(1)}, bf16[64,512]{1,0:T(8,128)(2,1)S(1)}, u32[]{:S(2)}, u32[]{:S(2)}) collective-permute-start(bf16[64,512]{1,0:T(8,128)(2,1)S(1)} %get-tuple-element.349), channel_id=1, source_target_pairs={{0,4},{1,5},{2,6},{3,7},{4,0},{5,1},{6,2},{7,3},{8,12},{9,13},{10,... | collective-permute-start | bytes 196616 | tf_op jit(solution)/shard_map/ppermute | solution.py:77
  150.9 2.1 %collective-permute-start.49 = (f32[80,512]{1,0:T(8,128)S(1)}, f32[80,512]{1,0:T(8,128)S(1)}, u32[]{:S(2)}, u32[]{:S(2)}) collective-permute-start(f32[80,512]{1,0:T(8,128)S(1)} %get-tuple-element.365), channel_id=1, source_target_pairs={{0,4},{1,5},{2,6},{3,7},{4,0},{5,1},{6,2},{7,3},{8,12},{9,13},{10,... | collective-permute-start | bytes 491528 | tf_op jit(solution)/shard_map/ppermute | solution.py:77
  153.2 1.3 collective-permute-start.51
  154.5 10.3 %all_to_all.47.refs_6_ = f32[32,1,640]{2,1,0:T(1,128)S(1)} all-to-all(f32[32,1,640]{2,1,0:T(1,128)S(1)} %get-tuple-element.368), channel_id=1, replica_groups=mesh['sx'=8,'sy'=4] {'sx','sy'}, dimensions={0} | all-to-all | bytes 163840 | tf_op jit(solution)/shard_map/all_to_all | solution.py:408
  164.8 1.4 shard_map.108
  (126 shorter events, 37.1 us)
Async XLA Ops:
  19.2 12.8 %collective-permute-start = (f32[80,512]{1,0:T(8,128)S(1)}, f32[80,512]{1,0:T(8,128)S(1)}, u32[]{:S(2)}, u32[]{:S(2)}) collective-permute-start(f32[80,512]{1,0:T(8,128)S(1)} %get-tuple-element.193), channel_id=1, source_target_pairs={{0,1},{1,0},{2,3},{3,2},{4,5},{5,4},{6,7},{7,6},{8,9},{9,8},{10,11... | collective-permute-start | bytes 491528 | tf_op jit(solution)/shard_map/ppermute | solution.py:77
  19.5 12.5 %collective-permute-start.1 = (f32[80,512]{1,0:T(8,128)S(1)}, f32[80,512]{1,0:T(8,128)S(1)}, u32[]{:S(2)}, u32[]{:S(2)}) collective-permute-start(f32[80,512]{1,0:T(8,128)S(1)} %get-tuple-element.194), channel_id=1, source_target_pairs={{0,4},{1,5},{2,6},{3,7},{4,0},{5,1},{6,2},{7,3},{8,12},{9,13},{10,... | collective-permute-start | bytes 491528 | tf_op jit(solution)/shard_map/ppermute | solution.py:77
  20.0 12.0 %collective-permute-start.2 = (f32[80,512]{1,0:T(8,128)S(1)}, f32[80,512]{1,0:T(8,128)S(1)}, u32[]{:S(2)}, u32[]{:S(2)}) collective-permute-start(f32[80,512]{1,0:T(8,128)S(1)} %get-tuple-element.195), channel_id=1, source_target_pairs={{0,1},{1,0},{2,3},{3,2},{4,8},{5,9},{6,10},{7,11},{8,4},{9,5},{10,... | collective-permute-start | bytes 491528 | tf_op jit(solution)/shard_map/ppermute | solution.py:77
  20.1 11.8 %collective-permute-start.3 = (f32[80,512]{1,0:T(8,128)S(1)}, f32[80,512]{1,0:T(8,128)S(1)}, u32[]{:S(2)}, u32[]{:S(2)}) collective-permute-start(f32[80,512]{1,0:T(8,128)S(1)} %get-tuple-element.196), channel_id=1, source_target_pairs={{0,3},{1,2},{2,1},{3,0},{4,7},{5,6},{6,5},{7,4},{8,11},{9,10},{10,... | collective-permute-start | bytes 491528 | tf_op jit(solution)/shard_map/ppermute | solution.py:77
  34.6 4.3 %collective-permute-start.4 = (bf16[64,512]{1,0:T(8,128)(2,1)S(1)}, bf16[64,512]{1,0:T(8,128)(2,1)S(1)}, u32[]{:S(2)}, u32[]{:S(2)}) collective-permute-start(bf16[64,512]{1,0:T(8,128)(2,1)S(1)} %get-tuple-element.206), channel_id=1, source_target_pairs={{0,4},{1,5},{2,6},{3,7},{4,0},{5,1},{6,2},{7,3},{8,12},{9,13},{10,... | collective-permute-start | bytes 196616 | tf_op jit(solution)/shard_map/ppermute | solution.py:77
  40.1 13.9 %collective-permute-start.8 = (f32[80,512]{1,0:T(8,128)S(1)}, f32[80,512]{1,0:T(8,128)S(1)}, u32[]{:S(2)}, u32[]{:S(2)}) collective-permute-start(f32[80,512]{1,0:T(8,128)S(1)} %get-tuple-element.216), channel_id=1, source_target_pairs={{0,1},{1,0},{2,3},{3,2},{4,5},{5,4},{6,7},{7,6},{8,9},{9,8},{10,11... | collective-permute-start | bytes 491528 | tf_op jit(solution)/shard_map/ppermute | solution.py:77
  40.2 13.9 %collective-permute-start.9 = (f32[80,512]{1,0:T(8,128)S(1)}, f32[80,512]{1,0:T(8,128)S(1)}, u32[]{:S(2)}, u32[]{:S(2)}) collective-permute-start(f32[80,512]{1,0:T(8,128)S(1)} %get-tuple-element.217), channel_id=1, source_target_pairs={{0,4},{1,5},{2,6},{3,7},{4,0},{5,1},{6,2},{7,3},{8,12},{9,13},{10,... | collective-permute-start | bytes 491528 | tf_op jit(solution)/shard_map/ppermute | solution.py:77
  42.2 11.8 %collective-permute-start.10 = (f32[80,512]{1,0:T(8,128)S(1)}, f32[80,512]{1,0:T(8,128)S(1)}, u32[]{:S(2)}, u32[]{:S(2)}) collective-permute-start(f32[80,512]{1,0:T(8,128)S(1)} %get-tuple-element.218), channel_id=1, source_target_pairs={{0,1},{1,0},{2,3},{3,2},{4,8},{5,9},{6,10},{7,11},{8,4},{9,5},{10,... | collective-permute-start | bytes 491528 | tf_op jit(solution)/shard_map/ppermute | solution.py:77
  42.4 11.6 %collective-permute-start.11 = (f32[80,512]{1,0:T(8,128)S(1)}, f32[80,512]{1,0:T(8,128)S(1)}, u32[]{:S(2)}, u32[]{:S(2)}) collective-permute-start(f32[80,512]{1,0:T(8,128)S(1)} %get-tuple-element.219), channel_id=1, source_target_pairs={{0,3},{1,2},{2,1},{3,0},{4,7},{5,6},{6,5},{7,4},{8,11},{9,10},{10,... | collective-permute-start | bytes 491528 | tf_op jit(solution)/shard_map/ppermute | solution.py:77
  56.6 4.3 %collective-permute-start.12 = (bf16[64,512]{1,0:T(8,128)(2,1)S(1)}, bf16[64,512]{1,0:T(8,128)(2,1)S(1)}, u32[]{:S(2)}, u32[]{:S(2)}) collective-permute-start(bf16[64,512]{1,0:T(8,128)(2,1)S(1)} %get-tuple-element.228), channel_id=1, source_target_pairs={{0,4},{1,5},{2,6},{3,7},{4,0},{5,1},{6,2},{7,3},{8,12},{9,13},{10,... | collective-permute-start | bytes 196616 | tf_op jit(solution)/shard_map/ppermute | solution.py:77
  62.1 14.0 %collective-permute-start.16 = (f32[80,512]{1,0:T(8,128)S(1)}, f32[80,512]{1,0:T(8,128)S(1)}, u32[]{:S(2)}, u32[]{:S(2)}) collective-permute-start(f32[80,512]{1,0:T(8,128)S(1)} %get-tuple-element.240), channel_id=1, source_target_pairs={{0,1},{1,0},{2,3},{3,2},{4,5},{5,4},{6,7},{7,6},{8,9},{9,8},{10,11... | collective-permute-start | bytes 491528 | tf_op jit(solution)/shard_map/ppermute | solution.py:77
  62.2 13.9 %collective-permute-start.17 = (f32[80,512]{1,0:T(8,128)S(1)}, f32[80,512]{1,0:T(8,128)S(1)}, u32[]{:S(2)}, u32[]{:S(2)}) collective-permute-start(f32[80,512]{1,0:T(8,128)S(1)} %get-tuple-element.241), channel_id=1, source_target_pairs={{0,4},{1,5},{2,6},{3,7},{4,0},{5,1},{6,2},{7,3},{8,12},{9,13},{10,... | collective-permute-start | bytes 491528 | tf_op jit(solution)/shard_map/ppermute | solution.py:77
  64.3 11.8 %collective-permute-start.18 = (f32[80,512]{1,0:T(8,128)S(1)}, f32[80,512]{1,0:T(8,128)S(1)}, u32[]{:S(2)}, u32[]{:S(2)}) collective-permute-start(f32[80,512]{1,0:T(8,128)S(1)} %get-tuple-element.242), channel_id=1, source_target_pairs={{0,1},{1,0},{2,3},{3,2},{4,8},{5,9},{6,10},{7,11},{8,4},{9,5},{10,... | collective-permute-start | bytes 491528 | tf_op jit(solution)/shard_map/ppermute | solution.py:77
  64.5 11.6 %collective-permute-start.19 = (f32[80,512]{1,0:T(8,128)S(1)}, f32[80,512]{1,0:T(8,128)S(1)}, u32[]{:S(2)}, u32[]{:S(2)}) collective-permute-start(f32[80,512]{1,0:T(8,128)S(1)} %get-tuple-element.243), channel_id=1, source_target_pairs={{0,3},{1,2},{2,1},{3,0},{4,7},{5,6},{6,5},{7,4},{8,11},{9,10},{10,... | collective-permute-start | bytes 491528 | tf_op jit(solution)/shard_map/ppermute | solution.py:77
  78.7 4.3 %collective-permute-start.20 = (bf16[64,512]{1,0:T(8,128)(2,1)S(1)}, bf16[64,512]{1,0:T(8,128)(2,1)S(1)}, u32[]{:S(2)}, u32[]{:S(2)}) collective-permute-start(bf16[64,512]{1,0:T(8,128)(2,1)S(1)} %get-tuple-element.256), channel_id=1, source_target_pairs={{0,4},{1,5},{2,6},{3,7},{4,0},{5,1},{6,2},{7,3},{8,12},{9,13},{10,... | collective-permute-start | bytes 196616 | tf_op jit(solution)/shard_map/ppermute | solution.py:77
  84.2 14.0 %collective-permute-start.24 = (f32[80,512]{1,0:T(8,128)S(1)}, f32[80,512]{1,0:T(8,128)S(1)}, u32[]{:S(2)}, u32[]{:S(2)}) collective-permute-start(f32[80,512]{1,0:T(8,128)S(1)} %get-tuple-element.271), channel_id=1, source_target_pairs={{0,1},{1,0},{2,3},{3,2},{4,5},{5,4},{6,7},{7,6},{8,9},{9,8},{10,11... | collective-permute-start | bytes 491528 | tf_op jit(solution)/shard_map/ppermute | solution.py:77
  84.3 13.9 %collective-permute-start.25 = (f32[80,512]{1,0:T(8,128)S(1)}, f32[80,512]{1,0:T(8,128)S(1)}, u32[]{:S(2)}, u32[]{:S(2)}) collective-permute-start(f32[80,512]{1,0:T(8,128)S(1)} %get-tuple-element.272), channel_id=1, source_target_pairs={{0,4},{1,5},{2,6},{3,7},{4,0},{5,1},{6,2},{7,3},{8,12},{9,13},{10,... | collective-permute-start | bytes 491528 | tf_op jit(solution)/shard_map/ppermute | solution.py:77
  86.4 11.8 %collective-permute-start.26 = (f32[80,512]{1,0:T(8,128)S(1)}, f32[80,512]{1,0:T(8,128)S(1)}, u32[]{:S(2)}, u32[]{:S(2)}) collective-permute-start(f32[80,512]{1,0:T(8,128)S(1)} %get-tuple-element.273), channel_id=1, source_target_pairs={{0,1},{1,0},{2,3},{3,2},{4,8},{5,9},{6,10},{7,11},{8,4},{9,5},{10,... | collective-permute-start | bytes 491528 | tf_op jit(solution)/shard_map/ppermute | solution.py:77
  86.6 11.6 %collective-permute-start.27 = (f32[80,512]{1,0:T(8,128)S(1)}, f32[80,512]{1,0:T(8,128)S(1)}, u32[]{:S(2)}, u32[]{:S(2)}) collective-permute-start(f32[80,512]{1,0:T(8,128)S(1)} %get-tuple-element.274), channel_id=1, source_target_pairs={{0,3},{1,2},{2,1},{3,0},{4,7},{5,6},{6,5},{7,4},{8,11},{9,10},{10,... | collective-permute-start | bytes 491528 | tf_op jit(solution)/shard_map/ppermute | solution.py:77
  100.8 4.3 %collective-permute-start.28 = (bf16[64,512]{1,0:T(8,128)(2,1)S(1)}, bf16[64,512]{1,0:T(8,128)(2,1)S(1)}, u32[]{:S(2)}, u32[]{:S(2)}) collective-permute-start(bf16[64,512]{1,0:T(8,128)(2,1)S(1)} %get-tuple-element.287), channel_id=1, source_target_pairs={{0,4},{1,5},{2,6},{3,7},{4,0},{5,1},{6,2},{7,3},{8,12},{9,13},{10,... | collective-permute-start | bytes 196616 | tf_op jit(solution)/shard_map/ppermute | solution.py:77
  106.3 14.0 %collective-permute-start.32 = (f32[80,512]{1,0:T(8,128)S(1)}, f32[80,512]{1,0:T(8,128)S(1)}, u32[]{:S(2)}, u32[]{:S(2)}) collective-permute-start(f32[80,512]{1,0:T(8,128)S(1)} %get-tuple-element.302), channel_id=1, source_target_pairs={{0,1},{1,0},{2,3},{3,2},{4,5},{5,4},{6,7},{7,6},{8,9},{9,8},{10,11... | collective-permute-start | bytes 491528 | tf_op jit(solution)/shard_map/ppermute | solution.py:77
  106.4 13.9 %collective-permute-start.33 = (f32[80,512]{1,0:T(8,128)S(1)}, f32[80,512]{1,0:T(8,128)S(1)}, u32[]{:S(2)}, u32[]{:S(2)}) collective-permute-start(f32[80,512]{1,0:T(8,128)S(1)} %get-tuple-element.303), channel_id=1, source_target_pairs={{0,4},{1,5},{2,6},{3,7},{4,0},{5,1},{6,2},{7,3},{8,12},{9,13},{10,... | collective-permute-start | bytes 491528 | tf_op jit(solution)/shard_map/ppermute | solution.py:77
  108.5 11.8 %collective-permute-start.34 = (f32[80,512]{1,0:T(8,128)S(1)}, f32[80,512]{1,0:T(8,128)S(1)}, u32[]{:S(2)}, u32[]{:S(2)}) collective-permute-start(f32[80,512]{1,0:T(8,128)S(1)} %get-tuple-element.304), channel_id=1, source_target_pairs={{0,1},{1,0},{2,3},{3,2},{4,8},{5,9},{6,10},{7,11},{8,4},{9,5},{10,... | collective-permute-start | bytes 491528 | tf_op jit(solution)/shard_map/ppermute | solution.py:77
  108.7 11.6 %collective-permute-start.35 = (f32[80,512]{1,0:T(8,128)S(1)}, f32[80,512]{1,0:T(8,128)S(1)}, u32[]{:S(2)}, u32[]{:S(2)}) collective-permute-start(f32[80,512]{1,0:T(8,128)S(1)} %get-tuple-element.305), channel_id=1, source_target_pairs={{0,3},{1,2},{2,1},{3,0},{4,7},{5,6},{6,5},{7,4},{8,11},{9,10},{10,... | collective-permute-start | bytes 491528 | tf_op jit(solution)/shard_map/ppermute | solution.py:77
  128.4 14.0 %collective-permute-start.40 = (f32[80,512]{1,0:T(8,128)S(1)}, f32[80,512]{1,0:T(8,128)S(1)}, u32[]{:S(2)}, u32[]{:S(2)}) collective-permute-start(f32[80,512]{1,0:T(8,128)S(1)} %get-tuple-element.333), channel_id=1, source_target_pairs={{0,1},{1,0},{2,3},{3,2},{4,5},{5,4},{6,7},{7,6},{8,9},{9,8},{10,11... | collective-permute-start | bytes 491528 | tf_op jit(solution)/shard_map/ppermute | solution.py:77
  128.5 13.9 %collective-permute-start.41 = (f32[80,512]{1,0:T(8,128)S(1)}, f32[80,512]{1,0:T(8,128)S(1)}, u32[]{:S(2)}, u32[]{:S(2)}) collective-permute-start(f32[80,512]{1,0:T(8,128)S(1)} %get-tuple-element.334), channel_id=1, source_target_pairs={{0,4},{1,5},{2,6},{3,7},{4,0},{5,1},{6,2},{7,3},{8,12},{9,13},{10,... | collective-permute-start | bytes 491528 | tf_op jit(solution)/shard_map/ppermute | solution.py:77
  130.6 11.8 %collective-permute-start.42 = (f32[80,512]{1,0:T(8,128)S(1)}, f32[80,512]{1,0:T(8,128)S(1)}, u32[]{:S(2)}, u32[]{:S(2)}) collective-permute-start(f32[80,512]{1,0:T(8,128)S(1)} %get-tuple-element.335), channel_id=1, source_target_pairs={{0,1},{1,0},{2,3},{3,2},{4,8},{5,9},{6,10},{7,11},{8,4},{9,5},{10,... | collective-permute-start | bytes 491528 | tf_op jit(solution)/shard_map/ppermute | solution.py:77
  130.8 11.6 %collective-permute-start.43 = (f32[80,512]{1,0:T(8,128)S(1)}, f32[80,512]{1,0:T(8,128)S(1)}, u32[]{:S(2)}, u32[]{:S(2)}) collective-permute-start(f32[80,512]{1,0:T(8,128)S(1)} %get-tuple-element.336), channel_id=1, source_target_pairs={{0,3},{1,2},{2,1},{3,0},{4,7},{5,6},{6,5},{7,4},{8,11},{9,10},{10,... | collective-permute-start | bytes 491528 | tf_op jit(solution)/shard_map/ppermute | solution.py:77
  150.9 14.0 %collective-permute-start.48 = (f32[80,512]{1,0:T(8,128)S(1)}, f32[80,512]{1,0:T(8,128)S(1)}, u32[]{:S(2)}, u32[]{:S(2)}) collective-permute-start(f32[80,512]{1,0:T(8,128)S(1)} %get-tuple-element.364), channel_id=1, source_target_pairs={{0,1},{1,0},{2,3},{3,2},{4,5},{5,4},{6,7},{7,6},{8,9},{9,8},{10,11... | collective-permute-start | bytes 491528 | tf_op jit(solution)/shard_map/ppermute | solution.py:77
  150.9 13.9 %collective-permute-start.49 = (f32[80,512]{1,0:T(8,128)S(1)}, f32[80,512]{1,0:T(8,128)S(1)}, u32[]{:S(2)}, u32[]{:S(2)}) collective-permute-start(f32[80,512]{1,0:T(8,128)S(1)} %get-tuple-element.365), channel_id=1, source_target_pairs={{0,4},{1,5},{2,6},{3,7},{4,0},{5,1},{6,2},{7,3},{8,12},{9,13},{10,... | collective-permute-start | bytes 491528 | tf_op jit(solution)/shard_map/ppermute | solution.py:77
  153.0 11.8 %collective-permute-start.50 = (f32[80,512]{1,0:T(8,128)S(1)}, f32[80,512]{1,0:T(8,128)S(1)}, u32[]{:S(2)}, u32[]{:S(2)}) collective-permute-start(f32[80,512]{1,0:T(8,128)S(1)} %get-tuple-element.366), channel_id=1, source_target_pairs={{0,1},{1,0},{2,3},{3,2},{4,8},{5,9},{6,10},{7,11},{8,4},{9,5},{10,... | collective-permute-start | bytes 491528 | tf_op jit(solution)/shard_map/ppermute | solution.py:77
  153.2 11.6 %collective-permute-start.51 = (f32[80,512]{1,0:T(8,128)S(1)}, f32[80,512]{1,0:T(8,128)S(1)}, u32[]{:S(2)}, u32[]{:S(2)}) collective-permute-start(f32[80,512]{1,0:T(8,128)S(1)} %get-tuple-element.367), channel_id=1, source_target_pairs={{0,3},{1,2},{2,1},{3,0},{4,7},{5,6},{6,5},{7,4},{8,11},{9,10},{10,... | collective-permute-start | bytes 491528 | tf_op jit(solution)/shard_map/ppermute | solution.py:77
  (26 other events, 171.4 us)

commit v8 on v7

--- a/solution.py
+++ b/solution.py
@@ -108,17 +108,18 @@
     return columns
 
 
-def write_message(message_ref, columns, gamma, delta):
-    rows = gamma.shape[0]
+def write_message(message_ref, columns, products):
+    found = [*zip((0, 8, 1, 9, 2, 10, 3, 11), columns), *zip((4, 12), products)]
+    rows = found[0][1].shape[0]
     lane = lax.broadcasted_iota(jnp.int32, (rows, LANES), 1)
     table = jnp.zeros((rows, LANES), F32)
-    order = [*columns[0::2], gamma, *columns[1::2], delta]
-    for i, column in enumerate(order):
-        table = jnp.where(lane == (i if i < 5 else i + 3), column, table)
+    for place, column in found:
+        table = jnp.where(lane == place, column, table)
     turned = table.T
     block = jnp.concatenate([turned[0:8], turned[8:16]], axis=1)
-    for i in range(5):
-        row = jnp.broadcast_to(block[i : i + 1][None], (message_ref.shape[0], 1, LANES))
+    sent = [*range(4 if columns else 0), *([4] if products else [])]
+    for i, source in enumerate(sent):
+        row = jnp.broadcast_to(block[source : source + 1][None], (message_ref.shape[0], 1, LANES))
         message_ref[:, :, i * LANES : (i + 1) * LANES] = row
 
 
@@ -200,8 +201,7 @@
             at = slot % 2 * edge_len + start
             halves[slot // 2][:, at : at + CHUNK] = load[:realiz]
             edge_ref[:realiz, start : start + CHUNK] = load[:realiz]
-    zero = jnp.zeros((realiz, 1), F32)
-    write_message(message_ref, project(halves), zero, zero)
+    write_message(message_ref, project(halves), ())
 
 
 def product(place, slots, vec_ref, matrix_ref, slot, start):
@@ -248,7 +248,8 @@
             delta = here if delta is None else delta + here
     gamma = jnp.sum(gamma_ref[...], axis=1, keepdims=True)
     delta = jnp.sum(delta, axis=1, keepdims=True)
-    write_message(message_ref, project(halves), gamma, delta)
+    columns = project(halves) if message_ref.shape[2] > LANES else ()
+    write_message(message_ref, columns, (gamma, delta))
 
 
 def coarse_table(gathered_ref, full):
@@ -258,7 +259,7 @@
 
 
 def scalars(mode, gathered_ref, state_in, state_ref, realiz):
-    total = jnp.sum(gathered_ref[:, 0, 4 * LANES : 5 * LANES], axis=0, keepdims=True)
+    total = jnp.sum(gathered_ref[:, 0, gathered_ref.shape[2] - LANES :], axis=0, keepdims=True)
     lane = lax.broadcasted_iota(jnp.int32, (1, LANES), 1)
     swapped = pltpu.roll(total, LANES // 2, 1)
     gamma = jnp.where(lane < realiz, total, swapped)
@@ -415,9 +416,9 @@
     devices = cols * rows
     capacity = max(2, 2 * obs_count // devices)
     edge = shape(realiz, size // 4, BF16)
-    exact = [shape(realiz + PAD, size // 4)] * 4
+    exact, padded = [shape(realiz, size // 4)] * 4, [shape(realiz + PAD, size // 4)] * 4
     half, whole = shape(realiz, size // 2), shape(realiz, size)
-    message = jax.ShapeDtypeStruct((devices, 1, 5 * LANES), F32)
+    first, message, last = (jax.ShapeDtypeStruct((devices, 1, rows_sent * LANES), F32) for rows_sent in (4, 5, 1))
     narrow, state_shape = shape(realiz, LANES), shape(8, LANES)
     coarse_state = shape(4 * devices, LANES)
     scratch_half = pltpu.VMEM((realiz, size // 2), BF16)
@@ -440,7 +441,7 @@
     got = lax.all_to_all(packed.reshape(devices, capacity, LANES), AXES, split_axis=0, concat_axis=0, tiled=True)
     *image, e0, e1, e2, e3, sent = call(
         functools.partial(load_kernel, realiz),
-        [half, half, *exact, message],
+        [half, half, *exact, first],
         (got.reshape(devices * capacity, LANES),),
         flops=COVER,
     )
@@ -480,7 +481,7 @@
         )
         z_near, *image, e0, e1, e2, e3, sent = call(
             image_near_kernel,
-            [half, half, half, *exact, message],
+            [half, half, half, *([*exact, last] if step == ITERS - 1 else [*padded, message])],
             (part_near, g[0], g[1], z_far, partial, gamma, schur_mat, *track[0][:1]),
             [scratch_half],
             flops // 2,

time: 167 us -> 166 us (level)
  no operation moved by 1% of the time
where the time goes in v8:
time: 166 us; the launch traced here: 165 us
  blocking collectives  87.8 us (53%)
  starting transfers between devices  37.7 us (23%)
  Pallas kernels  29.4 us (18%)
  waiting for transfers between devices  9.44 us (6%)
    all_to_all x7, blocking collectives, gather(): lax.all_to_all(message, AXES, split_axis=0, concat_axis=0, tiled=True)  72.3 us
    ppermute x52, starting transfers between devices, exchange(): got[slot] = lax.ppermute(edges[slot], AXES, plans[slot])  37.7 us
    pallas_call x32, Pallas kernels, call(): pl.pallas_call(kernel, out_shape=outs, in_specs=[spec] * len(args), out_s...  29.4 us
    all_to_all x1, blocking collectives, body(): lax.all_to_all(packed.reshape(devices, capacity, LANES), AXES, split_axis...  15.5 us
    ppermute x52, waiting for transfers between devices, exchange(): got[slot] = lax.ppermute(edges[slot], AXES, plans[slot])  9.44 us
  transfers between devices with their start and end apart: 52, of which 12 were waited for; matrix products, arithmetic and copies ran while one was open for 0% of the time, Pallas kernels for 7%

profile of v8, /device:TPU:0, one launch (start us, length us, event | category | flops | bytes accessed | tf_op | source)
XLA Modules:
  0.0 165.5 jit_solution(5318816119494158744)
XLA Ops:
  0.6 2.0 %shard_map.77 = (bf16[512,128]{1,0:T(8,128)(2,1)}, f32[8,128]{1,0:T(8,128)}, f32[8,128]{1,0:T(8,128)}) custom-call(bf16[64,256]{1,0:T(8,128)(2,1)} %bitcast.41, s32[1,256]{1,0:T(1,128)} %bitcast.42, s32[1,256]{1,0:T(1,128)} %bitcast.43, f32[8,256]{1,0:T(8,128)} %inverse_in.1), custom_call_target="tpu_custom_call" | custom-call | flops 8000000000 | bytes 43008 | tf_op jit(solution)/shard_map/pallas_call | solution.py:25
  2.7 15.5 %all_to_all.40 = bf16[32,16,128]{2,1,0:T(8,128)(2,1)S(1)} all-to-all(bf16[32,16,128]{2,1,0:T(8,128)(2,1)} %bitcast.38), channel_id=1, replica_groups=mesh['sx'=8,'sy'=4] {'sx','sy'}, dimensions={0} | all-to-all | bytes 262144 | tf_op jit(solution)/shard_map/all_to_all | solution.py:441
  20.9 10.9 %all_to_all.41.refs_6_ = f32[32,1,512]{2,1,0:T(1,128)S(1)} all-to-all(f32[32,1,512]{2,1,0:T(1,128)S(1)} %get-tuple-element.197), channel_id=1, replica_groups=mesh['sx'=8,'sy'=4] {'sx','sy'}, dimensions={0} | all-to-all | bytes 131072 | tf_op jit(solution)/shard_map/all_to_all | solution.py:409
  34.4 1.8 %collective-permute-start.4 = (bf16[64,512]{1,0:T(8,128)(2,1)S(1)}, bf16[64,512]{1,0:T(8,128)(2,1)S(1)}, u32[]{:S(2)}, u32[]{:S(2)}) collective-permute-start(bf16[64,512]{1,0:T(8,128)(2,1)S(1)} %get-tuple-element.206), channel_id=1, source_target_pairs={{0,4},{1,5},{2,6},{3,7},{4,0},{5,1},{6,2},{7,3},{8,12},{9,13},{10,... | collective-permute-start | bytes 196616 | tf_op jit(solution)/shard_map/ppermute | solution.py:77
  38.7 1.2 shard_map.82
  40.0 2.0 %collective-permute-start.9 = (f32[80,512]{1,0:T(8,128)S(1)}, f32[80,512]{1,0:T(8,128)S(1)}, u32[]{:S(2)}, u32[]{:S(2)}) collective-permute-start(f32[80,512]{1,0:T(8,128)S(1)} %get-tuple-element.217), channel_id=1, source_target_pairs={{0,4},{1,5},{2,6},{3,7},{4,0},{5,1},{6,2},{7,3},{8,12},{9,13},{10,... | collective-permute-start | bytes 491528 | tf_op jit(solution)/shard_map/ppermute | solution.py:77
  42.1 1.3 collective-permute-start.11
  43.4 10.3 %all_to_all.42.refs_6_ = f32[32,1,640]{2,1,0:T(1,128)S(1)} all-to-all(f32[32,1,640]{2,1,0:T(1,128)S(1)} %get-tuple-element.220), channel_id=1, replica_groups=mesh['sx'=8,'sy'=4] {'sx','sy'}, dimensions={0} | all-to-all | bytes 163840 | tf_op jit(solution)/shard_map/all_to_all | solution.py:409
  56.4 1.8 %collective-permute-start.12 = (bf16[64,512]{1,0:T(8,128)(2,1)S(1)}, bf16[64,512]{1,0:T(8,128)(2,1)S(1)}, u32[]{:S(2)}, u32[]{:S(2)}) collective-permute-start(bf16[64,512]{1,0:T(8,128)(2,1)S(1)} %get-tuple-element.228), channel_id=1, source_target_pairs={{0,4},{1,5},{2,6},{3,7},{4,0},{5,1},{6,2},{7,3},{8,12},{9,13},{10,... | collective-permute-start | bytes 196616 | tf_op jit(solution)/shard_map/ppermute | solution.py:77
  62.0 2.1 %collective-permute-start.17 = (f32[80,512]{1,0:T(8,128)S(1)}, f32[80,512]{1,0:T(8,128)S(1)}, u32[]{:S(2)}, u32[]{:S(2)}) collective-permute-start(f32[80,512]{1,0:T(8,128)S(1)} %get-tuple-element.241), channel_id=1, source_target_pairs={{0,4},{1,5},{2,6},{3,7},{4,0},{5,1},{6,2},{7,3},{8,12},{9,13},{10,... | collective-permute-start | bytes 491528 | tf_op jit(solution)/shard_map/ppermute | solution.py:77
  64.2 1.3 collective-permute-start.19
  65.6 10.3 %all_to_all.43.refs_6_ = f32[32,1,640]{2,1,0:T(1,128)S(1)} all-to-all(f32[32,1,640]{2,1,0:T(1,128)S(1)} %get-tuple-element.244), channel_id=1, replica_groups=mesh['sx'=8,'sy'=4] {'sx','sy'}, dimensions={0} | all-to-all | bytes 163840 | tf_op jit(solution)/shard_map/all_to_all | solution.py:409
  78.5 1.8 %collective-permute-start.20 = (bf16[64,512]{1,0:T(8,128)(2,1)S(1)}, bf16[64,512]{1,0:T(8,128)(2,1)S(1)}, u32[]{:S(2)}, u32[]{:S(2)}) collective-permute-start(bf16[64,512]{1,0:T(8,128)(2,1)S(1)} %get-tuple-element.256), channel_id=1, source_target_pairs={{0,4},{1,5},{2,6},{3,7},{4,0},{5,1},{6,2},{7,3},{8,12},{9,13},{10,... | collective-permute-start | bytes 196616 | tf_op jit(solution)/shard_map/ppermute | solution.py:77
  82.8 1.2 shard_map.92
  84.1 2.1 %collective-permute-start.25 = (f32[80,512]{1,0:T(8,128)S(1)}, f32[80,512]{1,0:T(8,128)S(1)}, u32[]{:S(2)}, u32[]{:S(2)}) collective-permute-start(f32[80,512]{1,0:T(8,128)S(1)} %get-tuple-element.272), channel_id=1, source_target_pairs={{0,4},{1,5},{2,6},{3,7},{4,0},{5,1},{6,2},{7,3},{8,12},{9,13},{10,... | collective-permute-start | bytes 491528 | tf_op jit(solution)/shard_map/ppermute | solution.py:77
  86.3 1.3 collective-permute-start.27
  87.7 10.3 %all_to_all.44.refs_6_ = f32[32,1,640]{2,1,0:T(1,128)S(1)} all-to-all(f32[32,1,640]{2,1,0:T(1,128)S(1)} %get-tuple-element.275), channel_id=1, replica_groups=mesh['sx'=8,'sy'=4] {'sx','sy'}, dimensions={0} | all-to-all | bytes 163840 | tf_op jit(solution)/shard_map/all_to_all | solution.py:409
  100.6 1.8 %collective-permute-start.28 = (bf16[64,512]{1,0:T(8,128)(2,1)S(1)}, bf16[64,512]{1,0:T(8,128)(2,1)S(1)}, u32[]{:S(2)}, u32[]{:S(2)}) collective-permute-start(bf16[64,512]{1,0:T(8,128)(2,1)S(1)} %get-tuple-element.287), channel_id=1, source_target_pairs={{0,4},{1,5},{2,6},{3,7},{4,0},{5,1},{6,2},{7,3},{8,12},{9,13},{10,... | collective-permute-start | bytes 196616 | tf_op jit(solution)/shard_map/ppermute | solution.py:77
  104.9 1.2 shard_map.97
  106.2 2.1 %collective-permute-start.33 = (f32[80,512]{1,0:T(8,128)S(1)}, f32[80,512]{1,0:T(8,128)S(1)}, u32[]{:S(2)}, u32[]{:S(2)}) collective-permute-start(f32[80,512]{1,0:T(8,128)S(1)} %get-tuple-element.303), channel_id=1, source_target_pairs={{0,4},{1,5},{2,6},{3,7},{4,0},{5,1},{6,2},{7,3},{8,12},{9,13},{10,... | collective-permute-start | bytes 491528 | tf_op jit(solution)/shard_map/ppermute | solution.py:77
  108.4 1.3 collective-permute-start.35
  109.7 10.3 %all_to_all.45.refs_6_ = f32[32,1,640]{2,1,0:T(1,128)S(1)} all-to-all(f32[32,1,640]{2,1,0:T(1,128)S(1)} %get-tuple-element.306), channel_id=1, replica_groups=mesh['sx'=8,'sy'=4] {'sx','sy'}, dimensions={0} | all-to-all | bytes 163840 | tf_op jit(solution)/shard_map/all_to_all | solution.py:409
  122.7 1.8 %collective-permute-start.36 = (bf16[64,512]{1,0:T(8,128)(2,1)S(1)}, bf16[64,512]{1,0:T(8,128)(2,1)S(1)}, u32[]{:S(2)}, u32[]{:S(2)}) collective-permute-start(bf16[64,512]{1,0:T(8,128)(2,1)S(1)} %get-tuple-element.318), channel_id=1, source_target_pairs={{0,4},{1,5},{2,6},{3,7},{4,0},{5,1},{6,2},{7,3},{8,12},{9,13},{10,... | collective-permute-start | bytes 196616 | tf_op jit(solution)/shard_map/ppermute | solution.py:77
  128.2 2.1 %collective-permute-start.41 = (f32[80,512]{1,0:T(8,128)S(1)}, f32[80,512]{1,0:T(8,128)S(1)}, u32[]{:S(2)}, u32[]{:S(2)}) collective-permute-start(f32[80,512]{1,0:T(8,128)S(1)} %get-tuple-element.334), channel_id=1, source_target_pairs={{0,4},{1,5},{2,6},{3,7},{4,0},{5,1},{6,2},{7,3},{8,12},{9,13},{10,... | collective-permute-start | bytes 491528 | tf_op jit(solution)/shard_map/ppermute | solution.py:77
  130.5 1.4 collective-permute-start.43
  131.9 10.3 %all_to_all.46.refs_6_ = f32[32,1,640]{2,1,0:T(1,128)S(1)} all-to-all(f32[32,1,640]{2,1,0:T(1,128)S(1)} %get-tuple-element.337), channel_id=1, replica_groups=mesh['sx'=8,'sy'=4] {'sx','sy'}, dimensions={0} | all-to-all | bytes 163840 | tf_op jit(solution)/shard_map/all_to_all | solution.py:409
  142.2 1.5 shard_map.103
  145.1 1.8 %collective-permute-start.44 = (bf16[64,512]{1,0:T(8,128)(2,1)S(1)}, bf16[64,512]{1,0:T(8,128)(2,1)S(1)}, u32[]{:S(2)}, u32[]{:S(2)}) collective-permute-start(bf16[64,512]{1,0:T(8,128)(2,1)S(1)} %get-tuple-element.349), channel_id=1, source_target_pairs={{0,4},{1,5},{2,6},{3,7},{4,0},{5,1},{6,2},{7,3},{8,12},{9,13},{10,... | collective-permute-start | bytes 196616 | tf_op jit(solution)/shard_map/ppermute | solution.py:77
  150.6 2.1 %collective-permute-start.49 = (f32[64,512]{1,0:T(8,128)S(1)}, f32[64,512]{1,0:T(8,128)S(1)}, u32[]{:S(2)}, u32[]{:S(2)}) collective-permute-start(f32[64,512]{1,0:T(8,128)S(1)} %get-tuple-element.365), channel_id=1, source_target_pairs={{0,4},{1,5},{2,6},{3,7},{4,0},{5,1},{6,2},{7,3},{8,12},{9,13},{10,... | collective-permute-start | bytes 393224 | tf_op jit(solution)/shard_map/ppermute | solution.py:77
  152.9 1.3 collective-permute-start.51
  154.2 9.9 %all_to_all.47.refs_6_ = f32[32,1,128]{2,1,0:T(1,128)S(1)} all-to-all(f32[32,1,128]{2,1,0:T(1,128)S(1)} %get-tuple-element.368), channel_id=1, replica_groups=mesh['sx'=8,'sy'=4] {'sx','sy'}, dimensions={0} | all-to-all | bytes 32768 | tf_op jit(solution)/shard_map/all_to_all | solution.py:409
  164.1 1.4 shard_map.108
  (126 shorter events, 36.9 us)
Async XLA Ops:
  19.2 12.6 %collective-permute-start = (f32[64,512]{1,0:T(8,128)S(1)}, f32[64,512]{1,0:T(8,128)S(1)}, u32[]{:S(2)}, u32[]{:S(2)}) collective-permute-start(f32[64,512]{1,0:T(8,128)S(1)} %get-tuple-element.193), channel_id=1, source_target_pairs={{0,1},{1,0},{2,3},{3,2},{4,5},{5,4},{6,7},{7,6},{8,9},{9,8},{10,11... | collective-permute-start | bytes 393224 | tf_op jit(solution)/shard_map/ppermute | solution.py:77
  19.4 12.3 %collective-permute-start.1 = (f32[64,512]{1,0:T(8,128)S(1)}, f32[64,512]{1,0:T(8,128)S(1)}, u32[]{:S(2)}, u32[]{:S(2)}) collective-permute-start(f32[64,512]{1,0:T(8,128)S(1)} %get-tuple-element.194), channel_id=1, source_target_pairs={{0,4},{1,5},{2,6},{3,7},{4,0},{5,1},{6,2},{7,3},{8,12},{9,13},{10,... | collective-permute-start | bytes 393224 | tf_op jit(solution)/shard_map/ppermute | solution.py:77
  20.0 11.8 %collective-permute-start.2 = (f32[64,512]{1,0:T(8,128)S(1)}, f32[64,512]{1,0:T(8,128)S(1)}, u32[]{:S(2)}, u32[]{:S(2)}) collective-permute-start(f32[64,512]{1,0:T(8,128)S(1)} %get-tuple-element.195), channel_id=1, source_target_pairs={{0,1},{1,0},{2,3},{3,2},{4,8},{5,9},{6,10},{7,11},{8,4},{9,5},{10,... | collective-permute-start | bytes 393224 | tf_op jit(solution)/shard_map/ppermute | solution.py:77
  20.1 11.6 %collective-permute-start.3 = (f32[64,512]{1,0:T(8,128)S(1)}, f32[64,512]{1,0:T(8,128)S(1)}, u32[]{:S(2)}, u32[]{:S(2)}) collective-permute-start(f32[64,512]{1,0:T(8,128)S(1)} %get-tuple-element.196), channel_id=1, source_target_pairs={{0,3},{1,2},{2,1},{3,0},{4,7},{5,6},{6,5},{7,4},{8,11},{9,10},{10,... | collective-permute-start | bytes 393224 | tf_op jit(solution)/shard_map/ppermute | solution.py:77
  34.4 4.3 %collective-permute-start.4 = (bf16[64,512]{1,0:T(8,128)(2,1)S(1)}, bf16[64,512]{1,0:T(8,128)(2,1)S(1)}, u32[]{:S(2)}, u32[]{:S(2)}) collective-permute-start(bf16[64,512]{1,0:T(8,128)(2,1)S(1)} %get-tuple-element.206), channel_id=1, source_target_pairs={{0,4},{1,5},{2,6},{3,7},{4,0},{5,1},{6,2},{7,3},{8,12},{9,13},{10,... | collective-permute-start | bytes 196616 | tf_op jit(solution)/shard_map/ppermute | solution.py:77
  39.9 13.9 %collective-permute-start.8 = (f32[80,512]{1,0:T(8,128)S(1)}, f32[80,512]{1,0:T(8,128)S(1)}, u32[]{:S(2)}, u32[]{:S(2)}) collective-permute-start(f32[80,512]{1,0:T(8,128)S(1)} %get-tuple-element.216), channel_id=1, source_target_pairs={{0,1},{1,0},{2,3},{3,2},{4,5},{5,4},{6,7},{7,6},{8,9},{9,8},{10,11... | collective-permute-start | bytes 491528 | tf_op jit(solution)/shard_map/ppermute | solution.py:77
  40.0 13.8 %collective-permute-start.9 = (f32[80,512]{1,0:T(8,128)S(1)}, f32[80,512]{1,0:T(8,128)S(1)}, u32[]{:S(2)}, u32[]{:S(2)}) collective-permute-start(f32[80,512]{1,0:T(8,128)S(1)} %get-tuple-element.217), channel_id=1, source_target_pairs={{0,4},{1,5},{2,6},{3,7},{4,0},{5,1},{6,2},{7,3},{8,12},{9,13},{10,... | collective-permute-start | bytes 491528 | tf_op jit(solution)/shard_map/ppermute | solution.py:77
  42.0 11.8 %collective-permute-start.10 = (f32[80,512]{1,0:T(8,128)S(1)}, f32[80,512]{1,0:T(8,128)S(1)}, u32[]{:S(2)}, u32[]{:S(2)}) collective-permute-start(f32[80,512]{1,0:T(8,128)S(1)} %get-tuple-element.218), channel_id=1, source_target_pairs={{0,1},{1,0},{2,3},{3,2},{4,8},{5,9},{6,10},{7,11},{8,4},{9,5},{10,... | collective-permute-start | bytes 491528 | tf_op jit(solution)/shard_map/ppermute | solution.py:77
  42.1 11.6 %collective-permute-start.11 = (f32[80,512]{1,0:T(8,128)S(1)}, f32[80,512]{1,0:T(8,128)S(1)}, u32[]{:S(2)}, u32[]{:S(2)}) collective-permute-start(f32[80,512]{1,0:T(8,128)S(1)} %get-tuple-element.219), channel_id=1, source_target_pairs={{0,3},{1,2},{2,1},{3,0},{4,7},{5,6},{6,5},{7,4},{8,11},{9,10},{10,... | collective-permute-start | bytes 491528 | tf_op jit(solution)/shard_map/ppermute | solution.py:77
  61.9 14.0 %collective-permute-start.16 = (f32[80,512]{1,0:T(8,128)S(1)}, f32[80,512]{1,0:T(8,128)S(1)}, u32[]{:S(2)}, u32[]{:S(2)}) collective-permute-start(f32[80,512]{1,0:T(8,128)S(1)} %get-tuple-element.240), channel_id=1, source_target_pairs={{0,1},{1,0},{2,3},{3,2},{4,5},{5,4},{6,7},{7,6},{8,9},{9,8},{10,11... | collective-permute-start | bytes 491528 | tf_op jit(solution)/shard_map/ppermute | solution.py:77
  62.0 13.9 %collective-permute-start.17 = (f32[80,512]{1,0:T(8,128)S(1)}, f32[80,512]{1,0:T(8,128)S(1)}, u32[]{:S(2)}, u32[]{:S(2)}) collective-permute-start(f32[80,512]{1,0:T(8,128)S(1)} %get-tuple-element.241), channel_id=1, source_target_pairs={{0,4},{1,5},{2,6},{3,7},{4,0},{5,1},{6,2},{7,3},{8,12},{9,13},{10,... | collective-permute-start | bytes 491528 | tf_op jit(solution)/shard_map/ppermute | solution.py:77
  64.1 11.8 %collective-permute-start.18 = (f32[80,512]{1,0:T(8,128)S(1)}, f32[80,512]{1,0:T(8,128)S(1)}, u32[]{:S(2)}, u32[]{:S(2)}) collective-permute-start(f32[80,512]{1,0:T(8,128)S(1)} %get-tuple-element.242), channel_id=1, source_target_pairs={{0,1},{1,0},{2,3},{3,2},{4,8},{5,9},{6,10},{7,11},{8,4},{9,5},{10,... | collective-permute-start | bytes 491528 | tf_op jit(solution)/shard_map/ppermute | solution.py:77
  64.2 11.6 %collective-permute-start.19 = (f32[80,512]{1,0:T(8,128)S(1)}, f32[80,512]{1,0:T(8,128)S(1)}, u32[]{:S(2)}, u32[]{:S(2)}) collective-permute-start(f32[80,512]{1,0:T(8,128)S(1)} %get-tuple-element.243), channel_id=1, source_target_pairs={{0,3},{1,2},{2,1},{3,0},{4,7},{5,6},{6,5},{7,4},{8,11},{9,10},{10,... | collective-permute-start | bytes 491528 | tf_op jit(solution)/shard_map/ppermute | solution.py:77
  84.0 14.0 %collective-permute-start.24 = (f32[80,512]{1,0:T(8,128)S(1)}, f32[80,512]{1,0:T(8,128)S(1)}, u32[]{:S(2)}, u32[]{:S(2)}) collective-permute-start(f32[80,512]{1,0:T(8,128)S(1)} %get-tuple-element.271), channel_id=1, source_target_pairs={{0,1},{1,0},{2,3},{3,2},{4,5},{5,4},{6,7},{7,6},{8,9},{9,8},{10,11... | collective-permute-start | bytes 491528 | tf_op jit(solution)/shard_map/ppermute | solution.py:77
  84.1 13.9 %collective-permute-start.25 = (f32[80,512]{1,0:T(8,128)S(1)}, f32[80,512]{1,0:T(8,128)S(1)}, u32[]{:S(2)}, u32[]{:S(2)}) collective-permute-start(f32[80,512]{1,0:T(8,128)S(1)} %get-tuple-element.272), channel_id=1, source_target_pairs={{0,4},{1,5},{2,6},{3,7},{4,0},{5,1},{6,2},{7,3},{8,12},{9,13},{10,... | collective-permute-start | bytes 491528 | tf_op jit(solution)/shard_map/ppermute | solution.py:77
  86.2 11.8 %collective-permute-start.26 = (f32[80,512]{1,0:T(8,128)S(1)}, f32[80,512]{1,0:T(8,128)S(1)}, u32[]{:S(2)}, u32[]{:S(2)}) collective-permute-start(f32[80,512]{1,0:T(8,128)S(1)} %get-tuple-element.273), channel_id=1, source_target_pairs={{0,1},{1,0},{2,3},{3,2},{4,8},{5,9},{6,10},{7,11},{8,4},{9,5},{10,... | collective-permute-start | bytes 491528 | tf_op jit(solution)/shard_map/ppermute | solution.py:77
  86.3 11.6 %collective-permute-start.27 = (f32[80,512]{1,0:T(8,128)S(1)}, f32[80,512]{1,0:T(8,128)S(1)}, u32[]{:S(2)}, u32[]{:S(2)}) collective-permute-start(f32[80,512]{1,0:T(8,128)S(1)} %get-tuple-element.274), channel_id=1, source_target_pairs={{0,3},{1,2},{2,1},{3,0},{4,7},{5,6},{6,5},{7,4},{8,11},{9,10},{10,... | collective-permute-start | bytes 491528 | tf_op jit(solution)/shard_map/ppermute | solution.py:77
  100.6 4.3 %collective-permute-start.28 = (bf16[64,512]{1,0:T(8,128)(2,1)S(1)}, bf16[64,512]{1,0:T(8,128)(2,1)S(1)}, u32[]{:S(2)}, u32[]{:S(2)}) collective-permute-start(bf16[64,512]{1,0:T(8,128)(2,1)S(1)} %get-tuple-element.287), channel_id=1, source_target_pairs={{0,4},{1,5},{2,6},{3,7},{4,0},{5,1},{6,2},{7,3},{8,12},{9,13},{10,... | collective-permute-start | bytes 196616 | tf_op jit(solution)/shard_map/ppermute | solution.py:77
  106.1 14.0 %collective-permute-start.32 = (f32[80,512]{1,0:T(8,128)S(1)}, f32[80,512]{1,0:T(8,128)S(1)}, u32[]{:S(2)}, u32[]{:S(2)}) collective-permute-start(f32[80,512]{1,0:T(8,128)S(1)} %get-tuple-element.302), channel_id=1, source_target_pairs={{0,1},{1,0},{2,3},{3,2},{4,5},{5,4},{6,7},{7,6},{8,9},{9,8},{10,11... | collective-permute-start | bytes 491528 | tf_op jit(solution)/shard_map/ppermute | solution.py:77
  106.2 13.9 %collective-permute-start.33 = (f32[80,512]{1,0:T(8,128)S(1)}, f32[80,512]{1,0:T(8,128)S(1)}, u32[]{:S(2)}, u32[]{:S(2)}) collective-permute-start(f32[80,512]{1,0:T(8,128)S(1)} %get-tuple-element.303), channel_id=1, source_target_pairs={{0,4},{1,5},{2,6},{3,7},{4,0},{5,1},{6,2},{7,3},{8,12},{9,13},{10,... | collective-permute-start | bytes 491528 | tf_op jit(solution)/shard_map/ppermute | solution.py:77
  108.3 11.8 %collective-permute-start.34 = (f32[80,512]{1,0:T(8,128)S(1)}, f32[80,512]{1,0:T(8,128)S(1)}, u32[]{:S(2)}, u32[]{:S(2)}) collective-permute-start(f32[80,512]{1,0:T(8,128)S(1)} %get-tuple-element.304), channel_id=1, source_target_pairs={{0,1},{1,0},{2,3},{3,2},{4,8},{5,9},{6,10},{7,11},{8,4},{9,5},{10,... | collective-permute-start | bytes 491528 | tf_op jit(solution)/shard_map/ppermute | solution.py:77
  108.4 11.6 %collective-permute-start.35 = (f32[80,512]{1,0:T(8,128)S(1)}, f32[80,512]{1,0:T(8,128)S(1)}, u32[]{:S(2)}, u32[]{:S(2)}) collective-permute-start(f32[80,512]{1,0:T(8,128)S(1)} %get-tuple-element.305), channel_id=1, source_target_pairs={{0,3},{1,2},{2,1},{3,0},{4,7},{5,6},{6,5},{7,4},{8,11},{9,10},{10,... | collective-permute-start | bytes 491528 | tf_op jit(solution)/shard_map/ppermute | solution.py:77
  122.7 4.3 %collective-permute-start.36 = (bf16[64,512]{1,0:T(8,128)(2,1)S(1)}, bf16[64,512]{1,0:T(8,128)(2,1)S(1)}, u32[]{:S(2)}, u32[]{:S(2)}) collective-permute-start(bf16[64,512]{1,0:T(8,128)(2,1)S(1)} %get-tuple-element.318), channel_id=1, source_target_pairs={{0,4},{1,5},{2,6},{3,7},{4,0},{5,1},{6,2},{7,3},{8,12},{9,13},{10,... | collective-permute-start | bytes 196616 | tf_op jit(solution)/shard_map/ppermute | solution.py:77
  128.2 14.0 %collective-permute-start.40 = (f32[80,512]{1,0:T(8,128)S(1)}, f32[80,512]{1,0:T(8,128)S(1)}, u32[]{:S(2)}, u32[]{:S(2)}) collective-permute-start(f32[80,512]{1,0:T(8,128)S(1)} %get-tuple-element.333), channel_id=1, source_target_pairs={{0,1},{1,0},{2,3},{3,2},{4,5},{5,4},{6,7},{7,6},{8,9},{9,8},{10,11... | collective-permute-start | bytes 491528 | tf_op jit(solution)/shard_map/ppermute | solution.py:77
  128.2 13.9 %collective-permute-start.41 = (f32[80,512]{1,0:T(8,128)S(1)}, f32[80,512]{1,0:T(8,128)S(1)}, u32[]{:S(2)}, u32[]{:S(2)}) collective-permute-start(f32[80,512]{1,0:T(8,128)S(1)} %get-tuple-element.334), channel_id=1, source_target_pairs={{0,4},{1,5},{2,6},{3,7},{4,0},{5,1},{6,2},{7,3},{8,12},{9,13},{10,... | collective-permute-start | bytes 491528 | tf_op jit(solution)/shard_map/ppermute | solution.py:77
  130.3 11.8 %collective-permute-start.42 = (f32[80,512]{1,0:T(8,128)S(1)}, f32[80,512]{1,0:T(8,128)S(1)}, u32[]{:S(2)}, u32[]{:S(2)}) collective-permute-start(f32[80,512]{1,0:T(8,128)S(1)} %get-tuple-element.335), channel_id=1, source_target_pairs={{0,1},{1,0},{2,3},{3,2},{4,8},{5,9},{6,10},{7,11},{8,4},{9,5},{10,... | collective-permute-start | bytes 491528 | tf_op jit(solution)/shard_map/ppermute | solution.py:77
  130.5 11.7 %collective-permute-start.43 = (f32[80,512]{1,0:T(8,128)S(1)}, f32[80,512]{1,0:T(8,128)S(1)}, u32[]{:S(2)}, u32[]{:S(2)}) collective-permute-start(f32[80,512]{1,0:T(8,128)S(1)} %get-tuple-element.336), channel_id=1, source_target_pairs={{0,3},{1,2},{2,1},{3,0},{4,7},{5,6},{6,5},{7,4},{8,11},{9,10},{10,... | collective-permute-start | bytes 491528 | tf_op jit(solution)/shard_map/ppermute | solution.py:77
  145.1 4.3 %collective-permute-start.44 = (bf16[64,512]{1,0:T(8,128)(2,1)S(1)}, bf16[64,512]{1,0:T(8,128)(2,1)S(1)}, u32[]{:S(2)}, u32[]{:S(2)}) collective-permute-start(bf16[64,512]{1,0:T(8,128)(2,1)S(1)} %get-tuple-element.349), channel_id=1, source_target_pairs={{0,4},{1,5},{2,6},{3,7},{4,0},{5,1},{6,2},{7,3},{8,12},{9,13},{10,... | collective-permute-start | bytes 196616 | tf_op jit(solution)/shard_map/ppermute | solution.py:77
  150.5 13.5 %collective-permute-start.48 = (f32[64,512]{1,0:T(8,128)S(1)}, f32[64,512]{1,0:T(8,128)S(1)}, u32[]{:S(2)}, u32[]{:S(2)}) collective-permute-start(f32[64,512]{1,0:T(8,128)S(1)} %get-tuple-element.364), channel_id=1, source_target_pairs={{0,1},{1,0},{2,3},{3,2},{4,5},{5,4},{6,7},{7,6},{8,9},{9,8},{10,11... | collective-permute-start | bytes 393224 | tf_op jit(solution)/shard_map/ppermute | solution.py:77
  150.6 13.4 %collective-permute-start.49 = (f32[64,512]{1,0:T(8,128)S(1)}, f32[64,512]{1,0:T(8,128)S(1)}, u32[]{:S(2)}, u32[]{:S(2)}) collective-permute-start(f32[64,512]{1,0:T(8,128)S(1)} %get-tuple-element.365), channel_id=1, source_target_pairs={{0,4},{1,5},{2,6},{3,7},{4,0},{5,1},{6,2},{7,3},{8,12},{9,13},{10,... | collective-permute-start | bytes 393224 | tf_op jit(solution)/shard_map/ppermute | solution.py:77
  152.7 11.3 %collective-permute-start.50 = (f32[64,512]{1,0:T(8,128)S(1)}, f32[64,512]{1,0:T(8,128)S(1)}, u32[]{:S(2)}, u32[]{:S(2)}) collective-permute-start(f32[64,512]{1,0:T(8,128)S(1)} %get-tuple-element.366), channel_id=1, source_target_pairs={{0,1},{1,0},{2,3},{3,2},{4,8},{5,9},{6,10},{7,11},{8,4},{9,5},{10,... | collective-permute-start | bytes 393224 | tf_op jit(solution)/shard_map/ppermute | solution.py:77
  152.9 11.2 %collective-permute-start.51 = (f32[64,512]{1,0:T(8,128)S(1)}, f32[64,512]{1,0:T(8,128)S(1)}, u32[]{:S(2)}, u32[]{:S(2)}) collective-permute-start(f32[64,512]{1,0:T(8,128)S(1)} %get-tuple-element.367), channel_id=1, source_target_pairs={{0,3},{1,2},{2,1},{3,0},{4,7},{5,6},{6,5},{7,4},{8,11},{9,10},{10,... | collective-permute-start | bytes 393224 | tf_op jit(solution)/shard_map/ppermute | solution.py:77
  (26 other events, 170.6 us)

commit v9 on v8

--- a/solution.py
+++ b/solution.py
@@ -8,11 +8,13 @@
 from jax.sharding import PartitionSpec as P
 
 ITERS = 6
+LOAD_ORDER = (2, 3, 0, 1)
 ORDER = (1, 0, 2, 3)
 PAD = 16
 COVER = 8e9
 LANES = 128
 CHUNK = 512
+STEP = 256
 HP = lax.Precision.HIGHEST
 F32 = jnp.float32
 BF16 = jnp.bfloat16
@@ -280,12 +282,12 @@
     return jnp.concatenate([*rows, jnp.zeros((LANES - count, LANES), F32)], axis=0).T[:realiz]
 
 
-def in_slots(refs):
-    return [refs[ORDER.index(slot)] for slot in range(4)]
+def in_slots(refs, order):
+    return [refs[order.index(slot)] for slot in range(4)]
 
 
 def new_residual(place, slot, mode, columns, image_ref, got_ref, old, at, start):
-    got = got_ref[: image_ref.shape[0], pl.ds(start, CHUNK)]
+    got = got_ref[: image_ref.shape[0], pl.ds(start, STEP)]
     shared = place.shared[slot]
     applied = image_ref[:, at] + (got if shared is None else jnp.where(shared, got, 0.0))
     if mode == "load":
@@ -326,7 +328,7 @@
     refs = list(refs)
     take = lambda n: [refs.pop(0) for _ in range(n)]
     place = Place()
-    images, edges, (gathered_ref,) = take(2), in_slots(take(4)), take(1)
+    images, edges, (gathered_ref,) = take(2), in_slots(take(4), LOAD_ORDER if mode == "load" else ORDER), take(1)
     olds = [take(OLD[mode]) for _ in range(2)]
     state_in, = take(1) if mode == "next" else (None,)
     coarse_in, = take(1) if mode != "load" else (None,)
@@ -352,13 +354,13 @@
         rows = [alpha, beta, jnp.zeros((6, LANES), F32)]
     for slot in range(4):
         half = slot // 2
-        for start in range(0, edge_len, CHUNK):
-            at = pl.ds(slot % 2 * edge_len + start, CHUNK)
+        for start in range(0, edge_len, STEP):
+            at = pl.ds(slot % 2 * edge_len + start, STEP)
             applied, resid = new_residual(place, slot, mode, columns, images[half], edges[slot], olds[half], at, start)
             news[half][0][:, at] = resid
             if applied is not None:
                 news[half][1][:, at] = applied
-            scaled[:, pl.ds(slot * edge_len + start, CHUNK)] = (place.weight(slot) * resid).astype(BF16)
+            scaled[:, pl.ds(slot * edge_len + start, STEP)] = (place.weight(slot) * resid).astype(BF16)
     level = jnp.dot(level_mat_ref[...], coarse, precision=HP, preferred_element_type=F32)
     ramp = jnp.dot(ramp_mat_ref[...], coarse, precision=HP, preferred_element_type=F32)
     rows.append(level + pltpu.roll(ramp, LANES // 2, 1))
@@ -382,8 +384,8 @@
     for half in range(2):
         precon_ref, *olds = refs[half * (1 + old) : (half + 1) * (1 + old)]
         direction_ref, field_ref = refs[2 * (1 + old) + 2 * half : 2 * (1 + old) + 2 * half + 2]
-        for start in range(0, precon_ref.shape[1], CHUNK):
-            at = pl.ds(start, CHUNK)
+        for start in range(0, precon_ref.shape[1], STEP):
+            at = pl.ds(start, STEP)
             direction_ref[:, at], field_ref[:, at] = new_field(mode, columns, precon_ref, olds, at)
 
 
@@ -391,16 +393,16 @@
     refs = list(refs)
     take = lambda n: [refs.pop(0) for _ in range(n)]
     place = Place()
-    images, edges, (gathered_ref,) = take(2), in_slots(take(4)), take(1)
+    images, edges, (gathered_ref,) = take(2), in_slots(take(4), ORDER), take(1)
     olds, (state_in,), tracks = [take(2) for _ in range(2)], take(1), [take(3) for _ in range(2)]
     field_ref, resid_ref = refs
     realiz, edge_len = images[0].shape[0], edges[0].shape[1]
     columns = turn(scalars("next", gathered_ref, state_in, None, realiz), realiz)
     for slot in range(4):
         half = slot // 2
-        for start in range(0, edge_len, CHUNK):
-            at = pl.ds(slot % 2 * edge_len + start, CHUNK)
-            to = pl.ds(pl.multiple_of(place.edges[slot] * edge_len + start, CHUNK), CHUNK)
+        for start in range(0, edge_len, STEP):
+            at = pl.ds(slot % 2 * edge_len + start, STEP)
+            to = pl.ds(pl.multiple_of(place.edges[slot] * edge_len + start, STEP), STEP)
             _, resid_ref[:, to] = new_residual(place, slot, "next", columns, images[half], edges[slot], olds[half], at, start)
             _, field_ref[:, to] = new_field("next", columns, tracks[half][0], tracks[half][1:], at)
 
@@ -448,7 +450,7 @@
     mode, olds, states = "load", ([], []), []
     for step in range(ITERS + 1):
         g, gathered = exchange((e0, e1, e2, e3)), gather(sent)
-        ins = [*image, *[g[slot] for slot in ORDER], gathered, *olds[0], *olds[1]]
+        ins = [*image, *[g[slot] for slot in (LOAD_ORDER if mode == "load" else ORDER)], gathered, *olds[0], *olds[1]]
         if step == ITERS:
             field, resid = call(last_kernel, [whole, whole], [*ins, states[0], z[0], *track[0], z[1], *track[1]])
             return field[None, None], resid[None, None]

time: 166 us -> 166 us (level)
  no operation moved by 1% of the time
where the time goes in v9:
time: 166 us
  blocking collectives  87.4 us (53%)
  starting transfers between devices  38.2 us (23%)
  Pallas kernels  29.3 us (18%)
  waiting for transfers between devices  9.45 us (6%)
    all_to_all x7, blocking collectives, gather(): lax.all_to_all(message, AXES, split_axis=0, concat_axis=0, tiled=True)  71.9 us
    ppermute x52, starting transfers between devices, exchange(): got[slot] = lax.ppermute(edges[slot], AXES, plans[slot])  38.2 us
    pallas_call x32, Pallas kernels, call(): pl.pallas_call(kernel, out_shape=outs, in_specs=[spec] * len(args), out_s...  29.3 us
    all_to_all x1, blocking collectives, body(): lax.all_to_all(packed.reshape(devices, capacity, LANES), AXES, split_axis...  15.5 us
    ppermute x52, waiting for transfers between devices, exchange(): got[slot] = lax.ppermute(edges[slot], AXES, plans[slot])  9.45 us
  transfers between devices with their start and end apart: 52, of which 12 were waited for; matrix products, arithmetic and copies ran while one was open for 0% of the time, Pallas kernels for 7%

profile of v9, /device:TPU:0, one launch (start us, length us, event | category | flops | bytes accessed | tf_op | source)
XLA Modules:
  0.0 165.6 jit_solution(11081460438610576350)
XLA Ops:
  0.6 2.0 %shard_map.77 = (bf16[512,128]{1,0:T(8,128)(2,1)}, f32[8,128]{1,0:T(8,128)}, f32[8,128]{1,0:T(8,128)}) custom-call(bf16[64,256]{1,0:T(8,128)(2,1)} %bitcast.41, s32[1,256]{1,0:T(1,128)} %bitcast.42, s32[1,256]{1,0:T(1,128)} %bitcast.43, f32[8,256]{1,0:T(8,128)} %inverse_in.1), custom_call_target="tpu_custom_call" | custom-call | flops 8000000000 | bytes 43008 | tf_op jit(solution)/shard_map/pallas_call | solution.py:27
  2.7 15.5 %all_to_all.40 = bf16[32,16,128]{2,1,0:T(8,128)(2,1)S(1)} all-to-all(bf16[32,16,128]{2,1,0:T(8,128)(2,1)} %bitcast.38), channel_id=1, replica_groups=mesh['sx'=8,'sy'=4] {'sx','sy'}, dimensions={0} | all-to-all | bytes 262144 | tf_op jit(solution)/shard_map/all_to_all | solution.py:443
  19.8 1.5 collective-permute-start.2
  21.4 10.5 %all_to_all.41.refs_6_ = f32[32,1,512]{2,1,0:T(1,128)S(1)} all-to-all(f32[32,1,512]{2,1,0:T(1,128)S(1)} %get-tuple-element.197), channel_id=1, replica_groups=mesh['sx'=8,'sy'=4] {'sx','sy'}, dimensions={0} | all-to-all | bytes 131072 | tf_op jit(solution)/shard_map/all_to_all | solution.py:411
  34.5 1.8 %collective-permute-start.4 = (bf16[64,512]{1,0:T(8,128)(2,1)S(1)}, bf16[64,512]{1,0:T(8,128)(2,1)S(1)}, u32[]{:S(2)}, u32[]{:S(2)}) collective-permute-start(bf16[64,512]{1,0:T(8,128)(2,1)S(1)} %get-tuple-element.206), channel_id=1, source_target_pairs={{0,4},{1,5},{2,6},{3,7},{4,0},{5,1},{6,2},{7,3},{8,12},{9,13},{10,... | collective-permute-start | bytes 196616 | tf_op jit(solution)/shard_map/ppermute | solution.py:79
  38.8 1.2 shard_map.82
  40.1 2.0 %collective-permute-start.9 = (f32[80,512]{1,0:T(8,128)S(1)}, f32[80,512]{1,0:T(8,128)S(1)}, u32[]{:S(2)}, u32[]{:S(2)}) collective-permute-start(f32[80,512]{1,0:T(8,128)S(1)} %get-tuple-element.217), channel_id=1, source_target_pairs={{0,4},{1,5},{2,6},{3,7},{4,0},{5,1},{6,2},{7,3},{8,12},{9,13},{10,... | collective-permute-start | bytes 491528 | tf_op jit(solution)/shard_map/ppermute | solution.py:79
  42.2 1.3 collective-permute-start.11
  43.5 10.3 %all_to_all.42.refs_6_ = f32[32,1,640]{2,1,0:T(1,128)S(1)} all-to-all(f32[32,1,640]{2,1,0:T(1,128)S(1)} %get-tuple-element.220), channel_id=1, replica_groups=mesh['sx'=8,'sy'=4] {'sx','sy'}, dimensions={0} | all-to-all | bytes 163840 | tf_op jit(solution)/shard_map/all_to_all | solution.py:411
  56.5 1.8 %collective-permute-start.12 = (bf16[64,512]{1,0:T(8,128)(2,1)S(1)}, bf16[64,512]{1,0:T(8,128)(2,1)S(1)}, u32[]{:S(2)}, u32[]{:S(2)}) collective-permute-start(bf16[64,512]{1,0:T(8,128)(2,1)S(1)} %get-tuple-element.228), channel_id=1, source_target_pairs={{0,4},{1,5},{2,6},{3,7},{4,0},{5,1},{6,2},{7,3},{8,12},{9,13},{10,... | collective-permute-start | bytes 196616 | tf_op jit(solution)/shard_map/ppermute | solution.py:79
  60.8 1.2 shard_map.87
  62.1 2.1 %collective-permute-start.17 = (f32[80,512]{1,0:T(8,128)S(1)}, f32[80,512]{1,0:T(8,128)S(1)}, u32[]{:S(2)}, u32[]{:S(2)}) collective-permute-start(f32[80,512]{1,0:T(8,128)S(1)} %get-tuple-element.241), channel_id=1, source_target_pairs={{0,4},{1,5},{2,6},{3,7},{4,0},{5,1},{6,2},{7,3},{8,12},{9,13},{10,... | collective-permute-start | bytes 491528 | tf_op jit(solution)/shard_map/ppermute | solution.py:79
  64.3 1.3 collective-permute-start.19
  65.7 10.3 %all_to_all.43.refs_6_ = f32[32,1,640]{2,1,0:T(1,128)S(1)} all-to-all(f32[32,1,640]{2,1,0:T(1,128)S(1)} %get-tuple-element.244), channel_id=1, replica_groups=mesh['sx'=8,'sy'=4] {'sx','sy'}, dimensions={0} | all-to-all | bytes 163840 | tf_op jit(solution)/shard_map/all_to_all | solution.py:411
  78.6 1.8 %collective-permute-start.20 = (bf16[64,512]{1,0:T(8,128)(2,1)S(1)}, bf16[64,512]{1,0:T(8,128)(2,1)S(1)}, u32[]{:S(2)}, u32[]{:S(2)}) collective-permute-start(bf16[64,512]{1,0:T(8,128)(2,1)S(1)} %get-tuple-element.256), channel_id=1, source_target_pairs={{0,4},{1,5},{2,6},{3,7},{4,0},{5,1},{6,2},{7,3},{8,12},{9,13},{10,... | collective-permute-start | bytes 196616 | tf_op jit(solution)/shard_map/ppermute | solution.py:79
  84.2 2.1 %collective-permute-start.25 = (f32[80,512]{1,0:T(8,128)S(1)}, f32[80,512]{1,0:T(8,128)S(1)}, u32[]{:S(2)}, u32[]{:S(2)}) collective-permute-start(f32[80,512]{1,0:T(8,128)S(1)} %get-tuple-element.272), channel_id=1, source_target_pairs={{0,4},{1,5},{2,6},{3,7},{4,0},{5,1},{6,2},{7,3},{8,12},{9,13},{10,... | collective-permute-start | bytes 491528 | tf_op jit(solution)/shard_map/ppermute | solution.py:79
  86.4 1.3 collective-permute-start.27
  87.8 10.3 %all_to_all.44.refs_6_ = f32[32,1,640]{2,1,0:T(1,128)S(1)} all-to-all(f32[32,1,640]{2,1,0:T(1,128)S(1)} %get-tuple-element.275), channel_id=1, replica_groups=mesh['sx'=8,'sy'=4] {'sx','sy'}, dimensions={0} | all-to-all | bytes 163840 | tf_op jit(solution)/shard_map/all_to_all | solution.py:411
  100.7 1.8 %collective-permute-start.28 = (bf16[64,512]{1,0:T(8,128)(2,1)S(1)}, bf16[64,512]{1,0:T(8,128)(2,1)S(1)}, u32[]{:S(2)}, u32[]{:S(2)}) collective-permute-start(bf16[64,512]{1,0:T(8,128)(2,1)S(1)} %get-tuple-element.287), channel_id=1, source_target_pairs={{0,4},{1,5},{2,6},{3,7},{4,0},{5,1},{6,2},{7,3},{8,12},{9,13},{10,... | collective-permute-start | bytes 196616 | tf_op jit(solution)/shard_map/ppermute | solution.py:79
  106.3 2.1 %collective-permute-start.33 = (f32[80,512]{1,0:T(8,128)S(1)}, f32[80,512]{1,0:T(8,128)S(1)}, u32[]{:S(2)}, u32[]{:S(2)}) collective-permute-start(f32[80,512]{1,0:T(8,128)S(1)} %get-tuple-element.303), channel_id=1, source_target_pairs={{0,4},{1,5},{2,6},{3,7},{4,0},{5,1},{6,2},{7,3},{8,12},{9,13},{10,... | collective-permute-start | bytes 491528 | tf_op jit(solution)/shard_map/ppermute | solution.py:79
  108.5 1.3 collective-permute-start.35
  109.8 10.3 %all_to_all.45.refs_6_ = f32[32,1,640]{2,1,0:T(1,128)S(1)} all-to-all(f32[32,1,640]{2,1,0:T(1,128)S(1)} %get-tuple-element.306), channel_id=1, replica_groups=mesh['sx'=8,'sy'=4] {'sx','sy'}, dimensions={0} | all-to-all | bytes 163840 | tf_op jit(solution)/shard_map/all_to_all | solution.py:411
  122.8 1.8 %collective-permute-start.36 = (bf16[64,512]{1,0:T(8,128)(2,1)S(1)}, bf16[64,512]{1,0:T(8,128)(2,1)S(1)}, u32[]{:S(2)}, u32[]{:S(2)}) collective-permute-start(bf16[64,512]{1,0:T(8,128)(2,1)S(1)} %get-tuple-element.318), channel_id=1, source_target_pairs={{0,4},{1,5},{2,6},{3,7},{4,0},{5,1},{6,2},{7,3},{8,12},{9,13},{10,... | collective-permute-start | bytes 196616 | tf_op jit(solution)/shard_map/ppermute | solution.py:79
  128.3 2.1 %collective-permute-start.41 = (f32[80,512]{1,0:T(8,128)S(1)}, f32[80,512]{1,0:T(8,128)S(1)}, u32[]{:S(2)}, u32[]{:S(2)}) collective-permute-start(f32[80,512]{1,0:T(8,128)S(1)} %get-tuple-element.334), channel_id=1, source_target_pairs={{0,4},{1,5},{2,6},{3,7},{4,0},{5,1},{6,2},{7,3},{8,12},{9,13},{10,... | collective-permute-start | bytes 491528 | tf_op jit(solution)/shard_map/ppermute | solution.py:79
  130.6 1.4 collective-permute-start.43
  132.0 10.3 %all_to_all.46.refs_6_ = f32[32,1,640]{2,1,0:T(1,128)S(1)} all-to-all(f32[32,1,640]{2,1,0:T(1,128)S(1)} %get-tuple-element.337), channel_id=1, replica_groups=mesh['sx'=8,'sy'=4] {'sx','sy'}, dimensions={0} | all-to-all | bytes 163840 | tf_op jit(solution)/shard_map/all_to_all | solution.py:411
  142.3 1.5 shard_map.103
  145.2 1.8 %collective-permute-start.44 = (bf16[64,512]{1,0:T(8,128)(2,1)S(1)}, bf16[64,512]{1,0:T(8,128)(2,1)S(1)}, u32[]{:S(2)}, u32[]{:S(2)}) collective-permute-start(bf16[64,512]{1,0:T(8,128)(2,1)S(1)} %get-tuple-element.349), channel_id=1, source_target_pairs={{0,4},{1,5},{2,6},{3,7},{4,0},{5,1},{6,2},{7,3},{8,12},{9,13},{10,... | collective-permute-start | bytes 196616 | tf_op jit(solution)/shard_map/ppermute | solution.py:79
  150.7 2.1 %collective-permute-start.49 = (f32[64,512]{1,0:T(8,128)S(1)}, f32[64,512]{1,0:T(8,128)S(1)}, u32[]{:S(2)}, u32[]{:S(2)}) collective-permute-start(f32[64,512]{1,0:T(8,128)S(1)} %get-tuple-element.365), channel_id=1, source_target_pairs={{0,4},{1,5},{2,6},{3,7},{4,0},{5,1},{6,2},{7,3},{8,12},{9,13},{10,... | collective-permute-start | bytes 393224 | tf_op jit(solution)/shard_map/ppermute | solution.py:79
  153.0 1.3 collective-permute-start.51
  154.3 9.9 %all_to_all.47.refs_6_ = f32[32,1,128]{2,1,0:T(1,128)S(1)} all-to-all(f32[32,1,128]{2,1,0:T(1,128)S(1)} %get-tuple-element.368), channel_id=1, replica_groups=mesh['sx'=8,'sy'=4] {'sx','sy'}, dimensions={0} | all-to-all | bytes 32768 | tf_op jit(solution)/shard_map/all_to_all | solution.py:411
  164.2 1.4 shard_map.108
  (126 shorter events, 37.1 us)
Async XLA Ops:
  19.2 12.7 %collective-permute-start = (f32[64,512]{1,0:T(8,128)S(1)}, f32[64,512]{1,0:T(8,128)S(1)}, u32[]{:S(2)}, u32[]{:S(2)}) collective-permute-start(f32[64,512]{1,0:T(8,128)S(1)} %get-tuple-element.193), channel_id=1, source_target_pairs={{0,1},{1,0},{2,3},{3,2},{4,8},{5,9},{6,10},{7,11},{8,4},{9,5},{10,... | collective-permute-start | bytes 393224 | tf_op jit(solution)/shard_map/ppermute | solution.py:79
  19.4 12.4 %collective-permute-start.1 = (f32[64,512]{1,0:T(8,128)S(1)}, f32[64,512]{1,0:T(8,128)S(1)}, u32[]{:S(2)}, u32[]{:S(2)}) collective-permute-start(f32[64,512]{1,0:T(8,128)S(1)} %get-tuple-element.194), channel_id=1, source_target_pairs={{0,3},{1,2},{2,1},{3,0},{4,7},{5,6},{6,5},{7,4},{8,11},{9,10},{10,... | collective-permute-start | bytes 393224 | tf_op jit(solution)/shard_map/ppermute | solution.py:79
  19.8 12.1 %collective-permute-start.2 = (f32[64,512]{1,0:T(8,128)S(1)}, f32[64,512]{1,0:T(8,128)S(1)}, u32[]{:S(2)}, u32[]{:S(2)}) collective-permute-start(f32[64,512]{1,0:T(8,128)S(1)} %get-tuple-element.195), channel_id=1, source_target_pairs={{0,4},{1,5},{2,6},{3,7},{4,0},{5,1},{6,2},{7,3},{8,12},{9,13},{10,... | collective-permute-start | bytes 393224 | tf_op jit(solution)/shard_map/ppermute | solution.py:79
  21.3 10.5 %collective-permute-start.3 = (f32[64,512]{1,0:T(8,128)S(1)}, f32[64,512]{1,0:T(8,128)S(1)}, u32[]{:S(2)}, u32[]{:S(2)}) collective-permute-start(f32[64,512]{1,0:T(8,128)S(1)} %get-tuple-element.196), channel_id=1, source_target_pairs={{0,1},{1,0},{2,3},{3,2},{4,5},{5,4},{6,7},{7,6},{8,9},{9,8},{10,11... | collective-permute-start | bytes 393224 | tf_op jit(solution)/shard_map/ppermute | solution.py:79
  34.5 4.3 %collective-permute-start.4 = (bf16[64,512]{1,0:T(8,128)(2,1)S(1)}, bf16[64,512]{1,0:T(8,128)(2,1)S(1)}, u32[]{:S(2)}, u32[]{:S(2)}) collective-permute-start(bf16[64,512]{1,0:T(8,128)(2,1)S(1)} %get-tuple-element.206), channel_id=1, source_target_pairs={{0,4},{1,5},{2,6},{3,7},{4,0},{5,1},{6,2},{7,3},{8,12},{9,13},{10,... | collective-permute-start | bytes 196616 | tf_op jit(solution)/shard_map/ppermute | solution.py:79
  40.0 13.9 %collective-permute-start.8 = (f32[80,512]{1,0:T(8,128)S(1)}, f32[80,512]{1,0:T(8,128)S(1)}, u32[]{:S(2)}, u32[]{:S(2)}) collective-permute-start(f32[80,512]{1,0:T(8,128)S(1)} %get-tuple-element.216), channel_id=1, source_target_pairs={{0,1},{1,0},{2,3},{3,2},{4,5},{5,4},{6,7},{7,6},{8,9},{9,8},{10,11... | collective-permute-start | bytes 491528 | tf_op jit(solution)/shard_map/ppermute | solution.py:79
  40.1 13.8 %collective-permute-start.9 = (f32[80,512]{1,0:T(8,128)S(1)}, f32[80,512]{1,0:T(8,128)S(1)}, u32[]{:S(2)}, u32[]{:S(2)}) collective-permute-start(f32[80,512]{1,0:T(8,128)S(1)} %get-tuple-element.217), channel_id=1, source_target_pairs={{0,4},{1,5},{2,6},{3,7},{4,0},{5,1},{6,2},{7,3},{8,12},{9,13},{10,... | collective-permute-start | bytes 491528 | tf_op jit(solution)/shard_map/ppermute | solution.py:79
  42.1 11.8 %collective-permute-start.10 = (f32[80,512]{1,0:T(8,128)S(1)}, f32[80,512]{1,0:T(8,128)S(1)}, u32[]{:S(2)}, u32[]{:S(2)}) collective-permute-start(f32[80,512]{1,0:T(8,128)S(1)} %get-tuple-element.218), channel_id=1, source_target_pairs={{0,1},{1,0},{2,3},{3,2},{4,8},{5,9},{6,10},{7,11},{8,4},{9,5},{10,... | collective-permute-start | bytes 491528 | tf_op jit(solution)/shard_map/ppermute | solution.py:79
  42.2 11.7 %collective-permute-start.11 = (f32[80,512]{1,0:T(8,128)S(1)}, f32[80,512]{1,0:T(8,128)S(1)}, u32[]{:S(2)}, u32[]{:S(2)}) collective-permute-start(f32[80,512]{1,0:T(8,128)S(1)} %get-tuple-element.219), channel_id=1, source_target_pairs={{0,3},{1,2},{2,1},{3,0},{4,7},{5,6},{6,5},{7,4},{8,11},{9,10},{10,... | collective-permute-start | bytes 491528 | tf_op jit(solution)/shard_map/ppermute | solution.py:79
  56.5 4.3 %collective-permute-start.12 = (bf16[64,512]{1,0:T(8,128)(2,1)S(1)}, bf16[64,512]{1,0:T(8,128)(2,1)S(1)}, u32[]{:S(2)}, u32[]{:S(2)}) collective-permute-start(bf16[64,512]{1,0:T(8,128)(2,1)S(1)} %get-tuple-element.228), channel_id=1, source_target_pairs={{0,4},{1,5},{2,6},{3,7},{4,0},{5,1},{6,2},{7,3},{8,12},{9,13},{10,... | collective-permute-start | bytes 196616 | tf_op jit(solution)/shard_map/ppermute | solution.py:79
  62.0 14.0 %collective-permute-start.16 = (f32[80,512]{1,0:T(8,128)S(1)}, f32[80,512]{1,0:T(8,128)S(1)}, u32[]{:S(2)}, u32[]{:S(2)}) collective-permute-start(f32[80,512]{1,0:T(8,128)S(1)} %get-tuple-element.240), channel_id=1, source_target_pairs={{0,1},{1,0},{2,3},{3,2},{4,5},{5,4},{6,7},{7,6},{8,9},{9,8},{10,11... | collective-permute-start | bytes 491528 | tf_op jit(solution)/shard_map/ppermute | solution.py:79
  62.1 13.9 %collective-permute-start.17 = (f32[80,512]{1,0:T(8,128)S(1)}, f32[80,512]{1,0:T(8,128)S(1)}, u32[]{:S(2)}, u32[]{:S(2)}) collective-permute-start(f32[80,512]{1,0:T(8,128)S(1)} %get-tuple-element.241), channel_id=1, source_target_pairs={{0,4},{1,5},{2,6},{3,7},{4,0},{5,1},{6,2},{7,3},{8,12},{9,13},{10,... | collective-permute-start | bytes 491528 | tf_op jit(solution)/shard_map/ppermute | solution.py:79
  64.2 11.8 %collective-permute-start.18 = (f32[80,512]{1,0:T(8,128)S(1)}, f32[80,512]{1,0:T(8,128)S(1)}, u32[]{:S(2)}, u32[]{:S(2)}) collective-permute-start(f32[80,512]{1,0:T(8,128)S(1)} %get-tuple-element.242), channel_id=1, source_target_pairs={{0,1},{1,0},{2,3},{3,2},{4,8},{5,9},{6,10},{7,11},{8,4},{9,5},{10,... | collective-permute-start | bytes 491528 | tf_op jit(solution)/shard_map/ppermute | solution.py:79
  64.3 11.6 %collective-permute-start.19 = (f32[80,512]{1,0:T(8,128)S(1)}, f32[80,512]{1,0:T(8,128)S(1)}, u32[]{:S(2)}, u32[]{:S(2)}) collective-permute-start(f32[80,512]{1,0:T(8,128)S(1)} %get-tuple-element.243), channel_id=1, source_target_pairs={{0,3},{1,2},{2,1},{3,0},{4,7},{5,6},{6,5},{7,4},{8,11},{9,10},{10,... | collective-permute-start | bytes 491528 | tf_op jit(solution)/shard_map/ppermute | solution.py:79
  78.6 4.3 %collective-permute-start.20 = (bf16[64,512]{1,0:T(8,128)(2,1)S(1)}, bf16[64,512]{1,0:T(8,128)(2,1)S(1)}, u32[]{:S(2)}, u32[]{:S(2)}) collective-permute-start(bf16[64,512]{1,0:T(8,128)(2,1)S(1)} %get-tuple-element.256), channel_id=1, source_target_pairs={{0,4},{1,5},{2,6},{3,7},{4,0},{5,1},{6,2},{7,3},{8,12},{9,13},{10,... | collective-permute-start | bytes 196616 | tf_op jit(solution)/shard_map/ppermute | solution.py:79
  84.1 14.0 %collective-permute-start.24 = (f32[80,512]{1,0:T(8,128)S(1)}, f32[80,512]{1,0:T(8,128)S(1)}, u32[]{:S(2)}, u32[]{:S(2)}) collective-permute-start(f32[80,512]{1,0:T(8,128)S(1)} %get-tuple-element.271), channel_id=1, source_target_pairs={{0,1},{1,0},{2,3},{3,2},{4,5},{5,4},{6,7},{7,6},{8,9},{9,8},{10,11... | collective-permute-start | bytes 491528 | tf_op jit(solution)/shard_map/ppermute | solution.py:79
  84.2 13.9 %collective-permute-start.25 = (f32[80,512]{1,0:T(8,128)S(1)}, f32[80,512]{1,0:T(8,128)S(1)}, u32[]{:S(2)}, u32[]{:S(2)}) collective-permute-start(f32[80,512]{1,0:T(8,128)S(1)} %get-tuple-element.272), channel_id=1, source_target_pairs={{0,4},{1,5},{2,6},{3,7},{4,0},{5,1},{6,2},{7,3},{8,12},{9,13},{10,... | collective-permute-start | bytes 491528 | tf_op jit(solution)/shard_map/ppermute | solution.py:79
  86.3 11.8 %collective-permute-start.26 = (f32[80,512]{1,0:T(8,128)S(1)}, f32[80,512]{1,0:T(8,128)S(1)}, u32[]{:S(2)}, u32[]{:S(2)}) collective-permute-start(f32[80,512]{1,0:T(8,128)S(1)} %get-tuple-element.273), channel_id=1, source_target_pairs={{0,1},{1,0},{2,3},{3,2},{4,8},{5,9},{6,10},{7,11},{8,4},{9,5},{10,... | collective-permute-start | bytes 491528 | tf_op jit(solution)/shard_map/ppermute | solution.py:79
  86.4 11.6 %collective-permute-start.27 = (f32[80,512]{1,0:T(8,128)S(1)}, f32[80,512]{1,0:T(8,128)S(1)}, u32[]{:S(2)}, u32[]{:S(2)}) collective-permute-start(f32[80,512]{1,0:T(8,128)S(1)} %get-tuple-element.274), channel_id=1, source_target_pairs={{0,3},{1,2},{2,1},{3,0},{4,7},{5,6},{6,5},{7,4},{8,11},{9,10},{10,... | collective-permute-start | bytes 491528 | tf_op jit(solution)/shard_map/ppermute | solution.py:79
  100.7 4.3 %collective-permute-start.28 = (bf16[64,512]{1,0:T(8,128)(2,1)S(1)}, bf16[64,512]{1,0:T(8,128)(2,1)S(1)}, u32[]{:S(2)}, u32[]{:S(2)}) collective-permute-start(bf16[64,512]{1,0:T(8,128)(2,1)S(1)} %get-tuple-element.287), channel_id=1, source_target_pairs={{0,4},{1,5},{2,6},{3,7},{4,0},{5,1},{6,2},{7,3},{8,12},{9,13},{10,... | collective-permute-start | bytes 196616 | tf_op jit(solution)/shard_map/ppermute | solution.py:79
  106.2 14.0 %collective-permute-start.32 = (f32[80,512]{1,0:T(8,128)S(1)}, f32[80,512]{1,0:T(8,128)S(1)}, u32[]{:S(2)}, u32[]{:S(2)}) collective-permute-start(f32[80,512]{1,0:T(8,128)S(1)} %get-tuple-element.302), channel_id=1, source_target_pairs={{0,1},{1,0},{2,3},{3,2},{4,5},{5,4},{6,7},{7,6},{8,9},{9,8},{10,11... | collective-permute-start | bytes 491528 | tf_op jit(solution)/shard_map/ppermute | solution.py:79
  106.3 13.9 %collective-permute-start.33 = (f32[80,512]{1,0:T(8,128)S(1)}, f32[80,512]{1,0:T(8,128)S(1)}, u32[]{:S(2)}, u32[]{:S(2)}) collective-permute-start(f32[80,512]{1,0:T(8,128)S(1)} %get-tuple-element.303), channel_id=1, source_target_pairs={{0,4},{1,5},{2,6},{3,7},{4,0},{5,1},{6,2},{7,3},{8,12},{9,13},{10,... | collective-permute-start | bytes 491528 | tf_op jit(solution)/shard_map/ppermute | solution.py:79
  108.4 11.8 %collective-permute-start.34 = (f32[80,512]{1,0:T(8,128)S(1)}, f32[80,512]{1,0:T(8,128)S(1)}, u32[]{:S(2)}, u32[]{:S(2)}) collective-permute-start(f32[80,512]{1,0:T(8,128)S(1)} %get-tuple-element.304), channel_id=1, source_target_pairs={{0,1},{1,0},{2,3},{3,2},{4,8},{5,9},{6,10},{7,11},{8,4},{9,5},{10,... | collective-permute-start | bytes 491528 | tf_op jit(solution)/shard_map/ppermute | solution.py:79
  108.5 11.6 %collective-permute-start.35 = (f32[80,512]{1,0:T(8,128)S(1)}, f32[80,512]{1,0:T(8,128)S(1)}, u32[]{:S(2)}, u32[]{:S(2)}) collective-permute-start(f32[80,512]{1,0:T(8,128)S(1)} %get-tuple-element.305), channel_id=1, source_target_pairs={{0,3},{1,2},{2,1},{3,0},{4,7},{5,6},{6,5},{7,4},{8,11},{9,10},{10,... | collective-permute-start | bytes 491528 | tf_op jit(solution)/shard_map/ppermute | solution.py:79
  128.3 14.0 %collective-permute-start.40 = (f32[80,512]{1,0:T(8,128)S(1)}, f32[80,512]{1,0:T(8,128)S(1)}, u32[]{:S(2)}, u32[]{:S(2)}) collective-permute-start(f32[80,512]{1,0:T(8,128)S(1)} %get-tuple-element.333), channel_id=1, source_target_pairs={{0,1},{1,0},{2,3},{3,2},{4,5},{5,4},{6,7},{7,6},{8,9},{9,8},{10,11... | collective-permute-start | bytes 491528 | tf_op jit(solution)/shard_map/ppermute | solution.py:79
  128.3 13.9 %collective-permute-start.41 = (f32[80,512]{1,0:T(8,128)S(1)}, f32[80,512]{1,0:T(8,128)S(1)}, u32[]{:S(2)}, u32[]{:S(2)}) collective-permute-start(f32[80,512]{1,0:T(8,128)S(1)} %get-tuple-element.334), channel_id=1, source_target_pairs={{0,4},{1,5},{2,6},{3,7},{4,0},{5,1},{6,2},{7,3},{8,12},{9,13},{10,... | collective-permute-start | bytes 491528 | tf_op jit(solution)/shard_map/ppermute | solution.py:79
  130.4 11.8 %collective-permute-start.42 = (f32[80,512]{1,0:T(8,128)S(1)}, f32[80,512]{1,0:T(8,128)S(1)}, u32[]{:S(2)}, u32[]{:S(2)}) collective-permute-start(f32[80,512]{1,0:T(8,128)S(1)} %get-tuple-element.335), channel_id=1, source_target_pairs={{0,1},{1,0},{2,3},{3,2},{4,8},{5,9},{6,10},{7,11},{8,4},{9,5},{10,... | collective-permute-start | bytes 491528 | tf_op jit(solution)/shard_map/ppermute | solution.py:79
  130.6 11.7 %collective-permute-start.43 = (f32[80,512]{1,0:T(8,128)S(1)}, f32[80,512]{1,0:T(8,128)S(1)}, u32[]{:S(2)}, u32[]{:S(2)}) collective-permute-start(f32[80,512]{1,0:T(8,128)S(1)} %get-tuple-element.336), channel_id=1, source_target_pairs={{0,3},{1,2},{2,1},{3,0},{4,7},{5,6},{6,5},{7,4},{8,11},{9,10},{10,... | collective-permute-start | bytes 491528 | tf_op jit(solution)/shard_map/ppermute | solution.py:79
  150.6 13.5 %collective-permute-start.48 = (f32[64,512]{1,0:T(8,128)S(1)}, f32[64,512]{1,0:T(8,128)S(1)}, u32[]{:S(2)}, u32[]{:S(2)}) collective-permute-start(f32[64,512]{1,0:T(8,128)S(1)} %get-tuple-element.364), channel_id=1, source_target_pairs={{0,1},{1,0},{2,3},{3,2},{4,5},{5,4},{6,7},{7,6},{8,9},{9,8},{10,11... | collective-permute-start | bytes 393224 | tf_op jit(solution)/shard_map/ppermute | solution.py:79
  150.7 13.4 %collective-permute-start.49 = (f32[64,512]{1,0:T(8,128)S(1)}, f32[64,512]{1,0:T(8,128)S(1)}, u32[]{:S(2)}, u32[]{:S(2)}) collective-permute-start(f32[64,512]{1,0:T(8,128)S(1)} %get-tuple-element.365), channel_id=1, source_target_pairs={{0,4},{1,5},{2,6},{3,7},{4,0},{5,1},{6,2},{7,3},{8,12},{9,13},{10,... | collective-permute-start | bytes 393224 | tf_op jit(solution)/shard_map/ppermute | solution.py:79
  152.8 11.3 %collective-permute-start.50 = (f32[64,512]{1,0:T(8,128)S(1)}, f32[64,512]{1,0:T(8,128)S(1)}, u32[]{:S(2)}, u32[]{:S(2)}) collective-permute-start(f32[64,512]{1,0:T(8,128)S(1)} %get-tuple-element.366), channel_id=1, source_target_pairs={{0,1},{1,0},{2,3},{3,2},{4,8},{5,9},{6,10},{7,11},{8,4},{9,5},{10,... | collective-permute-start | bytes 393224 | tf_op jit(solution)/shard_map/ppermute | solution.py:79
  153.0 11.2 %collective-permute-start.51 = (f32[64,512]{1,0:T(8,128)S(1)}, f32[64,512]{1,0:T(8,128)S(1)}, u32[]{:S(2)}, u32[]{:S(2)}) collective-permute-start(f32[64,512]{1,0:T(8,128)S(1)} %get-tuple-element.367), channel_id=1, source_target_pairs={{0,3},{1,2},{2,1},{3,0},{4,7},{5,6},{6,5},{7,4},{8,11},{9,10},{10,... | collective-permute-start | bytes 393224 | tf_op jit(solution)/shard_map/ppermute | solution.py:79
  (26 other events, 171.0 us)
